TPU v7x, 512 devices: a whole 4x8x8 slice. The times are simulated.
512 devices in a mesh: sec: 64 (over x, y, core), term: 8 (over z).
Axes of the slice: x: 4, y: 8, z: 8, core: 2. Of those that a mesh axis runs over, the one named last changes fastest.
Arguments:
- wavefunction: bfloat16 [64, 64, 128, 128], P('sec'), may hold values from -6 to 6
- left_env: bfloat16 [8, 5, 64, 128, 128], P('term', None, 'sec'), may hold values from -0.5 to 0.5
- right_env: bfloat16 [8, 64, 128, 128], P('term', 'sec'), may hold values from -0.5 to 0.5
- coupling: float32 [8, 5, 64, 64], P('term'), may hold values from -1 to 1
- left_shift: int32 [8, 5], P('term'), may hold values from -1 to 1
- allowed: int32 [64, 64], replicated, may hold values 0 or 1
Outputs:
- applied: bfloat16 [64, 64, 128, 128], P('term', 'sec')
All inputs are finite; a program needn't handle non-finite values.
Results may differ from a plain program's by a relative error of at most 0.0049.
Values may be sent and summed in bfloat16 or wider, within the bound.
No kernel may reach another device: no remote copies, remote signals or barrier semaphores. Data moves between devices by JAX's collectives and lax.ppermute only.
A program may use at most 128 MiB of HBM per device.

v0:
```python
import jax
import jax.numpy as jnp
from jax import lax
from jax.sharding import PartitionSpec as P


def on_device(wavefunction, left_env, right_env, coupling, left_shift, allowed):
    position = lax.axis_index("sec")
    sec_dev = wavefunction.shape[0]
    offset = position * sec_dev
    terms_here = left_env.shape[0]
    bond_count = left_env.shape[1]
    width = wavefunction.shape[2]
    rows_mask = lax.dynamic_slice_in_dim(allowed, offset, sec_dev, 0)
    masked_psi = wavefunction * rows_mask[:, :, None, None].astype(jnp.bfloat16)
    cols_mask = lax.dynamic_slice_in_dim(allowed, offset, sec_dev, 1).astype(jnp.float32)
    relaid = lax.all_to_all(masked_psi, "sec", split_axis=1, concat_axis=0, tiled=True)
    padded_col = jnp.pad(relaid, ((1, 1), (0, 0), (0, 0), (0, 0)))
    col_factor = lax.dynamic_slice_in_dim(coupling, offset, sec_dev, 3)
    segment = lax.all_gather(left_env, "sec", axis=2, tiled=True)
    begin_at = jnp.int32(0)
    amount = segment.shape[2]
    running = jnp.zeros((terms_here, amount, sec_dev, width, width), jnp.float32)
    for bond_index in range(bond_count):

        def pick_rows(moved_by):
            return lax.dynamic_slice_in_dim(padded_col, begin_at + 1 + moved_by, amount, 0)

        sources = jax.vmap(pick_rows)(left_shift[:, bond_index])
        product = jnp.einsum(
            "waik,wabkj->wabij", segment[:, bond_index], sources, preferred_element_type=jnp.float32
        )
        running = running + product * col_factor[:, bond_index, :, :, None, None]
    partial_value = running.astype(jnp.bfloat16)
    total_z = jnp.einsum(
        "wabij,wblj->abil", partial_value, right_env, preferred_element_type=jnp.float32
    )
    total_z = total_z * cols_mask[:, :, None, None]
    summed = lax.psum(total_z, "term")
    portion = summed.shape[0] // lax.axis_size("term")
    result = lax.dynamic_slice_in_dim(summed, lax.axis_index("term") * portion, portion, 0)
    return result.astype(jnp.bfloat16)


def solution(mesh):
    in_specs = (
        P("sec", None, None, None),
        P("term", None, "sec", None, None),
        P("term", "sec", None, None),
        P("term", None, None, None),
        P("term", None),
        P(),
    )
    out_specs = P("term", "sec", None, None)
    return jax.shard_map(
        on_device, mesh=mesh, in_specs=in_specs, out_specs=out_specs, check_vma=False
    )
```

profile of v0, /device:TPU:1, one launch (start us, length us, event | category | flops | bytes accessed | tf_op | source)
XLA Modules:
  0.0 242.2 jit_solution(2839699800486116718)
XLA Ops:
  6.5 0.0 copy-start
  6.5 0.0 all-gather.2.cloned.1.call-start
  6.5 0.7 all-gather.2.cloned.1.call-update
  7.3 0.7 fusion.40
  8.0 0.0 copy-start.3
  8.0 0.0 copy-start.2
  8.0 0.0 copy-start.1
  8.0 3.1 %bitcast_multiply_fusion.6 = bf16[1,64,128,128]{3,2,0,1:T(8,128)(2,1)} fusion(bf16[1,64,128,128]{3,2,1,0:T(8,128)(2,1)} %param.6, bf16[64]{0:T(256)(128)(2,1)S(1)} %fusion.40), kind=kLoop, calls=%fused_computation.27 | loop fusion | flops 1048576 | bytes 4194432 | tf_op jit(solution)/shard_map/mul | solution.py:15
  11.1 11.6 %all-to-all-start = ((bf16[1,64,128,128]{3,2,0,1:T(8,128)(2,1)}), bf16[1,64,128,128]{3,2,0,1:T(8,128)(2,1)S(1)}, u32[]{:S(2)}, u32[]{:S(2)}) async-start(bf16[1,64,128,128]{3,2,0,1:T(8,128)(2,1)} %bitcast_multiply_fusion.6), calls=%async_computation | async-start | bytes 4194304 | tf_op jit(solution)/shard_map/all_to_all | solution.py:17
  22.7 0.0 copy-done.3
  22.7 0.7 fusion.47
  29.9 0.0 copy-done.2
  29.9 0.2 convert_reduce_fusion
  30.1 0.0 copy-done.1
  30.1 0.3 dynamic-slice_reduce_fusion.4
  30.3 49.8 %all-to-all-done = bf16[1,64,128,128]{3,2,0,1:T(8,128)(2,1)S(1)} async-done(((bf16[1,64,128,128]{3,2,0,1:T(8,128)(2,1)}), bf16[1,64,128,128]{3,2,0,1:T(8,128)(2,1)S(1)}, u32[]{:S(2)}, u32[]{:S(2)}) %all-to-all-start) | async-done | bytes 2097184 | tf_op jit(solution)/shard_map/all_to_all | solution.py:17
  80.1 33.9 %all-gather.2.cloned.1.call-done = bf16[1,5,64,128,128]{4,3,2,1,0:T(8,128)(2,1)} async-done(((bf16[1,5,1,128,128]{4,3,2,1,0:T(8,128)(2,1)}), bf16[1,5,64,128,128]{4,3,2,1,0:T(8,128)(2,1)}) %all-gather.2.cloned.1.call-update) | async-done | bytes 10485776 | tf_op jit(solution)/shard_map/all_gather | solution.py:20
  114.0 5.2 %fusion.8 = f32[64,128,128]{2,1,0:T(8,128)} fusion(bf16[1,5,64,128,128]{4,3,2,1,0:T(8,128)(2,1)} %all-gather.2.cloned.1.call-done, s32[]{:T(128)} %bitcast.11, bf16[64,1,128,128]{3,2,0,1:T(8,128)(2,1)S(1)} %bitcast.131), kind=kOutput, calls=%fused_computation.18 | convolution fusion | flops 268435456 | bytes 8389120 | tf_op jit(solution)/shard_map/waik,wabkj->wabij/dot_general | solution.py:30
  119.2 5.1 %fusion.7 = f32[64,128,128]{2,1,0:T(8,128)} fusion(bf16[1,5,64,128,128]{4,3,2,1,0:T(8,128)(2,1)} %all-gather.2.cloned.1.call-done, s32[]{:T(128)} %bitcast.17, bf16[64,1,128,128]{3,2,0,1:T(8,128)(2,1)S(1)} %bitcast.132), kind=kOutput, calls=%fused_computation.16 | convolution fusion | flops 268435456 | bytes 8389120 | tf_op jit(solution)/shard_map/waik,wabkj->wabij/dot_general | solution.py:30
  124.4 5.2 %fusion.6 = f32[64,128,128]{2,1,0:T(8,128)} fusion(bf16[1,5,64,128,128]{4,3,2,1,0:T(8,128)(2,1)} %all-gather.2.cloned.1.call-done, s32[]{:T(128)} %bitcast.23, bf16[64,1,128,128]{3,2,0,1:T(8,128)(2,1)S(1)} %bitcast.133), kind=kOutput, calls=%fused_computation.14 | convolution fusion | flops 268435456 | bytes 8389120 | tf_op jit(solution)/shard_map/waik,wabkj->wabij/dot_general | solution.py:30
  129.6 5.2 %fusion.9 = f32[64,128,128]{2,1,0:T(8,128)} fusion(bf16[1,5,64,128,128]{4,3,2,1,0:T(8,128)(2,1)} %all-gather.2.cloned.1.call-done, s32[]{:T(128)} %bitcast.5, bf16[64,1,128,128]{3,2,0,1:T(8,128)(2,1)S(1)} %bitcast.134), kind=kOutput, calls=%fused_computation.20 | convolution fusion | flops 268435456 | bytes 8389120 | tf_op jit(solution)/shard_map/waik,wabkj->wabij/dot_general | solution.py:30
  134.8 0.0 copy-done
  134.8 9.7 %fusion = f32[64,1,128,128]{3,2,0,1:T(8,128)} fusion(f32[64]{0:T(128)S(1)} %convert_reduce_fusion, f32[64,128,128]{2,1,0:T(8,128)} %fusion.6, f32[64,128,128]{2,1,0:T(8,128)} %fusion.7, f32[64,128,128]{2,1,0:T(8,128)} %fusion.8, f32[64,128,128]{2,1,0:T(8,128)} %fusion.9, bf16[1,5,64,128,128]{4,3,2,1,0:T(8,128)(2,1)} %all-gather.2.cloned.1.call-done, ...), kind=kOutput, calls=%fused_computation.1 | convolution fusion | flops 548405248 | bytes 25200640 | tf_op jit(solution)/shard_map/wabij,wblj->abil/dot_general | solution.py:35
  144.5 90.1 %all-reduce.2 = bf16[64,1,128,128]{3,2,0,1:T(8,128)(2,1)S(1)} all-reduce(f32[64,1,128,128]{3,2,0,1:T(8,128)} %fusion), channel_id=1, replica_groups=mesh['sec'=64,'term'=8] {'term'}, use_global_device_ids=true, to_apply=%region_0.1 | all-reduce | flops 1048576 | bytes 6291456 | tf_op jit(solution)/shard_map/psum | solution.py:39
  234.7 0.7 fusion.31
Async XLA Ops:
  6.5 128.2 %copy-start = (bf16[1,1,128,128]{3,2,1,0:T(8,128)(2,1)S(1)}, bf16[1,1,128,128]{3,2,1,0:T(8,128)(2,1)}, u32[]{:S(2)}) copy-start(bf16[1,1,128,128]{3,2,1,0:T(8,128)(2,1)} %param.8) | copy-start | bytes 98308
  6.5 107.4 %all-gather.2.cloned.1.call-start = ((), (), s32[]{:S(2)}) async-start(), calls=%async_computation.1 | async-start | bytes 10649600 | tf_op jit(solution)/shard_map/all_gather | solution.py:20
  8.0 14.8 %copy-start.3 = (s32[1,5]{1,0:T(1,128)S(1)}, s32[1,5]{1,0:T(1,128)}, u32[]{:S(2)}) copy-start(s32[1,5]{1,0:T(1,128)} %param.10) | copy-start | bytes 64
  8.0 21.9 %copy-start.2 = (s32[64,64]{1,0:T(8,128)S(1)}, s32[64,64]{1,0:T(8,128)}, u32[]{:S(2)}) copy-start(s32[64,64]{1,0:T(8,128)} %param.11) | copy-start | bytes 49156
  8.0 22.1 %copy-start.1 = (f32[1,5,64,64]{3,2,1,0:T(8,128)S(1)}, f32[1,5,64,64]{3,2,1,0:T(8,128)}, u32[]{:S(2)}) copy-start(f32[1,5,64,64]{3,2,1,0:T(8,128)} %param.9) | copy-start | bytes 245764
  11.1 69.0 %all-to-all-start = ((bf16[1,64,128,128]{3,2,0,1:T(8,128)(2,1)}), bf16[1,64,128,128]{3,2,0,1:T(8,128)(2,1)S(1)}, u32[]{:S(2)}, u32[]{:S(2)}) async-start(bf16[1,64,128,128]{3,2,0,1:T(8,128)(2,1)} %bitcast_multiply_fusion.6), calls=%async_computation | async-start | bytes 4194304 | tf_op jit(solution)/shard_map/all_to_all | solution.py:17
Sparse Core Ops, SparseCore 0:
  10.7 103.1 all-gather.1
where the time goes:
time: 243 us; the launch traced here: 242 us
  blocking collectives  90.1 us (37%)
  waiting for transfers between devices  84.3 us (35%)
  matrix products  30.5 us (13%)
  between operations  19.9 us (8%)
  starting transfers between devices  11.6 us (5%)
  other arithmetic  4.02 us (2%)
    psum x1, blocking collectives, on_device(): summed = lax.psum(total_z, 'term')  90.1 us
    all_to_all x1, waiting for transfers between devices, on_device(): lax.all_to_all(masked_psi, 'sec', split_axis=1, concat_axis=0, tiled=True)  49.8 us
    all_gather x1, waiting for transfers between devices, on_device(): segment = lax.all_gather(left_env, 'sec', axis=2, tiled=True)  33.9 us
    dot_general x4, matrix products, on_device(): jnp.einsum('waik,wabkj->wabij', segment[:, bond_index], sources, preferre...  20.8 us
    all_to_all x1, starting transfers between devices, on_device(): lax.all_to_all(masked_psi, 'sec', split_axis=1, concat_axis=0, tiled=True)  11.6 us
    dot_general x1, matrix products, on_device(): jnp.einsum('wabij,wblj->abil', partial_value, right_env, preferred_elemen...  9.74 us
  transfers between devices with their start and end apart: 2, of which 2 were waited for; matrix products, arithmetic and copies ran while one was open for 2% of the time, Pallas kernels for 0%

commit v1 on v0

v1 whole, which is shorter than its diff:
```python
import functools

import jax
import jax.numpy as jnp
from jax import lax
from jax.experimental import pallas as pl
from jax.experimental.pallas import tpu as pltpu
from jax.sharding import PartitionSpec as P

M = 128
LB = 5
NW = 8
G = 8
BOTH = ("sec", "term")
OFFSETS = (0, -1, 1, -2, 2, -3, 3, -4)
ROWS = LB * M
F32 = jnp.float32
BF16 = jnp.bfloat16
VMEM = pl.BlockSpec(memory_space=pltpu.VMEM)
SMEM = pl.BlockSpec(memory_space=pltpu.SMEM)
PARAMS = pltpu.CompilerParams(vmem_limit_bytes=24 * 1024 * 1024)


def together(*arrays):
    return lax.optimization_barrier(arrays)


def slot_bond(t, k):
    return lax.rem(t + OFFSETS[k] + NW, NW)


def left_products(factor_ref, shift_ref, *refs):
    envs, psi_ref, out_ref = refs[:NW], refs[NW], refs[NW + 1]
    for k in range(NW):
        rows = [shift_ref[k, c] + 1 for c in range(LB)]

        @pl.loop(0, G)
        def _(j):
            total = None
            for c in range(LB):
                product = jnp.dot(
                    envs[k][c * M : (c + 1) * M, :], psi_ref[rows[c], j], preferred_element_type=F32
                )
                product = product * factor_ref[k * LB + c, j]
                total = product if total is None else total + product
            out_ref[k, j] = total.astype(BF16)


def right_sum(t, j, i, partial_ref, right_ref, keep_ref):
    total = None
    for k in range(NW):
        product = lax.dot_general(
            partial_ref[k, j],
            right_ref[slot_bond(t, k) * (G // 2) + i],
            (((1,), (1,)), ((), ())),
            preferred_element_type=F32,
        )
        total = product if total is None else total + product
    return (total * keep_ref[0, j]).astype(BF16)


def right_own(where_ref, keep_ref, partial_ref, right_ref, out_ref):
    t, core = where_ref[0], where_ref[1]

    @pl.loop(0, G // 2)
    def _(i):
        out_ref[i] = right_sum(t, 2 * i + core, i, partial_ref, right_ref, keep_ref)


def right_other(where_ref, keep_ref, partial_ref, right_ref, own_ref, out_ref):
    t, core = where_ref[0], where_ref[1]

    @pl.loop(0, G // 2)
    def _(i):
        j = 2 * i + 1 - core
        value = right_sum(t, j, i, partial_ref, right_ref, keep_ref)
        out_ref[j] = value
        out_ref[G + j] = value
        mine = own_ref[i]
        out_ref[2 * i + core] = mine
        out_ref[G + 2 * i + core] = mine


def bf16_pieces(x):
    pieces = []
    for _ in range(3):
        piece = lax.reduce_precision(x, 8, 7)
        pieces.append(piece)
        x = x - piece
    return pieces


def on_device(wavefunction, left_env, right_env, coupling, left_shift, allowed, *, n_sec, n_term):
    s, t = lax.axis_index("sec"), lax.axis_index("term")
    groups = n_sec // G

    def device(sec, term):
        return sec * n_term + term

    spread = [(device(b, w), device(w * G + b % G, b // G)) for b in range(n_sec) for w in range(n_term)]
    by_core = [[2 * chip + core for chip in range(n_sec // 2)] for core in range(2)]
    up = [(i, (i + 1) % n_term) for i in range(n_term)]
    down = [(i, (i - 1) % n_term) for i in range(n_term)]
    exchange = [
        [device(A * G + i, B) for i in range(G)] + [device(B * G + i, A) for i in range(G)]
        for A in range(groups)
        for B in range(A + 1, groups)
    ] + [
        [device(A * G + i, A) for i in range(G)] + [device((A + 1) * G + i, A + 1) for i in range(G)]
        for A in range(0, groups, 2)
    ]

    right = lax.ppermute(right_env[0], BOTH, spread)

    row = lax.dynamic_slice_in_dim(coupling[0], s, 1, 1)[:, 0, :]
    table = jnp.concatenate(bf16_pieces(row) + [jnp.pad(left_shift.astype(F32), ((0, 0), (0, n_sec - LB)))])
    table = jnp.pad(table, ((0, 0), (0, M - n_sec))).astype(BF16)
    payload = jnp.concatenate([left_env[0, :, 0].reshape(ROWS, M), table])
    own_psi = lax.dynamic_slice_in_dim(wavefunction[0], t * G, G, 0)

    u1 = lax.ppermute(payload, "term", up)
    d1 = lax.ppermute(payload, "term", down)
    right, u1, d1 = together(right, u1, d1)
    halves = lax.all_to_all(
        jnp.tile(right, (n_sec // 2, 1, 1)), "sec", 0, 0, axis_index_groups=by_core, tiled=True
    )
    u2 = lax.ppermute(u1, "term", up)
    d2 = lax.ppermute(d1, "term", down)
    below = lax.ppermute(own_psi, "sec", [(i, i + 1) for i in range(n_sec - 1)])
    above = lax.ppermute(own_psi, "sec", [(i + 1, i) for i in range(n_sec - 1)])
    u2, d2 = together(u2, d2)
    u3 = lax.ppermute(u2, "term", up)
    d3 = lax.ppermute(d2, "term", down)
    u3, d3 = together(u3, d3)
    u4 = lax.ppermute(u3, "term", up)
    slots = [payload, u1, d1, u2, d2, u3, d3, u4]
    psi = jnp.stack([below, own_psi, above])

    tables = jnp.stack([x[ROWS:] for x in slots]).astype(F32)
    couplings = tables[:, :LB, :n_sec] + tables[:, LB : 2 * LB, :n_sec] + tables[:, 2 * LB : 3 * LB, :n_sec]
    couplings = lax.dynamic_slice_in_dim(couplings, t * G, G, 2)
    shifts = tables[:, 3 * LB, :LB].astype(jnp.int32)
    near = lax.dynamic_slice(jnp.pad(allowed, ((1, 1), (0, 0))), (s, t * G), (3, G)).astype(F32)
    source = shifts[:, :, None, None] + 1 == jnp.arange(3)[:, None]
    factors = couplings * jnp.sum(jnp.where(source, near, 0.0), axis=2)

    partial = pl.pallas_call(
        left_products,
        out_shape=jax.ShapeDtypeStruct((NW, G, M, M), BF16),
        in_specs=[SMEM, SMEM] + [VMEM] * (NW + 1),
        out_specs=VMEM,
        compiler_params=PARAMS,
        cost_estimate=pl.CostEstimate(flops=2 * 320 * M**3, bytes_accessed=5 << 20, transcendentals=0),
    )(factors.reshape(NW * LB, G), shifts, *slots, psi)

    halves, partial = together(halves, partial)
    others = lax.ppermute(halves, "sec", [(i, i ^ 1) for i in range(n_sec)])
    where = jnp.stack([t, lax.rem(s, 2)]).astype(jnp.int32)
    keep = lax.dynamic_slice(allowed, (s, t * G), (1, G)).astype(F32)
    cost = pl.CostEstimate(flops=2 * 32 * M**3, bytes_accessed=2 << 20, transcendentals=0)
    own = pl.pallas_call(
        right_own,
        out_shape=jax.ShapeDtypeStruct((G // 2, M, M), BF16),
        in_specs=[SMEM, SMEM, VMEM, VMEM],
        out_specs=VMEM,
        compiler_params=PARAMS,
        cost_estimate=cost,
    )(where, keep, partial, halves)
    results = pl.pallas_call(
        right_other,
        out_shape=jax.ShapeDtypeStruct((2 * G, M, M), BF16),
        in_specs=[SMEM, SMEM, VMEM, VMEM, VMEM],
        out_specs=VMEM,
        compiler_params=PARAMS,
        cost_estimate=cost,
    )(where, keep, partial, others, own)

    received = lax.all_to_all(results, BOTH, 0, 0, axis_index_groups=exchange, tiled=True)
    A = s // G
    first = jnp.where(A < t, G, jnp.where(A > t, 0, lax.rem(A, 2) * G))
    return lax.dynamic_slice_in_dim(received, first, G, 0)[:, None]


def solution(mesh):
    in_specs = (
        P("sec", None, None, None),
        P("term", None, "sec", None, None),
        P("term", "sec", None, None),
        P("term", None, None, None),
        P("term", None),
        P(),
    )
    body = functools.partial(on_device, n_sec=mesh.shape["sec"], n_term=mesh.shape["term"])
    return jax.shard_map(
        body, mesh=mesh, in_specs=in_specs, out_specs=P("term", "sec", None, None), check_vma=False
    )
```

time: 243 us -> 139 us (0.57)
  the two profiles are of different devices: /device:TPU:1 before, /device:TPU:256 now
where the time goes in v1:
time: 139 us; the launch traced here: 138 us
  starting transfers between devices  64.1 us (46%)
  waiting for transfers between devices  33.9 us (24%)
  Pallas kernels  18.8 us (14%)
  local copies, waits for them, and re-layouts  15.2 us (11%)
  other arithmetic  5.67 us (4%)
    all_to_all x1, waiting for transfers between devices, on_device(): lax.all_to_all(results, BOTH, 0, 0, axis_index_groups=exchange, tiled=True)  26.1 us
    pallas_call x1, Pallas kernels, on_device(): pl.pallas_call(left_products, out_shape=jax.ShapeDtypeStruct((NW, G, M, M...  13.7 us
    all_to_all x1, starting transfers between devices, on_device(): lax.all_to_all(results, BOTH, 0, 0, axis_index_groups=exchange, tiled=True)  13.3 us
    unnamed x27, local copies, waits for them, and re-layouts  10.9 us
    ppermute x1, starting transfers between devices, on_device(): right = lax.ppermute(right_env[0], BOTH, spread)  9.75 us
    all_to_all x1, starting transfers between devices, on_device(): lax.all_to_all(jnp.tile(right, (n_sec // 2, 1, 1)), 'sec', 0, 0, axis_ind...  8.74 us
    ppermute x1, starting transfers between devices, on_device(): u2 = lax.ppermute(u1, 'term', up)  6.49 us
    ppermute x1, starting transfers between devices, on_device(): d3 = lax.ppermute(d2, 'term', down)  4.65 us
  transfers between devices with their start and end apart: 13, of which 5 were waited for; matrix products, arithmetic and copies ran while one was open for 6% of the time, Pallas kernels for 11%

profile of v1, /device:TPU:256, one launch (start us, length us, event | category | flops | bytes accessed | tf_op | source)
XLA Modules:
  0.0 137.9 jit_solution(733953897186690799)
XLA Ops:
  0.0 0.0 copy-start
  0.0 0.8 convert_convert_fusion
  0.8 0.7 constant_dynamic-slice_fusion.1
  1.6 0.9 pad_maximum_fusion.1.refs_0_
  2.5 1.9 %collective-permute-start.2 = (bf16[656,128]{1,0:T(8,128)(2,1)S(1)}, bf16[656,128]{1,0:T(8,128)(2,1)S(1)}, u32[]{:S(2)}, u32[]{:S(2)}) collective-permute-start(bf16[656,128]{1,0:T(8,128)(2,1)S(1)} %pad_maximum_fusion.1.refs_0_), channel_id=1, source_target_pairs={{0,7},{1,0},{2,1},{3,2},{4,3},{5,4},{6,5},{7,6},{8,15},{9,8},{10,9... | collective-permute-start | bytes 503816 | tf_op jit(solution)/shard_map/ppermute | solution.py:122
  4.4 3.9 %collective-permute-start.1 = (bf16[656,128]{1,0:T(8,128)(2,1)S(1)}, bf16[656,128]{1,0:T(8,128)(2,1)}, u32[]{:S(2)}, u32[]{:S(2)}) collective-permute-start(bf16[656,128]{1,0:T(8,128)(2,1)S(1)} %pad_maximum_fusion.1.refs_0_), channel_id=1, source_target_pairs={{0,1},{1,2},{2,3},{3,4},{4,5},{5,6},{6,7},{7,0},{8,9},{9,10},{10,1... | collective-permute-start | bytes 503816 | tf_op jit(solution)/shard_map/ppermute | solution.py:121
  8.4 0.0 copy-done
  8.4 0.7 fusion.7
  9.1 1.3 collective-permute-start.9
  10.4 3.7 %collective-permute-start.8 = (bf16[8,128,128]{2,1,0:T(8,128)(2,1)}, bf16[8,128,128]{2,1,0:T(8,128)(2,1)}, u32[]{:S(2)}, u32[]{:S(2)}) collective-permute-start(bf16[8,128,128]{2,1,0:T(8,128)(2,1)} %fusion.7), channel_id=1, source_target_pairs={{0,8},{8,16},{16,24},{24,32},{32,40},{40,48},{48,56},{56,64},{64,7... | collective-permute-start | bytes 786440 | tf_op jit(solution)/shard_map/ppermute | solution.py:129
  14.1 9.7 %collective-permute-start = (bf16[1,128,128]{2,1,0:T(8,128)(2,1)}, bf16[1,128,128]{2,1,0:T(8,128)(2,1)S(1)}, u32[]{:S(2)}, u32[]{:S(2)}) collective-permute-start(bf16[1,128,128]{2,1,0:T(8,128)(2,1)} %bitcast.44), channel_id=1, source_target_pairs={{0,0},{1,64},{2,128},{3,192},{4,256},{5,320},{6,384},{7,448},{8,8}... | collective-permute-start | bytes 98312 | tf_op jit(solution)/shard_map/ppermute | solution.py:113
  23.9 0.7 constant_dynamic-slice_fusion
  24.6 0.8 fusion.5
  25.4 1.8 %collective-permute-done = bf16[1,128,128]{2,1,0:T(8,128)(2,1)S(1)} collective-permute-done((bf16[1,128,128]{2,1,0:T(8,128)(2,1)}, bf16[1,128,128]{2,1,0:T(8,128)(2,1)S(1)}, u32[]{:S(2)}, u32[]{:S(2)}) %collective-permute-start) | collective-permute-done | bytes 32800 | tf_op jit(solution)/shard_map/ppermute | solution.py:113
  27.2 0.0 collective-permute-done.2.refs_2_
  27.3 0.0 collective-permute-done.1.refs_1_
  27.3 6.5 %collective-permute-start.3 = (bf16[656,128]{1,0:T(8,128)(2,1)}, bf16[656,128]{1,0:T(8,128)(2,1)}, u32[]{:S(2)}, u32[]{:S(2)}) collective-permute-start(bf16[656,128]{1,0:T(8,128)(2,1)} %collective-permute-done.1.refs_1_), channel_id=1, source_target_pairs={{0,1},{1,2},{2,3},{3,4},{4,5},{5,6},{6,7},{7,0},{8,9},{9,10},{10,1... | collective-permute-start | bytes 503816 | tf_op jit(solution)/shard_map/ppermute | solution.py:127
  33.8 0.7 constant_dynamic-update-slice_fusion.6
  34.4 1.9 %collective-permute-start.4 = (bf16[656,128]{1,0:T(8,128)(2,1)S(1)}, bf16[656,128]{1,0:T(8,128)(2,1)}, u32[]{:S(2)}, u32[]{:S(2)}) collective-permute-start(bf16[656,128]{1,0:T(8,128)(2,1)S(1)} %collective-permute-done.2.refs_2_), channel_id=1, source_target_pairs={{0,7},{1,0},{2,1},{3,2},{4,3},{5,4},{6,5},{7,6},{8,15},{9,8},{10,9... | collective-permute-start | bytes 503816 | tf_op jit(solution)/shard_map/ppermute | solution.py:128
  36.4 1.2 tile.10
  37.6 8.7 %all-to-all-start = ((bf16[32,128,128]{2,1,0:T(8,128)(2,1)}), bf16[32,128,128]{2,1,0:T(8,128)(2,1)S(1)}, u32[]{:S(2)}, u32[]{:S(2)}) async-start(bf16[32,128,128]{2,1,0:T(8,128)(2,1)} %tile.10), calls=%async_computation | async-start | bytes 2097152 | tf_op jit(solution)/shard_map/all_to_all | solution.py:124
  46.4 0.0 collective-permute-done.9
  46.4 0.0 collective-permute-done.8
  46.4 2.1 %pad_maximum_fusion.refs_8_ = bf16[3,8,128,128]{3,2,1,0:T(8,128)(2,1)} fusion(bf16[1,8,128,128]{3,2,1,0:T(8,128)(2,1)} %bitcast.17, bf16[1,8,128,128]{3,2,1,0:T(8,128)(2,1)} %constant_dynamic-slice_fusion, bf16[1,8,128,128]{3,2,1,0:T(8,128)(2,1)} %bitcast.16), kind=kLoop, calls=%fused_computation | loop fusion | flops 786432 | bytes 1572864 | tf_op jit(solution)/shard_map/stack | solution.py:137
  48.5 0.0 collective-permute-done.3.refs_3_
  48.5 0.0 collective-permute-done.4.refs_4_
  48.5 2.4 %collective-permute-start.5 = (bf16[656,128]{1,0:T(8,128)(2,1)}, bf16[656,128]{1,0:T(8,128)(2,1)S(1)}, u32[]{:S(2)}, u32[]{:S(2)}) collective-permute-start(bf16[656,128]{1,0:T(8,128)(2,1)} %collective-permute-done.3.refs_3_), channel_id=1, source_target_pairs={{0,1},{1,2},{2,3},{3,4},{4,5},{5,6},{6,7},{7,0},{8,9},{9,10},{10,1... | collective-permute-start | bytes 503816 | tf_op jit(solution)/shard_map/ppermute | solution.py:132
  50.8 0.7 constant_dynamic-update-slice_fusion.4
  51.5 4.7 %collective-permute-start.6 = (bf16[656,128]{1,0:T(8,128)(2,1)}, bf16[656,128]{1,0:T(8,128)(2,1)S(1)}, u32[]{:S(2)}, u32[]{:S(2)}) collective-permute-start(bf16[656,128]{1,0:T(8,128)(2,1)} %collective-permute-done.4.refs_4_), channel_id=1, source_target_pairs={{0,7},{1,0},{2,1},{3,2},{4,3},{5,4},{6,5},{7,6},{8,15},{9,8},{10,9... | collective-permute-start | bytes 503816 | tf_op jit(solution)/shard_map/ppermute | solution.py:133
  56.2 0.7 constant_dynamic-update-slice_fusion.3
  56.9 0.2 collective-permute-done.5.refs_5_
  57.1 2.3 %collective-permute-done.6.refs_6_ = bf16[656,128]{1,0:T(8,128)(2,1)S(1)} collective-permute-done((bf16[656,128]{1,0:T(8,128)(2,1)}, bf16[656,128]{1,0:T(8,128)(2,1)S(1)}, u32[]{:S(2)}, u32[]{:S(2)}) %collective-permute-start.6) | collective-permute-done | bytes 167968 | tf_op jit(solution)/shard_map/ppermute | solution.py:133
  59.4 4.1 %collective-permute-start.7 = (bf16[656,128]{1,0:T(8,128)(2,1)S(1)}, bf16[656,128]{1,0:T(8,128)(2,1)S(1)}, u32[]{:S(2)}, u32[]{:S(2)}) collective-permute-start(bf16[656,128]{1,0:T(8,128)(2,1)S(1)} %collective-permute-done.5.refs_5_), channel_id=1, source_target_pairs={{0,1},{1,2},{2,3},{3,4},{4,5},{5,6},{6,7},{7,0},{8,9},{9,10},{10,1... | collective-permute-start | bytes 503816 | tf_op jit(solution)/shard_map/ppermute | solution.py:135
  63.5 0.0 copy-start.4
  63.5 0.7 copy-done.4
  64.2 0.0 copy-start.6
  64.2 0.7 copy-done.6
  64.8 3.4 %collective-permute-done.7.refs_7_ = bf16[656,128]{1,0:T(8,128)(2,1)S(1)} collective-permute-done((bf16[656,128]{1,0:T(8,128)(2,1)S(1)}, bf16[656,128]{1,0:T(8,128)(2,1)S(1)}, u32[]{:S(2)}, u32[]{:S(2)}) %collective-permute-start.7) | collective-permute-done | bytes 167968 | tf_op jit(solution)/shard_map/ppermute | solution.py:135
  68.2 0.0 copy-start.8
  68.2 0.7 copy-done.8
  68.9 0.1 copy.16
  69.0 0.1 select_reduce_fusion
  69.1 0.1 fusion
  69.2 0.0 copy-start.3
  69.2 1.1 copy-done.3
  70.4 0.0 copy-start.5
  70.4 0.9 copy-done.5
  71.3 0.0 copy-start.7
  71.3 0.9 copy-done.7
  72.2 0.9 copy-done.9
  73.1 13.7 %shard_map.64.partial_ref = bf16[8,8,128,128]{3,2,1,0:T(8,128)(2,1)S(1)} custom-call(f32[40,8]{1,0:T(8,128)S(1)} %reshape.26.factor_ref, s32[8,5]{1,0:T(8,128)S(1)} %bitcast.41, bf16[656,128]{1,0:T(8,128)(2,1)S(1)} %pad_maximum_fusion.1.refs_0_, bf16[656,128]{1,0:T(8,128)(2,1)} %collective-permute-done.1.refs_1_, ...), custom_call_target="tpu_custom_call" | custom-call | flops 1342177280 | bytes 5242880 | tf_op jit(solution)/shard_map/pallas_call | solution.py:147
  86.8 0.0 copy-start.1
  86.8 1.3 copy-done.1
  88.2 0.0 all-to-all-done.right_ref
  88.2 1.9 %collective-permute-start.10 = (bf16[32,128,128]{2,1,0:T(8,128)(2,1)S(1)}, bf16[32,128,128]{2,1,0:T(8,128)(2,1)}, u32[]{:S(2)}, u32[]{:S(2)}) collective-permute-start(bf16[32,128,128]{2,1,0:T(8,128)(2,1)S(1)} %all-to-all-done.right_ref), channel_id=1, source_target_pairs={{0,8},{8,0},{16,24},{24,16},{32,40},{40,32},{48,56},{56,48},{64,72... | collective-permute-start | bytes 3145736 | tf_op jit(solution)/shard_map/ppermute | solution.py:157
  90.1 0.8 dynamic-slice_convert_fusion.keep_ref
  90.8 0.1 pad_add_fusion.where_ref
  90.9 1.6 %copy-done.2 = bf16[8,8,128,128]{3,2,1,0:T(8,128)(2,1)S(1)} copy-done((bf16[8,8,128,128]{3,2,1,0:T(8,128)(2,1)S(1)}, bf16[8,8,128,128]{3,2,1,0:T(8,128)(2,1)}, u32[]{:S(2)}) %copy-start.2) | copy-done | bytes 2097176
  92.5 1.8 %shard_map.65.own_ref = bf16[4,128,128]{2,1,0:T(8,128)(2,1)S(1)} custom-call(s32[2]{0:T(128)S(1)} %pad_add_fusion.where_ref, f32[1,8]{1,0:T(1,128)S(1)} %dynamic-slice_convert_fusion.keep_ref, bf16[8,8,128,128]{3,2,1,0:T(8,128)(2,1)S(1)} %copy-done.2, bf16[32,128,128]{2,1,0:T(8,128)(2,1)S(1)} %all-to-all-done.right_ref), custom_call_target="tpu_custom_call" | custom-call | flops 134217728 | bytes 2097152 | tf_op jit(solution)/shard_map/pallas_call | solution.py:161
  94.3 0.0 collective-permute-done.10.right_ref
  94.3 3.3 %shard_map.66 = bf16[16,128,128]{2,1,0:T(8,128)(2,1)} custom-call(s32[2]{0:T(128)S(1)} %pad_add_fusion.where_ref, f32[1,8]{1,0:T(1,128)S(1)} %dynamic-slice_convert_fusion.keep_ref, bf16[8,8,128,128]{3,2,1,0:T(8,128)(2,1)S(1)} %copy-done.2, bf16[32,128,128]{2,1,0:T(8,128)(2,1)} %collective-permute-done.10.right_ref, bf16[4,128,128]{2,1,0:T(8,128)(2,1)S(1)} %shard_map.65.own_ref), custom_call_target="tpu_custom_call" | custom-call | flops 134217728 | bytes 2097152 | tf_op jit(solution)/shard_map/pallas_call | solution.py:169
  97.6 13.3 %all-to-all-start.1 = ((bf16[16,128,128]{2,1,0:T(8,128)(2,1)}), bf16[16,128,128]{2,1,0:T(8,128)(2,1)S(1)}, u32[]{:S(2)}, u32[]{:S(2)}) async-start(bf16[16,128,128]{2,1,0:T(8,128)(2,1)} %shard_map.66), calls=%async_computation.1 | async-start | bytes 1048576 | tf_op jit(solution)/shard_map/all_to_all | solution.py:178
  111.0 26.1 %all-to-all-done.1 = bf16[16,128,128]{2,1,0:T(8,128)(2,1)S(1)} async-done(((bf16[16,128,128]{2,1,0:T(8,128)(2,1)}), bf16[16,128,128]{2,1,0:T(8,128)(2,1)S(1)}, u32[]{:S(2)}, u32[]{:S(2)}) %all-to-all-start.1) | async-done | bytes 524320 | tf_op jit(solution)/shard_map/all_to_all | solution.py:178
  137.1 0.7 dynamic-slice_bitcast_fusion
  (16 shorter events, 0.1 us)
Async XLA Ops:
  0.0 8.4 %copy-start = (bf16[1,64,128,128]{3,2,1,0:T(8,128)(2,1)S(1)}, bf16[1,64,128,128]{3,2,1,0:T(8,128)(2,1)}, u32[]{:S(2)}) copy-start(bf16[1,64,128,128]{3,2,1,0:T(8,128)(2,1)} %param.6) | copy-start | bytes 6291460
  2.5 24.7 %collective-permute-start.2 = (bf16[656,128]{1,0:T(8,128)(2,1)S(1)}, bf16[656,128]{1,0:T(8,128)(2,1)S(1)}, u32[]{:S(2)}, u32[]{:S(2)}) collective-permute-start(bf16[656,128]{1,0:T(8,128)(2,1)S(1)} %pad_maximum_fusion.1.refs_0_), channel_id=1, source_target_pairs={{0,7},{1,0},{2,1},{3,2},{4,3},{5,4},{6,5},{7,6},{8,15},{9,8},{10,9... | collective-permute-start | bytes 503816 | tf_op jit(solution)/shard_map/ppermute | solution.py:122
  4.4 22.8 %collective-permute-start.1 = (bf16[656,128]{1,0:T(8,128)(2,1)S(1)}, bf16[656,128]{1,0:T(8,128)(2,1)}, u32[]{:S(2)}, u32[]{:S(2)}) collective-permute-start(bf16[656,128]{1,0:T(8,128)(2,1)S(1)} %pad_maximum_fusion.1.refs_0_), channel_id=1, source_target_pairs={{0,1},{1,2},{2,3},{3,4},{4,5},{5,6},{6,7},{7,0},{8,9},{9,10},{10,1... | collective-permute-start | bytes 503816 | tf_op jit(solution)/shard_map/ppermute | solution.py:121
  9.1 37.2 %collective-permute-start.9 = (bf16[8,128,128]{2,1,0:T(8,128)(2,1)}, bf16[8,128,128]{2,1,0:T(8,128)(2,1)}, u32[]{:S(2)}, u32[]{:S(2)}) collective-permute-start(bf16[8,128,128]{2,1,0:T(8,128)(2,1)} %fusion.7), channel_id=1, source_target_pairs={{8,0},{16,8},{24,16},{32,24},{40,32},{48,40},{56,48},{64,56},{72,6... | collective-permute-start | bytes 786440 | tf_op jit(solution)/shard_map/ppermute | solution.py:130
  10.4 36.0 %collective-permute-start.8 = (bf16[8,128,128]{2,1,0:T(8,128)(2,1)}, bf16[8,128,128]{2,1,0:T(8,128)(2,1)}, u32[]{:S(2)}, u32[]{:S(2)}) collective-permute-start(bf16[8,128,128]{2,1,0:T(8,128)(2,1)} %fusion.7), channel_id=1, source_target_pairs={{0,8},{8,16},{16,24},{24,32},{32,40},{40,48},{48,56},{56,64},{64,7... | collective-permute-start | bytes 786440 | tf_op jit(solution)/shard_map/ppermute | solution.py:129
  14.1 13.1 %collective-permute-start = (bf16[1,128,128]{2,1,0:T(8,128)(2,1)}, bf16[1,128,128]{2,1,0:T(8,128)(2,1)S(1)}, u32[]{:S(2)}, u32[]{:S(2)}) collective-permute-start(bf16[1,128,128]{2,1,0:T(8,128)(2,1)} %bitcast.44), channel_id=1, source_target_pairs={{0,0},{1,64},{2,128},{3,192},{4,256},{5,320},{6,384},{7,448},{8,8}... | collective-permute-start | bytes 98312 | tf_op jit(solution)/shard_map/ppermute | solution.py:113
  27.3 21.2 %collective-permute-start.3 = (bf16[656,128]{1,0:T(8,128)(2,1)}, bf16[656,128]{1,0:T(8,128)(2,1)}, u32[]{:S(2)}, u32[]{:S(2)}) collective-permute-start(bf16[656,128]{1,0:T(8,128)(2,1)} %collective-permute-done.1.refs_1_), channel_id=1, source_target_pairs={{0,1},{1,2},{2,3},{3,4},{4,5},{5,6},{6,7},{7,0},{8,9},{9,10},{10,1... | collective-permute-start | bytes 503816 | tf_op jit(solution)/shard_map/ppermute | solution.py:127
  34.4 14.0 %collective-permute-start.4 = (bf16[656,128]{1,0:T(8,128)(2,1)S(1)}, bf16[656,128]{1,0:T(8,128)(2,1)}, u32[]{:S(2)}, u32[]{:S(2)}) collective-permute-start(bf16[656,128]{1,0:T(8,128)(2,1)S(1)} %collective-permute-done.2.refs_2_), channel_id=1, source_target_pairs={{0,7},{1,0},{2,1},{3,2},{4,3},{5,4},{6,5},{7,6},{8,15},{9,8},{10,9... | collective-permute-start | bytes 503816 | tf_op jit(solution)/shard_map/ppermute | solution.py:128
  37.6 50.5 %all-to-all-start = ((bf16[32,128,128]{2,1,0:T(8,128)(2,1)}), bf16[32,128,128]{2,1,0:T(8,128)(2,1)S(1)}, u32[]{:S(2)}, u32[]{:S(2)}) async-start(bf16[32,128,128]{2,1,0:T(8,128)(2,1)} %tile.10), calls=%async_computation | async-start | bytes 2097152 | tf_op jit(solution)/shard_map/all_to_all | solution.py:124
  48.5 8.7 %collective-permute-start.5 = (bf16[656,128]{1,0:T(8,128)(2,1)}, bf16[656,128]{1,0:T(8,128)(2,1)S(1)}, u32[]{:S(2)}, u32[]{:S(2)}) collective-permute-start(bf16[656,128]{1,0:T(8,128)(2,1)} %collective-permute-done.3.refs_3_), channel_id=1, source_target_pairs={{0,1},{1,2},{2,3},{3,4},{4,5},{5,6},{6,7},{7,0},{8,9},{9,10},{10,1... | collective-permute-start | bytes 503816 | tf_op jit(solution)/shard_map/ppermute | solution.py:132
  51.5 7.8 %collective-permute-start.6 = (bf16[656,128]{1,0:T(8,128)(2,1)}, bf16[656,128]{1,0:T(8,128)(2,1)S(1)}, u32[]{:S(2)}, u32[]{:S(2)}) collective-permute-start(bf16[656,128]{1,0:T(8,128)(2,1)} %collective-permute-done.4.refs_4_), channel_id=1, source_target_pairs={{0,7},{1,0},{2,1},{3,2},{4,3},{5,4},{6,5},{7,6},{8,15},{9,8},{10,9... | collective-permute-start | bytes 503816 | tf_op jit(solution)/shard_map/ppermute | solution.py:133
  59.4 8.8 %collective-permute-start.7 = (bf16[656,128]{1,0:T(8,128)(2,1)S(1)}, bf16[656,128]{1,0:T(8,128)(2,1)S(1)}, u32[]{:S(2)}, u32[]{:S(2)}) collective-permute-start(bf16[656,128]{1,0:T(8,128)(2,1)S(1)} %collective-permute-done.5.refs_5_), channel_id=1, source_target_pairs={{0,1},{1,2},{2,3},{3,4},{4,5},{5,6},{6,7},{7,0},{8,9},{9,10},{10,1... | collective-permute-start | bytes 503816 | tf_op jit(solution)/shard_map/ppermute | solution.py:135
  63.5 0.7 copy-start.4
  64.2 0.7 copy-start.6
  68.2 0.7 copy-start.8
  69.2 1.1 copy-start.3
  70.4 0.9 copy-start.5
  71.3 0.9 copy-start.7
  72.2 0.9 copy-start.9
  86.8 1.3 copy-start.1
  88.2 6.1 %collective-permute-start.10 = (bf16[32,128,128]{2,1,0:T(8,128)(2,1)S(1)}, bf16[32,128,128]{2,1,0:T(8,128)(2,1)}, u32[]{:S(2)}, u32[]{:S(2)}) collective-permute-start(bf16[32,128,128]{2,1,0:T(8,128)(2,1)S(1)} %all-to-all-done.right_ref), channel_id=1, source_target_pairs={{0,8},{8,0},{16,24},{24,16},{32,40},{40,32},{48,56},{56,48},{64,72... | collective-permute-start | bytes 3145736 | tf_op jit(solution)/shard_map/ppermute | solution.py:157
  90.9 1.6 %copy-start.2 = (bf16[8,8,128,128]{3,2,1,0:T(8,128)(2,1)S(1)}, bf16[8,8,128,128]{3,2,1,0:T(8,128)(2,1)}, u32[]{:S(2)}) copy-start(bf16[8,8,128,128]{3,2,1,0:T(8,128)(2,1)} %copy-done.1) | copy-start | bytes 6291460
  97.6 39.5 %all-to-all-start.1 = ((bf16[16,128,128]{2,1,0:T(8,128)(2,1)}), bf16[16,128,128]{2,1,0:T(8,128)(2,1)S(1)}, u32[]{:S(2)}, u32[]{:S(2)}) async-start(bf16[16,128,128]{2,1,0:T(8,128)(2,1)} %shard_map.66), calls=%async_computation.1 | async-start | bytes 1048576 | tf_op jit(solution)/shard_map/all_to_all | solution.py:178

commit v2 on v1

v2 whole, which is shorter than its diff:
```python
import functools

import jax
import jax.numpy as jnp
from jax import lax
from jax.experimental import pallas as pl
from jax.experimental.pallas import tpu as pltpu
from jax.sharding import PartitionSpec as P

M = 128
LB = 5
NW = 8
G = 8
BOTH = ("sec", "term")
OFFSETS = (0, -1, 1, -2, 2, -3, 3, -4)
ROWS = LB * M
F32 = jnp.float32
BF16 = jnp.bfloat16
VMEM = pl.BlockSpec(memory_space=pltpu.VMEM)
SMEM = pl.BlockSpec(memory_space=pltpu.SMEM)
PARAMS = pltpu.CompilerParams(vmem_limit_bytes=56 * 1024 * 1024)


def together(*arrays):
    return lax.optimization_barrier(arrays)


def slot_bond(t, k):
    return lax.rem(t + OFFSETS[k] + NW, NW)


def left_products(count, first, t_ref, *refs):
    slots = refs[:count]
    if first:
        below_ref, own_ref, above_ref, out_ref, psi_ref, factor_ref = refs[count:]
        for row, ref in enumerate((below_ref, own_ref, above_ref)):
            psi_ref[row] = ref[...]
    else:
        psi_ref, out_ref, factor_ref = refs[count:]
    sector = lax.broadcasted_iota(jnp.int32, (M, G * M), 0)
    wanted = lax.broadcasted_iota(jnp.int32, (M, G * M), 1) // M + t_ref[0] * G
    pick = jnp.where((sector == wanted) | (sector == wanted + M // 2), 1.0, 0.0).astype(BF16)
    for q, slot in enumerate(slots):
        table = slot[ROWS : ROWS + 16, :]
        spread = jnp.dot(table, pick, preferred_element_type=F32)
        factor_ref[q] = spread[:8] + spread[8:]
        shifts = table.astype(F32)[15:16, :]
        rows = [shifts[0, c].astype(jnp.int32) + 1 for c in range(LB)]
        envs = [slot[c * M : (c + 1) * M, :] for c in range(LB)]
        for start in range(0, G * M, 2 * M):
            totals = [None, None]
            for c in range(LB):
                product = lax.dot_general(
                    psi_ref[rows[c], start : start + 2 * M, :],
                    envs[c],
                    (((1,), (1,)), ((), ())),
                    preferred_element_type=F32,
                )
                for h in range(2):
                    at = start + h * M
                    term = product[h * M : (h + 1) * M] * factor_ref[q, c : c + 1, at : at + M]
                    totals[h] = term if totals[h] is None else totals[h] + term
            for h in range(2):
                at = start + h * M
                out_ref[q, at : at + M, :] = totals[h].astype(BF16)


def left_call(t, slots, psi, first):
    count = len(slots)
    out_shape = [jax.ShapeDtypeStruct((count, G * M, M), BF16)]
    if first:
        out_shape.append(jax.ShapeDtypeStruct((3, G * M, M), BF16))
    return pl.pallas_call(
        functools.partial(left_products, count, first),
        out_shape=out_shape,
        in_specs=[SMEM] + [VMEM] * (count + len(psi)),
        out_specs=[VMEM] * len(out_shape),
        scratch_shapes=[pltpu.VMEM((count, 8, G * M), F32)],
        compiler_params=PARAMS,
        cost_estimate=pl.CostEstimate(flops=2 * 40 * count * M**3, bytes_accessed=2 << 20, transcendentals=0),
    )(t, *slots, *psi)


def right_sum(t, j, i, partials, right_ref, keep_ref):
    total, k = None, 0
    for ref in partials:
        for q in range(ref.shape[0]):
            product = jnp.dot(
                right_ref[slot_bond(t, k) * (G // 2) + i],
                ref[q, pl.ds(pl.multiple_of(j * M, M), M), :],
                preferred_element_type=F32,
            )
            total = product if total is None else total + product
            k += 1
    return (total * keep_ref[0, j]).T.astype(BF16)


def right_own(where_ref, keep_ref, right_ref, *refs):
    partials, out_ref = refs[:-1], refs[-1]
    t, core = where_ref[0], where_ref[1]
    for i in range(G // 2):
        out_ref[i] = right_sum(t, 2 * i + core, i, partials, right_ref, keep_ref)


def right_other(where_ref, keep_ref, right_ref, own_ref, *refs):
    partials, out_ref = refs[:-1], refs[-1]
    t, core = where_ref[0], where_ref[1]
    for i in range(G // 2):
        j = 2 * i + 1 - core
        value = right_sum(t, j, i, partials, right_ref, keep_ref)
        out_ref[j] = value
        out_ref[G + j] = value
        mine = own_ref[i]
        out_ref[2 * i + core] = mine
        out_ref[G + 2 * i + core] = mine


def bf16_pieces(x):
    pieces = []
    for _ in range(3):
        piece = lax.reduce_precision(x, 8, 7)
        pieces.append(piece)
        x = x - piece
    return pieces


def on_device(wavefunction, left_env, right_env, coupling, left_shift, allowed, *, n_sec, n_term):
    s, t = lax.axis_index("sec"), lax.axis_index("term")
    groups = n_sec // G

    def device(sec, term):
        return sec * n_term + term

    spread = [(device(b, w), device(w * G + b % G, b // G)) for b in range(n_sec) for w in range(n_term)]
    by_core = [[2 * chip + core for chip in range(n_sec // 2)] for core in range(2)]
    up = [(i, (i + 1) % n_term) for i in range(n_term)]
    down = [(i, (i - 1) % n_term) for i in range(n_term)]
    exchange = [
        [device(A * G + i, B) for i in range(G)] + [device(B * G + i, A) for i in range(G)]
        for A in range(groups)
        for B in range(A + 1, groups)
    ] + [
        [device(A * G + i, A) for i in range(G)] + [device((A + 1) * G + i, A + 1) for i in range(G)]
        for A in range(0, groups, 2)
    ]

    right = lax.ppermute(right_env[0], BOTH, spread)

    near = lax.dynamic_slice_in_dim(jnp.pad(allowed, ((1, 1), (0, 0))), s, 3, 0)
    source = left_shift[0, :, None] + 1 == jnp.arange(3)
    kept = jnp.sum(jnp.where(source[:, :, None], near, 0), axis=1)
    factors = lax.dynamic_slice_in_dim(coupling[0], s, 1, 1)[:, 0, :] * kept.astype(F32)
    high, middle, low = bf16_pieces(factors)
    table = jnp.concatenate(
        [
            jnp.pad(jnp.concatenate([high, middle], axis=1), ((0, 8 - LB), (0, 0))),
            jnp.pad(low, ((0, 7 - LB), (0, M - n_sec))),
            jnp.pad(left_shift.astype(F32), ((0, 0), (0, M - LB))),
        ]
    ).astype(BF16)
    payload = jnp.concatenate([left_env[0, :, 0].reshape(ROWS, M), table])
    own_psi = lax.dynamic_slice_in_dim(wavefunction[0], t * G, G, 0)
    own_psi = jnp.swapaxes(own_psi, 1, 2).reshape(G * M, M)
    here = t.astype(jnp.int32)[None]

    u1 = lax.ppermute(payload, "term", up)
    d1 = lax.ppermute(payload, "term", down)
    right, own_psi = together(right, own_psi)
    below = lax.ppermute(own_psi, "sec", [(i, i + 1) for i in range(n_sec - 1)])
    above = lax.ppermute(own_psi, "sec", [(i + 1, i) for i in range(n_sec - 1)])
    right, u1, d1 = together(right, u1, d1)
    halves = lax.all_to_all(
        jnp.tile(right, (n_sec // 2, 1, 1)), "sec", 0, 0, axis_index_groups=by_core, tiled=True
    )
    u2 = lax.ppermute(u1, "term", up)
    d2 = lax.ppermute(d1, "term", down)
    part0, psi = left_call(here, [payload], [below, own_psi, above], True)
    (part1,) = left_call(here, [u1, d1], [psi], False)
    u2, d2, part1 = together(u2, d2, part1)
    u3 = lax.ppermute(u2, "term", up)
    d3 = lax.ppermute(d2, "term", down)
    (part2,) = left_call(here, [u2, d2], [psi], False)
    u3, d3, part2 = together(u3, d3, part2)
    u4 = lax.ppermute(u3, "term", up)
    (part3,) = left_call(here, [u3, d3], [psi], False)
    u4, part3 = together(u4, part3)
    (part4,) = left_call(here, [u4], [psi], False)
    parts = [part0, part1, part2, part3, part4]

    halves, parts[-1] = together(halves, parts[-1])
    others = lax.ppermute(halves, "sec", [(i, i ^ 1) for i in range(n_sec)])
    where = jnp.stack([t, lax.rem(s, 2)]).astype(jnp.int32)
    keep = lax.dynamic_slice(allowed, (s, t * G), (1, G)).astype(F32)
    cost = pl.CostEstimate(flops=2 * 32 * M**3, bytes_accessed=2 << 20, transcendentals=0)
    own = pl.pallas_call(
        right_own,
        out_shape=jax.ShapeDtypeStruct((G // 2, M, M), BF16),
        in_specs=[SMEM, SMEM] + [VMEM] * (1 + len(parts)),
        out_specs=VMEM,
        compiler_params=PARAMS,
        cost_estimate=cost,
    )(where, keep, halves, *parts)
    results = pl.pallas_call(
        right_other,
        out_shape=jax.ShapeDtypeStruct((2 * G, M, M), BF16),
        in_specs=[SMEM, SMEM] + [VMEM] * (2 + len(parts)),
        out_specs=VMEM,
        compiler_params=PARAMS,
        cost_estimate=cost,
    )(where, keep, others, own, *parts)

    received = lax.all_to_all(results, BOTH, 0, 0, axis_index_groups=exchange, tiled=True)
    A = s // G
    first = jnp.where(A < t, G, jnp.where(A > t, 0, lax.rem(A, 2) * G))
    return lax.dynamic_slice_in_dim(received, first, G, 0)[:, None]


def solution(mesh):
    in_specs = (
        P("sec", None, None, None),
        P("term", None, "sec", None, None),
        P("term", "sec", None, None),
        P("term", None, None, None),
        P("term", None),
        P(),
    )
    body = functools.partial(on_device, n_sec=mesh.shape["sec"], n_term=mesh.shape["term"])
    return jax.shard_map(
        body, mesh=mesh, in_specs=in_specs, out_specs=P("term", "sec", None, None), check_vma=False
    )
```

time: 139 us -> 142 us (1.022)
  the two profiles are of different devices: /device:TPU:256 before, /device:TPU:4 now
where the time goes in v2:
time: 142 us; the launch traced here: 140 us
  starting transfers between devices  70.7 us (50%)
  waiting for transfers between devices  38.6 us (27%)
  Pallas kernels  21.2 us (15%)
  local copies, waits for them, and re-layouts  5.1 us (4%)
  other arithmetic  4.02 us (3%)
    all_to_all x1, waiting for transfers between devices, on_device(): lax.all_to_all(results, BOTH, 0, 0, axis_index_groups=exchange, tiled=True)  16.2 us
    pallas_call x5, Pallas kernels, left_call(): pl.pallas_call(functools.partial(left_products, count, first), out_shape=...  14.9 us
    all_to_all x1, starting transfers between devices, on_device(): lax.all_to_all(jnp.tile(right, (n_sec // 2, 1, 1)), 'sec', 0, 0, axis_ind...  14.1 us
    all_to_all x1, starting transfers between devices, on_device(): lax.all_to_all(results, BOTH, 0, 0, axis_index_groups=exchange, tiled=True)  13 us
    ppermute x1, waiting for transfers between devices, on_device(): below = lax.ppermute(own_psi, 'sec', [(i, i + 1) for i in range(n_sec - 1)])  12.1 us
    ppermute x1, starting transfers between devices, on_device(): d1 = lax.ppermute(payload, 'term', down)  8.59 us
    ppermute x1, waiting for transfers between devices, on_device(): right = lax.ppermute(right_env[0], BOTH, spread)  7.04 us
    ppermute x1, starting transfers between devices, on_device(): above = lax.ppermute(own_psi, 'sec', [(i + 1, i) for i in range(n_sec - 1)])  5.75 us
  transfers between devices with their start and end apart: 13, of which 4 were waited for; matrix products, arithmetic and copies ran while one was open for 2% of the time, Pallas kernels for 13%

profile of v2, /device:TPU:4, one launch (start us, length us, event | category | flops | bytes accessed | tf_op | source)
XLA Modules:
  0.0 139.9 jit_solution(8655616007180069232)
XLA Ops:
  0.0 0.0 copy-start
  0.0 0.8 add_bitcast_fusion
  0.8 0.1 iota_compare_fusion.4
  0.9 0.7 pad_dynamic-slice_fusion
  1.6 0.1 select_reduce_fusion
  1.7 0.7 constant_dynamic-slice_fusion
  2.5 0.1 fusion.10
  2.5 0.9 fusion.4.refs_0_
  3.5 0.0 copy-start.3
  3.5 4.3 %collective-permute-start.1 = (bf16[656,128]{1,0:T(8,128)(2,1)S(1)}, bf16[656,128]{1,0:T(8,128)(2,1)S(1)}, u32[]{:S(2)}, u32[]{:S(2)}) collective-permute-start(bf16[656,128]{1,0:T(8,128)(2,1)S(1)} %fusion.4.refs_0_), channel_id=1, source_target_pairs={{0,1},{1,2},{2,3},{3,4},{4,5},{5,6},{6,7},{7,0},{8,9},{9,10},{10,1... | collective-permute-start | bytes 503816 | tf_op jit(solution)/shard_map/ppermute | solution.py:166
  7.8 8.6 %collective-permute-start.2 = (bf16[656,128]{1,0:T(8,128)(2,1)S(1)}, bf16[656,128]{1,0:T(8,128)(2,1)S(1)}, u32[]{:S(2)}, u32[]{:S(2)}) collective-permute-start(bf16[656,128]{1,0:T(8,128)(2,1)S(1)} %fusion.4.refs_0_), channel_id=1, source_target_pairs={{0,7},{1,0},{2,1},{3,2},{4,3},{5,4},{6,5},{7,6},{8,15},{9,8},{10,9... | collective-permute-start | bytes 503816 | tf_op jit(solution)/shard_map/ppermute | solution.py:167
  16.4 5.0 %collective-permute-start = (bf16[1,128,128]{2,1,0:T(8,128)(2,1)}, bf16[1,128,128]{2,1,0:T(8,128)(2,1)S(1)}, u32[]{:S(2)}, u32[]{:S(2)}) collective-permute-start(bf16[1,128,128]{2,1,0:T(8,128)(2,1)} %bitcast.29), channel_id=1, source_target_pairs={{0,0},{1,64},{2,128},{3,192},{4,256},{5,320},{6,384},{7,448},{8,8}... | collective-permute-start | bytes 98312 | tf_op jit(solution)/shard_map/ppermute | solution.py:147
  21.4 0.0 copy-done
  21.5 0.2 copy.9
  21.6 0.0 copy-start.2
  21.7 7.0 %collective-permute-done = bf16[1,128,128]{2,1,0:T(8,128)(2,1)S(1)} collective-permute-done((bf16[1,128,128]{2,1,0:T(8,128)(2,1)}, bf16[1,128,128]{2,1,0:T(8,128)(2,1)S(1)}, u32[]{:S(2)}, u32[]{:S(2)}) %collective-permute-start) | collective-permute-done | bytes 32800 | tf_op jit(solution)/shard_map/ppermute | solution.py:147
  28.7 0.0 collective-permute-done.1.refs_0_
  28.7 0.0 collective-permute-done.2.refs_1_
  28.7 0.0 copy-start.7
  28.7 1.2 tile.10
  30.0 0.0 copy-done.3
  30.0 0.0 copy-done.6
  30.0 0.0 copy-done.7
  30.0 14.1 %all-to-all-start = ((bf16[32,128,128]{2,1,0:T(8,128)(2,1)}), bf16[32,128,128]{2,1,0:T(8,128)(2,1)S(1)}, u32[]{:S(2)}, u32[]{:S(2)}) async-start(bf16[32,128,128]{2,1,0:T(8,128)(2,1)} %tile.10), calls=%async_computation | async-start | bytes 2097152 | tf_op jit(solution)/shard_map/all_to_all | solution.py:172
  44.1 1.9 %collective-permute-start.5 = (bf16[1024,128]{1,0:T(8,128)(2,1)S(1)}, bf16[1024,128]{1,0:T(8,128)(2,1)S(1)}, u32[]{:S(2)}, u32[]{:S(2)}) collective-permute-start(bf16[1024,128]{1,0:T(8,128)(2,1)S(1)} %bitcast.24), channel_id=1, source_target_pairs={{0,8},{8,16},{16,24},{24,32},{32,40},{40,48},{48,56},{56,64},{64,7... | collective-permute-start | bytes 786440 | tf_op jit(solution)/shard_map/ppermute | solution.py:169
  46.1 5.8 %collective-permute-start.6 = (bf16[1024,128]{1,0:T(8,128)(2,1)S(1)}, bf16[1024,128]{1,0:T(8,128)(2,1)S(1)}, u32[]{:S(2)}, u32[]{:S(2)}) collective-permute-start(bf16[1024,128]{1,0:T(8,128)(2,1)S(1)} %bitcast.25), channel_id=1, source_target_pairs={{8,0},{16,8},{24,16},{32,24},{40,32},{48,40},{56,48},{64,56},{72,6... | collective-permute-start | bytes 786440 | tf_op jit(solution)/shard_map/ppermute | solution.py:170
  51.8 1.9 %collective-permute-start.3 = (bf16[656,128]{1,0:T(8,128)(2,1)}, bf16[656,128]{1,0:T(8,128)(2,1)S(1)}, u32[]{:S(2)}, u32[]{:S(2)}) collective-permute-start(bf16[656,128]{1,0:T(8,128)(2,1)} %copy-done.6), channel_id=1, source_target_pairs={{0,1},{1,2},{2,3},{3,4},{4,5},{5,6},{6,7},{7,0},{8,9},{9,10},{10,1... | collective-permute-start | bytes 503816 | tf_op jit(solution)/shard_map/ppermute | solution.py:175
  53.7 5.1 %collective-permute-start.4 = (bf16[656,128]{1,0:T(8,128)(2,1)}, bf16[656,128]{1,0:T(8,128)(2,1)S(1)}, u32[]{:S(2)}, u32[]{:S(2)}) collective-permute-start(bf16[656,128]{1,0:T(8,128)(2,1)} %copy-done.7), channel_id=1, source_target_pairs={{0,7},{1,0},{2,1},{3,2},{4,3},{5,4},{6,5},{7,6},{8,15},{9,8},{10,9... | collective-permute-start | bytes 503816 | tf_op jit(solution)/shard_map/ppermute | solution.py:176
  58.9 12.1 %collective-permute-done.5.refs_1_ = bf16[1024,128]{1,0:T(8,128)(2,1)S(1)} collective-permute-done((bf16[1024,128]{1,0:T(8,128)(2,1)S(1)}, bf16[1024,128]{1,0:T(8,128)(2,1)S(1)}, u32[]{:S(2)}, u32[]{:S(2)}) %collective-permute-start.5) | collective-permute-done | bytes 262176 | tf_op jit(solution)/shard_map/ppermute | solution.py:169
  71.0 0.0 collective-permute-done.6.refs_3_
  71.0 0.0 copy-done.2
  71.0 0.7 copy-done.4
  71.7 0.1 copy-done.5
  71.8 2.6 %shard_map.64 = (bf16[1,1024,128]{2,1,0:T(8,128)(2,1)}, bf16[3,1024,128]{2,1,0:T(8,128)(2,1)}) custom-call(s32[1]{0:T(128)} %bitcast.t_ref, bf16[656,128]{1,0:T(8,128)(2,1)} %copy-done.3, bf16[1024,128]{1,0:T(8,128)(2,1)} %copy-done.4, bf16[1024,128]{1,0:T(8,128)(2,1)} %bitcast.26, bf16[1024,128]{1,0:T(8,128)(2,1)} %copy-done.5), custom_call_target="tpu_custom_call" | custom-call | flops 167772160 | bytes 2097152 | tf_op jit(solution)/shard_map/pallas_call | solution.py:73
  74.3 3.2 %shard_map.65.refs_1_ = bf16[2,1024,128]{2,1,0:T(8,128)(2,1)} custom-call(s32[1]{0:T(128)} %bitcast.t_ref, bf16[656,128]{1,0:T(8,128)(2,1)} %copy-done.6, bf16[656,128]{1,0:T(8,128)(2,1)} %copy-done.7, bf16[3,1024,128]{2,1,0:T(8,128)(2,1)} %get-tuple-element.27.refs_2_.refs_1_), custom_call_target="tpu_custom_call" | custom-call | flops 335544320 | bytes 2097152 | tf_op jit(solution)/shard_map/pallas_call | solution.py:73
  77.6 0.0 collective-permute-done.3.refs_0_
  77.6 0.0 collective-permute-done.4.refs_1_
  77.6 0.0 copy-start.9
  77.6 1.9 %collective-permute-start.7 = (bf16[656,128]{1,0:T(8,128)(2,1)S(1)}, bf16[656,128]{1,0:T(8,128)(2,1)S(1)}, u32[]{:S(2)}, u32[]{:S(2)}) collective-permute-start(bf16[656,128]{1,0:T(8,128)(2,1)S(1)} %collective-permute-done.3.refs_0_), channel_id=1, source_target_pairs={{0,1},{1,2},{2,3},{3,4},{4,5},{5,6},{6,7},{7,0},{8,9},{9,10},{10,1... | collective-permute-start | bytes 503816 | tf_op jit(solution)/shard_map/ppermute | solution.py:180
  79.5 5.1 %collective-permute-start.8 = (bf16[656,128]{1,0:T(8,128)(2,1)S(1)}, bf16[656,128]{1,0:T(8,128)(2,1)S(1)}, u32[]{:S(2)}, u32[]{:S(2)}) collective-permute-start(bf16[656,128]{1,0:T(8,128)(2,1)S(1)} %collective-permute-done.4.refs_1_), channel_id=1, source_target_pairs={{0,7},{1,0},{2,1},{3,2},{4,3},{5,4},{6,5},{7,6},{8,15},{9,8},{10,9... | collective-permute-start | bytes 503816 | tf_op jit(solution)/shard_map/ppermute | solution.py:181
  84.7 0.0 copy-done.8
  84.7 0.0 copy-done.9
  84.7 3.2 %shard_map.66.refs_2_ = bf16[2,1024,128]{2,1,0:T(8,128)(2,1)} custom-call(s32[1]{0:T(128)} %bitcast.t_ref, bf16[656,128]{1,0:T(8,128)(2,1)} %copy-done.8, bf16[656,128]{1,0:T(8,128)(2,1)} %copy-done.9, bf16[3,1024,128]{2,1,0:T(8,128)(2,1)} %get-tuple-element.27.refs_2_.refs_1_), custom_call_target="tpu_custom_call" | custom-call | flops 335544320 | bytes 2097152 | tf_op jit(solution)/shard_map/pallas_call | solution.py:73
  87.9 0.0 collective-permute-done.7.refs_0_
  87.9 0.0 collective-permute-done.8.refs_1_
  87.9 0.0 copy-start.11
  88.0 1.9 %collective-permute-start.9 = (bf16[656,128]{1,0:T(8,128)(2,1)S(1)}, bf16[656,128]{1,0:T(8,128)(2,1)S(1)}, u32[]{:S(2)}, u32[]{:S(2)}) collective-permute-start(bf16[656,128]{1,0:T(8,128)(2,1)S(1)} %collective-permute-done.7.refs_0_), channel_id=1, source_target_pairs={{0,1},{1,2},{2,3},{3,4},{4,5},{5,6},{6,7},{7,0},{8,9},{9,10},{10,1... | collective-permute-start | bytes 503816 | tf_op jit(solution)/shard_map/ppermute | solution.py:184
  89.9 0.0 copy-done.10
  89.9 0.0 copy-done.11
  89.9 3.2 %shard_map.67.refs_3_ = bf16[2,1024,128]{2,1,0:T(8,128)(2,1)} custom-call(s32[1]{0:T(128)} %bitcast.t_ref, bf16[656,128]{1,0:T(8,128)(2,1)} %copy-done.10, bf16[656,128]{1,0:T(8,128)(2,1)} %copy-done.11, bf16[3,1024,128]{2,1,0:T(8,128)(2,1)} %get-tuple-element.27.refs_2_.refs_1_), custom_call_target="tpu_custom_call" | custom-call | flops 335544320 | bytes 2097152 | tf_op jit(solution)/shard_map/pallas_call | solution.py:73
  93.1 3.3 %collective-permute-done.9.refs_0_ = bf16[656,128]{1,0:T(8,128)(2,1)S(1)} collective-permute-done((bf16[656,128]{1,0:T(8,128)(2,1)S(1)}, bf16[656,128]{1,0:T(8,128)(2,1)S(1)}, u32[]{:S(2)}, u32[]{:S(2)}) %collective-permute-start.9) | collective-permute-done | bytes 167968 | tf_op jit(solution)/shard_map/ppermute | solution.py:184
  96.5 0.7 copy-done.12
  97.1 2.6 %shard_map.68.refs_4_ = bf16[1,1024,128]{2,1,0:T(8,128)(2,1)} custom-call(s32[1]{0:T(128)} %bitcast.t_ref, bf16[656,128]{1,0:T(8,128)(2,1)} %copy-done.12, bf16[3,1024,128]{2,1,0:T(8,128)(2,1)} %get-tuple-element.27.refs_2_.refs_1_), custom_call_target="tpu_custom_call" | custom-call | flops 167772160 | bytes 2097152 | tf_op jit(solution)/shard_map/pallas_call | solution.py:73
  99.7 0.0 all-to-all-done.right_ref
  99.7 1.9 %collective-permute-start.10 = (bf16[32,128,128]{2,1,0:T(8,128)(2,1)S(1)}, bf16[32,128,128]{2,1,0:T(8,128)(2,1)}, u32[]{:S(2)}, u32[]{:S(2)}) collective-permute-start(bf16[32,128,128]{2,1,0:T(8,128)(2,1)S(1)} %all-to-all-done.right_ref), channel_id=1, source_target_pairs={{0,8},{8,0},{16,24},{24,16},{32,40},{40,32},{48,56},{56,48},{64,72... | collective-permute-start | bytes 3145736 | tf_op jit(solution)/shard_map/ppermute | solution.py:191
  101.6 1.4 dynamic-slice_convert_fusion.keep_ref
  103.0 0.6 pad_add_fusion.where_ref
  103.7 0.0 copy-done.1
  103.7 3.0 %shard_map.69.own_ref = bf16[4,128,128]{2,1,0:T(8,128)(2,1)} custom-call(s32[2]{0:T(128)} %pad_add_fusion.where_ref, f32[1,8]{1,0:T(1,128)} %dynamic-slice_convert_fusion.keep_ref, bf16[32,128,128]{2,1,0:T(8,128)(2,1)} %copy-done.1, bf16[1,1024,128]{2,1,0:T(8,128)(2,1)} %get-tuple-element.34.refs_0_, bf16[2,1024,128]{2,1,0:T(8,128)(2,1)} %shard_map.65.refs_1_, ...), custom_call_target="tpu_custom_call" | custom-call | flops 134217728 | bytes 2097152 | tf_op jit(solution)/shard_map/pallas_call | solution.py:195
  106.7 0.0 collective-permute-done.10.right_ref
  106.7 3.2 %shard_map.70 = bf16[16,128,128]{2,1,0:T(8,128)(2,1)} custom-call(s32[2]{0:T(128)} %pad_add_fusion.where_ref, f32[1,8]{1,0:T(1,128)} %dynamic-slice_convert_fusion.keep_ref, bf16[32,128,128]{2,1,0:T(8,128)(2,1)} %collective-permute-done.10.right_ref, bf16[4,128,128]{2,1,0:T(8,128)(2,1)} %shard_map.69.own_ref, ...), custom_call_target="tpu_custom_call" | custom-call | flops 134217728 | bytes 2097152 | tf_op jit(solution)/shard_map/pallas_call | solution.py:203
  109.9 13.0 %all-to-all-start.1 = ((bf16[16,128,128]{2,1,0:T(8,128)(2,1)}), bf16[16,128,128]{2,1,0:T(8,128)(2,1)S(1)}, u32[]{:S(2)}, u32[]{:S(2)}) async-start(bf16[16,128,128]{2,1,0:T(8,128)(2,1)} %shard_map.70), calls=%async_computation.1 | async-start | bytes 1048576 | tf_op jit(solution)/shard_map/all_to_all | solution.py:212
  123.0 16.2 %all-to-all-done.1 = bf16[16,128,128]{2,1,0:T(8,128)(2,1)S(1)} async-done(((bf16[16,128,128]{2,1,0:T(8,128)(2,1)}), bf16[16,128,128]{2,1,0:T(8,128)(2,1)S(1)}, u32[]{:S(2)}, u32[]{:S(2)}) %all-to-all-start.1) | async-done | bytes 524320 | tf_op jit(solution)/shard_map/all_to_all | solution.py:212
  139.1 0.7 dynamic-slice_bitcast_fusion
  (9 shorter events, 0.0 us)
Async XLA Ops:
  0.0 21.4 %copy-start = (bf16[1,64,128,128]{3,2,1,0:T(8,128)(2,1)S(1)}, bf16[1,64,128,128]{3,2,1,0:T(8,128)(2,1)}, u32[]{:S(2)}) copy-start(bf16[1,64,128,128]{3,2,1,0:T(8,128)(2,1)} %param.6) | copy-start | bytes 6291460
  3.5 26.5 %copy-start.3 = (bf16[656,128]{1,0:T(8,128)(2,1)}, bf16[656,128]{1,0:T(8,128)(2,1)S(1)}, u32[]{:S(2)}) copy-start(bf16[656,128]{1,0:T(8,128)(2,1)S(1)} %fusion.4.refs_0_) | copy-start | bytes 503812
  3.5 25.2 %collective-permute-start.1 = (bf16[656,128]{1,0:T(8,128)(2,1)S(1)}, bf16[656,128]{1,0:T(8,128)(2,1)S(1)}, u32[]{:S(2)}, u32[]{:S(2)}) collective-permute-start(bf16[656,128]{1,0:T(8,128)(2,1)S(1)} %fusion.4.refs_0_), channel_id=1, source_target_pairs={{0,1},{1,2},{2,3},{3,4},{4,5},{5,6},{6,7},{7,0},{8,9},{9,10},{10,1... | collective-permute-start | bytes 503816 | tf_op jit(solution)/shard_map/ppermute | solution.py:166
  7.8 20.9 %collective-permute-start.2 = (bf16[656,128]{1,0:T(8,128)(2,1)S(1)}, bf16[656,128]{1,0:T(8,128)(2,1)S(1)}, u32[]{:S(2)}, u32[]{:S(2)}) collective-permute-start(bf16[656,128]{1,0:T(8,128)(2,1)S(1)} %fusion.4.refs_0_), channel_id=1, source_target_pairs={{0,7},{1,0},{2,1},{3,2},{4,3},{5,4},{6,5},{7,6},{8,15},{9,8},{10,9... | collective-permute-start | bytes 503816 | tf_op jit(solution)/shard_map/ppermute | solution.py:167
  16.4 12.3 %collective-permute-start = (bf16[1,128,128]{2,1,0:T(8,128)(2,1)}, bf16[1,128,128]{2,1,0:T(8,128)(2,1)S(1)}, u32[]{:S(2)}, u32[]{:S(2)}) collective-permute-start(bf16[1,128,128]{2,1,0:T(8,128)(2,1)} %bitcast.29), channel_id=1, source_target_pairs={{0,0},{1,64},{2,128},{3,192},{4,256},{5,320},{6,384},{7,448},{8,8}... | collective-permute-start | bytes 98312 | tf_op jit(solution)/shard_map/ppermute | solution.py:147
  21.6 49.3 %copy-start.2 = (bf16[8,128,128]{2,1,0:T(8,128)(2,1)}, bf16[8,128,128]{2,1,0:T(8,128)(2,1)S(1)}, u32[]{:S(2)}) copy-start(bf16[8,128,128]{2,1,0:T(8,128)(2,1)S(1)} %copy.9) | copy-start | bytes 786436
  28.7 1.3 copy-start.6
  28.7 1.3 copy-start.7
  30.0 69.8 %all-to-all-start = ((bf16[32,128,128]{2,1,0:T(8,128)(2,1)}), bf16[32,128,128]{2,1,0:T(8,128)(2,1)S(1)}, u32[]{:S(2)}, u32[]{:S(2)}) async-start(bf16[32,128,128]{2,1,0:T(8,128)(2,1)} %tile.10), calls=%async_computation | async-start | bytes 2097152 | tf_op jit(solution)/shard_map/all_to_all | solution.py:172
  44.1 26.8 %collective-permute-start.5 = (bf16[1024,128]{1,0:T(8,128)(2,1)S(1)}, bf16[1024,128]{1,0:T(8,128)(2,1)S(1)}, u32[]{:S(2)}, u32[]{:S(2)}) collective-permute-start(bf16[1024,128]{1,0:T(8,128)(2,1)S(1)} %bitcast.24), channel_id=1, source_target_pairs={{0,8},{8,16},{16,24},{24,32},{32,40},{40,48},{48,56},{56,64},{64,7... | collective-permute-start | bytes 786440 | tf_op jit(solution)/shard_map/ppermute | solution.py:169
  46.1 24.9 %collective-permute-start.6 = (bf16[1024,128]{1,0:T(8,128)(2,1)S(1)}, bf16[1024,128]{1,0:T(8,128)(2,1)S(1)}, u32[]{:S(2)}, u32[]{:S(2)}) collective-permute-start(bf16[1024,128]{1,0:T(8,128)(2,1)S(1)} %bitcast.25), channel_id=1, source_target_pairs={{8,0},{16,8},{24,16},{32,24},{40,32},{48,40},{56,48},{64,56},{72,6... | collective-permute-start | bytes 786440 | tf_op jit(solution)/shard_map/ppermute | solution.py:170
  51.8 25.8 %collective-permute-start.3 = (bf16[656,128]{1,0:T(8,128)(2,1)}, bf16[656,128]{1,0:T(8,128)(2,1)S(1)}, u32[]{:S(2)}, u32[]{:S(2)}) collective-permute-start(bf16[656,128]{1,0:T(8,128)(2,1)} %copy-done.6), channel_id=1, source_target_pairs={{0,1},{1,2},{2,3},{3,4},{4,5},{5,6},{6,7},{7,0},{8,9},{9,10},{10,1... | collective-permute-start | bytes 503816 | tf_op jit(solution)/shard_map/ppermute | solution.py:175
  53.7 23.8 %collective-permute-start.4 = (bf16[656,128]{1,0:T(8,128)(2,1)}, bf16[656,128]{1,0:T(8,128)(2,1)S(1)}, u32[]{:S(2)}, u32[]{:S(2)}) collective-permute-start(bf16[656,128]{1,0:T(8,128)(2,1)} %copy-done.7), channel_id=1, source_target_pairs={{0,7},{1,0},{2,1},{3,2},{4,3},{5,4},{6,5},{7,6},{8,15},{9,8},{10,9... | collective-permute-start | bytes 503816 | tf_op jit(solution)/shard_map/ppermute | solution.py:176
  71.0 0.7 copy-start.4
  71.0 0.8 copy-start.5
  77.6 7.1 %copy-start.8 = (bf16[656,128]{1,0:T(8,128)(2,1)}, bf16[656,128]{1,0:T(8,128)(2,1)S(1)}, u32[]{:S(2)}) copy-start(bf16[656,128]{1,0:T(8,128)(2,1)S(1)} %collective-permute-done.3.refs_0_) | copy-start | bytes 503812
  77.6 7.1 %copy-start.9 = (bf16[656,128]{1,0:T(8,128)(2,1)}, bf16[656,128]{1,0:T(8,128)(2,1)S(1)}, u32[]{:S(2)}) copy-start(bf16[656,128]{1,0:T(8,128)(2,1)S(1)} %collective-permute-done.4.refs_1_) | copy-start | bytes 503812
  77.6 10.3 %collective-permute-start.7 = (bf16[656,128]{1,0:T(8,128)(2,1)S(1)}, bf16[656,128]{1,0:T(8,128)(2,1)S(1)}, u32[]{:S(2)}, u32[]{:S(2)}) collective-permute-start(bf16[656,128]{1,0:T(8,128)(2,1)S(1)} %collective-permute-done.3.refs_0_), channel_id=1, source_target_pairs={{0,1},{1,2},{2,3},{3,4},{4,5},{5,6},{6,7},{7,0},{8,9},{9,10},{10,1... | collective-permute-start | bytes 503816 | tf_op jit(solution)/shard_map/ppermute | solution.py:180
  79.5 8.4 %collective-permute-start.8 = (bf16[656,128]{1,0:T(8,128)(2,1)S(1)}, bf16[656,128]{1,0:T(8,128)(2,1)S(1)}, u32[]{:S(2)}, u32[]{:S(2)}) collective-permute-start(bf16[656,128]{1,0:T(8,128)(2,1)S(1)} %collective-permute-done.4.refs_1_), channel_id=1, source_target_pairs={{0,7},{1,0},{2,1},{3,2},{4,3},{5,4},{6,5},{7,6},{8,15},{9,8},{10,9... | collective-permute-start | bytes 503816 | tf_op jit(solution)/shard_map/ppermute | solution.py:181
  87.9 1.9 %copy-start.10 = (bf16[656,128]{1,0:T(8,128)(2,1)}, bf16[656,128]{1,0:T(8,128)(2,1)S(1)}, u32[]{:S(2)}) copy-start(bf16[656,128]{1,0:T(8,128)(2,1)S(1)} %collective-permute-done.7.refs_0_) | copy-start | bytes 503812
  87.9 2.0 %copy-start.11 = (bf16[656,128]{1,0:T(8,128)(2,1)}, bf16[656,128]{1,0:T(8,128)(2,1)S(1)}, u32[]{:S(2)}) copy-start(bf16[656,128]{1,0:T(8,128)(2,1)S(1)} %collective-permute-done.8.refs_1_) | copy-start | bytes 503812
  88.0 8.5 %collective-permute-start.9 = (bf16[656,128]{1,0:T(8,128)(2,1)S(1)}, bf16[656,128]{1,0:T(8,128)(2,1)S(1)}, u32[]{:S(2)}, u32[]{:S(2)}) collective-permute-start(bf16[656,128]{1,0:T(8,128)(2,1)S(1)} %collective-permute-done.7.refs_0_), channel_id=1, source_target_pairs={{0,1},{1,2},{2,3},{3,4},{4,5},{5,6},{6,7},{7,0},{8,9},{9,10},{10,1... | collective-permute-start | bytes 503816 | tf_op jit(solution)/shard_map/ppermute | solution.py:184
  96.5 0.7 copy-start.12
  99.7 3.9 %copy-start.1 = (bf16[32,128,128]{2,1,0:T(8,128)(2,1)}, bf16[32,128,128]{2,1,0:T(8,128)(2,1)S(1)}, u32[]{:S(2)}) copy-start(bf16[32,128,128]{2,1,0:T(8,128)(2,1)S(1)} %all-to-all-done.right_ref) | copy-start | bytes 3145732
  99.7 6.9 %collective-permute-start.10 = (bf16[32,128,128]{2,1,0:T(8,128)(2,1)S(1)}, bf16[32,128,128]{2,1,0:T(8,128)(2,1)}, u32[]{:S(2)}, u32[]{:S(2)}) collective-permute-start(bf16[32,128,128]{2,1,0:T(8,128)(2,1)S(1)} %all-to-all-done.right_ref), channel_id=1, source_target_pairs={{0,8},{8,0},{16,24},{24,16},{32,40},{40,32},{48,56},{56,48},{64,72... | collective-permute-start | bytes 3145736 | tf_op jit(solution)/shard_map/ppermute | solution.py:191
  109.9 29.2 %all-to-all-start.1 = ((bf16[16,128,128]{2,1,0:T(8,128)(2,1)}), bf16[16,128,128]{2,1,0:T(8,128)(2,1)S(1)}, u32[]{:S(2)}, u32[]{:S(2)}) async-start(bf16[16,128,128]{2,1,0:T(8,128)(2,1)} %shard_map.70), calls=%async_computation.1 | async-start | bytes 1048576 | tf_op jit(solution)/shard_map/all_to_all | solution.py:212

commit v3 on v1

v3 whole, which is shorter than its diff:
```python
import functools

import jax
import jax.numpy as jnp
from jax import lax
from jax.experimental import pallas as pl
from jax.experimental.pallas import tpu as pltpu
from jax.sharding import PartitionSpec as P

M = 128
LB = 5
NW = 8
G = 8
BOTH = ("sec", "term")
ROWS = LB * M
F32 = jnp.float32
BF16 = jnp.bfloat16
VMEM = pl.BlockSpec(memory_space=pltpu.VMEM)
SMEM = pl.BlockSpec(memory_space=pltpu.SMEM)
PARAMS = pltpu.CompilerParams(vmem_limit_bytes=56 * 1024 * 1024)


def together(*arrays):
    return lax.optimization_barrier(arrays)


def prepare(place_ref, shift_ref, psi_ref, env_ref, coupling_ref, allowed_ref, payload_ref, turned_ref, table_ref):
    for j in range(G):
        turned_ref[j * M : (j + 1) * M, :] = psi_ref[0, j].T
    s = place_ref[0]
    n_sec = allowed_ref.shape[0]
    payload_ref[:ROWS, :] = env_ref[...]
    table_ref[...] = jnp.zeros_like(table_ref)
    lane = lax.broadcasted_iota(jnp.int32, (1, M), 1)
    shifts = jnp.zeros((1, M), F32)
    for c in range(LB):
        shift = shift_ref[0, c]
        source = s + shift
        inside = jnp.logical_and(source >= 0, source < n_sec).astype(F32)
        kept = allowed_ref[pl.ds(jnp.clip(source, 0, n_sec - 1), 1), :].astype(F32) * inside
        factor = coupling_ref[c, pl.ds(s, 1), :] * kept
        high = factor.astype(BF16).astype(F32)
        middle = (factor - high).astype(BF16).astype(F32)
        low = (factor - high - middle).astype(BF16).astype(F32)
        table_ref[c : c + 1, :] = jnp.concatenate([high, middle], axis=1)
        table_ref[8 + c : 9 + c, :n_sec] = low
        shifts = jnp.where(lane == c, shift.astype(F32), shifts)
    table_ref[15:16, :] = shifts
    payload_ref[ROWS:, :] = table_ref[...].astype(BF16)


def left_products(t_ref, slots, below_ref, own_ref, above_ref, out_ref, psi_ref, factor_ref):
    for row, ref in enumerate((below_ref, own_ref, above_ref)):
        psi_ref[row] = ref[...]
    sector = lax.broadcasted_iota(jnp.int32, (M, G * M), 0)
    wanted = lax.broadcasted_iota(jnp.int32, (M, G * M), 1) // M + t_ref[0] * G
    pick = jnp.where((sector == wanted) | (sector == wanted + M // 2), 1.0, 0.0).astype(BF16)

    @pl.loop(0, NW)
    def _(w):
        table = slots[w, ROWS : ROWS + 16, :]
        spread = jnp.dot(table, pick, preferred_element_type=F32)
        factor_ref[...] = spread[:8] + spread[8:]
        shifts = table.astype(F32)[15:16, :]
        rows = [shifts[0, c].astype(jnp.int32) + 1 for c in range(LB)]
        envs = [slots[w, c * M : (c + 1) * M, :] for c in range(LB)]
        for start in range(0, G * M, 2 * M):
            totals = [None, None]
            for c in range(LB):
                product = lax.dot_general(
                    psi_ref[rows[c], start : start + 2 * M, :],
                    envs[c],
                    (((1,), (1,)), ((), ())),
                    preferred_element_type=F32,
                )
                for h in range(2):
                    at = start + h * M
                    term = product[h * M : (h + 1) * M] * factor_ref[c : c + 1, at : at + M]
                    totals[h] = term if totals[h] is None else totals[h] + term
            for h in range(2):
                at = start + h * M
                out_ref[w, at : at + M, :] = totals[h].astype(BF16)


def right_sum(j, i, partial_ref, right_ref, keep_ref):
    total = None
    for w in range(NW):
        product = jnp.dot(
            right_ref[w * (G // 2) + i],
            partial_ref[w, pl.ds(pl.multiple_of(j * M, M), M), :],
            preferred_element_type=F32,
        )
        total = product if total is None else total + product
    return (total * keep_ref[0, j]).T.astype(BF16)


def right_own(core_ref, keep_ref, right_ref, partial_ref, out_ref):
    core = core_ref[0]
    for i in range(G // 2):
        out_ref[i] = right_sum(2 * i + core, i, partial_ref, right_ref, keep_ref)


def right_other(core_ref, keep_ref, right_ref, own_ref, partial_ref, out_ref):
    core = core_ref[0]
    for i in range(G // 2):
        j = 2 * i + 1 - core
        value = right_sum(j, i, partial_ref, right_ref, keep_ref)
        out_ref[j] = value
        out_ref[G + j] = value
        mine = own_ref[i]
        out_ref[2 * i + core] = mine
        out_ref[G + 2 * i + core] = mine


def on_device(wavefunction, left_env, right_env, coupling, left_shift, allowed, *, n_sec, n_term):
    s, t = lax.axis_index("sec"), lax.axis_index("term")
    groups = n_sec // G

    def device(sec, term):
        return sec * n_term + term

    spread = [(device(b, w), device(w * G + b % G, b // G)) for b in range(n_sec) for w in range(n_term)]
    by_core = [[2 * chip + core for chip in range(n_sec // 2)] for core in range(2)]
    exchange = [
        [device(A * G + i, B) for i in range(G)] + [device(B * G + i, A) for i in range(G)]
        for A in range(groups)
        for B in range(A + 1, groups)
    ] + [
        [device(A * G + i, A) for i in range(G)] + [device((A + 1) * G + i, A + 1) for i in range(G)]
        for A in range(0, groups, 2)
    ]

    right = lax.ppermute(right_env[0], BOTH, spread)

    place = jnp.stack([s, t]).astype(jnp.int32)
    payload, own_psi = pl.pallas_call(
        prepare,
        grid_spec=pltpu.PrefetchScalarGridSpec(
            num_scalar_prefetch=2,
            grid=(1,),
            in_specs=[
                pl.BlockSpec((1, G, M, M), lambda i, place, shift: (0, place[1], 0, 0)),
                pl.BlockSpec((ROWS, M), lambda i, place, shift: (0, 0)),
                pl.BlockSpec(coupling.shape[1:], lambda i, place, shift: (0, 0, 0)),
                pl.BlockSpec(allowed.shape, lambda i, place, shift: (0, 0)),
            ],
            out_specs=[
                pl.BlockSpec((ROWS + 16, M), lambda i, place, shift: (0, 0)),
                pl.BlockSpec((G * M, M), lambda i, place, shift: (0, 0)),
            ],
            scratch_shapes=[pltpu.VMEM((16, M), F32)],
        ),
        out_shape=[jax.ShapeDtypeStruct((ROWS + 16, M), BF16), jax.ShapeDtypeStruct((G * M, M), BF16)],
        compiler_params=PARAMS,
    )(place, left_shift, wavefunction, left_env.reshape(ROWS, M), coupling[0], allowed)
    here = t.astype(jnp.int32)[None]

    payloads = lax.all_gather(payload, "term")
    below = lax.ppermute(own_psi, "sec", [(i, i + 1) for i in range(n_sec - 1)])
    above = lax.ppermute(own_psi, "sec", [(i + 1, i) for i in range(n_sec - 1)])
    right, below, above = together(right, below, above)
    halves = lax.all_to_all(
        jnp.tile(right, (n_sec // 2, 1, 1)), "sec", 0, 0, axis_index_groups=by_core, tiled=True
    )
    partial = pl.pallas_call(
        left_products,
        out_shape=jax.ShapeDtypeStruct((NW, G * M, M), BF16),
        in_specs=[SMEM] + [VMEM] * 4,
        out_specs=VMEM,
        scratch_shapes=[pltpu.VMEM((3, G * M, M), BF16), pltpu.VMEM((8, G * M), F32)],
        compiler_params=PARAMS,
        cost_estimate=pl.CostEstimate(flops=2 * 320 * M**3, bytes_accessed=5 << 20, transcendentals=0),
    )(here, payloads, below, own_psi, above)

    halves, partial = together(halves, partial)
    others = lax.ppermute(halves, "sec", [(i, i ^ 1) for i in range(n_sec)])
    core = lax.rem(s, 2).astype(jnp.int32)[None]
    keep = lax.dynamic_slice(allowed, (s, t * G), (1, G)).astype(F32)
    cost = pl.CostEstimate(flops=2 * 32 * M**3, bytes_accessed=2 << 20, transcendentals=0)
    own = pl.pallas_call(
        right_own,
        out_shape=jax.ShapeDtypeStruct((G // 2, M, M), BF16),
        in_specs=[SMEM, SMEM] + [VMEM] * 2,
        out_specs=VMEM,
        compiler_params=PARAMS,
        cost_estimate=cost,
    )(core, keep, halves, partial)
    results = pl.pallas_call(
        right_other,
        out_shape=jax.ShapeDtypeStruct((2 * G, M, M), BF16),
        in_specs=[SMEM, SMEM] + [VMEM] * 3,
        out_specs=VMEM,
        compiler_params=PARAMS,
        cost_estimate=cost,
    )(core, keep, others, own, partial)

    received = lax.all_to_all(results, BOTH, 0, 0, axis_index_groups=exchange, tiled=True)
    A = s // G
    first = jnp.where(A < t, G, jnp.where(A > t, 0, lax.rem(A, 2) * G))
    return lax.dynamic_slice_in_dim(received, first, G, 0)[:, None]


def solution(mesh):
    in_specs = (
        P("sec", None, None, None),
        P("term", None, "sec", None, None),
        P("term", "sec", None, None),
        P("term", None, None, None),
        P("term", None),
        P(),
    )
    body = functools.partial(on_device, n_sec=mesh.shape["sec"], n_term=mesh.shape["term"])
    return jax.shard_map(
        body, mesh=mesh, in_specs=in_specs, out_specs=P("term", "sec", None, None), check_vma=False
    )
```

time: 139 us -> 118 us (0.85)
  the two profiles are of different devices: /device:TPU:256 before, /device:TPU:4 now
where the time goes in v3:
time: 118 us
  starting transfers between devices  41.9 us (36%)
  waiting for transfers between devices  40.4 us (34%)
  Pallas kernels  17.1 us (14%)
  between operations  13.5 us (11%)
  local copies, waits for them, and re-layouts  2.92 us (2%)
  other arithmetic  1.95 us (2%)
    all_to_all x1, waiting for transfers between devices, on_device(): lax.all_to_all(results, BOTH, 0, 0, axis_index_groups=exchange, tiled=True)  18.5 us
    all_gather x1, waiting for transfers between devices, on_device(): payloads = lax.all_gather(payload, 'term')  15.5 us
    all_to_all x1, starting transfers between devices, on_device(): lax.all_to_all(results, BOTH, 0, 0, axis_index_groups=exchange, tiled=True)  12.7 us
    all_to_all x1, starting transfers between devices, on_device(): lax.all_to_all(jnp.tile(right, (n_sec // 2, 1, 1)), 'sec', 0, 0, axis_ind...  12.1 us
    ppermute x1, starting transfers between devices, on_device(): right = lax.ppermute(right_env[0], BOTH, spread)  8.49 us
    pallas_call x1, Pallas kernels, on_device(): pl.pallas_call(left_products, out_shape=jax.ShapeDtypeStruct((NW, G * M,...  8.01 us
    ppermute x1, starting transfers between devices, on_device(): above = lax.ppermute(own_psi, 'sec', [(i + 1, i) for i in range(n_sec - 1)])  4.79 us
    ppermute x1, waiting for transfers between devices, on_device(): right = lax.ppermute(right_env[0], BOTH, spread)  3.62 us
  transfers between devices with their start and end apart: 7, of which 4 were waited for; matrix products, arithmetic and copies ran while one was open for 2% of the time, Pallas kernels for 9%

profile of v3, /device:TPU:4, one launch (start us, length us, event | category | flops | bytes accessed | tf_op | source)
XLA Modules:
  0.0 117.7 jit_solution(10522350312648528275)
XLA Ops:
  6.5 0.0 copy-start.4
  6.5 0.0 all-gather.3.cloned.1.call-start
  6.5 0.6 pad_add_fusion.place_ref
  7.2 2.6 %shard_map.64 = (bf16[656,128]{1,0:T(8,128)(2,1)}, bf16[1024,128]{1,0:T(8,128)(2,1)}) custom-call(s32[2]{0:T(128)} %pad_add_fusion.place_ref, s32[1,5]{1,0:T(1,128)} %shift_ref.1, bf16[1,64,128,128]{3,2,1,0:T(8,128)(2,1)} %psi_ref.1, bf16[640,128]{1,0:T(8,128)(2,1)} %bitcast.10, f32[5,64,64]{2,1,0:T(8,128)} %bitcast.11, s32[64,64]{1,0:T(8,128)} %allowed_ref.1), custom_call_target="tpu_custom_call" | custom-call | tf_op jit(solution)/shard_map/pallas_call | solution.py:136
  9.8 0.0 all-gather.3.cloned.1.call-update
  9.8 4.8 %collective-permute-start.2 = (bf16[1024,128]{1,0:T(8,128)(2,1)}, bf16[1024,128]{1,0:T(8,128)(2,1)S(1)}, u32[]{:S(2)}, u32[]{:S(2)}) collective-permute-start(bf16[1024,128]{1,0:T(8,128)(2,1)} %get-tuple-element.12.own_ref), channel_id=1, source_target_pairs={{8,0},{16,8},{24,16},{32,24},{40,32},{48,40},{56,48},{64,56},{72,6... | collective-permute-start | bytes 786440 | tf_op jit(solution)/shard_map/ppermute | solution.py:160
  14.6 1.9 %collective-permute-start.1 = (bf16[1024,128]{1,0:T(8,128)(2,1)}, bf16[1024,128]{1,0:T(8,128)(2,1)S(1)}, u32[]{:S(2)}, u32[]{:S(2)}) collective-permute-start(bf16[1024,128]{1,0:T(8,128)(2,1)} %get-tuple-element.12.own_ref), channel_id=1, source_target_pairs={{0,8},{8,16},{16,24},{24,32},{32,40},{40,48},{48,56},{56,64},{64,7... | collective-permute-start | bytes 786440 | tf_op jit(solution)/shard_map/ppermute | solution.py:159
  16.6 0.0 copy-done.4
  16.6 8.5 %collective-permute-start = (bf16[1,128,128]{2,1,0:T(8,128)(2,1)S(1)}, bf16[1,128,128]{2,1,0:T(8,128)(2,1)S(1)}, u32[]{:S(2)}, u32[]{:S(2)}) collective-permute-start(bf16[1,128,128]{2,1,0:T(8,128)(2,1)S(1)} %bitcast.14), channel_id=1, source_target_pairs={{0,0},{1,64},{2,128},{3,192},{4,256},{5,320},{6,384},{7,448},{8,8}... | collective-permute-start | bytes 98312 | tf_op jit(solution)/shard_map/ppermute | solution.py:133
  25.1 3.6 %collective-permute-done = bf16[1,128,128]{2,1,0:T(8,128)(2,1)S(1)} collective-permute-done((bf16[1,128,128]{2,1,0:T(8,128)(2,1)S(1)}, bf16[1,128,128]{2,1,0:T(8,128)(2,1)S(1)}, u32[]{:S(2)}, u32[]{:S(2)}) %collective-permute-start) | collective-permute-done | bytes 32800 | tf_op jit(solution)/shard_map/ppermute | solution.py:133
  28.7 0.0 collective-permute-done.2.above_ref
  28.7 0.0 copy-start.2
  28.7 0.0 collective-permute-done.1.below_ref
  28.7 0.0 copy-start.3
  28.7 1.2 %tile.10 = bf16[32,128,128]{2,1,0:T(8,128)(2,1)} broadcast(bf16[128,128]{1,0:T(8,128)(2,1)S(1)} %bitcast.12), dimensions={1,2} | broadcast | bytes 1081344 | tf_op jit(solution)/shard_map/tile | solution.py:163
  29.9 12.1 %all-to-all-start = ((bf16[32,128,128]{2,1,0:T(8,128)(2,1)}), bf16[32,128,128]{2,1,0:T(8,128)(2,1)S(1)}, u32[]{:S(2)}, u32[]{:S(2)}) async-start(bf16[32,128,128]{2,1,0:T(8,128)(2,1)} %tile.10), calls=%async_computation | async-start | bytes 2097152 | tf_op jit(solution)/shard_map/all_to_all | solution.py:162
  42.0 15.5 %all-gather.3.cloned.1.call-done = bf16[5248,128]{1,0:T(8,128)(2,1)} async-done(((bf16[656,128]{1,0:T(8,128)(2,1)}), bf16[5248,128]{1,0:T(8,128)(2,1)}) %all-gather.3.cloned.1.call-update) | async-done | bytes 1343504 | tf_op jit(solution)/shard_map/all_gather | solution.py:158
  57.5 0.0 copy-done.2
  57.5 0.0 copy-done.3
  57.5 8.0 %shard_map.65.partial_ref = bf16[8,1024,128]{2,1,0:T(8,128)(2,1)} custom-call(s32[1]{0:T(128)} %bitcast.3.t_ref, bf16[8,656,128]{2,1,0:T(8,128)(2,1)} %bitcast.13, bf16[1024,128]{1,0:T(8,128)(2,1)} %copy-done.3, bf16[1024,128]{1,0:T(8,128)(2,1)} %get-tuple-element.12.own_ref, bf16[1024,128]{1,0:T(8,128)(2,1)} %copy-done.2), custom_call_target="tpu_custom_call" | custom-call | flops 1342177280 | bytes 5242880 | tf_op jit(solution)/shard_map/pallas_call | solution.py:165
  65.5 2.8 %all-to-all-done.right_ref = bf16[32,128,128]{2,1,0:T(8,128)(2,1)S(1)} async-done(((bf16[32,128,128]{2,1,0:T(8,128)(2,1)}), bf16[32,128,128]{2,1,0:T(8,128)(2,1)S(1)}, u32[]{:S(2)}, u32[]{:S(2)}) %all-to-all-start) | async-done | bytes 1048608 | tf_op jit(solution)/shard_map/all_to_all | solution.py:162
  68.3 0.0 copy-start
  68.3 1.9 %collective-permute-start.3 = (bf16[32,128,128]{2,1,0:T(8,128)(2,1)S(1)}, bf16[32,128,128]{2,1,0:T(8,128)(2,1)S(1)}, u32[]{:S(2)}, u32[]{:S(2)}) collective-permute-start(bf16[32,128,128]{2,1,0:T(8,128)(2,1)S(1)} %all-to-all-done.right_ref), channel_id=1, source_target_pairs={{0,8},{8,0},{16,24},{24,16},{32,40},{40,32},{48,56},{56,48},{64,72... | collective-permute-start | bytes 3145736 | tf_op jit(solution)/shard_map/ppermute | solution.py:176
  70.2 1.3 %dynamic-slice_convert_fusion.keep_ref = f32[1,8]{1,0:T(1,128)} fusion(s32[64,64]{1,0:T(8,128)} %allowed_ref.1, s32[]{:T(128)S(6)} %select_n.21, s32[]{:T(128)S(6)} %select_n.22), kind=kLoop, calls=%fused_computation.2 | loop fusion | flops 8 | bytes 72 | tf_op jit(solution)/shard_map/convert_element_type | solution.py:178
  71.5 0.0 copy-done
  71.5 3.1 %shard_map.66.own_ref = bf16[4,128,128]{2,1,0:T(8,128)(2,1)} custom-call(s32[1]{0:T(128)} %bitcast.core_ref, f32[1,8]{1,0:T(1,128)} %dynamic-slice_convert_fusion.keep_ref, bf16[32,128,128]{2,1,0:T(8,128)(2,1)} %copy-done, bf16[8,1024,128]{2,1,0:T(8,128)(2,1)} %shard_map.65.partial_ref), custom_call_target="tpu_custom_call" | custom-call | flops 134217728 | bytes 2097152 | tf_op jit(solution)/shard_map/pallas_call | solution.py:180
  74.6 0.0 collective-permute-done.3.right_ref
  74.6 0.0 copy-start.1
  74.6 1.0 copy-done.1
  75.6 3.3 %shard_map.67 = bf16[16,128,128]{2,1,0:T(8,128)(2,1)} custom-call(s32[1]{0:T(128)} %bitcast.core_ref, f32[1,8]{1,0:T(1,128)} %dynamic-slice_convert_fusion.keep_ref, bf16[32,128,128]{2,1,0:T(8,128)(2,1)} %copy-done.1, bf16[4,128,128]{2,1,0:T(8,128)(2,1)} %shard_map.66.own_ref, bf16[8,1024,128]{2,1,0:T(8,128)(2,1)} %shard_map.65.partial_ref), custom_call_target="tpu_custom_call" | custom-call | flops 134217728 | bytes 2097152 | tf_op jit(solution)/shard_map/pallas_call | solution.py:188
  78.9 12.7 %all-to-all-start.1 = ((bf16[16,128,128]{2,1,0:T(8,128)(2,1)}), bf16[16,128,128]{2,1,0:T(8,128)(2,1)S(1)}, u32[]{:S(2)}, u32[]{:S(2)}) async-start(bf16[16,128,128]{2,1,0:T(8,128)(2,1)} %shard_map.67), calls=%async_computation.1 | async-start | bytes 1048576 | tf_op jit(solution)/shard_map/all_to_all | solution.py:197
  91.6 18.5 %all-to-all-done.1 = bf16[16,128,128]{2,1,0:T(8,128)(2,1)S(1)} async-done(((bf16[16,128,128]{2,1,0:T(8,128)(2,1)}), bf16[16,128,128]{2,1,0:T(8,128)(2,1)S(1)}, u32[]{:S(2)}, u32[]{:S(2)}) %all-to-all-start.1) | async-done | bytes 524320 | tf_op jit(solution)/shard_map/all_to_all | solution.py:197
  110.1 0.7 dynamic-slice_bitcast_fusion
Async XLA Ops:
  6.5 10.0 %copy-start.4 = (bf16[1,1,128,128]{3,2,1,0:T(8,128)(2,1)S(1)}, bf16[1,1,128,128]{3,2,1,0:T(8,128)(2,1)}, u32[]{:S(2)}) copy-start(bf16[1,1,128,128]{3,2,1,0:T(8,128)(2,1)} %param.8) | copy-start | bytes 98308
  6.5 51.0 %all-gather.3.cloned.1.call-start = ((), (), s32[]{:S(2)}) async-start(), calls=%async_computation.2 | async-start | bytes 1511424 | tf_op jit(solution)/shard_map/all_gather | solution.py:158
  9.8 18.9 %collective-permute-start.2 = (bf16[1024,128]{1,0:T(8,128)(2,1)}, bf16[1024,128]{1,0:T(8,128)(2,1)S(1)}, u32[]{:S(2)}, u32[]{:S(2)}) collective-permute-start(bf16[1024,128]{1,0:T(8,128)(2,1)} %get-tuple-element.12.own_ref), channel_id=1, source_target_pairs={{8,0},{16,8},{24,16},{32,24},{40,32},{48,40},{56,48},{64,56},{72,6... | collective-permute-start | bytes 786440 | tf_op jit(solution)/shard_map/ppermute | solution.py:160
  14.6 14.1 %collective-permute-start.1 = (bf16[1024,128]{1,0:T(8,128)(2,1)}, bf16[1024,128]{1,0:T(8,128)(2,1)S(1)}, u32[]{:S(2)}, u32[]{:S(2)}) collective-permute-start(bf16[1024,128]{1,0:T(8,128)(2,1)} %get-tuple-element.12.own_ref), channel_id=1, source_target_pairs={{0,8},{8,16},{16,24},{24,32},{32,40},{40,48},{48,56},{56,64},{64,7... | collective-permute-start | bytes 786440 | tf_op jit(solution)/shard_map/ppermute | solution.py:159
  16.6 12.1 %collective-permute-start = (bf16[1,128,128]{2,1,0:T(8,128)(2,1)S(1)}, bf16[1,128,128]{2,1,0:T(8,128)(2,1)S(1)}, u32[]{:S(2)}, u32[]{:S(2)}) collective-permute-start(bf16[1,128,128]{2,1,0:T(8,128)(2,1)S(1)} %bitcast.14), channel_id=1, source_target_pairs={{0,0},{1,64},{2,128},{3,192},{4,256},{5,320},{6,384},{7,448},{8,8}... | collective-permute-start | bytes 98312 | tf_op jit(solution)/shard_map/ppermute | solution.py:133
  28.7 28.8 %copy-start.2 = (bf16[1024,128]{1,0:T(8,128)(2,1)}, bf16[1024,128]{1,0:T(8,128)(2,1)S(1)}, u32[]{:S(2)}) copy-start(bf16[1024,128]{1,0:T(8,128)(2,1)S(1)} %collective-permute-done.2.above_ref) | copy-start | bytes 786436
  28.7 28.8 %copy-start.3 = (bf16[1024,128]{1,0:T(8,128)(2,1)}, bf16[1024,128]{1,0:T(8,128)(2,1)S(1)}, u32[]{:S(2)}) copy-start(bf16[1024,128]{1,0:T(8,128)(2,1)S(1)} %collective-permute-done.1.below_ref) | copy-start | bytes 786436
  29.9 38.4 %all-to-all-start = ((bf16[32,128,128]{2,1,0:T(8,128)(2,1)}), bf16[32,128,128]{2,1,0:T(8,128)(2,1)S(1)}, u32[]{:S(2)}, u32[]{:S(2)}) async-start(bf16[32,128,128]{2,1,0:T(8,128)(2,1)} %tile.10), calls=%async_computation | async-start | bytes 2097152 | tf_op jit(solution)/shard_map/all_to_all | solution.py:162
  68.3 3.2 %copy-start = (bf16[32,128,128]{2,1,0:T(8,128)(2,1)}, bf16[32,128,128]{2,1,0:T(8,128)(2,1)S(1)}, u32[]{:S(2)}) copy-start(bf16[32,128,128]{2,1,0:T(8,128)(2,1)S(1)} %all-to-all-done.right_ref) | copy-start | bytes 3145732
  68.3 6.3 %collective-permute-start.3 = (bf16[32,128,128]{2,1,0:T(8,128)(2,1)S(1)}, bf16[32,128,128]{2,1,0:T(8,128)(2,1)S(1)}, u32[]{:S(2)}, u32[]{:S(2)}) collective-permute-start(bf16[32,128,128]{2,1,0:T(8,128)(2,1)S(1)} %all-to-all-done.right_ref), channel_id=1, source_target_pairs={{0,8},{8,0},{16,24},{24,16},{32,40},{40,32},{48,56},{56,48},{64,72... | collective-permute-start | bytes 3145736 | tf_op jit(solution)/shard_map/ppermute | solution.py:176
  74.6 1.0 copy-start.1
  78.9 31.2 %all-to-all-start.1 = ((bf16[16,128,128]{2,1,0:T(8,128)(2,1)}), bf16[16,128,128]{2,1,0:T(8,128)(2,1)S(1)}, u32[]{:S(2)}, u32[]{:S(2)}) async-start(bf16[16,128,128]{2,1,0:T(8,128)(2,1)} %shard_map.67), calls=%async_computation.1 | async-start | bytes 1048576 | tf_op jit(solution)/shard_map/all_to_all | solution.py:197
Sparse Core Ops, SparseCore 0:
  9.9 47.5 all-gather.2

commit v4 on v3

--- a/solution.py
+++ b/solution.py
@@ -78,19 +78,12 @@
                     term = product[h * M : (h + 1) * M] * factor_ref[c : c + 1, at : at + M]
                     totals[h] = term if totals[h] is None else totals[h] + term
             for h in range(2):
-                at = start + h * M
-                out_ref[w, at : at + M, :] = totals[h].astype(BF16)
+                out_ref[start // M + h, pl.ds(pl.multiple_of(w * M, M), M), :] = totals[h].astype(BF16)
 
 
 def right_sum(j, i, partial_ref, right_ref, keep_ref):
-    total = None
-    for w in range(NW):
-        product = jnp.dot(
-            right_ref[w * (G // 2) + i],
-            partial_ref[w, pl.ds(pl.multiple_of(j * M, M), M), :],
-            preferred_element_type=F32,
-        )
-        total = product if total is None else total + product
+    right = jnp.concatenate([right_ref[w * (G // 2) + i] for w in range(NW)], axis=1)
+    total = jnp.dot(right, partial_ref[j], preferred_element_type=F32)
     return (total * keep_ref[0, j]).T.astype(BF16)
 
 
@@ -156,15 +149,15 @@
     here = t.astype(jnp.int32)[None]
 
     payloads = lax.all_gather(payload, "term")
+    right, own_psi = together(right, own_psi)
     below = lax.ppermute(own_psi, "sec", [(i, i + 1) for i in range(n_sec - 1)])
     above = lax.ppermute(own_psi, "sec", [(i + 1, i) for i in range(n_sec - 1)])
-    right, below, above = together(right, below, above)
     halves = lax.all_to_all(
         jnp.tile(right, (n_sec // 2, 1, 1)), "sec", 0, 0, axis_index_groups=by_core, tiled=True
     )
     partial = pl.pallas_call(
         left_products,
-        out_shape=jax.ShapeDtypeStruct((NW, G * M, M), BF16),
+        out_shape=jax.ShapeDtypeStruct((G, NW * M, M), BF16),
         in_specs=[SMEM] + [VMEM] * 4,
         out_specs=VMEM,
         scratch_shapes=[pltpu.VMEM((3, G * M, M), BF16), pltpu.VMEM((8, G * M), F32)],

time: 118 us -> 122 us (1.034)
  the two profiles are of different devices: /device:TPU:4 before, /device:TPU:7 now
where the time goes in v4:
time: 122 us
  starting transfers between devices  45.3 us (37%)
  waiting for transfers between devices  40.4 us (33%)
  Pallas kernels  17 us (14%)
  between operations  13.5 us (11%)
  local copies, waits for them, and re-layouts  3.69 us (3%)
  other arithmetic  1.97 us (2%)
    ppermute x1, waiting for transfers between devices, on_device(): above = lax.ppermute(own_psi, 'sec', [(i + 1, i) for i in range(n_sec - 1)])  20.5 us
    all_to_all x1, waiting for transfers between devices, on_device(): lax.all_to_all(results, BOTH, 0, 0, axis_index_groups=exchange, tiled=True)  18.2 us
    all_to_all x1, starting transfers between devices, on_device(): lax.all_to_all(jnp.tile(right, (n_sec // 2, 1, 1)), 'sec', 0, 0, axis_ind...  12.4 us
    all_to_all x1, starting transfers between devices, on_device(): lax.all_to_all(results, BOTH, 0, 0, axis_index_groups=exchange, tiled=True)  11.3 us
    ppermute x1, starting transfers between devices, on_device(): right = lax.ppermute(right_env[0], BOTH, spread)  10.7 us
    pallas_call x1, Pallas kernels, on_device(): pl.pallas_call(left_products, out_shape=jax.ShapeDtypeStruct((G, NW * M,...  8.03 us
    ppermute x1, starting transfers between devices, on_device(): above = lax.ppermute(own_psi, 'sec', [(i + 1, i) for i in range(n_sec - 1)])  4.29 us
    ppermute x1, starting transfers between devices, on_device(): others = lax.ppermute(halves, 'sec', [(i, i ^ 1) for i in range(n_sec)])  3.63 us
  transfers between devices with their start and end apart: 7, of which 3 were waited for; matrix products, arithmetic and copies ran while one was open for 2% of the time, Pallas kernels for 9%

profile of v4, /device:TPU:7, one launch (start us, length us, event | category | flops | bytes accessed | tf_op | source)
XLA Modules:
  0.0 121.8 jit_solution(8493923072550010957)
XLA Ops:
  6.5 0.0 copy-start.5
  6.5 0.0 all-gather.3.cloned.1.call-start
  6.5 0.7 pad_add_fusion.place_ref
  7.2 2.6 %shard_map.64 = (bf16[656,128]{1,0:T(8,128)(2,1)}, bf16[1024,128]{1,0:T(8,128)(2,1)}) custom-call(s32[2]{0:T(128)} %pad_add_fusion.place_ref, s32[1,5]{1,0:T(1,128)} %shift_ref.1, bf16[1,64,128,128]{3,2,1,0:T(8,128)(2,1)} %psi_ref.1, bf16[640,128]{1,0:T(8,128)(2,1)} %bitcast.10, f32[5,64,64]{2,1,0:T(8,128)} %bitcast.11, s32[64,64]{1,0:T(8,128)} %allowed_ref.1), custom_call_target="tpu_custom_call" | custom-call | tf_op jit(solution)/shard_map/pallas_call | solution.py:129
  9.8 0.0 copy-start.2
  9.8 0.0 all-gather.3.cloned.1.call-update
  9.8 0.0 copy-done.5
  9.9 10.7 %collective-permute-start = (bf16[1,128,128]{2,1,0:T(8,128)(2,1)S(1)}, bf16[1,128,128]{2,1,0:T(8,128)(2,1)S(1)}, u32[]{:S(2)}, u32[]{:S(2)}) collective-permute-start(bf16[1,128,128]{2,1,0:T(8,128)(2,1)S(1)} %bitcast.14), channel_id=1, source_target_pairs={{0,0},{1,64},{2,128},{3,192},{4,256},{5,320},{6,384},{7,448},{8,8}... | collective-permute-start | bytes 98312 | tf_op jit(solution)/shard_map/ppermute | solution.py:126
  20.6 1.6 %collective-permute-done = bf16[1,128,128]{2,1,0:T(8,128)(2,1)S(1)} collective-permute-done((bf16[1,128,128]{2,1,0:T(8,128)(2,1)S(1)}, bf16[1,128,128]{2,1,0:T(8,128)(2,1)S(1)}, u32[]{:S(2)}, u32[]{:S(2)}) %collective-permute-start) | collective-permute-done | bytes 32800 | tf_op jit(solution)/shard_map/ppermute | solution.py:126
  22.2 1.2 tile.10
  23.4 12.4 %all-to-all-start = ((bf16[32,128,128]{2,1,0:T(8,128)(2,1)}), bf16[32,128,128]{2,1,0:T(8,128)(2,1)S(1)}, u32[]{:S(2)}, u32[]{:S(2)}) async-start(bf16[32,128,128]{2,1,0:T(8,128)(2,1)} %tile.10), calls=%async_computation | async-start | bytes 2097152 | tf_op jit(solution)/shard_map/all_to_all | solution.py:155
  35.8 0.0 copy-done.2
  35.8 4.3 %collective-permute-start.2 = (bf16[1024,128]{1,0:T(8,128)(2,1)S(1)}, bf16[1024,128]{1,0:T(8,128)(2,1)S(1)}, u32[]{:S(2)}, u32[]{:S(2)}) collective-permute-start(bf16[1024,128]{1,0:T(8,128)(2,1)S(1)} %copy-done.2), channel_id=1, source_target_pairs={{8,0},{16,8},{24,16},{32,24},{40,32},{48,40},{56,48},{64,56},{72,6... | collective-permute-start | bytes 786440 | tf_op jit(solution)/shard_map/ppermute | solution.py:154
  40.1 3.0 %collective-permute-start.1 = (bf16[1024,128]{1,0:T(8,128)(2,1)S(1)}, bf16[1024,128]{1,0:T(8,128)(2,1)S(1)}, u32[]{:S(2)}, u32[]{:S(2)}) collective-permute-start(bf16[1024,128]{1,0:T(8,128)(2,1)S(1)} %copy-done.2), channel_id=1, source_target_pairs={{0,8},{8,16},{16,24},{24,32},{32,40},{40,48},{48,56},{56,64},{64,7... | collective-permute-start | bytes 786440 | tf_op jit(solution)/shard_map/ppermute | solution.py:153
  43.1 20.5 %collective-permute-done.2.above_ref = bf16[1024,128]{1,0:T(8,128)(2,1)S(1)} collective-permute-done((bf16[1024,128]{1,0:T(8,128)(2,1)S(1)}, bf16[1024,128]{1,0:T(8,128)(2,1)S(1)}, u32[]{:S(2)}, u32[]{:S(2)}) %collective-permute-start.2) | collective-permute-done | bytes 262176 | tf_op jit(solution)/shard_map/ppermute | solution.py:154
  63.6 0.0 copy-start.3
  63.6 0.0 collective-permute-done.1.below_ref
  63.6 0.0 copy-start.4
  63.6 0.0 all-gather.3.cloned.1.call-done
  63.6 0.7 copy-done.3
  64.3 0.1 copy-done.4
  64.4 8.0 %shard_map.65.partial_ref = bf16[8,1024,128]{2,1,0:T(8,128)(2,1)} custom-call(s32[1]{0:T(128)} %bitcast.3.t_ref, bf16[8,656,128]{2,1,0:T(8,128)(2,1)} %bitcast.13, bf16[1024,128]{1,0:T(8,128)(2,1)} %copy-done.4, bf16[1024,128]{1,0:T(8,128)(2,1)} %get-tuple-element.14.own_ref, bf16[1024,128]{1,0:T(8,128)(2,1)} %copy-done.3), custom_call_target="tpu_custom_call" | custom-call | flops 1342177280 | bytes 5242880 | tf_op jit(solution)/shard_map/pallas_call | solution.py:158
  72.5 0.0 all-to-all-done.right_ref
  72.5 0.0 copy-start
  72.5 3.6 %collective-permute-start.3 = (bf16[32,128,128]{2,1,0:T(8,128)(2,1)S(1)}, bf16[32,128,128]{2,1,0:T(8,128)(2,1)S(1)}, u32[]{:S(2)}, u32[]{:S(2)}) collective-permute-start(bf16[32,128,128]{2,1,0:T(8,128)(2,1)S(1)} %all-to-all-done.right_ref), channel_id=1, source_target_pairs={{0,8},{8,0},{16,24},{24,16},{32,40},{40,32},{48,56},{56,48},{64,72... | collective-permute-start | bytes 3145736 | tf_op jit(solution)/shard_map/ppermute | solution.py:169
  76.1 1.3 %dynamic-slice_convert_fusion.keep_ref = f32[1,8]{1,0:T(1,128)} fusion(s32[64,64]{1,0:T(8,128)} %allowed_ref.1, s32[]{:T(128)S(6)} %select_n.21, s32[]{:T(128)S(6)} %select_n.22), kind=kLoop, calls=%fused_computation.2 | loop fusion | flops 8 | bytes 72 | tf_op jit(solution)/shard_map/convert_element_type | solution.py:171
  77.4 0.0 copy-done
  77.4 3.1 %shard_map.66.own_ref = bf16[4,128,128]{2,1,0:T(8,128)(2,1)} custom-call(s32[1]{0:T(128)} %bitcast.core_ref, f32[1,8]{1,0:T(1,128)} %dynamic-slice_convert_fusion.keep_ref, bf16[32,128,128]{2,1,0:T(8,128)(2,1)} %copy-done, bf16[8,1024,128]{2,1,0:T(8,128)(2,1)} %shard_map.65.partial_ref), custom_call_target="tpu_custom_call" | custom-call | flops 134217728 | bytes 2097152 | tf_op jit(solution)/shard_map/pallas_call | solution.py:173
  80.5 0.0 collective-permute-done.3.right_ref
  80.5 0.0 copy-start.1
  80.5 1.0 copy-done.1
  81.5 3.3 %shard_map.67 = bf16[16,128,128]{2,1,0:T(8,128)(2,1)} custom-call(s32[1]{0:T(128)} %bitcast.core_ref, f32[1,8]{1,0:T(1,128)} %dynamic-slice_convert_fusion.keep_ref, bf16[32,128,128]{2,1,0:T(8,128)(2,1)} %copy-done.1, bf16[4,128,128]{2,1,0:T(8,128)(2,1)} %shard_map.66.own_ref, bf16[8,1024,128]{2,1,0:T(8,128)(2,1)} %shard_map.65.partial_ref), custom_call_target="tpu_custom_call" | custom-call | flops 134217728 | bytes 2097152 | tf_op jit(solution)/shard_map/pallas_call | solution.py:181
  84.8 11.3 %all-to-all-start.1 = ((bf16[16,128,128]{2,1,0:T(8,128)(2,1)}), bf16[16,128,128]{2,1,0:T(8,128)(2,1)S(1)}, u32[]{:S(2)}, u32[]{:S(2)}) async-start(bf16[16,128,128]{2,1,0:T(8,128)(2,1)} %shard_map.67), calls=%async_computation.1 | async-start | bytes 1048576 | tf_op jit(solution)/shard_map/all_to_all | solution.py:190
  96.1 18.2 %all-to-all-done.1 = bf16[16,128,128]{2,1,0:T(8,128)(2,1)S(1)} async-done(((bf16[16,128,128]{2,1,0:T(8,128)(2,1)}), bf16[16,128,128]{2,1,0:T(8,128)(2,1)S(1)}, u32[]{:S(2)}, u32[]{:S(2)}) %all-to-all-start.1) | async-done | bytes 524320 | tf_op jit(solution)/shard_map/all_to_all | solution.py:190
  114.3 0.7 dynamic-slice_bitcast_fusion
Async XLA Ops:
  6.5 3.3 %copy-start.5 = (bf16[1,1,128,128]{3,2,1,0:T(8,128)(2,1)S(1)}, bf16[1,1,128,128]{3,2,1,0:T(8,128)(2,1)}, u32[]{:S(2)}) copy-start(bf16[1,1,128,128]{3,2,1,0:T(8,128)(2,1)} %param.8) | copy-start | bytes 98308
  6.5 57.1 %all-gather.3.cloned.1.call-start = ((), (), s32[]{:S(2)}) async-start(), calls=%async_computation.2 | async-start | bytes 1511424 | tf_op jit(solution)/shard_map/all_gather | solution.py:151
  9.8 25.9 %copy-start.2 = (bf16[1024,128]{1,0:T(8,128)(2,1)S(1)}, bf16[1024,128]{1,0:T(8,128)(2,1)}, u32[]{:S(2)}) copy-start(bf16[1024,128]{1,0:T(8,128)(2,1)} %get-tuple-element.14.own_ref) | copy-start | bytes 786436
  9.9 12.3 %collective-permute-start = (bf16[1,128,128]{2,1,0:T(8,128)(2,1)S(1)}, bf16[1,128,128]{2,1,0:T(8,128)(2,1)S(1)}, u32[]{:S(2)}, u32[]{:S(2)}) collective-permute-start(bf16[1,128,128]{2,1,0:T(8,128)(2,1)S(1)} %bitcast.14), channel_id=1, source_target_pairs={{0,0},{1,64},{2,128},{3,192},{4,256},{5,320},{6,384},{7,448},{8,8}... | collective-permute-start | bytes 98312 | tf_op jit(solution)/shard_map/ppermute | solution.py:126
  23.4 49.1 %all-to-all-start = ((bf16[32,128,128]{2,1,0:T(8,128)(2,1)}), bf16[32,128,128]{2,1,0:T(8,128)(2,1)S(1)}, u32[]{:S(2)}, u32[]{:S(2)}) async-start(bf16[32,128,128]{2,1,0:T(8,128)(2,1)} %tile.10), calls=%async_computation | async-start | bytes 2097152 | tf_op jit(solution)/shard_map/all_to_all | solution.py:155
  35.8 27.8 %collective-permute-start.2 = (bf16[1024,128]{1,0:T(8,128)(2,1)S(1)}, bf16[1024,128]{1,0:T(8,128)(2,1)S(1)}, u32[]{:S(2)}, u32[]{:S(2)}) collective-permute-start(bf16[1024,128]{1,0:T(8,128)(2,1)S(1)} %copy-done.2), channel_id=1, source_target_pairs={{8,0},{16,8},{24,16},{32,24},{40,32},{48,40},{56,48},{64,56},{72,6... | collective-permute-start | bytes 786440 | tf_op jit(solution)/shard_map/ppermute | solution.py:154
  40.1 23.5 %collective-permute-start.1 = (bf16[1024,128]{1,0:T(8,128)(2,1)S(1)}, bf16[1024,128]{1,0:T(8,128)(2,1)S(1)}, u32[]{:S(2)}, u32[]{:S(2)}) collective-permute-start(bf16[1024,128]{1,0:T(8,128)(2,1)S(1)} %copy-done.2), channel_id=1, source_target_pairs={{0,8},{8,16},{16,24},{24,32},{32,40},{40,48},{48,56},{56,64},{64,7... | collective-permute-start | bytes 786440 | tf_op jit(solution)/shard_map/ppermute | solution.py:153
  63.6 0.7 copy-start.3
  63.6 0.8 copy-start.4
  72.5 5.0 %copy-start = (bf16[32,128,128]{2,1,0:T(8,128)(2,1)}, bf16[32,128,128]{2,1,0:T(8,128)(2,1)S(1)}, u32[]{:S(2)}) copy-start(bf16[32,128,128]{2,1,0:T(8,128)(2,1)S(1)} %all-to-all-done.right_ref) | copy-start | bytes 3145732
  72.5 8.0 %collective-permute-start.3 = (bf16[32,128,128]{2,1,0:T(8,128)(2,1)S(1)}, bf16[32,128,128]{2,1,0:T(8,128)(2,1)S(1)}, u32[]{:S(2)}, u32[]{:S(2)}) collective-permute-start(bf16[32,128,128]{2,1,0:T(8,128)(2,1)S(1)} %all-to-all-done.right_ref), channel_id=1, source_target_pairs={{0,8},{8,0},{16,24},{24,16},{32,40},{40,32},{48,56},{56,48},{64,72... | collective-permute-start | bytes 3145736 | tf_op jit(solution)/shard_map/ppermute | solution.py:169
  80.5 1.0 copy-start.1
  84.8 29.5 %all-to-all-start.1 = ((bf16[16,128,128]{2,1,0:T(8,128)(2,1)}), bf16[16,128,128]{2,1,0:T(8,128)(2,1)S(1)}, u32[]{:S(2)}, u32[]{:S(2)}) async-start(bf16[16,128,128]{2,1,0:T(8,128)(2,1)} %shard_map.67), calls=%async_computation.1 | async-start | bytes 1048576 | tf_op jit(solution)/shard_map/all_to_all | solution.py:190
Sparse Core Ops, SparseCore 0:
  10.0 42.8 all-gather.2

commit v5 on v4

v5 whole, which is shorter than its diff:
```python
import functools

import jax
import jax.numpy as jnp
from jax import lax
from jax.experimental import pallas as pl
from jax.experimental.pallas import tpu as pltpu
from jax.sharding import PartitionSpec as P

M = 128
LB = 5
NW = 8
G = 8
H = G // 2
BOTH = ("sec", "term")
ROWS = LB * M
F32 = jnp.float32
BF16 = jnp.bfloat16
VMEM = pl.BlockSpec(memory_space=pltpu.VMEM)
SMEM = pl.BlockSpec(memory_space=pltpu.SMEM)
PARAMS = pltpu.CompilerParams(vmem_limit_bytes=56 * 1024 * 1024)


def together(*arrays):
    return lax.optimization_barrier(arrays)


def right_chip(t, w, i):
    return w // 2 * G + (t % 2 * H + 2 * i + w % 2 + G - 2) % G


def prepare(place_ref, shift_ref, psi_ref, env_ref, coupling_ref, allowed_ref, payload_ref, turned_ref, table_ref):
    s = place_ref[0]
    core = lax.rem(s, 2)
    for i in range(H):
        turned_ref[i * M : (i + 1) * M, :] = psi_ref[0, 2 * i + core].T
        turned_ref[(H + i) * M : (H + i + 1) * M, :] = psi_ref[0, 2 * i + 1 - core].T
    n_sec = allowed_ref.shape[0]
    payload_ref[:ROWS, :] = env_ref[...]
    table_ref[...] = jnp.zeros_like(table_ref)
    lane = lax.broadcasted_iota(jnp.int32, (1, M), 1)
    shifts = jnp.zeros((1, M), F32)
    for c in range(LB):
        shift = shift_ref[0, c]
        source = s + shift
        inside = jnp.logical_and(source >= 0, source < n_sec).astype(F32)
        kept = allowed_ref[pl.ds(jnp.clip(source, 0, n_sec - 1), 1), :].astype(F32) * inside
        factor = coupling_ref[c, pl.ds(s, 1), :] * kept
        high = factor.astype(BF16).astype(F32)
        middle = (factor - high).astype(BF16).astype(F32)
        low = (factor - high - middle).astype(BF16).astype(F32)
        table_ref[c : c + 1, :] = jnp.concatenate([high, middle], axis=1)
        table_ref[8 + c : 9 + c, :n_sec] = low
        shifts = jnp.where(lane == c, shift.astype(F32), shifts)
    table_ref[15:16, :] = shifts
    payload_ref[ROWS:, :] = table_ref[...].astype(BF16)


def left_products(first_row, place_ref, slots, *refs):
    near_ref, turned_ref, inner_ref, far_ref, out_ref, psi_ref, factor_ref = refs
    psi_ref[0] = near_ref[H * M :, :]
    psi_ref[1] = turned_ref[: H * M, :]
    psi_ref[2] = inner_ref[...]
    psi_ref[3] = far_ref[...]
    s, t = place_ref[0], place_ref[1]
    core = lax.rem(s, 2)
    sector = lax.broadcasted_iota(jnp.int32, (M, H * M), 0)
    wanted = lax.broadcasted_iota(jnp.int32, (M, H * M), 1) // M * 2 + t * G + core
    pick = jnp.where((sector == wanted) | (sector == wanted + M // 2), 1.0, 0.0).astype(BF16)

    @pl.loop(0, NW)
    def _(w):
        table = slots[w, ROWS : ROWS + 16, :]
        spread = jnp.dot(table, pick, preferred_element_type=F32)
        factor_ref[...] = spread[:8] + spread[8:]
        shifts = table.astype(F32)[15:16, :]
        rows = [first_row + shifts[0, c].astype(jnp.int32) * (1 - 2 * core) for c in range(LB)]
        envs = [slots[w, c * M : (c + 1) * M, :] for c in range(LB)]
        for start in range(0, H * M, 2 * M):
            totals = [None, None]
            for c in range(LB):
                product = lax.dot_general(
                    psi_ref[rows[c], start : start + 2 * M, :],
                    envs[c],
                    (((1,), (1,)), ((), ())),
                    preferred_element_type=F32,
                )
                for h in range(2):
                    at = start + h * M
                    term = product[h * M : (h + 1) * M] * factor_ref[c : c + 1, at : at + M]
                    totals[h] = term if totals[h] is None else totals[h] + term
            for h in range(2):
                out_ref[start // M + h, pl.ds(pl.multiple_of(w * M, M), M), :] = totals[h].astype(BF16)


def right_products(place_ref, allowed_ref, right_ref, own_ref, other_ref, out_ref):
    s, t = place_ref[0], place_ref[1]
    core = lax.rem(s, 2)
    for i in range(H):
        right = jnp.concatenate([right_ref[right_chip(t, w, i)] for w in range(NW)], axis=1)
        for partial_ref, which in ((own_ref, core), (other_ref, 1 - core)):
            total = jnp.dot(right, partial_ref[i], preferred_element_type=F32)
            keep = allowed_ref[s - core + which, t * G + 2 * i + core].astype(F32)
            value = (total * keep).T.astype(BF16)
            out_ref[i, which] = value
            out_ref[H + i, which] = value


def on_device(wavefunction, left_env, right_env, coupling, left_shift, allowed, *, n_sec, n_term):
    s, t = lax.axis_index("sec"), lax.axis_index("term")
    groups = n_sec // G

    def device(sec, term):
        return sec * n_term + term

    spread = [
        (device(b, w), device(2 * right_chip(b // G, w, b % G // 2) + b % 2, b // G))
        for b in range(n_sec)
        for w in range(n_term)
    ]
    by_core = [[2 * chip + core for chip in range(n_sec // 2)] for core in range(2)]
    exchange = []
    for core in range(2):

        def members(A, B):
            return [device(A * G + 2 * i + core, B) for i in range(H)]

        exchange += [members(A, B) + members(B, A) for A in range(groups) for B in range(A + 1, groups)]
        exchange += [members(A, A) + members(A + 1, A + 1) for A in range(0, groups, 2)]

    right = lax.ppermute(right_env[0], BOTH, spread)
    place = jnp.stack([s, t]).astype(jnp.int32)
    payload, turned = pl.pallas_call(
        prepare,
        grid_spec=pltpu.PrefetchScalarGridSpec(
            num_scalar_prefetch=2,
            grid=(1,),
            in_specs=[
                pl.BlockSpec((1, G, M, M), lambda i, place, shift: (0, place[1], 0, 0)),
                pl.BlockSpec((ROWS, M), lambda i, place, shift: (0, 0)),
                pl.BlockSpec(coupling.shape[1:], lambda i, place, shift: (0, 0, 0)),
                pl.BlockSpec(allowed.shape, lambda i, place, shift: (0, 0)),
            ],
            out_specs=[
                pl.BlockSpec((ROWS + 16, M), lambda i, place, shift: (0, 0)),
                pl.BlockSpec((G * M, M), lambda i, place, shift: (0, 0)),
            ],
            scratch_shapes=[pltpu.VMEM((16, M), F32)],
        ),
        out_shape=[jax.ShapeDtypeStruct((ROWS + 16, M), BF16), jax.ShapeDtypeStruct((G * M, M), BF16)],
        compiler_params=PARAMS,
    )(place, left_shift, wavefunction, left_env.reshape(ROWS, M), coupling[0], allowed)

    payloads = lax.all_gather(payload, "term")
    across = [(i, i ^ 1) for i in range(n_sec)]
    near = lax.ppermute(turned, "sec", [(i, i + 1) if i % 2 else (i, i - 1) for i in range(1, n_sec - 1)])
    right, near = together(right, near)
    inner = lax.ppermute(turned[H * M :], "sec", across)
    far = lax.ppermute(near[: H * M], "sec", across)
    right = lax.all_to_all(
        jnp.tile(right, (n_sec // 2, 1, 1)), "sec", 0, 0, axis_index_groups=by_core, tiled=True
    )
    payloads, inner, far = together(payloads, inner, far)
    other_payloads = lax.ppermute(payloads, "sec", across)

    def left_call(first_row, slots):
        return pl.pallas_call(
            functools.partial(left_products, first_row),
            out_shape=jax.ShapeDtypeStruct((H, NW * M, M), BF16),
            in_specs=[SMEM] + [VMEM] * 5,
            out_specs=VMEM,
            scratch_shapes=[pltpu.VMEM((4, H * M, M), BF16), pltpu.VMEM((8, H * M), F32)],
            compiler_params=PARAMS,
            cost_estimate=pl.CostEstimate(flops=2 * 160 * M**3, bytes_accessed=3 << 20, transcendentals=0),
        )(place, slots, near, turned, inner, far)

    own = left_call(1, payloads)
    other = left_call(2, other_payloads)
    right, other = together(right, other)
    results = pl.pallas_call(
        right_products,
        out_shape=jax.ShapeDtypeStruct((G, 2, M, M), BF16),
        in_specs=[SMEM, SMEM] + [VMEM] * 3,
        out_specs=VMEM,
        compiler_params=PARAMS,
        cost_estimate=pl.CostEstimate(flops=2 * 64 * M**3, bytes_accessed=4 << 20, transcendentals=0),
    )(place, allowed, right, own, other)

    received = lax.all_to_all(results, BOTH, 0, 0, axis_index_groups=exchange, tiled=True)
    A = s // G
    first = jnp.where(A < t, H, jnp.where(A > t, 0, lax.rem(A, 2) * H))
    return lax.dynamic_slice_in_dim(received, first, H, 0).reshape(G, 1, M, M)


def solution(mesh):
    in_specs = (
        P("sec", None, None, None),
        P("term", None, "sec", None, None),
        P("term", "sec", None, None),
        P("term", None, None, None),
        P("term", None),
        P(),
    )
    body = functools.partial(on_device, n_sec=mesh.shape["sec"], n_term=mesh.shape["term"])
    return jax.shard_map(
        body, mesh=mesh, in_specs=in_specs, out_specs=P("term", "sec", None, None), check_vma=False
    )
```

time: 122 us -> 115 us (0.943)
  the two profiles are of different devices: /device:TPU:7 before, /device:TPU:4 now
where the time goes in v5:
time: 115 us
  starting transfers between devices  44.2 us (38%)
  waiting for transfers between devices  34.5 us (30%)
  Pallas kernels  18.2 us (16%)
  between operations  13.5 us (12%)
  local copies, waits for them, and re-layouts  4.03 us (4%)
    all_to_all x1, waiting for transfers between devices, on_device(): lax.all_to_all(results, BOTH, 0, 0, axis_index_groups=exchange, tiled=True)  18 us
    all_gather x1, waiting for transfers between devices, on_device(): payloads = lax.all_gather(payload, 'term')  13.6 us
    ppermute x1, starting transfers between devices, on_device(): right = lax.ppermute(right_env[0], BOTH, spread)  12.5 us
    all_to_all x1, starting transfers between devices, on_device(): lax.all_to_all(results, BOTH, 0, 0, axis_index_groups=exchange, tiled=True)  12.3 us
    pallas_call x2, Pallas kernels, left_call(): pl.pallas_call(functools.partial(left_products, first_row), out_shape=jax...  12.1 us
    all_to_all x1, starting transfers between devices, on_device(): lax.all_to_all(jnp.tile(right, (n_sec // 2, 1, 1)), 'sec', 0, 0, axis_ind...  7.91 us
    ppermute x1, starting transfers between devices, on_device(): lax.ppermute(turned, 'sec', [(i, i + 1) if i % 2 else (i, i - 1) for i in...  4.79 us
    pallas_call x1, Pallas kernels, on_device(): pl.pallas_call(right_products, out_shape=jax.ShapeDtypeStruct((G, 2, M, M...  3.45 us
  transfers between devices with their start and end apart: 8, of which 4 were waited for; matrix products, arithmetic and copies ran while one was open for 1% of the time, Pallas kernels for 11%

profile of v5, /device:TPU:4, one launch (start us, length us, event | category | flops | bytes accessed | tf_op | source)
XLA Modules:
  0.0 115.0 jit_solution(17477053209033194470)
XLA Ops:
  6.5 0.0 copy-start.6
  6.5 0.0 all-gather.3.cloned.1.call-start
  6.5 0.6 pad_add_fusion.place_ref
  7.1 2.6 %shard_map.64 = (bf16[656,128]{1,0:T(8,128)(2,1)}, bf16[1024,128]{1,0:T(8,128)(2,1)}) custom-call(s32[2]{0:T(128)} %pad_add_fusion.place_ref, s32[1,5]{1,0:T(1,128)} %shift_ref.1, bf16[1,64,128,128]{3,2,1,0:T(8,128)(2,1)} %psi_ref.1, bf16[640,128]{1,0:T(8,128)(2,1)} %bitcast.10, f32[5,64,64]{2,1,0:T(8,128)} %bitcast.11, s32[64,64]{1,0:T(8,128)} %allowed_ref.3), custom_call_target="tpu_custom_call" | custom-call | tf_op jit(solution)/shard_map/pallas_call | solution.py:133
  9.7 0.0 all-gather.3.cloned.1.call-update
  9.8 4.8 %collective-permute-start.1 = (bf16[1024,128]{1,0:T(8,128)(2,1)}, bf16[1024,128]{1,0:T(8,128)(2,1)S(1)}, u32[]{:S(2)}, u32[]{:S(2)}) collective-permute-start(bf16[1024,128]{1,0:T(8,128)(2,1)} %get-tuple-element.14.refs_1_), channel_id=1, source_target_pairs={{8,16},{16,8},{24,32},{32,24},{40,48},{48,40},{56,64},{64,56},{72,... | collective-permute-start | bytes 786440 | tf_op jit(solution)/shard_map/ppermute | solution.py:156
  14.6 0.0 copy-done.6
  14.6 12.5 %collective-permute-start = (bf16[1,128,128]{2,1,0:T(8,128)(2,1)S(1)}, bf16[1,128,128]{2,1,0:T(8,128)(2,1)S(1)}, u32[]{:S(2)}, u32[]{:S(2)}) collective-permute-start(bf16[1,128,128]{2,1,0:T(8,128)(2,1)S(1)} %bitcast.13), channel_id=1, source_target_pairs={{0,96},{1,112},{2,224},{3,240},{4,352},{5,368},{6,480},{7,496},{8,... | collective-permute-start | bytes 98312 | tf_op jit(solution)/shard_map/ppermute | solution.py:131
  27.0 1.6 %collective-permute-done = bf16[1,128,128]{2,1,0:T(8,128)(2,1)S(1)} collective-permute-done((bf16[1,128,128]{2,1,0:T(8,128)(2,1)S(1)}, bf16[1,128,128]{2,1,0:T(8,128)(2,1)S(1)}, u32[]{:S(2)}, u32[]{:S(2)}) %collective-permute-start) | collective-permute-done | bytes 32800 | tf_op jit(solution)/shard_map/ppermute | solution.py:131
  28.6 0.0 collective-permute-done.1.refs_0_
  28.6 0.0 copy-start.2
  28.6 0.0 copy-start.1
  28.6 1.2 %tile.10 = bf16[32,128,128]{2,1,0:T(8,128)(2,1)} broadcast(bf16[128,128]{1,0:T(8,128)(2,1)S(1)} %bitcast.12), dimensions={1,2} | broadcast | bytes 1081344 | tf_op jit(solution)/shard_map/tile | solution.py:161
  29.8 7.9 %all-to-all-start = ((bf16[32,128,128]{2,1,0:T(8,128)(2,1)}), bf16[32,128,128]{2,1,0:T(8,128)(2,1)S(1)}, u32[]{:S(2)}, u32[]{:S(2)}) async-start(bf16[32,128,128]{2,1,0:T(8,128)(2,1)} %tile.10), calls=%async_computation | async-start | bytes 2097152 | tf_op jit(solution)/shard_map/all_to_all | solution.py:160
  37.8 0.0 copy-done.1
  37.8 2.9 %collective-permute-start.2 = (bf16[512,128]{1,0:T(8,128)(2,1)S(1)}, bf16[512,128]{1,0:T(8,128)(2,1)S(1)}, u32[]{:S(2)}, u32[]{:S(2)}) collective-permute-start(bf16[512,128]{1,0:T(8,128)(2,1)S(1)} %slice.6), channel_id=1, source_target_pairs={{0,8},{8,0},{16,24},{24,16},{32,40},{40,32},{48,56},{56,48},{64,72... | collective-permute-start | bytes 393224 | tf_op jit(solution)/shard_map/ppermute | solution.py:158
  40.7 0.0 copy-done.2
  40.7 1.9 %collective-permute-start.3 = (bf16[512,128]{1,0:T(8,128)(2,1)S(1)}, bf16[512,128]{1,0:T(8,128)(2,1)S(1)}, u32[]{:S(2)}, u32[]{:S(2)}) collective-permute-start(bf16[512,128]{1,0:T(8,128)(2,1)S(1)} %slice.7), channel_id=1, source_target_pairs={{0,8},{8,0},{16,24},{24,16},{32,40},{40,32},{48,56},{56,48},{64,72... | collective-permute-start | bytes 393224 | tf_op jit(solution)/shard_map/ppermute | solution.py:159
  42.6 0.0 collective-permute-done.2.refs_2_
  42.6 0.0 copy-start.4
  42.6 1.3 %collective-permute-done.3.refs_3_ = bf16[512,128]{1,0:T(8,128)(2,1)S(1)} collective-permute-done((bf16[512,128]{1,0:T(8,128)(2,1)S(1)}, bf16[512,128]{1,0:T(8,128)(2,1)S(1)}, u32[]{:S(2)}, u32[]{:S(2)}) %collective-permute-start.3) | collective-permute-done | bytes 131104 | tf_op jit(solution)/shard_map/ppermute | solution.py:159
  43.9 0.0 copy-start.5
  43.9 13.6 %all-gather.3.cloned.1.call-done = bf16[5248,128]{1,0:T(8,128)(2,1)} async-done(((bf16[656,128]{1,0:T(8,128)(2,1)}), bf16[5248,128]{1,0:T(8,128)(2,1)}) %all-gather.3.cloned.1.call-update) | async-done | bytes 1343504 | tf_op jit(solution)/shard_map/all_gather | solution.py:154
  57.5 1.9 %collective-permute-start.4 = (bf16[8,656,128]{2,1,0:T(8,128)(2,1)}, bf16[8,656,128]{2,1,0:T(8,128)(2,1)S(1)}, u32[]{:S(2)}, u32[]{:S(2)}) collective-permute-start(bf16[8,656,128]{2,1,0:T(8,128)(2,1)} %bitcast.8), channel_id=1, source_target_pairs={{0,8},{8,0},{16,24},{24,16},{32,40},{40,32},{48,56},{56,48},{64,72... | collective-permute-start | bytes 4030472 | tf_op jit(solution)/shard_map/ppermute | solution.py:164
  59.4 0.0 copy-done.4
  59.4 0.0 copy-done.5
  59.5 6.0 %shard_map.66.own_ref = bf16[4,1024,128]{2,1,0:T(8,128)(2,1)} custom-call(s32[2]{0:T(128)} %pad_add_fusion.place_ref, bf16[8,656,128]{2,1,0:T(8,128)(2,1)} %bitcast.9, bf16[1024,128]{1,0:T(8,128)(2,1)} %copy-done.2, bf16[1024,128]{1,0:T(8,128)(2,1)} %get-tuple-element.14.refs_1_, bf16[512,128]{1,0:T(8,128)(2,1)} %copy-done.4, bf16[512,128]{1,0:T(8,128)(2,1)} %copy-done.5), custom_call_target="tpu_custom_call" | custom-call | flops 671088640 | bytes 3145728 | tf_op jit(solution)/shard_map/pallas_call | solution.py:167
  65.5 0.0 collective-permute-done.4.slots
  65.5 0.0 copy-start.3
  65.5 1.1 copy-done.3
  66.6 6.0 %shard_map.65.other_ref = bf16[4,1024,128]{2,1,0:T(8,128)(2,1)} custom-call(s32[2]{0:T(128)} %pad_add_fusion.place_ref, bf16[8,656,128]{2,1,0:T(8,128)(2,1)} %copy-done.3, bf16[1024,128]{1,0:T(8,128)(2,1)} %copy-done.2, bf16[1024,128]{1,0:T(8,128)(2,1)} %get-tuple-element.14.refs_1_, bf16[512,128]{1,0:T(8,128)(2,1)} %copy-done.4, bf16[512,128]{1,0:T(8,128)(2,1)} %copy-done.5), custom_call_target="tpu_custom_call" | custom-call | flops 671088640 | bytes 3145728 | tf_op jit(solution)/shard_map/pallas_call | solution.py:167
  72.6 0.0 all-to-all-done.right_ref
  72.6 0.0 copy-start
  72.6 1.0 copy-done
  73.6 3.5 %shard_map.67 = bf16[8,2,128,128]{3,2,1,0:T(8,128)(2,1)} custom-call(s32[2]{0:T(128)} %pad_add_fusion.place_ref, s32[64,64]{1,0:T(8,128)} %allowed_ref.3, bf16[32,128,128]{2,1,0:T(8,128)(2,1)} %copy-done, bf16[4,1024,128]{2,1,0:T(8,128)(2,1)} %shard_map.66.own_ref, bf16[4,1024,128]{2,1,0:T(8,128)(2,1)} %shard_map.65.other_ref), custom_call_target="tpu_custom_call" | custom-call | flops 268435456 | bytes 4194304 | tf_op jit(solution)/shard_map/pallas_call | solution.py:180
  77.1 12.3 %all-to-all-start.1 = ((bf16[8,2,128,128]{3,2,1,0:T(8,128)(2,1)}), bf16[8,2,128,128]{3,2,1,0:T(8,128)(2,1)S(1)}, u32[]{:S(2)}, u32[]{:S(2)}) async-start(bf16[8,2,128,128]{3,2,1,0:T(8,128)(2,1)} %shard_map.67), calls=%async_computation.1 | async-start | bytes 1048576 | tf_op jit(solution)/shard_map/all_to_all | solution.py:189
  89.4 18.0 %all-to-all-done.1 = bf16[8,2,128,128]{3,2,1,0:T(8,128)(2,1)S(1)} async-done(((bf16[8,2,128,128]{3,2,1,0:T(8,128)(2,1)}), bf16[8,2,128,128]{3,2,1,0:T(8,128)(2,1)S(1)}, u32[]{:S(2)}, u32[]{:S(2)}) %all-to-all-start.1) | async-done | bytes 524320 | tf_op jit(solution)/shard_map/all_to_all | solution.py:189
  107.4 0.7 constant_dynamic-slice_fusion
  (2 shorter events, 0.0 us)
Async XLA Ops:
  6.5 8.0 %copy-start.6 = (bf16[1,1,128,128]{3,2,1,0:T(8,128)(2,1)S(1)}, bf16[1,1,128,128]{3,2,1,0:T(8,128)(2,1)}, u32[]{:S(2)}) copy-start(bf16[1,1,128,128]{3,2,1,0:T(8,128)(2,1)} %param.8) | copy-start | bytes 98308
  6.5 51.0 %all-gather.3.cloned.1.call-start = ((), (), s32[]{:S(2)}) async-start(), calls=%async_computation.2 | async-start | bytes 1511424 | tf_op jit(solution)/shard_map/all_gather | solution.py:154
  9.8 18.9 %collective-permute-start.1 = (bf16[1024,128]{1,0:T(8,128)(2,1)}, bf16[1024,128]{1,0:T(8,128)(2,1)S(1)}, u32[]{:S(2)}, u32[]{:S(2)}) collective-permute-start(bf16[1024,128]{1,0:T(8,128)(2,1)} %get-tuple-element.14.refs_1_), channel_id=1, source_target_pairs={{8,16},{16,8},{24,32},{32,24},{40,48},{48,40},{56,64},{64,56},{72,... | collective-permute-start | bytes 786440 | tf_op jit(solution)/shard_map/ppermute | solution.py:156
  14.6 14.0 %collective-permute-start = (bf16[1,128,128]{2,1,0:T(8,128)(2,1)S(1)}, bf16[1,128,128]{2,1,0:T(8,128)(2,1)S(1)}, u32[]{:S(2)}, u32[]{:S(2)}) collective-permute-start(bf16[1,128,128]{2,1,0:T(8,128)(2,1)S(1)} %bitcast.13), channel_id=1, source_target_pairs={{0,96},{1,112},{2,224},{3,240},{4,352},{5,368},{6,480},{7,496},{8,... | collective-permute-start | bytes 98312 | tf_op jit(solution)/shard_map/ppermute | solution.py:131
  28.6 12.0 %copy-start.2 = (bf16[1024,128]{1,0:T(8,128)(2,1)}, bf16[1024,128]{1,0:T(8,128)(2,1)S(1)}, u32[]{:S(2)}) copy-start(bf16[1024,128]{1,0:T(8,128)(2,1)S(1)} %collective-permute-done.1.refs_0_) | copy-start | bytes 786436
  28.6 9.1 %copy-start.1 = (bf16[1024,128]{1,0:T(8,128)(2,1)S(1)}, bf16[1024,128]{1,0:T(8,128)(2,1)}, u32[]{:S(2)}) copy-start(bf16[1024,128]{1,0:T(8,128)(2,1)} %get-tuple-element.14.refs_1_) | copy-start | bytes 786436
  29.8 42.8 %all-to-all-start = ((bf16[32,128,128]{2,1,0:T(8,128)(2,1)}), bf16[32,128,128]{2,1,0:T(8,128)(2,1)S(1)}, u32[]{:S(2)}, u32[]{:S(2)}) async-start(bf16[32,128,128]{2,1,0:T(8,128)(2,1)} %tile.10), calls=%async_computation | async-start | bytes 2097152 | tf_op jit(solution)/shard_map/all_to_all | solution.py:160
  37.8 4.8 %collective-permute-start.2 = (bf16[512,128]{1,0:T(8,128)(2,1)S(1)}, bf16[512,128]{1,0:T(8,128)(2,1)S(1)}, u32[]{:S(2)}, u32[]{:S(2)}) collective-permute-start(bf16[512,128]{1,0:T(8,128)(2,1)S(1)} %slice.6), channel_id=1, source_target_pairs={{0,8},{8,0},{16,24},{24,16},{32,40},{40,32},{48,56},{56,48},{64,72... | collective-permute-start | bytes 393224 | tf_op jit(solution)/shard_map/ppermute | solution.py:158
  40.7 3.2 %collective-permute-start.3 = (bf16[512,128]{1,0:T(8,128)(2,1)S(1)}, bf16[512,128]{1,0:T(8,128)(2,1)S(1)}, u32[]{:S(2)}, u32[]{:S(2)}) collective-permute-start(bf16[512,128]{1,0:T(8,128)(2,1)S(1)} %slice.7), channel_id=1, source_target_pairs={{0,8},{8,0},{16,24},{24,16},{32,40},{40,32},{48,56},{56,48},{64,72... | collective-permute-start | bytes 393224 | tf_op jit(solution)/shard_map/ppermute | solution.py:159
  42.6 16.8 %copy-start.4 = (bf16[512,128]{1,0:T(8,128)(2,1)}, bf16[512,128]{1,0:T(8,128)(2,1)S(1)}, u32[]{:S(2)}) copy-start(bf16[512,128]{1,0:T(8,128)(2,1)S(1)} %collective-permute-done.2.refs_2_) | copy-start | bytes 393220
  43.9 15.5 %copy-start.5 = (bf16[512,128]{1,0:T(8,128)(2,1)}, bf16[512,128]{1,0:T(8,128)(2,1)S(1)}, u32[]{:S(2)}) copy-start(bf16[512,128]{1,0:T(8,128)(2,1)S(1)} %collective-permute-done.3.refs_3_) | copy-start | bytes 393220
  57.5 8.0 %collective-permute-start.4 = (bf16[8,656,128]{2,1,0:T(8,128)(2,1)}, bf16[8,656,128]{2,1,0:T(8,128)(2,1)S(1)}, u32[]{:S(2)}, u32[]{:S(2)}) collective-permute-start(bf16[8,656,128]{2,1,0:T(8,128)(2,1)} %bitcast.8), channel_id=1, source_target_pairs={{0,8},{8,0},{16,24},{24,16},{32,40},{40,32},{48,56},{56,48},{64,72... | collective-permute-start | bytes 4030472 | tf_op jit(solution)/shard_map/ppermute | solution.py:164
  65.5 1.1 copy-start.3
  72.6 1.0 copy-start
  77.1 30.4 %all-to-all-start.1 = ((bf16[8,2,128,128]{3,2,1,0:T(8,128)(2,1)}), bf16[8,2,128,128]{3,2,1,0:T(8,128)(2,1)S(1)}, u32[]{:S(2)}, u32[]{:S(2)}) async-start(bf16[8,2,128,128]{3,2,1,0:T(8,128)(2,1)} %shard_map.67), calls=%async_computation.1 | async-start | bytes 1048576 | tf_op jit(solution)/shard_map/all_to_all | solution.py:189
Sparse Core Ops, SparseCore 0:
  9.9 47.5 all-gather.2

commit v6 on v5

v6 whole, which is shorter than its diff:
```python
import functools

import jax
import jax.numpy as jnp
from jax import lax
from jax.experimental import pallas as pl
from jax.experimental.pallas import tpu as pltpu
from jax.sharding import PartitionSpec as P

M = 128
LB = 5
NW = 8
G = 8
H = G // 2
BOTH = ("sec", "term")
ROWS = LB * M
F32 = jnp.float32
BF16 = jnp.bfloat16
VMEM = pl.BlockSpec(memory_space=pltpu.VMEM)
SMEM = pl.BlockSpec(memory_space=pltpu.SMEM)
PARAMS = pltpu.CompilerParams(vmem_limit_bytes=56 * 1024 * 1024)


def together(*arrays):
    return lax.optimization_barrier(arrays)


def right_chip(t, w, i):
    return w // 2 * G + (t % 2 * H + 2 * i + w % 2 + G - 2) % G


def pack(shift_ref, env_ref, coupling_ref, allowed_ref, payload_ref, table_ref):
    s = lax.axis_index("sec")
    n_sec = allowed_ref.shape[0]
    payload_ref[:ROWS, :] = env_ref[...]
    table_ref[...] = jnp.zeros_like(table_ref)
    lane = lax.broadcasted_iota(jnp.int32, (1, M), 1)
    shifts = jnp.zeros((1, M), F32)
    for c in range(LB):
        shift = shift_ref[0, c]
        source = s + shift
        inside = jnp.logical_and(source >= 0, source < n_sec).astype(F32)
        kept = allowed_ref[pl.ds(jnp.clip(source, 0, n_sec - 1), 1), :].astype(F32) * inside
        factor = coupling_ref[c, pl.ds(s, 1), :] * kept
        high = factor.astype(BF16).astype(F32)
        middle = (factor - high).astype(BF16).astype(F32)
        low = (factor - high - middle).astype(BF16).astype(F32)
        table_ref[c : c + 1, :] = jnp.concatenate([high, middle], axis=1)
        table_ref[8 + c : 9 + c, :n_sec] = low
        shifts = jnp.where(lane == c, shift.astype(F32), shifts)
    table_ref[15:16, :] = shifts
    payload_ref[ROWS:, :] = table_ref[...].astype(BF16)


def turn(psi_ref, turned_ref, block_ref, sem):
    core = lax.rem(lax.axis_index("sec"), 2)
    copy = pltpu.make_async_copy(psi_ref.at[0, pl.ds(lax.axis_index("term") * G, G)], block_ref, sem)
    copy.start()
    copy.wait()
    for i in range(H):
        turned_ref[i * M : (i + 1) * M, :] = block_ref[2 * i + core].T
        turned_ref[(H + i) * M : (H + i + 1) * M, :] = block_ref[2 * i + 1 - core].T


def fill(psi_ref, near_ref, turned_ref, inner_ref, far_ref):
    psi_ref[0] = near_ref[H * M :, :]
    psi_ref[1] = turned_ref[: H * M, :]
    psi_ref[2] = inner_ref[...]
    psi_ref[3] = far_ref[...]


def left_sums(first_row, slots, psi_ref, out_ref):
    t = lax.axis_index("term")
    core = lax.rem(lax.axis_index("sec"), 2)
    sector = lax.broadcasted_iota(jnp.int32, (M, H * M), 0)
    wanted = lax.broadcasted_iota(jnp.int32, (M, H * M), 1) // M * 2 + t * G + core
    pick = jnp.where((sector == wanted) | (sector == wanted + M // 2), 1.0, 0.0).astype(BF16)
    for w in range(slots.shape[0]):
        table = slots[w, ROWS : ROWS + 16, :]
        spread = jnp.dot(table, pick, preferred_element_type=F32)
        factors = spread[:8] + spread[8:]
        shifts = table.astype(F32)[15:16, :]
        rows = [first_row + shifts[0, c].astype(jnp.int32) * (1 - 2 * core) for c in range(LB)]
        for start in range(0, H * M, 2 * M):
            totals = [None, None]
            for c in range(LB):
                product = lax.dot_general(
                    psi_ref[rows[c], start : start + 2 * M, :],
                    slots[w, c * M : (c + 1) * M, :],
                    (((1,), (1,)), ((), ())),
                    preferred_element_type=F32,
                )
                for h in range(2):
                    at = start + h * M
                    term = product[h * M : (h + 1) * M] * factors[c : c + 1, at : at + M]
                    totals[h] = term if totals[h] is None else totals[h] + term
            for h in range(2):
                out_ref[start // M + h, w * M : (w + 1) * M, :] = totals[h].astype(BF16)


def left_products(own_slots, other_slots, near_ref, turned_ref, inner_ref, far_ref, own_ref, other_ref, psi_ref):
    fill(psi_ref, near_ref, turned_ref, inner_ref, far_ref)
    left_sums(1, own_slots, psi_ref, own_ref)
    left_sums(2, other_slots, psi_ref, other_ref)


def right_products(allowed_ref, right_ref, own_same, other_same, own_next, other_next, out_ref):
    s, t = lax.axis_index("sec"), lax.axis_index("term")
    core = lax.rem(s, 2)
    parity = lax.rem(t, 2)
    for i in range(H):
        same = jnp.concatenate([right_ref[right_chip(t, 2 * m + parity, i)] for m in range(NW // 2)], axis=1)
        following = jnp.concatenate([right_ref[right_chip(t, 2 * m + 1 - parity, i)] for m in range(NW // 2)], axis=1)
        for same_ref, next_ref, which in ((own_same, own_next, core), (other_same, other_next, 1 - core)):
            total = jnp.dot(same, same_ref[i], preferred_element_type=F32)
            total += jnp.dot(following, next_ref[i], preferred_element_type=F32)
            keep = allowed_ref[s - core + which, t * G + 2 * i + core].astype(F32)
            value = (total * keep).T.astype(BF16)
            out_ref[i, which] = value
            out_ref[H + i, which] = value


def on_device(wavefunction, left_env, right_env, coupling, left_shift, allowed, *, n_sec, n_term):
    s, t = lax.axis_index("sec"), lax.axis_index("term")
    groups = n_sec // G

    def device(sec, term):
        return sec * n_term + term

    spread = [
        (device(b, w), device(2 * right_chip(b // G, w, b % G // 2) + b % 2, b // G))
        for b in range(n_sec)
        for w in range(n_term)
    ]
    by_core = [[2 * chip + core for chip in range(n_sec // 2)] for core in range(2)]
    exchange = []
    for core in range(2):

        def members(A, B):
            return [device(A * G + 2 * i + core, B) for i in range(H)]

        exchange += [members(A, B) + members(B, A) for A in range(groups) for B in range(A + 1, groups)]
        exchange += [members(A, A) + members(A + 1, A + 1) for A in range(0, groups, 2)]

    right = lax.ppermute(right_env[0], BOTH, spread)
    payload = pl.pallas_call(
        pack,
        out_shape=jax.ShapeDtypeStruct((ROWS + 16, M), BF16),
        in_specs=[SMEM] + [VMEM] * 3,
        out_specs=VMEM,
        scratch_shapes=[pltpu.VMEM((16, M), F32)],
        compiler_params=PARAMS,
    )(left_shift, left_env.reshape(ROWS, M), coupling[0], allowed)
    turned = pl.pallas_call(
        turn,
        out_shape=jax.ShapeDtypeStruct((G * M, M), BF16),
        in_specs=[pl.BlockSpec(memory_space=pl.ANY)],
        out_specs=VMEM,
        scratch_shapes=[pltpu.VMEM((G, M, M), BF16), pltpu.SemaphoreType.DMA],
        compiler_params=PARAMS,
    )(wavefunction)

    across = [(i, i ^ 1) for i in range(n_sec)]
    near = lax.ppermute(turned, "sec", [(i, i + 1) if i % 2 else (i, i - 1) for i in range(1, n_sec - 1)])
    same = lax.all_gather(
        payload, "term", axis_index_groups=[list(range(parity, n_term, 2)) for parity in range(2)]
    )
    right, near, same = together(right, near, same)
    following = lax.ppermute(same, "term", [(i, i ^ 1) for i in range(n_term)])
    right = lax.all_to_all(
        jnp.tile(right, (n_sec // 2, 1, 1)), "sec", 0, 0, axis_index_groups=by_core, tiled=True
    )
    inner = lax.ppermute(turned[H * M :], "sec", across)
    far = lax.ppermute(near[: H * M], "sec", across)

    def left_call(slots):
        return pl.pallas_call(
            left_products,
            out_shape=[jax.ShapeDtypeStruct((H, NW // 2 * M, M), BF16)] * 2,
            in_specs=[VMEM] * 6,
            out_specs=[VMEM] * 2,
            scratch_shapes=[pltpu.VMEM((4, H * M, M), BF16)],
            compiler_params=PARAMS,
            cost_estimate=pl.CostEstimate(flops=2 * 160 * M**3, bytes_accessed=3 << 20, transcendentals=0),
        )(slots, lax.ppermute(slots, "sec", across), near, turned, inner, far)

    own_same, other_same = left_call(same)
    following, own_same = together(following, own_same)
    own_next, other_next = left_call(following)
    right, own_next = together(right, own_next)
    results = pl.pallas_call(
        right_products,
        out_shape=jax.ShapeDtypeStruct((G, 2, M, M), BF16),
        in_specs=[SMEM] + [VMEM] * 5,
        out_specs=VMEM,
        compiler_params=PARAMS,
        cost_estimate=pl.CostEstimate(flops=2 * 64 * M**3, bytes_accessed=4 << 20, transcendentals=0),
    )(allowed, right, own_same, other_same, own_next, other_next)

    received = lax.all_to_all(results, BOTH, 0, 0, axis_index_groups=exchange, tiled=True)
    A = s // G
    first = jnp.where(A < t, H, jnp.where(A > t, 0, lax.rem(A, 2) * H))
    return lax.dynamic_slice_in_dim(received, first, H, 0).reshape(G, 1, M, M)


def solution(mesh):
    in_specs = (
        P("sec", None, None, None),
        P("term", None, "sec", None, None),
        P("term", "sec", None, None),
        P("term", None, None, None),
        P("term", None),
        P(),
    )
    body = functools.partial(on_device, n_sec=mesh.shape["sec"], n_term=mesh.shape["term"])
    return jax.shard_map(
        body, mesh=mesh, in_specs=in_specs, out_specs=P("term", "sec", None, None), check_vma=False
    )
```

time: 115 us -> 114 us (level)
  blocking collectives: 0 us -> 17.5 us
  between operations: 13.5 us -> 0.16 us
  waiting for transfers between devices: 34.5 us -> 25.6 us
  starting transfers between devices: 44.2 us -> 49.2 us
  Pallas kernels: 18.2 us -> 15.6 us
  local copies, waits for them, and re-layouts: 4.03 us -> 5.36 us
    all_gather x0 -> x1, blocking collectives: none -> 17.5 us  [on_device(): lax.all_gather(payload, 'term', axis_index_groups=[list(range(parity, n_t...]
    all_gather x1 -> x0, waiting for transfers between devices: 13.6 us -> none  [on_device(): payloads = lax.all_gather(payload, 'term')]
    ppermute x1 -> x3, waiting for transfers between devices: 0.01 us -> 6.62 us  [the longest x1 4.53 us: on_device(): following = lax.ppermute(same, 'term', [(i, i ^ 1) for i in range(n_term)])]
    ppermute x1 -> x3, starting transfers between devices: 1.91 us -> 7.52 us  [the longest x2 3.83 us: left_call(): lax.ppermute(slots, 'sec', across)]
    pallas_call x3 -> x4, Pallas kernels: 14.7 us -> 12.1 us  [the longest x2 8.56 us: left_call(): pl.pallas_call(left_products, out_shape=[jax.ShapeDtypeStruct((H, NW // 2...]
    ppermute x1, waiting for transfers between devices: 1.58 us -> 0.01 us  [on_device(): right = lax.ppermute(right_env[0], BOTH, spread)]
    unnamed x14 -> x20, local copies, waits for them, and re-layouts: 2.09 us -> 3.36 us
  transfers between devices with their start and end apart: 8 -> 9, of which waited for: 4 -> 4; matrix products, arithmetic and copies ran while one was open for 1% -> 0% of each run, Pallas kernels for 11% -> 9%
where the time goes in v6:
time: 114 us; the launch traced here: 113 us
  starting transfers between devices  49.2 us (43%)
  waiting for transfers between devices  25.6 us (22%)
  blocking collectives  17.5 us (15%)
  Pallas kernels  15.6 us (14%)
  local copies, waits for them, and re-layouts  5.36 us (5%)
    all_to_all x1, waiting for transfers between devices, on_device(): lax.all_to_all(results, BOTH, 0, 0, axis_index_groups=exchange, tiled=True)  17.9 us
    all_gather x1, blocking collectives, on_device(): lax.all_gather(payload, 'term', axis_index_groups=[list(range(parity, n_t...  17.5 us
    ppermute x1, starting transfers between devices, on_device(): right = lax.ppermute(right_env[0], BOTH, spread)  12.5 us
    all_to_all x1, starting transfers between devices, on_device(): lax.all_to_all(results, BOTH, 0, 0, axis_index_groups=exchange, tiled=True)  12.3 us
    pallas_call x2, Pallas kernels, left_call(): pl.pallas_call(left_products, out_shape=[jax.ShapeDtypeStruct((H, NW // 2...  8.56 us
    all_to_all x1, starting transfers between devices, on_device(): lax.all_to_all(jnp.tile(right, (n_sec // 2, 1, 1)), 'sec', 0, 0, axis_ind...  7.78 us
    ppermute x1, starting transfers between devices, on_device(): lax.ppermute(turned, 'sec', [(i, i + 1) if i % 2 else (i, i - 1) for i in...  4.79 us
    ppermute x1, waiting for transfers between devices, on_device(): following = lax.ppermute(same, 'term', [(i, i ^ 1) for i in range(n_term)])  4.53 us
  transfers between devices with their start and end apart: 9, of which 4 were waited for; matrix products, arithmetic and copies ran while one was open for 0% of the time, Pallas kernels for 9%

profile of v6, /device:TPU:4, one launch (start us, length us, event | category | flops | bytes accessed | tf_op | source)
XLA Modules:
  0.0 113.4 jit_solution(1898078329422959769)
XLA Ops:
  0.0 0.0 copy-start.9
  0.0 1.8 %shard_map.64.turned_ref = bf16[1024,128]{1,0:T(8,128)(2,1)} custom-call(bf16[1,64,128,128]{3,2,1,0:T(8,128)(2,1)} %psi_ref.1), custom_call_target="tpu_custom_call" | custom-call | tf_op jit(solution)/shard_map/pallas_call | solution.py:154
  1.8 4.8 %collective-permute-start.1 = (bf16[1024,128]{1,0:T(8,128)(2,1)}, bf16[1024,128]{1,0:T(8,128)(2,1)S(1)}, u32[]{:S(2)}, u32[]{:S(2)}) collective-permute-start(bf16[1024,128]{1,0:T(8,128)(2,1)} %shard_map.64.turned_ref), channel_id=1, source_target_pairs={{8,16},{16,8},{24,32},{32,24},{40,48},{48,40},{56,64},{64,56},{72,... | collective-permute-start | bytes 786440 | tf_op jit(solution)/shard_map/ppermute | solution.py:164
  6.6 0.0 copy-done.9
  6.6 12.5 %collective-permute-start = (bf16[1,128,128]{2,1,0:T(8,128)(2,1)S(1)}, bf16[1,128,128]{2,1,0:T(8,128)(2,1)S(1)}, u32[]{:S(2)}, u32[]{:S(2)}) collective-permute-start(bf16[1,128,128]{2,1,0:T(8,128)(2,1)S(1)} %bitcast.12), channel_id=1, source_target_pairs={{0,96},{1,112},{2,224},{3,240},{4,352},{5,368},{6,480},{7,496},{8,... | collective-permute-start | bytes 98312 | tf_op jit(solution)/shard_map/ppermute | solution.py:145
  19.1 1.8 %shard_map.65 = bf16[656,128]{1,0:T(8,128)(2,1)} custom-call(s32[1,5]{1,0:T(1,128)} %shift_ref.1, bf16[640,128]{1,0:T(8,128)(2,1)} %bitcast.9, f32[5,64,64]{2,1,0:T(8,128)} %bitcast.10, s32[64,64]{1,0:T(8,128)} %allowed_ref.3), custom_call_target="tpu_custom_call" | custom-call | tf_op jit(solution)/shard_map/pallas_call | solution.py:146
  20.8 0.0 copy-start.2
  20.9 17.5 %all-gather = bf16[2624,128]{1,0:T(8,128)(2,1)S(1)} all-gather(bf16[656,128]{1,0:T(8,128)(2,1)} %shard_map.65), channel_id=2, replica_groups={{0,2,4,6},{1,3,5,7},{8,10,12,14},{9,11,13,15},{16,18,20,22},{17,19,21,2..., dimensions={0}, use_global_device_ids=true | all-gather | bytes 839680 | tf_op jit(solution)/shard_map/all_gather | solution.py:165
  38.4 0.0 copy-start.1
  38.4 0.0 collective-permute-done
  38.4 0.0 collective-permute-done.1.near_ref
  38.4 0.0 copy-start.3
  38.4 1.3 %tile.10 = bf16[32,128,128]{2,1,0:T(8,128)(2,1)} broadcast(bf16[128,128]{1,0:T(8,128)(2,1)S(1)} %bitcast.11), dimensions={1,2} | broadcast | bytes 1081344 | tf_op jit(solution)/shard_map/tile | solution.py:171
  39.7 7.8 %all-to-all-start = ((bf16[32,128,128]{2,1,0:T(8,128)(2,1)}), bf16[32,128,128]{2,1,0:T(8,128)(2,1)S(1)}, u32[]{:S(2)}, u32[]{:S(2)}) async-start(bf16[32,128,128]{2,1,0:T(8,128)(2,1)} %tile.10), calls=%async_computation | async-start | bytes 2097152 | tf_op jit(solution)/shard_map/all_to_all | solution.py:170
  47.5 1.9 %collective-permute-start.3 = (bf16[4,656,128]{2,1,0:T(8,128)(2,1)S(1)}, bf16[4,656,128]{2,1,0:T(8,128)(2,1)S(1)}, u32[]{:S(2)}, u32[]{:S(2)}) collective-permute-start(bf16[4,656,128]{2,1,0:T(8,128)(2,1)S(1)} %bitcast.6), channel_id=1, source_target_pairs={{0,8},{8,0},{16,24},{24,16},{32,40},{40,32},{48,56},{56,48},{64,72... | collective-permute-start | bytes 2015240 | tf_op jit(solution)/shard_map/ppermute | solution.py:185
  49.4 3.7 %collective-permute-start.2 = (bf16[4,656,128]{2,1,0:T(8,128)(2,1)S(1)}, bf16[4,656,128]{2,1,0:T(8,128)(2,1)S(1)}, u32[]{:S(2)}, u32[]{:S(2)}) collective-permute-start(bf16[4,656,128]{2,1,0:T(8,128)(2,1)S(1)} %bitcast.7), channel_id=1, source_target_pairs={{0,1},{1,0},{2,3},{3,2},{4,5},{5,4},{6,7},{7,6},{8,9},{9,8},{10,11... | collective-permute-start | bytes 2015240 | tf_op jit(solution)/shard_map/ppermute | solution.py:169
  53.1 0.0 copy-done.2
  53.1 2.1 %collective-permute-start.4 = (bf16[512,128]{1,0:T(8,128)(2,1)S(1)}, bf16[512,128]{1,0:T(8,128)(2,1)S(1)}, u32[]{:S(2)}, u32[]{:S(2)}) collective-permute-start(bf16[512,128]{1,0:T(8,128)(2,1)S(1)} %slice.8), channel_id=1, source_target_pairs={{0,8},{8,0},{16,24},{24,16},{32,40},{40,32},{48,56},{56,48},{64,72... | collective-permute-start | bytes 393224 | tf_op jit(solution)/shard_map/ppermute | solution.py:173
  55.3 2.2 %collective-permute-start.5 = (bf16[512,128]{1,0:T(8,128)(2,1)S(1)}, bf16[512,128]{1,0:T(8,128)(2,1)S(1)}, u32[]{:S(2)}, u32[]{:S(2)}) collective-permute-start(bf16[512,128]{1,0:T(8,128)(2,1)S(1)} %slice.7), channel_id=1, source_target_pairs={{0,8},{8,0},{16,24},{24,16},{32,40},{40,32},{48,56},{56,48},{64,72... | collective-permute-start | bytes 393224 | tf_op jit(solution)/shard_map/ppermute | solution.py:174
  57.5 0.0 collective-permute-done.4.inner_ref
  57.5 0.0 copy-start.7
  57.5 1.0 collective-permute-done.5.far_ref
  58.5 0.0 copy-start.8
  58.5 0.0 collective-permute-done.3.other_slots
  58.5 0.0 copy-done.1
  58.5 0.0 copy-done.3
  58.5 0.0 copy-done.7
  58.5 0.6 copy-done.8
  59.2 0.0 copy-start.5
  59.2 0.9 copy-done.5
  60.0 4.3 %shard_map.66 = (bf16[4,512,128]{2,1,0:T(8,128)(2,1)}, bf16[4,512,128]{2,1,0:T(8,128)(2,1)}) custom-call(bf16[4,656,128]{2,1,0:T(8,128)(2,1)} %bitcast.8, bf16[4,656,128]{2,1,0:T(8,128)(2,1)} %copy-done.5, bf16[1024,128]{1,0:T(8,128)(2,1)} %copy-done.3, bf16[1024,128]{1,0:T(8,128)(2,1)} %shard_map.64.turned_ref, bf16[512,128]{1,0:T(8,128)(2,1)} %copy-done.7, ...), custom_call_target="tpu_custom_call" | custom-call | flops 671088640 | bytes 3145728 | tf_op jit(solution)/shard_map/pallas_call | solution.py:177
  64.3 4.5 %collective-permute-done.2.own_slots = bf16[4,656,128]{2,1,0:T(8,128)(2,1)S(1)} collective-permute-done((bf16[4,656,128]{2,1,0:T(8,128)(2,1)S(1)}, bf16[4,656,128]{2,1,0:T(8,128)(2,1)S(1)}, u32[]{:S(2)}, u32[]{:S(2)}) %collective-permute-start.2) | collective-permute-done | bytes 671776 | tf_op jit(solution)/shard_map/ppermute | solution.py:169
  68.8 0.0 copy-start.4
  68.8 1.9 %collective-permute-start.6 = (bf16[4,656,128]{2,1,0:T(8,128)(2,1)S(1)}, bf16[4,656,128]{2,1,0:T(8,128)(2,1)S(1)}, u32[]{:S(2)}, u32[]{:S(2)}) collective-permute-start(bf16[4,656,128]{2,1,0:T(8,128)(2,1)S(1)} %collective-permute-done.2.own_slots), channel_id=1, source_target_pairs={{0,8},{8,0},{16,24},{24,16},{32,40},{40,32},{48,56},{56,48},{64,72... | collective-permute-start | bytes 2015240 | tf_op jit(solution)/shard_map/ppermute | solution.py:185
  70.7 2.1 %collective-permute-done.6.other_slots = bf16[4,656,128]{2,1,0:T(8,128)(2,1)S(1)} collective-permute-done((bf16[4,656,128]{2,1,0:T(8,128)(2,1)S(1)}, bf16[4,656,128]{2,1,0:T(8,128)(2,1)S(1)}, u32[]{:S(2)}, u32[]{:S(2)}) %collective-permute-start.6) | collective-permute-done | bytes 671776 | tf_op jit(solution)/shard_map/ppermute | solution.py:185
  72.8 0.0 copy-done.4
  72.8 0.0 copy-start.6
  72.8 0.9 copy-done.6
  73.7 4.3 %shard_map.67 = (bf16[4,512,128]{2,1,0:T(8,128)(2,1)}, bf16[4,512,128]{2,1,0:T(8,128)(2,1)}) custom-call(bf16[4,656,128]{2,1,0:T(8,128)(2,1)} %copy-done.4, bf16[4,656,128]{2,1,0:T(8,128)(2,1)} %copy-done.6, bf16[1024,128]{1,0:T(8,128)(2,1)} %copy-done.3, bf16[1024,128]{1,0:T(8,128)(2,1)} %shard_map.64.turned_ref, bf16[512,128]{1,0:T(8,128)(2,1)} %copy-done.7, ...), custom_call_target="tpu_custom_call" | custom-call | flops 671088640 | bytes 3145728 | tf_op jit(solution)/shard_map/pallas_call | solution.py:177
  78.0 0.0 all-to-all-done.right_ref
  78.0 0.0 copy-start
  78.0 1.0 copy-done
  79.0 3.4 %shard_map.68 = bf16[8,2,128,128]{3,2,1,0:T(8,128)(2,1)} custom-call(s32[64,64]{1,0:T(8,128)} %allowed_ref.3, bf16[32,128,128]{2,1,0:T(8,128)(2,1)} %copy-done, bf16[4,512,128]{2,1,0:T(8,128)(2,1)} %get-tuple-element.23.own_same, bf16[4,512,128]{2,1,0:T(8,128)(2,1)} %get-tuple-element.24.other_same, bf16[4,512,128]{2,1,0:T(8,128)(2,1)} %get-tuple-element.25.own_next, ...), custom_call_target="tpu_custom_call" | custom-call | flops 268435456 | bytes 4194304 | tf_op jit(solution)/shard_map/pallas_call | solution.py:191
  82.4 12.3 %all-to-all-start.1 = ((bf16[8,2,128,128]{3,2,1,0:T(8,128)(2,1)}), bf16[8,2,128,128]{3,2,1,0:T(8,128)(2,1)S(1)}, u32[]{:S(2)}, u32[]{:S(2)}) async-start(bf16[8,2,128,128]{3,2,1,0:T(8,128)(2,1)} %shard_map.68), calls=%async_computation.1 | async-start | bytes 1048576 | tf_op jit(solution)/shard_map/all_to_all | solution.py:200
  94.8 17.9 %all-to-all-done.1 = bf16[8,2,128,128]{3,2,1,0:T(8,128)(2,1)S(1)} async-done(((bf16[8,2,128,128]{3,2,1,0:T(8,128)(2,1)}), bf16[8,2,128,128]{3,2,1,0:T(8,128)(2,1)S(1)}, u32[]{:S(2)}, u32[]{:S(2)}) %all-to-all-start.1) | async-done | bytes 524320 | tf_op jit(solution)/shard_map/all_to_all | solution.py:200
  112.7 0.7 constant_dynamic-slice_fusion
  (2 shorter events, 0.0 us)
Async XLA Ops:
  0.0 6.6 %copy-start.9 = (bf16[1,1,128,128]{3,2,1,0:T(8,128)(2,1)S(1)}, bf16[1,1,128,128]{3,2,1,0:T(8,128)(2,1)}, u32[]{:S(2)}) copy-start(bf16[1,1,128,128]{3,2,1,0:T(8,128)(2,1)} %param.8) | copy-start | bytes 98308
  1.8 36.6 %collective-permute-start.1 = (bf16[1024,128]{1,0:T(8,128)(2,1)}, bf16[1024,128]{1,0:T(8,128)(2,1)S(1)}, u32[]{:S(2)}, u32[]{:S(2)}) collective-permute-start(bf16[1024,128]{1,0:T(8,128)(2,1)} %shard_map.64.turned_ref), channel_id=1, source_target_pairs={{8,16},{16,8},{24,32},{32,24},{40,48},{48,40},{56,64},{64,56},{72,... | collective-permute-start | bytes 786440 | tf_op jit(solution)/shard_map/ppermute | solution.py:164
  6.6 31.8 %collective-permute-start = (bf16[1,128,128]{2,1,0:T(8,128)(2,1)S(1)}, bf16[1,128,128]{2,1,0:T(8,128)(2,1)S(1)}, u32[]{:S(2)}, u32[]{:S(2)}) collective-permute-start(bf16[1,128,128]{2,1,0:T(8,128)(2,1)S(1)} %bitcast.12), channel_id=1, source_target_pairs={{0,96},{1,112},{2,224},{3,240},{4,352},{5,368},{6,480},{7,496},{8,... | collective-permute-start | bytes 98312 | tf_op jit(solution)/shard_map/ppermute | solution.py:145
  20.8 32.2 %copy-start.2 = (bf16[1024,128]{1,0:T(8,128)(2,1)S(1)}, bf16[1024,128]{1,0:T(8,128)(2,1)}, u32[]{:S(2)}) copy-start(bf16[1024,128]{1,0:T(8,128)(2,1)} %shard_map.64.turned_ref) | copy-start | bytes 786436
  38.4 20.1 %copy-start.1 = (bf16[2624,128]{1,0:T(8,128)(2,1)}, bf16[2624,128]{1,0:T(8,128)(2,1)S(1)}, u32[]{:S(2)}) copy-start(bf16[2624,128]{1,0:T(8,128)(2,1)S(1)} %all-gather) | copy-start | bytes 2015236
  38.4 20.1 %copy-start.3 = (bf16[1024,128]{1,0:T(8,128)(2,1)}, bf16[1024,128]{1,0:T(8,128)(2,1)S(1)}, u32[]{:S(2)}) copy-start(bf16[1024,128]{1,0:T(8,128)(2,1)S(1)} %collective-permute-done.1.near_ref) | copy-start | bytes 786436
  39.7 38.3 %all-to-all-start = ((bf16[32,128,128]{2,1,0:T(8,128)(2,1)}), bf16[32,128,128]{2,1,0:T(8,128)(2,1)S(1)}, u32[]{:S(2)}, u32[]{:S(2)}) async-start(bf16[32,128,128]{2,1,0:T(8,128)(2,1)} %tile.10), calls=%async_computation | async-start | bytes 2097152 | tf_op jit(solution)/shard_map/all_to_all | solution.py:170
  47.5 11.1 %collective-permute-start.3 = (bf16[4,656,128]{2,1,0:T(8,128)(2,1)S(1)}, bf16[4,656,128]{2,1,0:T(8,128)(2,1)S(1)}, u32[]{:S(2)}, u32[]{:S(2)}) collective-permute-start(bf16[4,656,128]{2,1,0:T(8,128)(2,1)S(1)} %bitcast.6), channel_id=1, source_target_pairs={{0,8},{8,0},{16,24},{24,16},{32,40},{40,32},{48,56},{56,48},{64,72... | collective-permute-start | bytes 2015240 | tf_op jit(solution)/shard_map/ppermute | solution.py:185
  49.4 19.4 %collective-permute-start.2 = (bf16[4,656,128]{2,1,0:T(8,128)(2,1)S(1)}, bf16[4,656,128]{2,1,0:T(8,128)(2,1)S(1)}, u32[]{:S(2)}, u32[]{:S(2)}) collective-permute-start(bf16[4,656,128]{2,1,0:T(8,128)(2,1)S(1)} %bitcast.7), channel_id=1, source_target_pairs={{0,1},{1,0},{2,3},{3,2},{4,5},{5,4},{6,7},{7,6},{8,9},{9,8},{10,11... | collective-permute-start | bytes 2015240 | tf_op jit(solution)/shard_map/ppermute | solution.py:169
  53.1 4.4 %collective-permute-start.4 = (bf16[512,128]{1,0:T(8,128)(2,1)S(1)}, bf16[512,128]{1,0:T(8,128)(2,1)S(1)}, u32[]{:S(2)}, u32[]{:S(2)}) collective-permute-start(bf16[512,128]{1,0:T(8,128)(2,1)S(1)} %slice.8), channel_id=1, source_target_pairs={{0,8},{8,0},{16,24},{24,16},{32,40},{40,32},{48,56},{56,48},{64,72... | collective-permute-start | bytes 393224 | tf_op jit(solution)/shard_map/ppermute | solution.py:173
  55.3 3.2 %collective-permute-start.5 = (bf16[512,128]{1,0:T(8,128)(2,1)S(1)}, bf16[512,128]{1,0:T(8,128)(2,1)S(1)}, u32[]{:S(2)}, u32[]{:S(2)}) collective-permute-start(bf16[512,128]{1,0:T(8,128)(2,1)S(1)} %slice.7), channel_id=1, source_target_pairs={{0,8},{8,0},{16,24},{24,16},{32,40},{40,32},{48,56},{56,48},{64,72... | collective-permute-start | bytes 393224 | tf_op jit(solution)/shard_map/ppermute | solution.py:174
  57.5 1.0 copy-start.7
  58.5 0.6 copy-start.8
  59.2 0.9 copy-start.5
  68.8 4.0 %copy-start.4 = (bf16[4,656,128]{2,1,0:T(8,128)(2,1)}, bf16[4,656,128]{2,1,0:T(8,128)(2,1)S(1)}, u32[]{:S(2)}) copy-start(bf16[4,656,128]{2,1,0:T(8,128)(2,1)S(1)} %collective-permute-done.2.own_slots) | copy-start | bytes 2015236
  68.8 4.0 %collective-permute-start.6 = (bf16[4,656,128]{2,1,0:T(8,128)(2,1)S(1)}, bf16[4,656,128]{2,1,0:T(8,128)(2,1)S(1)}, u32[]{:S(2)}, u32[]{:S(2)}) collective-permute-start(bf16[4,656,128]{2,1,0:T(8,128)(2,1)S(1)} %collective-permute-done.2.own_slots), channel_id=1, source_target_pairs={{0,8},{8,0},{16,24},{24,16},{32,40},{40,32},{48,56},{56,48},{64,72... | collective-permute-start | bytes 2015240 | tf_op jit(solution)/shard_map/ppermute | solution.py:185
  72.8 0.9 copy-start.6
  78.0 1.0 copy-start
  82.4 30.2 %all-to-all-start.1 = ((bf16[8,2,128,128]{3,2,1,0:T(8,128)(2,1)}), bf16[8,2,128,128]{3,2,1,0:T(8,128)(2,1)S(1)}, u32[]{:S(2)}, u32[]{:S(2)}) async-start(bf16[8,2,128,128]{3,2,1,0:T(8,128)(2,1)} %shard_map.68), calls=%async_computation.1 | async-start | bytes 1048576 | tf_op jit(solution)/shard_map/all_to_all | solution.py:200

commit v7 on v6

--- a/solution.py
+++ b/solution.py
@@ -18,6 +18,8 @@
 BF16 = jnp.bfloat16
 VMEM = pl.BlockSpec(memory_space=pltpu.VMEM)
 SMEM = pl.BlockSpec(memory_space=pltpu.SMEM)
+ANY = pl.BlockSpec(memory_space=pl.ANY)
+WEIGHTS = (320, 4000)
 PARAMS = pltpu.CompilerParams(vmem_limit_bytes=56 * 1024 * 1024)
 
 
@@ -26,7 +28,12 @@
 
 
 def right_chip(t, w, i):
-    return w // 2 * G + (t % 2 * H + 2 * i + w % 2 + G - 2) % G
+    ahead = (w - t) & 7
+    far = ahead >> 2
+    pair = far * (ahead - 4) + (1 - far) * (3 - ahead)
+    x = ((t >> 1) + (pair ^ (pair >> 1))) & 3
+    y = (4 * (t & 1) + far * (-1, 1, 2, 4)[i] + (1 - far) * (-2, 0, 3, 5)[i]) & 7
+    return x * 8 + y
 
 
 def pack(shift_ref, env_ref, coupling_ref, allowed_ref, payload_ref, table_ref):
@@ -98,13 +105,25 @@
                 out_ref[start // M + h, w * M : (w + 1) * M, :] = totals[h].astype(BF16)
 
 
-def left_products(own_slots, other_slots, near_ref, turned_ref, inner_ref, far_ref, own_ref, other_ref, psi_ref):
+def left_products(
+    own_slots, other_hbm, near_ref, turned_ref, inner_ref, far_ref, own_ref, other_ref, psi_ref, other_slots, sem
+):
+    copy = pltpu.make_async_copy(other_hbm, other_slots, sem)
+    copy.start()
     fill(psi_ref, near_ref, turned_ref, inner_ref, far_ref)
     left_sums(1, own_slots, psi_ref, own_ref)
+    copy.wait()
     left_sums(2, other_slots, psi_ref, other_ref)
 
 
-def right_products(allowed_ref, right_ref, own_same, other_same, own_next, other_next, out_ref):
+def right_products(allowed_ref, *refs):
+    arrays, out_ref, held, sems = refs[:5], refs[5], refs[6:11], refs[11]
+    copies = [pltpu.make_async_copy(arrays[n], held[n], sems.at[n]) for n in range(5)]
+    for copy in copies:
+        copy.start()
+    for copy in copies:
+        copy.wait()
+    right_ref, own_same, other_same, own_next, other_next = held
     s, t = lax.axis_index("sec"), lax.axis_index("term")
     core = lax.rem(s, 2)
     parity = lax.rem(t, 2)
@@ -154,7 +173,7 @@
     turned = pl.pallas_call(
         turn,
         out_shape=jax.ShapeDtypeStruct((G * M, M), BF16),
-        in_specs=[pl.BlockSpec(memory_space=pl.ANY)],
+        in_specs=[ANY],
         out_specs=VMEM,
         scratch_shapes=[pltpu.VMEM((G, M, M), BF16), pltpu.SemaphoreType.DMA],
         compiler_params=PARAMS,
@@ -173,26 +192,33 @@
     inner = lax.ppermute(turned[H * M :], "sec", across)
     far = lax.ppermute(near[: H * M], "sec", across)
 
-    def left_call(slots):
+    def left_call(slots, weight):
         return pl.pallas_call(
             left_products,
             out_shape=[jax.ShapeDtypeStruct((H, NW // 2 * M, M), BF16)] * 2,
-            in_specs=[VMEM] * 6,
+            in_specs=[VMEM, ANY] + [VMEM] * 4,
             out_specs=[VMEM] * 2,
-            scratch_shapes=[pltpu.VMEM((4, H * M, M), BF16)],
+            scratch_shapes=[
+                pltpu.VMEM((4, H * M, M), BF16),
+                pltpu.VMEM((NW // 2, ROWS + 16, M), BF16),
+                pltpu.SemaphoreType.DMA,
+            ],
             compiler_params=PARAMS,
-            cost_estimate=pl.CostEstimate(flops=2 * 160 * M**3, bytes_accessed=3 << 20, transcendentals=0),
+            cost_estimate=pl.CostEstimate(flops=weight * M**3, bytes_accessed=3 << 20, transcendentals=0),
         )(slots, lax.ppermute(slots, "sec", across), near, turned, inner, far)
 
-    own_same, other_same = left_call(same)
+    own_same, other_same = left_call(same, WEIGHTS[0])
     following, own_same = together(following, own_same)
-    own_next, other_next = left_call(following)
+    own_next, other_next = left_call(following, WEIGHTS[1])
     right, own_next = together(right, own_next)
     results = pl.pallas_call(
         right_products,
         out_shape=jax.ShapeDtypeStruct((G, 2, M, M), BF16),
-        in_specs=[SMEM] + [VMEM] * 5,
+        in_specs=[SMEM] + [ANY] * 5,
         out_specs=VMEM,
+        scratch_shapes=[pltpu.VMEM((n_sec // 2, M, M), BF16)]
+        + [pltpu.VMEM((H, NW // 2 * M, M), BF16)] * 4
+        + [pltpu.SemaphoreType.DMA((5,))],
         compiler_params=PARAMS,
         cost_estimate=pl.CostEstimate(flops=2 * 64 * M**3, bytes_accessed=4 << 20, transcendentals=0),
     )(allowed, right, own_same, other_same, own_next, other_next)

time: 114 us -> 115 us (level)
  Pallas kernels: 15.6 us -> 18.6 us
    all_to_all x1, waiting for transfers between devices: 0.01 us -> 5.19 us  [on_device(): lax.all_to_all(jnp.tile(right, (n_sec // 2, 1, 1)), 'sec', 0, 0, axis_ind...]
    ppermute x1, waiting for transfers between devices: 4.53 us -> 0.01 us  [on_device(): following = lax.ppermute(same, 'term', [(i, i ^ 1) for i in range(n_term)])]
    pallas_call x2, Pallas kernels: 8.56 us -> 10.4 us  [left_call(): pl.pallas_call(left_products, out_shape=[jax.ShapeDtypeStruct((H, NW // 2...]
    pallas_call x1, Pallas kernels: 3.45 us -> 4.65 us  [on_device(): pl.pallas_call(right_products, out_shape=jax.ShapeDtypeStruct((G, 2, M, M...]
    unnamed x20 -> x18, local copies, waits for them, and re-layouts: 3.36 us -> 2.48 us
  transfers between devices with their start and end apart: 9 -> 9, of which waited for: 4 -> 4; matrix products, arithmetic and copies ran while one was open for 0% -> 1% of each run, Pallas kernels for 9% -> 11%
where the time goes in v7:
time: 115 us; the launch traced here: 114 us
  starting transfers between devices  49.2 us (43%)
  waiting for transfers between devices  24.8 us (22%)
  Pallas kernels  18.6 us (16%)
  blocking collectives  17.1 us (15%)
  local copies, waits for them, and re-layouts  4.44 us (4%)
    all_gather x1, blocking collectives, on_device(): lax.all_gather(payload, 'term', axis_index_groups=[list(range(parity, n_t...  17.1 us
    all_to_all x1, waiting for transfers between devices, on_device(): lax.all_to_all(results, BOTH, 0, 0, axis_index_groups=exchange, tiled=True)  16.9 us
    all_to_all x1, starting transfers between devices, on_device(): lax.all_to_all(results, BOTH, 0, 0, axis_index_groups=exchange, tiled=True)  12.3 us
    ppermute x1, starting transfers between devices, on_device(): right = lax.ppermute(right_env[0], BOTH, spread)  11.7 us
    pallas_call x2, Pallas kernels, left_call(): pl.pallas_call(left_products, out_shape=[jax.ShapeDtypeStruct((H, NW // 2...  10.4 us
    all_to_all x1, starting transfers between devices, on_device(): lax.all_to_all(jnp.tile(right, (n_sec // 2, 1, 1)), 'sec', 0, 0, axis_ind...  7.83 us
    all_to_all x1, waiting for transfers between devices, on_device(): lax.all_to_all(jnp.tile(right, (n_sec // 2, 1, 1)), 'sec', 0, 0, axis_ind...  5.19 us
    ppermute x1, starting transfers between devices, on_device(): lax.ppermute(turned, 'sec', [(i, i + 1) if i % 2 else (i, i - 1) for i in...  4.79 us
  transfers between devices with their start and end apart: 9, of which 4 were waited for; matrix products, arithmetic and copies ran while one was open for 1% of the time, Pallas kernels for 11%

profile of v7, /device:TPU:4, one launch (start us, length us, event | category | flops | bytes accessed | tf_op | source)
XLA Modules:
  0.0 114.3 jit_solution(11291269287489105671)
XLA Ops:
  0.0 0.0 copy-start.8
  0.0 1.8 %shard_map.64.turned_ref = bf16[1024,128]{1,0:T(8,128)(2,1)} custom-call(bf16[1,64,128,128]{3,2,1,0:T(8,128)(2,1)} %psi_ref.1), custom_call_target="tpu_custom_call" | custom-call | tf_op jit(solution)/shard_map/pallas_call | solution.py:173
  1.8 4.8 %collective-permute-start.1 = (bf16[1024,128]{1,0:T(8,128)(2,1)}, bf16[1024,128]{1,0:T(8,128)(2,1)S(1)}, u32[]{:S(2)}, u32[]{:S(2)}) collective-permute-start(bf16[1024,128]{1,0:T(8,128)(2,1)} %shard_map.64.turned_ref), channel_id=1, source_target_pairs={{8,16},{16,8},{24,32},{32,24},{40,48},{48,40},{56,64},{64,56},{72,... | collective-permute-start | bytes 786440 | tf_op jit(solution)/shard_map/ppermute | solution.py:183
  6.6 0.0 copy-done.8
  6.6 11.7 %collective-permute-start = (bf16[1,128,128]{2,1,0:T(8,128)(2,1)S(1)}, bf16[1,128,128]{2,1,0:T(8,128)(2,1)S(1)}, u32[]{:S(2)}, u32[]{:S(2)}) collective-permute-start(bf16[1,128,128]{2,1,0:T(8,128)(2,1)S(1)} %bitcast.12), channel_id=1, source_target_pairs={{0,352},{1,480},{2,224},{3,96},{4,112},{5,240},{6,496},{7,368},{8,... | collective-permute-start | bytes 98312 | tf_op jit(solution)/shard_map/ppermute | solution.py:164
  18.3 1.8 %shard_map.65 = bf16[656,128]{1,0:T(8,128)(2,1)} custom-call(s32[1,5]{1,0:T(1,128)} %shift_ref.1, bf16[640,128]{1,0:T(8,128)(2,1)} %bitcast.9, f32[5,64,64]{2,1,0:T(8,128)} %bitcast.10, s32[64,64]{1,0:T(8,128)} %allowed_ref.3), custom_call_target="tpu_custom_call" | custom-call | tf_op jit(solution)/shard_map/pallas_call | solution.py:165
  20.1 0.0 copy-start.2
  20.1 17.1 %all-gather = bf16[2624,128]{1,0:T(8,128)(2,1)S(1)} all-gather(bf16[656,128]{1,0:T(8,128)(2,1)} %shard_map.65), channel_id=2, replica_groups={{0,2,4,6},{1,3,5,7},{8,10,12,14},{9,11,13,15},{16,18,20,22},{17,19,21,2..., dimensions={0}, use_global_device_ids=true | all-gather | bytes 839680 | tf_op jit(solution)/shard_map/all_gather | solution.py:184
  37.2 0.0 copy-start.1
  37.2 0.0 collective-permute-done
  37.2 0.0 collective-permute-done.1.near_ref
  37.2 0.0 copy-start.3
  37.2 1.9 %collective-permute-start.3 = (bf16[4,656,128]{2,1,0:T(8,128)(2,1)S(1)}, bf16[4,656,128]{2,1,0:T(8,128)(2,1)}, u32[]{:S(2)}, u32[]{:S(2)}) collective-permute-start(bf16[4,656,128]{2,1,0:T(8,128)(2,1)S(1)} %bitcast.6), channel_id=1, source_target_pairs={{0,8},{8,0},{16,24},{24,16},{32,40},{40,32},{48,56},{56,48},{64,72... | collective-permute-start | bytes 2015240 | tf_op jit(solution)/shard_map/ppermute | solution.py:208
  39.2 4.0 %collective-permute-start.2 = (bf16[4,656,128]{2,1,0:T(8,128)(2,1)S(1)}, bf16[4,656,128]{2,1,0:T(8,128)(2,1)S(1)}, u32[]{:S(2)}, u32[]{:S(2)}) collective-permute-start(bf16[4,656,128]{2,1,0:T(8,128)(2,1)S(1)} %bitcast.7), channel_id=1, source_target_pairs={{0,1},{1,0},{2,3},{3,2},{4,5},{5,4},{6,7},{7,6},{8,9},{9,8},{10,11... | collective-permute-start | bytes 2015240 | tf_op jit(solution)/shard_map/ppermute | solution.py:188
  43.2 1.2 %tile.10 = bf16[32,128,128]{2,1,0:T(8,128)(2,1)} broadcast(bf16[128,128]{1,0:T(8,128)(2,1)S(1)} %bitcast.11), dimensions={1,2} | broadcast | bytes 1081344 | tf_op jit(solution)/shard_map/tile | solution.py:190
  44.4 7.8 %all-to-all-start = ((bf16[32,128,128]{2,1,0:T(8,128)(2,1)}), bf16[32,128,128]{2,1,0:T(8,128)(2,1)S(1)}, u32[]{:S(2)}, u32[]{:S(2)}) async-start(bf16[32,128,128]{2,1,0:T(8,128)(2,1)} %tile.10), calls=%async_computation | async-start | bytes 2097152 | tf_op jit(solution)/shard_map/all_to_all | solution.py:189
  52.2 0.0 copy-done.2
  52.3 1.9 %collective-permute-start.4 = (bf16[512,128]{1,0:T(8,128)(2,1)S(1)}, bf16[512,128]{1,0:T(8,128)(2,1)S(1)}, u32[]{:S(2)}, u32[]{:S(2)}) collective-permute-start(bf16[512,128]{1,0:T(8,128)(2,1)S(1)} %slice.8), channel_id=1, source_target_pairs={{0,8},{8,0},{16,24},{24,16},{32,40},{40,32},{48,56},{56,48},{64,72... | collective-permute-start | bytes 393224 | tf_op jit(solution)/shard_map/ppermute | solution.py:192
  54.2 2.4 %collective-permute-start.5 = (bf16[512,128]{1,0:T(8,128)(2,1)S(1)}, bf16[512,128]{1,0:T(8,128)(2,1)S(1)}, u32[]{:S(2)}, u32[]{:S(2)}) collective-permute-start(bf16[512,128]{1,0:T(8,128)(2,1)S(1)} %slice.7), channel_id=1, source_target_pairs={{0,8},{8,0},{16,24},{24,16},{32,40},{40,32},{48,56},{56,48},{64,72... | collective-permute-start | bytes 393224 | tf_op jit(solution)/shard_map/ppermute | solution.py:193
  56.6 0.0 collective-permute-done.4.inner_ref
  56.6 0.0 copy-start.6
  56.7 0.9 collective-permute-done.5.far_ref
  57.6 0.0 copy-start.7
  57.6 0.0 collective-permute-done.3.other_hbm
  57.6 0.0 copy-done.1
  57.6 0.0 copy-done.3
  57.6 0.0 copy-done.6
  57.6 0.6 copy-done.7
  58.2 5.2 %shard_map.66 = (bf16[4,512,128]{2,1,0:T(8,128)(2,1)}, bf16[4,512,128]{2,1,0:T(8,128)(2,1)}) custom-call(bf16[4,656,128]{2,1,0:T(8,128)(2,1)} %bitcast.8, bf16[4,656,128]{2,1,0:T(8,128)(2,1)} %collective-permute-done.3.other_hbm, bf16[1024,128]{1,0:T(8,128)(2,1)} %copy-done.3, bf16[1024,128]{1,0:T(8,128)(2,1)} %shard_map.64.turned_ref, ...), custom_call_target="tpu_custom_call" | custom-call | flops 671088640 | bytes 3145728 | tf_op jit(solution)/shard_map/pallas_call | solution.py:196
  63.4 0.0 collective-permute-done.2.own_slots
  63.4 0.0 copy-start.4
  63.4 2.3 %collective-permute-start.6 = (bf16[4,656,128]{2,1,0:T(8,128)(2,1)S(1)}, bf16[4,656,128]{2,1,0:T(8,128)(2,1)S(1)}, u32[]{:S(2)}, u32[]{:S(2)}) collective-permute-start(bf16[4,656,128]{2,1,0:T(8,128)(2,1)S(1)} %collective-permute-done.2.own_slots), channel_id=1, source_target_pairs={{0,8},{8,0},{16,24},{24,16},{32,40},{40,32},{48,56},{56,48},{64,72... | collective-permute-start | bytes 2015240 | tf_op jit(solution)/shard_map/ppermute | solution.py:208
  65.7 1.7 %collective-permute-done.6.other_hbm = bf16[4,656,128]{2,1,0:T(8,128)(2,1)S(1)} collective-permute-done((bf16[4,656,128]{2,1,0:T(8,128)(2,1)S(1)}, bf16[4,656,128]{2,1,0:T(8,128)(2,1)S(1)}, u32[]{:S(2)}, u32[]{:S(2)}) %collective-permute-start.6) | collective-permute-done | bytes 671776 | tf_op jit(solution)/shard_map/ppermute | solution.py:208
  67.5 0.0 copy-done.4
  67.5 0.0 copy-start.5
  67.5 0.8 copy-done.5
  68.3 5.2 %shard_map.67 = (bf16[4,512,128]{2,1,0:T(8,128)(2,1)}, bf16[4,512,128]{2,1,0:T(8,128)(2,1)}) custom-call(bf16[4,656,128]{2,1,0:T(8,128)(2,1)} %copy-done.4, bf16[4,656,128]{2,1,0:T(8,128)(2,1)} %copy-done.5, bf16[1024,128]{1,0:T(8,128)(2,1)} %copy-done.3, bf16[1024,128]{1,0:T(8,128)(2,1)} %shard_map.64.turned_ref, bf16[512,128]{1,0:T(8,128)(2,1)} %copy-done.6, ...), custom_call_target="tpu_custom_call" | custom-call | flops 8388608000 | bytes 3145728 | tf_op jit(solution)/shard_map/pallas_call | solution.py:196
  73.5 5.2 %all-to-all-done.refs_0_ = bf16[32,128,128]{2,1,0:T(8,128)(2,1)S(1)} async-done(((bf16[32,128,128]{2,1,0:T(8,128)(2,1)}), bf16[32,128,128]{2,1,0:T(8,128)(2,1)S(1)}, u32[]{:S(2)}, u32[]{:S(2)}) %all-to-all-start) | async-done | bytes 1048608 | tf_op jit(solution)/shard_map/all_to_all | solution.py:189
  78.7 0.0 copy-start
  78.7 1.0 copy-done
  79.7 4.7 %shard_map.68 = bf16[8,2,128,128]{3,2,1,0:T(8,128)(2,1)} custom-call(s32[64,64]{1,0:T(8,128)} %allowed_ref.3, bf16[32,128,128]{2,1,0:T(8,128)(2,1)} %copy-done, bf16[4,512,128]{2,1,0:T(8,128)(2,1)} %get-tuple-element.23.refs_1_, bf16[4,512,128]{2,1,0:T(8,128)(2,1)} %get-tuple-element.24.refs_2_, bf16[4,512,128]{2,1,0:T(8,128)(2,1)} %get-tuple-element.25.refs_3_, ...), custom_call_target="tpu_custom_call" | custom-call | flops 268435456 | bytes 4194304 | tf_op jit(solution)/shard_map/pallas_call | solution.py:214
  84.4 12.3 %all-to-all-start.1 = ((bf16[8,2,128,128]{3,2,1,0:T(8,128)(2,1)}), bf16[8,2,128,128]{3,2,1,0:T(8,128)(2,1)S(1)}, u32[]{:S(2)}, u32[]{:S(2)}) async-start(bf16[8,2,128,128]{3,2,1,0:T(8,128)(2,1)} %shard_map.68), calls=%async_computation.1 | async-start | bytes 1048576 | tf_op jit(solution)/shard_map/all_to_all | solution.py:226
  96.6 16.9 %all-to-all-done.1 = bf16[8,2,128,128]{3,2,1,0:T(8,128)(2,1)S(1)} async-done(((bf16[8,2,128,128]{3,2,1,0:T(8,128)(2,1)}), bf16[8,2,128,128]{3,2,1,0:T(8,128)(2,1)S(1)}, u32[]{:S(2)}, u32[]{:S(2)}) %all-to-all-start.1) | async-done | bytes 524320 | tf_op jit(solution)/shard_map/all_to_all | solution.py:226
  113.6 0.7 constant_dynamic-slice_fusion
  (2 shorter events, 0.0 us)
Async XLA Ops:
  0.0 6.6 %copy-start.8 = (bf16[1,1,128,128]{3,2,1,0:T(8,128)(2,1)S(1)}, bf16[1,1,128,128]{3,2,1,0:T(8,128)(2,1)}, u32[]{:S(2)}) copy-start(bf16[1,1,128,128]{3,2,1,0:T(8,128)(2,1)} %param.8) | copy-start | bytes 98308
  1.8 35.4 %collective-permute-start.1 = (bf16[1024,128]{1,0:T(8,128)(2,1)}, bf16[1024,128]{1,0:T(8,128)(2,1)S(1)}, u32[]{:S(2)}, u32[]{:S(2)}) collective-permute-start(bf16[1024,128]{1,0:T(8,128)(2,1)} %shard_map.64.turned_ref), channel_id=1, source_target_pairs={{8,16},{16,8},{24,32},{32,24},{40,48},{48,40},{56,64},{64,56},{72,... | collective-permute-start | bytes 786440 | tf_op jit(solution)/shard_map/ppermute | solution.py:183
  6.6 30.6 %collective-permute-start = (bf16[1,128,128]{2,1,0:T(8,128)(2,1)S(1)}, bf16[1,128,128]{2,1,0:T(8,128)(2,1)S(1)}, u32[]{:S(2)}, u32[]{:S(2)}) collective-permute-start(bf16[1,128,128]{2,1,0:T(8,128)(2,1)S(1)} %bitcast.12), channel_id=1, source_target_pairs={{0,352},{1,480},{2,224},{3,96},{4,112},{5,240},{6,496},{7,368},{8,... | collective-permute-start | bytes 98312 | tf_op jit(solution)/shard_map/ppermute | solution.py:164
  20.1 32.1 %copy-start.2 = (bf16[1024,128]{1,0:T(8,128)(2,1)S(1)}, bf16[1024,128]{1,0:T(8,128)(2,1)}, u32[]{:S(2)}) copy-start(bf16[1024,128]{1,0:T(8,128)(2,1)} %shard_map.64.turned_ref) | copy-start | bytes 786436
  37.2 20.4 %copy-start.1 = (bf16[2624,128]{1,0:T(8,128)(2,1)}, bf16[2624,128]{1,0:T(8,128)(2,1)S(1)}, u32[]{:S(2)}) copy-start(bf16[2624,128]{1,0:T(8,128)(2,1)S(1)} %all-gather) | copy-start | bytes 2015236
  37.2 20.4 %copy-start.3 = (bf16[1024,128]{1,0:T(8,128)(2,1)}, bf16[1024,128]{1,0:T(8,128)(2,1)S(1)}, u32[]{:S(2)}) copy-start(bf16[1024,128]{1,0:T(8,128)(2,1)S(1)} %collective-permute-done.1.near_ref) | copy-start | bytes 786436
  37.2 20.4 %collective-permute-start.3 = (bf16[4,656,128]{2,1,0:T(8,128)(2,1)S(1)}, bf16[4,656,128]{2,1,0:T(8,128)(2,1)}, u32[]{:S(2)}, u32[]{:S(2)}) collective-permute-start(bf16[4,656,128]{2,1,0:T(8,128)(2,1)S(1)} %bitcast.6), channel_id=1, source_target_pairs={{0,8},{8,0},{16,24},{24,16},{32,40},{40,32},{48,56},{56,48},{64,72... | collective-permute-start | bytes 2015240 | tf_op jit(solution)/shard_map/ppermute | solution.py:208
  39.2 24.3 %collective-permute-start.2 = (bf16[4,656,128]{2,1,0:T(8,128)(2,1)S(1)}, bf16[4,656,128]{2,1,0:T(8,128)(2,1)S(1)}, u32[]{:S(2)}, u32[]{:S(2)}) collective-permute-start(bf16[4,656,128]{2,1,0:T(8,128)(2,1)S(1)} %bitcast.7), channel_id=1, source_target_pairs={{0,1},{1,0},{2,3},{3,2},{4,5},{5,4},{6,7},{7,6},{8,9},{9,8},{10,11... | collective-permute-start | bytes 2015240 | tf_op jit(solution)/shard_map/ppermute | solution.py:188
  44.4 34.3 %all-to-all-start = ((bf16[32,128,128]{2,1,0:T(8,128)(2,1)}), bf16[32,128,128]{2,1,0:T(8,128)(2,1)S(1)}, u32[]{:S(2)}, u32[]{:S(2)}) async-start(bf16[32,128,128]{2,1,0:T(8,128)(2,1)} %tile.10), calls=%async_computation | async-start | bytes 2097152 | tf_op jit(solution)/shard_map/all_to_all | solution.py:189
  52.3 4.4 %collective-permute-start.4 = (bf16[512,128]{1,0:T(8,128)(2,1)S(1)}, bf16[512,128]{1,0:T(8,128)(2,1)S(1)}, u32[]{:S(2)}, u32[]{:S(2)}) collective-permute-start(bf16[512,128]{1,0:T(8,128)(2,1)S(1)} %slice.8), channel_id=1, source_target_pairs={{0,8},{8,0},{16,24},{24,16},{32,40},{40,32},{48,56},{56,48},{64,72... | collective-permute-start | bytes 393224 | tf_op jit(solution)/shard_map/ppermute | solution.py:192
  54.2 3.4 %collective-permute-start.5 = (bf16[512,128]{1,0:T(8,128)(2,1)S(1)}, bf16[512,128]{1,0:T(8,128)(2,1)S(1)}, u32[]{:S(2)}, u32[]{:S(2)}) collective-permute-start(bf16[512,128]{1,0:T(8,128)(2,1)S(1)} %slice.7), channel_id=1, source_target_pairs={{0,8},{8,0},{16,24},{24,16},{32,40},{40,32},{48,56},{56,48},{64,72... | collective-permute-start | bytes 393224 | tf_op jit(solution)/shard_map/ppermute | solution.py:193
  56.6 1.0 copy-start.6
  57.6 0.6 copy-start.7
  63.4 4.0 %copy-start.4 = (bf16[4,656,128]{2,1,0:T(8,128)(2,1)}, bf16[4,656,128]{2,1,0:T(8,128)(2,1)S(1)}, u32[]{:S(2)}) copy-start(bf16[4,656,128]{2,1,0:T(8,128)(2,1)S(1)} %collective-permute-done.2.own_slots) | copy-start | bytes 2015236
  63.4 4.0 %collective-permute-start.6 = (bf16[4,656,128]{2,1,0:T(8,128)(2,1)S(1)}, bf16[4,656,128]{2,1,0:T(8,128)(2,1)S(1)}, u32[]{:S(2)}, u32[]{:S(2)}) collective-permute-start(bf16[4,656,128]{2,1,0:T(8,128)(2,1)S(1)} %collective-permute-done.2.own_slots), channel_id=1, source_target_pairs={{0,8},{8,0},{16,24},{24,16},{32,40},{40,32},{48,56},{56,48},{64,72... | collective-permute-start | bytes 2015240 | tf_op jit(solution)/shard_map/ppermute | solution.py:208
  67.5 0.9 copy-start.5
  78.7 1.0 copy-start
  84.4 29.2 %all-to-all-start.1 = ((bf16[8,2,128,128]{3,2,1,0:T(8,128)(2,1)}), bf16[8,2,128,128]{3,2,1,0:T(8,128)(2,1)S(1)}, u32[]{:S(2)}, u32[]{:S(2)}) async-start(bf16[8,2,128,128]{3,2,1,0:T(8,128)(2,1)} %shard_map.68), calls=%async_computation.1 | async-start | bytes 1048576 | tf_op jit(solution)/shard_map/all_to_all | solution.py:226

commit v8 on v6

--- a/solution.py
+++ b/solution.py
@@ -26,7 +26,12 @@
 
 
 def right_chip(t, w, i):
-    return w // 2 * G + (t % 2 * H + 2 * i + w % 2 + G - 2) % G
+    ahead = (w - t) & 7
+    far = ahead >> 2
+    pair = far * (ahead - 4) + (1 - far) * (3 - ahead)
+    x = ((t >> 1) + (pair ^ (pair >> 1))) & 3
+    y = (4 * (t & 1) + far * (-1, 1, 2, 4)[i] + (1 - far) * (-2, 0, 3, 5)[i]) & 7
+    return x * 8 + y
 
 
 def pack(shift_ref, env_ref, coupling_ref, allowed_ref, payload_ref, table_ref):
@@ -75,7 +80,7 @@
     sector = lax.broadcasted_iota(jnp.int32, (M, H * M), 0)
     wanted = lax.broadcasted_iota(jnp.int32, (M, H * M), 1) // M * 2 + t * G + core
     pick = jnp.where((sector == wanted) | (sector == wanted + M // 2), 1.0, 0.0).astype(BF16)
-    for w in range(slots.shape[0]):
+    for w in range(NW):
         table = slots[w, ROWS : ROWS + 16, :]
         spread = jnp.dot(table, pick, preferred_element_type=F32)
         factors = spread[:8] + spread[8:]
@@ -98,22 +103,20 @@
                 out_ref[start // M + h, w * M : (w + 1) * M, :] = totals[h].astype(BF16)
 
 
-def left_products(own_slots, other_slots, near_ref, turned_ref, inner_ref, far_ref, own_ref, other_ref, psi_ref):
+def own_products(slots, near_ref, turned_ref, inner_ref, far_ref, out_ref, psi_ref):
     fill(psi_ref, near_ref, turned_ref, inner_ref, far_ref)
-    left_sums(1, own_slots, psi_ref, own_ref)
-    left_sums(2, other_slots, psi_ref, other_ref)
-
-
-def right_products(allowed_ref, right_ref, own_same, other_same, own_next, other_next, out_ref):
+    left_sums(1, slots, psi_ref, out_ref)
+
+
+def all_products(allowed_ref, slots, near_ref, turned_ref, inner_ref, far_ref, right_ref, own_ref, out_ref, psi_ref, other_ref):
+    fill(psi_ref, near_ref, turned_ref, inner_ref, far_ref)
+    left_sums(2, slots, psi_ref, other_ref)
     s, t = lax.axis_index("sec"), lax.axis_index("term")
     core = lax.rem(s, 2)
-    parity = lax.rem(t, 2)
     for i in range(H):
-        same = jnp.concatenate([right_ref[right_chip(t, 2 * m + parity, i)] for m in range(NW // 2)], axis=1)
-        following = jnp.concatenate([right_ref[right_chip(t, 2 * m + 1 - parity, i)] for m in range(NW // 2)], axis=1)
-        for same_ref, next_ref, which in ((own_same, own_next, core), (other_same, other_next, 1 - core)):
-            total = jnp.dot(same, same_ref[i], preferred_element_type=F32)
-            total += jnp.dot(following, next_ref[i], preferred_element_type=F32)
+        right = jnp.concatenate([right_ref[right_chip(t, w, i)] for w in range(NW)], axis=1)
+        for partial_ref, which in ((own_ref, core), (other_ref, 1 - core)):
+            total = jnp.dot(right, partial_ref[i], preferred_element_type=F32)
             keep = allowed_ref[s - core + which, t * G + 2 * i + core].astype(F32)
             value = (total * keep).T.astype(BF16)
             out_ref[i, which] = value
@@ -160,42 +163,36 @@
         compiler_params=PARAMS,
     )(wavefunction)
 
+    payloads = lax.all_gather(payload, "term")
     across = [(i, i ^ 1) for i in range(n_sec)]
     near = lax.ppermute(turned, "sec", [(i, i + 1) if i % 2 else (i, i - 1) for i in range(1, n_sec - 1)])
-    same = lax.all_gather(
-        payload, "term", axis_index_groups=[list(range(parity, n_term, 2)) for parity in range(2)]
-    )
-    right, near, same = together(right, near, same)
-    following = lax.ppermute(same, "term", [(i, i ^ 1) for i in range(n_term)])
+    right, near = together(right, near)
+    inner = lax.ppermute(turned[H * M :], "sec", across)
+    far = lax.ppermute(near[: H * M], "sec", across)
     right = lax.all_to_all(
         jnp.tile(right, (n_sec // 2, 1, 1)), "sec", 0, 0, axis_index_groups=by_core, tiled=True
     )
-    inner = lax.ppermute(turned[H * M :], "sec", across)
-    far = lax.ppermute(near[: H * M], "sec", across)
-
-    def left_call(slots):
-        return pl.pallas_call(
-            left_products,
-            out_shape=[jax.ShapeDtypeStruct((H, NW // 2 * M, M), BF16)] * 2,
-            in_specs=[VMEM] * 6,
-            out_specs=[VMEM] * 2,
-            scratch_shapes=[pltpu.VMEM((4, H * M, M), BF16)],
-            compiler_params=PARAMS,
-            cost_estimate=pl.CostEstimate(flops=2 * 160 * M**3, bytes_accessed=3 << 20, transcendentals=0),
-        )(slots, lax.ppermute(slots, "sec", across), near, turned, inner, far)
-
-    own_same, other_same = left_call(same)
-    following, own_same = together(following, own_same)
-    own_next, other_next = left_call(following)
-    right, own_next = together(right, own_next)
+    payloads, inner, far = together(payloads, inner, far)
+    other_payloads = lax.ppermute(payloads, "sec", across)
+
+    own = pl.pallas_call(
+        own_products,
+        out_shape=jax.ShapeDtypeStruct((H, NW * M, M), BF16),
+        in_specs=[VMEM] * 5,
+        out_specs=VMEM,
+        scratch_shapes=[pltpu.VMEM((4, H * M, M), BF16)],
+        compiler_params=PARAMS,
+        cost_estimate=pl.CostEstimate(flops=2 * 160 * M**3, bytes_accessed=3 << 20, transcendentals=0),
+    )(payloads, near, turned, inner, far)
     results = pl.pallas_call(
-        right_products,
+        all_products,
         out_shape=jax.ShapeDtypeStruct((G, 2, M, M), BF16),
-        in_specs=[SMEM] + [VMEM] * 5,
-        out_specs=VMEM,
-        compiler_params=PARAMS,
-        cost_estimate=pl.CostEstimate(flops=2 * 64 * M**3, bytes_accessed=4 << 20, transcendentals=0),
-    )(allowed, right, own_same, other_same, own_next, other_next)
+        in_specs=[SMEM] + [VMEM] * 7,
+        out_specs=VMEM,
+        scratch_shapes=[pltpu.VMEM((4, H * M, M), BF16), pltpu.VMEM((H, NW * M, M), BF16)],
+        compiler_params=PARAMS,
+        cost_estimate=pl.CostEstimate(flops=2 * 224 * M**3, bytes_accessed=6 << 20, transcendentals=0),
+    )(allowed, other_payloads, near, turned, inner, far, right, own)
 
     received = lax.all_to_all(results, BOTH, 0, 0, axis_index_groups=exchange, tiled=True)
     A = s // G

time: 114 us -> 110 us (0.965)
  blocking collectives: 17.5 us -> 0 us
  between operations: 0.16 us -> 13.5 us
  waiting for transfers between devices: 25.6 us -> 32.7 us
  starting transfers between devices: 49.2 us -> 45.4 us
  Pallas kernels: 15.6 us -> 13.6 us
  local copies, waits for them, and re-layouts: 5.36 us -> 4.06 us
    all_gather x1 -> x0, blocking collectives: 17.5 us -> none  [on_device(): lax.all_gather(payload, 'term', axis_index_groups=[list(range(parity, n_t...]
    all_gather x0 -> x1, waiting for transfers between devices: none -> 12.5 us  [on_device(): payloads = lax.all_gather(payload, 'term')]
    ppermute x3 -> x1, waiting for transfers between devices: 6.62 us -> 0.01 us  [on_device(): other_payloads = lax.ppermute(payloads, 'sec', across)]
    ppermute x3 -> x1, starting transfers between devices: 7.52 us -> 1.91 us  [on_device(): other_payloads = lax.ppermute(payloads, 'sec', across)]
    ppermute x1, starting transfers between devices: 2.13 us -> 4.45 us  [on_device(): inner = lax.ppermute(turned[H * M:], 'sec', across)]
    pallas_call x3 -> x2, Pallas kernels: 12 us -> 10.1 us  [the longest x1 5.6 us: on_device(): pl.pallas_call(all_products, out_shape=jax.ShapeDtypeStruct((G, 2, M, M),...]
    ppermute x1, waiting for transfers between devices: 0.01 us -> 1.58 us  [on_device(): right = lax.ppermute(right_env[0], BOTH, spread)]
    unnamed x20 -> x14, local copies, waits for them, and re-layouts: 3.36 us -> 2.09 us
  transfers between devices with their start and end apart: 9 -> 8, of which waited for: 4 -> 4; matrix products, arithmetic and copies ran while one was open for 0% -> 1% of each run, Pallas kernels for 9% -> 6%
where the time goes in v8:
time: 110 us; the launch traced here: 109 us
  starting transfers between devices  45.4 us (41%)
  waiting for transfers between devices  32.7 us (30%)
  Pallas kernels  13.6 us (12%)
  between operations  13.5 us (12%)
  local copies, waits for them, and re-layouts  4.06 us (4%)
    all_to_all x1, waiting for transfers between devices, on_device(): lax.all_to_all(results, BOTH, 0, 0, axis_index_groups=exchange, tiled=True)  17.4 us
    all_to_all x1, starting transfers between devices, on_device(): lax.all_to_all(results, BOTH, 0, 0, axis_index_groups=exchange, tiled=True)  13.4 us
    all_gather x1, waiting for transfers between devices, on_device(): payloads = lax.all_gather(payload, 'term')  12.5 us
    ppermute x1, starting transfers between devices, on_device(): right = lax.ppermute(right_env[0], BOTH, spread)  11.7 us
    all_to_all x1, starting transfers between devices, on_device(): lax.all_to_all(jnp.tile(right, (n_sec // 2, 1, 1)), 'sec', 0, 0, axis_ind...  7.22 us
    pallas_call x1, Pallas kernels, on_device(): pl.pallas_call(all_products, out_shape=jax.ShapeDtypeStruct((G, 2, M, M),...  5.6 us
    ppermute x1, starting transfers between devices, on_device(): lax.ppermute(turned, 'sec', [(i, i + 1) if i % 2 else (i, i - 1) for i in...  4.79 us
    pallas_call x1, Pallas kernels, on_device(): pl.pallas_call(own_products, out_shape=jax.ShapeDtypeStruct((H, NW * M, M...  4.45 us
  transfers between devices with their start and end apart: 8, of which 4 were waited for; matrix products, arithmetic and copies ran while one was open for 1% of the time, Pallas kernels for 6%

profile of v8, /device:TPU:4, one launch (start us, length us, event | category | flops | bytes accessed | tf_op | source)
XLA Modules:
  0.0 109.4 jit_solution(10652560436043683562)
XLA Ops:
  6.5 0.0 all-gather.3.cloned.1.call-start
  6.5 1.8 %shard_map.64 = bf16[656,128]{1,0:T(8,128)(2,1)} custom-call(s32[1,5]{1,0:T(1,128)} %shift_ref.1, bf16[640,128]{1,0:T(8,128)(2,1)} %bitcast.8, f32[5,64,64]{2,1,0:T(8,128)} %bitcast.9, s32[64,64]{1,0:T(8,128)} %allowed_ref.3), custom_call_target="tpu_custom_call" | custom-call | tf_op jit(solution)/shard_map/pallas_call | solution.py:149
  8.3 0.0 copy-start.6
  8.3 0.0 all-gather.3.cloned.1.call-update
  8.3 1.8 %shard_map.65.turned_ref = bf16[1024,128]{1,0:T(8,128)(2,1)} custom-call(bf16[1,64,128,128]{3,2,1,0:T(8,128)(2,1)} %psi_ref.1), custom_call_target="tpu_custom_call" | custom-call | tf_op jit(solution)/shard_map/pallas_call | solution.py:157
  10.1 4.8 %collective-permute-start.2 = (bf16[1024,128]{1,0:T(8,128)(2,1)}, bf16[1024,128]{1,0:T(8,128)(2,1)S(1)}, u32[]{:S(2)}, u32[]{:S(2)}) collective-permute-start(bf16[1024,128]{1,0:T(8,128)(2,1)} %shard_map.65.turned_ref), channel_id=1, source_target_pairs={{8,16},{16,8},{24,32},{32,24},{40,48},{48,40},{56,64},{64,56},{72,... | collective-permute-start | bytes 786440 | tf_op jit(solution)/shard_map/ppermute | solution.py:168
  14.9 0.0 copy-done.6
  15.0 11.7 %collective-permute-start.1 = (bf16[1,128,128]{2,1,0:T(8,128)(2,1)S(1)}, bf16[1,128,128]{2,1,0:T(8,128)(2,1)S(1)}, u32[]{:S(2)}, u32[]{:S(2)}) collective-permute-start(bf16[1,128,128]{2,1,0:T(8,128)(2,1)S(1)} %bitcast.11), channel_id=1, source_target_pairs={{0,352},{1,480},{2,224},{3,96},{4,112},{5,240},{6,496},{7,368},{8,... | collective-permute-start | bytes 98312 | tf_op jit(solution)/shard_map/ppermute | solution.py:148
  26.7 1.6 %collective-permute-done.1 = bf16[1,128,128]{2,1,0:T(8,128)(2,1)S(1)} collective-permute-done((bf16[1,128,128]{2,1,0:T(8,128)(2,1)S(1)}, bf16[1,128,128]{2,1,0:T(8,128)(2,1)S(1)}, u32[]{:S(2)}, u32[]{:S(2)}) %collective-permute-start.1) | collective-permute-done | bytes 32800 | tf_op jit(solution)/shard_map/ppermute | solution.py:148
  28.3 0.0 collective-permute-done.2.near_ref
  28.3 0.0 copy-start.2
  28.3 0.0 copy-start.1
  28.3 1.2 %tile.10 = bf16[32,128,128]{2,1,0:T(8,128)(2,1)} broadcast(bf16[128,128]{1,0:T(8,128)(2,1)S(1)} %bitcast.10), dimensions={1,2} | broadcast | bytes 1081344 | tf_op jit(solution)/shard_map/tile | solution.py:173
  29.5 7.2 %all-to-all-start = ((bf16[32,128,128]{2,1,0:T(8,128)(2,1)}), bf16[32,128,128]{2,1,0:T(8,128)(2,1)S(1)}, u32[]{:S(2)}, u32[]{:S(2)}) async-start(bf16[32,128,128]{2,1,0:T(8,128)(2,1)} %tile.10), calls=%async_computation | async-start | bytes 2097152 | tf_op jit(solution)/shard_map/all_to_all | solution.py:172
  36.7 0.0 copy-done.1
  36.8 4.5 %collective-permute-start = (bf16[512,128]{1,0:T(8,128)(2,1)S(1)}, bf16[512,128]{1,0:T(8,128)(2,1)S(1)}, u32[]{:S(2)}, u32[]{:S(2)}) collective-permute-start(bf16[512,128]{1,0:T(8,128)(2,1)S(1)} %slice.8), channel_id=1, source_target_pairs={{0,8},{8,0},{16,24},{24,16},{32,40},{40,32},{48,56},{56,48},{64,72... | collective-permute-start | bytes 393224 | tf_op jit(solution)/shard_map/ppermute | solution.py:170
  41.2 0.0 copy-done.2
  41.2 1.9 %collective-permute-start.3 = (bf16[512,128]{1,0:T(8,128)(2,1)S(1)}, bf16[512,128]{1,0:T(8,128)(2,1)S(1)}, u32[]{:S(2)}, u32[]{:S(2)}) collective-permute-start(bf16[512,128]{1,0:T(8,128)(2,1)S(1)} %slice.7), channel_id=1, source_target_pairs={{0,8},{8,0},{16,24},{24,16},{32,40},{40,32},{48,56},{56,48},{64,72... | collective-permute-start | bytes 393224 | tf_op jit(solution)/shard_map/ppermute | solution.py:171
  43.2 0.0 collective-permute-done.inner_ref
  43.2 0.0 copy-start.4
  43.2 1.3 %collective-permute-done.3.far_ref = bf16[512,128]{1,0:T(8,128)(2,1)S(1)} collective-permute-done((bf16[512,128]{1,0:T(8,128)(2,1)S(1)}, bf16[512,128]{1,0:T(8,128)(2,1)S(1)}, u32[]{:S(2)}, u32[]{:S(2)}) %collective-permute-start.3) | collective-permute-done | bytes 131104 | tf_op jit(solution)/shard_map/ppermute | solution.py:171
  44.5 0.0 copy-start.5
  44.5 12.5 %all-gather.3.cloned.1.call-done = bf16[5248,128]{1,0:T(8,128)(2,1)} async-done(((bf16[656,128]{1,0:T(8,128)(2,1)}), bf16[5248,128]{1,0:T(8,128)(2,1)}) %all-gather.3.cloned.1.call-update) | async-done | bytes 1343504 | tf_op jit(solution)/shard_map/all_gather | solution.py:166
  57.0 1.9 %collective-permute-start.4 = (bf16[8,656,128]{2,1,0:T(8,128)(2,1)}, bf16[8,656,128]{2,1,0:T(8,128)(2,1)S(1)}, u32[]{:S(2)}, u32[]{:S(2)}) collective-permute-start(bf16[8,656,128]{2,1,0:T(8,128)(2,1)} %bitcast.6), channel_id=1, source_target_pairs={{0,8},{8,0},{16,24},{24,16},{32,40},{40,32},{48,56},{56,48},{64,72... | collective-permute-start | bytes 4030472 | tf_op jit(solution)/shard_map/ppermute | solution.py:176
  58.9 0.0 copy-done.4
  58.9 0.0 copy-done.5
  58.9 4.5 %shard_map.66.own_ref = bf16[4,1024,128]{2,1,0:T(8,128)(2,1)} custom-call(bf16[8,656,128]{2,1,0:T(8,128)(2,1)} %bitcast.7, bf16[1024,128]{1,0:T(8,128)(2,1)} %copy-done.2, bf16[1024,128]{1,0:T(8,128)(2,1)} %shard_map.65.turned_ref, bf16[512,128]{1,0:T(8,128)(2,1)} %copy-done.4, bf16[512,128]{1,0:T(8,128)(2,1)} %copy-done.5), custom_call_target="tpu_custom_call" | custom-call | flops 671088640 | bytes 3145728 | tf_op jit(solution)/shard_map/pallas_call | solution.py:178
  63.4 0.0 all-to-all-done.right_ref
  63.4 0.0 copy-start
  63.4 0.0 collective-permute-done.4.slots
  63.4 1.0 copy-done
  64.4 0.0 copy-start.3
  64.4 1.1 copy-done.3
  65.5 5.6 %shard_map.67 = bf16[8,2,128,128]{3,2,1,0:T(8,128)(2,1)} custom-call(s32[64,64]{1,0:T(8,128)} %allowed_ref.3, bf16[8,656,128]{2,1,0:T(8,128)(2,1)} %copy-done.3, bf16[1024,128]{1,0:T(8,128)(2,1)} %copy-done.2, bf16[1024,128]{1,0:T(8,128)(2,1)} %shard_map.65.turned_ref, bf16[512,128]{1,0:T(8,128)(2,1)} %copy-done.4, bf16[512,128]{1,0:T(8,128)(2,1)} %copy-done.5, ...), custom_call_target="tpu_custom_call" | custom-call | flops 939524096 | bytes 6291456 | tf_op jit(solution)/shard_map/pallas_call | solution.py:187
  71.1 13.4 %all-to-all-start.1 = ((bf16[8,2,128,128]{3,2,1,0:T(8,128)(2,1)}), bf16[8,2,128,128]{3,2,1,0:T(8,128)(2,1)S(1)}, u32[]{:S(2)}, u32[]{:S(2)}) async-start(bf16[8,2,128,128]{3,2,1,0:T(8,128)(2,1)} %shard_map.67), calls=%async_computation.1 | async-start | bytes 1048576 | tf_op jit(solution)/shard_map/all_to_all | solution.py:197
  84.5 17.4 %all-to-all-done.1 = bf16[8,2,128,128]{3,2,1,0:T(8,128)(2,1)S(1)} async-done(((bf16[8,2,128,128]{3,2,1,0:T(8,128)(2,1)}), bf16[8,2,128,128]{3,2,1,0:T(8,128)(2,1)S(1)}, u32[]{:S(2)}, u32[]{:S(2)}) %all-to-all-start.1) | async-done | bytes 524320 | tf_op jit(solution)/shard_map/all_to_all | solution.py:197
  101.8 0.7 constant_dynamic-slice_fusion
  (2 shorter events, 0.0 us)
Async XLA Ops:
  6.5 50.5 %all-gather.3.cloned.1.call-start = ((), (), s32[]{:S(2)}) async-start(), calls=%async_computation.2 | async-start | bytes 1511424 | tf_op jit(solution)/shard_map/all_gather | solution.py:166
  8.3 6.6 %copy-start.6 = (bf16[1,1,128,128]{3,2,1,0:T(8,128)(2,1)S(1)}, bf16[1,1,128,128]{3,2,1,0:T(8,128)(2,1)}, u32[]{:S(2)}) copy-start(bf16[1,1,128,128]{3,2,1,0:T(8,128)(2,1)} %param.8) | copy-start | bytes 98308
  10.1 18.1 %collective-permute-start.2 = (bf16[1024,128]{1,0:T(8,128)(2,1)}, bf16[1024,128]{1,0:T(8,128)(2,1)S(1)}, u32[]{:S(2)}, u32[]{:S(2)}) collective-permute-start(bf16[1024,128]{1,0:T(8,128)(2,1)} %shard_map.65.turned_ref), channel_id=1, source_target_pairs={{8,16},{16,8},{24,32},{32,24},{40,48},{48,40},{56,64},{64,56},{72,... | collective-permute-start | bytes 786440 | tf_op jit(solution)/shard_map/ppermute | solution.py:168
  15.0 13.3 %collective-permute-start.1 = (bf16[1,128,128]{2,1,0:T(8,128)(2,1)S(1)}, bf16[1,128,128]{2,1,0:T(8,128)(2,1)S(1)}, u32[]{:S(2)}, u32[]{:S(2)}) collective-permute-start(bf16[1,128,128]{2,1,0:T(8,128)(2,1)S(1)} %bitcast.11), channel_id=1, source_target_pairs={{0,352},{1,480},{2,224},{3,96},{4,112},{5,240},{6,496},{7,368},{8,... | collective-permute-start | bytes 98312 | tf_op jit(solution)/shard_map/ppermute | solution.py:148
  28.3 12.9 %copy-start.2 = (bf16[1024,128]{1,0:T(8,128)(2,1)}, bf16[1024,128]{1,0:T(8,128)(2,1)S(1)}, u32[]{:S(2)}) copy-start(bf16[1024,128]{1,0:T(8,128)(2,1)S(1)} %collective-permute-done.2.near_ref) | copy-start | bytes 786436
  28.3 8.5 %copy-start.1 = (bf16[1024,128]{1,0:T(8,128)(2,1)S(1)}, bf16[1024,128]{1,0:T(8,128)(2,1)}, u32[]{:S(2)}) copy-start(bf16[1024,128]{1,0:T(8,128)(2,1)} %shard_map.65.turned_ref) | copy-start | bytes 786436
  29.5 33.9 %all-to-all-start = ((bf16[32,128,128]{2,1,0:T(8,128)(2,1)}), bf16[32,128,128]{2,1,0:T(8,128)(2,1)S(1)}, u32[]{:S(2)}, u32[]{:S(2)}) async-start(bf16[32,128,128]{2,1,0:T(8,128)(2,1)} %tile.10), calls=%async_computation | async-start | bytes 2097152 | tf_op jit(solution)/shard_map/all_to_all | solution.py:172
  36.8 6.4 %collective-permute-start = (bf16[512,128]{1,0:T(8,128)(2,1)S(1)}, bf16[512,128]{1,0:T(8,128)(2,1)S(1)}, u32[]{:S(2)}, u32[]{:S(2)}) collective-permute-start(bf16[512,128]{1,0:T(8,128)(2,1)S(1)} %slice.8), channel_id=1, source_target_pairs={{0,8},{8,0},{16,24},{24,16},{32,40},{40,32},{48,56},{56,48},{64,72... | collective-permute-start | bytes 393224 | tf_op jit(solution)/shard_map/ppermute | solution.py:170
  41.2 3.2 %collective-permute-start.3 = (bf16[512,128]{1,0:T(8,128)(2,1)S(1)}, bf16[512,128]{1,0:T(8,128)(2,1)S(1)}, u32[]{:S(2)}, u32[]{:S(2)}) collective-permute-start(bf16[512,128]{1,0:T(8,128)(2,1)S(1)} %slice.7), channel_id=1, source_target_pairs={{0,8},{8,0},{16,24},{24,16},{32,40},{40,32},{48,56},{56,48},{64,72... | collective-permute-start | bytes 393224 | tf_op jit(solution)/shard_map/ppermute | solution.py:171
  43.2 15.7 %copy-start.4 = (bf16[512,128]{1,0:T(8,128)(2,1)}, bf16[512,128]{1,0:T(8,128)(2,1)S(1)}, u32[]{:S(2)}) copy-start(bf16[512,128]{1,0:T(8,128)(2,1)S(1)} %collective-permute-done.inner_ref) | copy-start | bytes 393220
  44.5 14.4 %copy-start.5 = (bf16[512,128]{1,0:T(8,128)(2,1)}, bf16[512,128]{1,0:T(8,128)(2,1)S(1)}, u32[]{:S(2)}) copy-start(bf16[512,128]{1,0:T(8,128)(2,1)S(1)} %collective-permute-done.3.far_ref) | copy-start | bytes 393220
  57.0 6.4 %collective-permute-start.4 = (bf16[8,656,128]{2,1,0:T(8,128)(2,1)}, bf16[8,656,128]{2,1,0:T(8,128)(2,1)S(1)}, u32[]{:S(2)}, u32[]{:S(2)}) collective-permute-start(bf16[8,656,128]{2,1,0:T(8,128)(2,1)} %bitcast.6), channel_id=1, source_target_pairs={{0,8},{8,0},{16,24},{24,16},{32,40},{40,32},{48,56},{56,48},{64,72... | collective-permute-start | bytes 4030472 | tf_op jit(solution)/shard_map/ppermute | solution.py:176
  63.4 1.0 copy-start
  64.4 1.1 copy-start.3
  71.1 30.7 %all-to-all-start.1 = ((bf16[8,2,128,128]{3,2,1,0:T(8,128)(2,1)}), bf16[8,2,128,128]{3,2,1,0:T(8,128)(2,1)S(1)}, u32[]{:S(2)}, u32[]{:S(2)}) async-start(bf16[8,2,128,128]{3,2,1,0:T(8,128)(2,1)} %shard_map.67), calls=%async_computation.1 | async-start | bytes 1048576 | tf_op jit(solution)/shard_map/all_to_all | solution.py:197
Sparse Core Ops, SparseCore 0:
  9.4 47.5 all-gather.2

commit v9 on v8

--- a/solution.py
+++ b/solution.py
@@ -18,7 +18,7 @@
 BF16 = jnp.bfloat16
 VMEM = pl.BlockSpec(memory_space=pltpu.VMEM)
 SMEM = pl.BlockSpec(memory_space=pltpu.SMEM)
-PARAMS = pltpu.CompilerParams(vmem_limit_bytes=56 * 1024 * 1024)
+PARAMS = pltpu.CompilerParams(vmem_limit_bytes=16 * 1024 * 1024)
 
 
 def together(*arrays):

time: 110 us -> 110 us (level)
  Pallas kernels: 13.6 us -> 8.22 us
  local copies, waits for them, and re-layouts: 4.06 us -> 8.11 us
  starting transfers between devices: 45.4 us -> 47.3 us
    unnamed x14 -> x16, local copies, waits for them, and re-layouts: 2.09 us -> 6.16 us
    pallas_call x1, Pallas kernels: 4.45 us -> 2.02 us  [on_device(): pl.pallas_call(own_products, out_shape=jax.ShapeDtypeStruct((H, NW * M, M...]
    all_to_all x1, starting transfers between devices: 13.4 us -> 15.4 us  [on_device(): lax.all_to_all(results, BOTH, 0, 0, axis_index_groups=exchange, tiled=True)]
    pallas_call x1, Pallas kernels: 1.79 us -> 0.15 us  [on_device(): pl.pallas_call(turn, out_shape=jax.ShapeDtypeStruct((G * M, M), BF16), in...]
  transfers between devices with their start and end apart: 8 -> 8, of which waited for: 4 -> 4; matrix products, arithmetic and copies ran while one was open for 1% -> 1% of each run, Pallas kernels for 6% -> 2%
where the time goes in v9:
time: 110 us; the launch traced here: 109 us
  starting transfers between devices  47.3 us (43%)
  waiting for transfers between devices  32.1 us (29%)
  between operations  13.5 us (12%)
  Pallas kernels  8.22 us (7%)
  local copies, waits for them, and re-layouts  8.11 us (7%)
    all_to_all x1, waiting for transfers between devices, on_device(): lax.all_to_all(results, BOTH, 0, 0, axis_index_groups=exchange, tiled=True)  17.4 us
    all_to_all x1, starting transfers between devices, on_device(): lax.all_to_all(results, BOTH, 0, 0, axis_index_groups=exchange, tiled=True)  15.4 us
    all_gather x1, waiting for transfers between devices, on_device(): payloads = lax.all_gather(payload, 'term')  11.7 us
    ppermute x1, starting transfers between devices, on_device(): right = lax.ppermute(right_env[0], BOTH, spread)  11.7 us
    all_to_all x1, starting transfers between devices, on_device(): lax.all_to_all(jnp.tile(right, (n_sec // 2, 1, 1)), 'sec', 0, 0, axis_ind...  7.33 us
    unnamed x16, local copies, waits for them, and re-layouts  6.16 us
    ppermute x1, starting transfers between devices, on_device(): lax.ppermute(turned, 'sec', [(i, i + 1) if i % 2 else (i, i - 1) for i in...  4.79 us
    pallas_call x1, Pallas kernels, on_device(): pl.pallas_call(all_products, out_shape=jax.ShapeDtypeStruct((G, 2, M, M),...  4.73 us
  transfers between devices with their start and end apart: 8, of which 4 were waited for; matrix products, arithmetic and copies ran while one was open for 1% of the time, Pallas kernels for 2%

profile of v9, /device:TPU:4, one launch (start us, length us, event | category | flops | bytes accessed | tf_op | source)
XLA Modules:
  0.0 109.2 jit_solution(15485237656718052194)
XLA Ops:
  6.5 0.0 all-gather.3.cloned.1.call-start
  6.5 0.0 copy-start.2
  6.5 0.9 copy-done.2
  7.5 0.0 copy-start.3
  7.5 0.9 copy-done.3
  8.4 0.0 copy-start.4
  8.4 0.8 copy-done.4
  9.1 0.0 copy-start.6
  9.1 0.7 copy-done.6
  9.8 1.3 %shard_map.64 = bf16[656,128]{1,0:T(8,128)(2,1)} custom-call(s32[1,5]{1,0:T(1,128)S(1)} %copy-done.6, bf16[640,128]{1,0:T(8,128)(2,1)S(1)} %bitcast.8, f32[5,64,64]{2,1,0:T(8,128)S(1)} %bitcast.9, s32[64,64]{1,0:T(8,128)S(1)} %copy-done.4), custom_call_target="tpu_custom_call" | custom-call | tf_op jit(solution)/shard_map/pallas_call | solution.py:149
  11.1 0.0 copy-start.7
  11.1 0.0 all-gather.3.cloned.1.call-update
  11.1 0.0 copy-start
  11.1 1.6 %copy-done = bf16[1,64,128,128]{3,2,1,0:T(8,128)(2,1)S(1)} copy-done((bf16[1,64,128,128]{3,2,1,0:T(8,128)(2,1)S(1)}, bf16[1,64,128,128]{3,2,1,0:T(8,128)(2,1)}, u32[]{:S(2)}) %copy-start) | copy-done | bytes 2097176
  12.7 0.2 shard_map.65.turned_ref
  12.9 4.8 %collective-permute-start.2 = (bf16[1024,128]{1,0:T(8,128)(2,1)S(1)}, bf16[1024,128]{1,0:T(8,128)(2,1)S(1)}, u32[]{:S(2)}, u32[]{:S(2)}) collective-permute-start(bf16[1024,128]{1,0:T(8,128)(2,1)S(1)} %shard_map.65.turned_ref), channel_id=1, source_target_pairs={{8,16},{16,8},{24,32},{32,24},{40,48},{48,40},{56,64},{64,56},{72,... | collective-permute-start | bytes 786440 | tf_op jit(solution)/shard_map/ppermute | solution.py:168
  17.7 0.0 copy-done.7
  17.7 11.7 %collective-permute-start.1 = (bf16[1,128,128]{2,1,0:T(8,128)(2,1)S(1)}, bf16[1,128,128]{2,1,0:T(8,128)(2,1)S(1)}, u32[]{:S(2)}, u32[]{:S(2)}) collective-permute-start(bf16[1,128,128]{2,1,0:T(8,128)(2,1)S(1)} %bitcast.11), channel_id=1, source_target_pairs={{0,352},{1,480},{2,224},{3,96},{4,112},{5,240},{6,496},{7,368},{8,... | collective-permute-start | bytes 98312 | tf_op jit(solution)/shard_map/ppermute | solution.py:148
  29.4 1.6 %collective-permute-done.1 = bf16[1,128,128]{2,1,0:T(8,128)(2,1)S(1)} collective-permute-done((bf16[1,128,128]{2,1,0:T(8,128)(2,1)S(1)}, bf16[1,128,128]{2,1,0:T(8,128)(2,1)S(1)}, u32[]{:S(2)}, u32[]{:S(2)}) %collective-permute-start.1) | collective-permute-done | bytes 32800 | tf_op jit(solution)/shard_map/ppermute | solution.py:148
  31.0 0.0 collective-permute-done.2.near_ref
  31.0 1.2 %tile.10 = bf16[32,128,128]{2,1,0:T(8,128)(2,1)} broadcast(bf16[128,128]{1,0:T(8,128)(2,1)S(1)} %bitcast.10), dimensions={1,2} | broadcast | bytes 1081344 | tf_op jit(solution)/shard_map/tile | solution.py:173
  32.2 7.3 %all-to-all-start = ((bf16[32,128,128]{2,1,0:T(8,128)(2,1)}), bf16[32,128,128]{2,1,0:T(8,128)(2,1)S(1)}, u32[]{:S(2)}, u32[]{:S(2)}) async-start(bf16[32,128,128]{2,1,0:T(8,128)(2,1)} %tile.10), calls=%async_computation | async-start | bytes 2097152 | tf_op jit(solution)/shard_map/all_to_all | solution.py:172
  39.6 4.2 %collective-permute-start = (bf16[512,128]{1,0:T(8,128)(2,1)S(1)}, bf16[512,128]{1,0:T(8,128)(2,1)S(1)}, u32[]{:S(2)}, u32[]{:S(2)}) collective-permute-start(bf16[512,128]{1,0:T(8,128)(2,1)S(1)} %slice.8), channel_id=1, source_target_pairs={{0,8},{8,0},{16,24},{24,16},{32,40},{40,32},{48,56},{56,48},{64,72... | collective-permute-start | bytes 393224 | tf_op jit(solution)/shard_map/ppermute | solution.py:170
  43.8 1.9 %collective-permute-start.3 = (bf16[512,128]{1,0:T(8,128)(2,1)S(1)}, bf16[512,128]{1,0:T(8,128)(2,1)S(1)}, u32[]{:S(2)}, u32[]{:S(2)}) collective-permute-start(bf16[512,128]{1,0:T(8,128)(2,1)S(1)} %slice.7), channel_id=1, source_target_pairs={{0,8},{8,0},{16,24},{24,16},{32,40},{40,32},{48,56},{56,48},{64,72... | collective-permute-start | bytes 393224 | tf_op jit(solution)/shard_map/ppermute | solution.py:171
  45.8 0.0 collective-permute-done.inner_ref
  45.8 1.3 %collective-permute-done.3.far_ref = bf16[512,128]{1,0:T(8,128)(2,1)S(1)} collective-permute-done((bf16[512,128]{1,0:T(8,128)(2,1)S(1)}, bf16[512,128]{1,0:T(8,128)(2,1)S(1)}, u32[]{:S(2)}, u32[]{:S(2)}) %collective-permute-start.3) | collective-permute-done | bytes 131104 | tf_op jit(solution)/shard_map/ppermute | solution.py:171
  47.1 11.7 %all-gather.3.cloned.1.call-done = bf16[5248,128]{1,0:T(8,128)(2,1)} async-done(((bf16[656,128]{1,0:T(8,128)(2,1)}), bf16[5248,128]{1,0:T(8,128)(2,1)}) %all-gather.3.cloned.1.call-update) | async-done | bytes 1343504 | tf_op jit(solution)/shard_map/all_gather | solution.py:166
  58.8 1.9 %collective-permute-start.4 = (bf16[8,656,128]{2,1,0:T(8,128)(2,1)}, bf16[8,656,128]{2,1,0:T(8,128)(2,1)}, u32[]{:S(2)}, u32[]{:S(2)}) collective-permute-start(bf16[8,656,128]{2,1,0:T(8,128)(2,1)} %bitcast.6), channel_id=1, source_target_pairs={{0,8},{8,0},{16,24},{24,16},{32,40},{40,32},{48,56},{56,48},{64,72... | collective-permute-start | bytes 4030472 | tf_op jit(solution)/shard_map/ppermute | solution.py:176
  60.7 0.0 copy-start.1
  60.7 1.3 %copy-done.1 = bf16[5248,128]{1,0:T(8,128)(2,1)S(1)} copy-done((bf16[5248,128]{1,0:T(8,128)(2,1)S(1)}, bf16[5248,128]{1,0:T(8,128)(2,1)}, u32[]{:S(2)}) %copy-start.1) | copy-done | bytes 1343512
  62.1 0.0 copy-start.5
  62.1 2.0 %shard_map.66.own_ref = bf16[4,1024,128]{2,1,0:T(8,128)(2,1)S(1)} custom-call(bf16[8,656,128]{2,1,0:T(8,128)(2,1)S(1)} %bitcast.7, bf16[1024,128]{1,0:T(8,128)(2,1)S(1)} %collective-permute-done.2.near_ref, bf16[1024,128]{1,0:T(8,128)(2,1)S(1)} %shard_map.65.turned_ref, bf16[512,128]{1,0:T(8,128)(2,1)S(1)} %collective-permute-done.inner_ref, ...), custom_call_target="tpu_custom_call" | custom-call | flops 671088640 | bytes 3145728 | tf_op jit(solution)/shard_map/pallas_call | solution.py:178
  64.1 0.0 all-to-all-done.right_ref
  64.1 0.0 collective-permute-done.4.slots
  64.1 0.0 copy-done.5
  64.1 4.7 %shard_map.67 = bf16[8,2,128,128]{3,2,1,0:T(8,128)(2,1)} custom-call(s32[64,64]{1,0:T(8,128)S(1)} %copy-done.5, bf16[8,656,128]{2,1,0:T(8,128)(2,1)} %collective-permute-done.4.slots, bf16[1024,128]{1,0:T(8,128)(2,1)S(1)} %collective-permute-done.2.near_ref, bf16[1024,128]{1,0:T(8,128)(2,1)S(1)} %shard_map.65.turned_ref, ...), custom_call_target="tpu_custom_call" | custom-call | flops 939524096 | bytes 6291456 | tf_op jit(solution)/shard_map/pallas_call | solution.py:187
  68.9 15.4 %all-to-all-start.1 = ((bf16[8,2,128,128]{3,2,1,0:T(8,128)(2,1)}), bf16[8,2,128,128]{3,2,1,0:T(8,128)(2,1)S(1)}, u32[]{:S(2)}, u32[]{:S(2)}) async-start(bf16[8,2,128,128]{3,2,1,0:T(8,128)(2,1)} %shard_map.67), calls=%async_computation.1 | async-start | bytes 1048576 | tf_op jit(solution)/shard_map/all_to_all | solution.py:197
  84.2 17.4 %all-to-all-done.1 = bf16[8,2,128,128]{3,2,1,0:T(8,128)(2,1)S(1)} async-done(((bf16[8,2,128,128]{3,2,1,0:T(8,128)(2,1)}), bf16[8,2,128,128]{3,2,1,0:T(8,128)(2,1)S(1)}, u32[]{:S(2)}, u32[]{:S(2)}) %all-to-all-start.1) | async-done | bytes 524320 | tf_op jit(solution)/shard_map/all_to_all | solution.py:197
  101.7 0.7 constant_dynamic-slice_fusion
  (2 shorter events, 0.0 us)
Async XLA Ops:
  6.5 52.3 %all-gather.3.cloned.1.call-start = ((), (), s32[]{:S(2)}) async-start(), calls=%async_computation.2 | async-start | bytes 1511424 | tf_op jit(solution)/shard_map/all_gather | solution.py:166
  6.5 0.9 copy-start.2
  7.5 0.9 copy-start.3
  8.4 0.8 copy-start.4
  9.1 0.7 copy-start.6
  11.1 6.6 %copy-start.7 = (bf16[1,1,128,128]{3,2,1,0:T(8,128)(2,1)S(1)}, bf16[1,1,128,128]{3,2,1,0:T(8,128)(2,1)}, u32[]{:S(2)}) copy-start(bf16[1,1,128,128]{3,2,1,0:T(8,128)(2,1)} %param.8) | copy-start | bytes 98308
  11.1 1.6 %copy-start = (bf16[1,64,128,128]{3,2,1,0:T(8,128)(2,1)S(1)}, bf16[1,64,128,128]{3,2,1,0:T(8,128)(2,1)}, u32[]{:S(2)}) copy-start(bf16[1,64,128,128]{3,2,1,0:T(8,128)(2,1)} %psi_ref.1) | copy-start | bytes 6291460
  12.9 18.1 %collective-permute-start.2 = (bf16[1024,128]{1,0:T(8,128)(2,1)S(1)}, bf16[1024,128]{1,0:T(8,128)(2,1)S(1)}, u32[]{:S(2)}, u32[]{:S(2)}) collective-permute-start(bf16[1024,128]{1,0:T(8,128)(2,1)S(1)} %shard_map.65.turned_ref), channel_id=1, source_target_pairs={{8,16},{16,8},{24,32},{32,24},{40,48},{48,40},{56,64},{64,56},{72,... | collective-permute-start | bytes 786440 | tf_op jit(solution)/shard_map/ppermute | solution.py:168
  17.7 13.3 %collective-permute-start.1 = (bf16[1,128,128]{2,1,0:T(8,128)(2,1)S(1)}, bf16[1,128,128]{2,1,0:T(8,128)(2,1)S(1)}, u32[]{:S(2)}, u32[]{:S(2)}) collective-permute-start(bf16[1,128,128]{2,1,0:T(8,128)(2,1)S(1)} %bitcast.11), channel_id=1, source_target_pairs={{0,352},{1,480},{2,224},{3,96},{4,112},{5,240},{6,496},{7,368},{8,... | collective-permute-start | bytes 98312 | tf_op jit(solution)/shard_map/ppermute | solution.py:148
  32.2 31.9 %all-to-all-start = ((bf16[32,128,128]{2,1,0:T(8,128)(2,1)}), bf16[32,128,128]{2,1,0:T(8,128)(2,1)S(1)}, u32[]{:S(2)}, u32[]{:S(2)}) async-start(bf16[32,128,128]{2,1,0:T(8,128)(2,1)} %tile.10), calls=%async_computation | async-start | bytes 2097152 | tf_op jit(solution)/shard_map/all_to_all | solution.py:172
  39.6 6.2 %collective-permute-start = (bf16[512,128]{1,0:T(8,128)(2,1)S(1)}, bf16[512,128]{1,0:T(8,128)(2,1)S(1)}, u32[]{:S(2)}, u32[]{:S(2)}) collective-permute-start(bf16[512,128]{1,0:T(8,128)(2,1)S(1)} %slice.8), channel_id=1, source_target_pairs={{0,8},{8,0},{16,24},{24,16},{32,40},{40,32},{48,56},{56,48},{64,72... | collective-permute-start | bytes 393224 | tf_op jit(solution)/shard_map/ppermute | solution.py:170
  43.8 3.2 %collective-permute-start.3 = (bf16[512,128]{1,0:T(8,128)(2,1)S(1)}, bf16[512,128]{1,0:T(8,128)(2,1)S(1)}, u32[]{:S(2)}, u32[]{:S(2)}) collective-permute-start(bf16[512,128]{1,0:T(8,128)(2,1)S(1)} %slice.7), channel_id=1, source_target_pairs={{0,8},{8,0},{16,24},{24,16},{32,40},{40,32},{48,56},{56,48},{64,72... | collective-permute-start | bytes 393224 | tf_op jit(solution)/shard_map/ppermute | solution.py:171
  58.8 5.3 %collective-permute-start.4 = (bf16[8,656,128]{2,1,0:T(8,128)(2,1)}, bf16[8,656,128]{2,1,0:T(8,128)(2,1)}, u32[]{:S(2)}, u32[]{:S(2)}) collective-permute-start(bf16[8,656,128]{2,1,0:T(8,128)(2,1)} %bitcast.6), channel_id=1, source_target_pairs={{0,8},{8,0},{16,24},{24,16},{32,40},{40,32},{48,56},{56,48},{64,72... | collective-permute-start | bytes 4030472 | tf_op jit(solution)/shard_map/ppermute | solution.py:176
  60.7 1.3 %copy-start.1 = (bf16[5248,128]{1,0:T(8,128)(2,1)S(1)}, bf16[5248,128]{1,0:T(8,128)(2,1)}, u32[]{:S(2)}) copy-start(bf16[5248,128]{1,0:T(8,128)(2,1)} %all-gather.3.cloned.1.call-done) | copy-start | bytes 4030468
  62.1 2.1 %copy-start.5 = (s32[64,64]{1,0:T(8,128)S(1)}, s32[64,64]{1,0:T(8,128)}, u32[]{:S(2)}) copy-start(s32[64,64]{1,0:T(8,128)} %allowed_ref.3) | copy-start | bytes 49156
  68.9 32.8 %all-to-all-start.1 = ((bf16[8,2,128,128]{3,2,1,0:T(8,128)(2,1)}), bf16[8,2,128,128]{3,2,1,0:T(8,128)(2,1)S(1)}, u32[]{:S(2)}, u32[]{:S(2)}) async-start(bf16[8,2,128,128]{3,2,1,0:T(8,128)(2,1)} %shard_map.67), calls=%async_computation.1 | async-start | bytes 1048576 | tf_op jit(solution)/shard_map/all_to_all | solution.py:197
Sparse Core Ops, SparseCore 0:
  11.2 47.5 all-gather.2

commit v10 on v9

--- a/solution.py
+++ b/solution.py
@@ -19,6 +19,8 @@
 VMEM = pl.BlockSpec(memory_space=pltpu.VMEM)
 SMEM = pl.BlockSpec(memory_space=pltpu.SMEM)
 PARAMS = pltpu.CompilerParams(vmem_limit_bytes=16 * 1024 * 1024)
+FIRST = pltpu.CompilerParams(vmem_limit_bytes=56 * 1024 * 1024)
+SPREAD_COST = 3000
 
 
 def together(*arrays):
@@ -65,6 +67,11 @@
     for i in range(H):
         turned_ref[i * M : (i + 1) * M, :] = block_ref[2 * i + core].T
         turned_ref[(H + i) * M : (H + i + 1) * M, :] = block_ref[2 * i + 1 - core].T
+
+
+def copies(block_ref, out_ref):
+    for n in range(out_ref.shape[0]):
+        out_ref[n] = block_ref[0]
 
 
 def fill(psi_ref, near_ref, turned_ref, inner_ref, far_ref):
@@ -152,7 +159,7 @@
         in_specs=[SMEM] + [VMEM] * 3,
         out_specs=VMEM,
         scratch_shapes=[pltpu.VMEM((16, M), F32)],
-        compiler_params=PARAMS,
+        compiler_params=FIRST,
     )(left_shift, left_env.reshape(ROWS, M), coupling[0], allowed)
     turned = pl.pallas_call(
         turn,
@@ -160,18 +167,24 @@
         in_specs=[pl.BlockSpec(memory_space=pl.ANY)],
         out_specs=VMEM,
         scratch_shapes=[pltpu.VMEM((G, M, M), BF16), pltpu.SemaphoreType.DMA],
-        compiler_params=PARAMS,
+        compiler_params=FIRST,
     )(wavefunction)
 
     payloads = lax.all_gather(payload, "term")
     across = [(i, i ^ 1) for i in range(n_sec)]
     near = lax.ppermute(turned, "sec", [(i, i + 1) if i % 2 else (i, i - 1) for i in range(1, n_sec - 1)])
-    right, near = together(right, near)
+    sent = pl.pallas_call(
+        copies,
+        out_shape=jax.ShapeDtypeStruct((n_sec // 2, M, M), BF16),
+        in_specs=[VMEM],
+        out_specs=VMEM,
+        compiler_params=PARAMS,
+        cost_estimate=pl.CostEstimate(flops=SPREAD_COST * M**3, bytes_accessed=1 << 20, transcendentals=0),
+    )(right)
+    sent, near = together(sent, near)
     inner = lax.ppermute(turned[H * M :], "sec", across)
     far = lax.ppermute(near[: H * M], "sec", across)
-    right = lax.all_to_all(
-        jnp.tile(right, (n_sec // 2, 1, 1)), "sec", 0, 0, axis_index_groups=by_core, tiled=True
-    )
+    right = lax.all_to_all(sent, "sec", 0, 0, axis_index_groups=by_core, tiled=True)
     payloads, inner, far = together(payloads, inner, far)
     other_payloads = lax.ppermute(payloads, "sec", across)
 

time: 110 us -> 107 us (0.973)
  waiting for transfers between devices: 32.1 us -> 39.4 us
  starting transfers between devices: 47.3 us -> 40.4 us
  local copies, waits for them, and re-layouts: 8.11 us -> 2.07 us
  Pallas kernels: 8.22 us -> 11.4 us
    ppermute x1, waiting for transfers between devices: 0.01 us -> 6.97 us  [on_device(): lax.ppermute(turned, 'sec', [(i, i + 1) if i % 2 else (i, i - 1) for i in...]
    unnamed x16 -> x6, local copies, waits for them, and re-layouts: 6.16 us -> 1.33 us
    all_to_all x1, waiting for transfers between devices: 0.01 us -> 4.03 us  [on_device(): lax.all_to_all(sent, 'sec', 0, 0, axis_index_groups=by_core, tiled=True)]
    all_to_all x1, starting transfers between devices: 15.4 us -> 12.2 us  [on_device(): lax.all_to_all(results, BOTH, 0, 0, axis_index_groups=exchange, tiled=True)]
    ppermute x1, starting transfers between devices: 4.79 us -> 1.92 us  [on_device(): lax.ppermute(turned, 'sec', [(i, i + 1) if i % 2 else (i, i - 1) for i in...]
    ppermute x1, starting transfers between devices: 4.23 us -> 1.92 us  [on_device(): inner = lax.ppermute(turned[H * M:], 'sec', across)]
    ppermute x1, starting transfers between devices: 11.7 us -> 13.8 us  [on_device(): right = lax.ppermute(right_env[0], BOTH, spread)]
    pallas_call x1, Pallas kernels: 0.15 us -> 1.79 us  [on_device(): pl.pallas_call(turn, out_shape=jax.ShapeDtypeStruct((G * M, M), BF16), in...]
  transfers between devices with their start and end apart: 8 -> 8, of which waited for: 4 -> 5; matrix products, arithmetic and copies ran while one was open for 1% -> 0% of each run, Pallas kernels for 2% -> 5%
where the time goes in v10:
time: 107 us
  starting transfers between devices  40.4 us (38%)
  waiting for transfers between devices  39.4 us (37%)
  between operations  13.5 us (13%)
  Pallas kernels  11.4 us (11%)
  local copies, waits for them, and re-layouts  2.07 us (2%)
    all_to_all x1, waiting for transfers between devices, on_device(): lax.all_to_all(results, BOTH, 0, 0, axis_index_groups=exchange, tiled=True)  16 us
    ppermute x1, starting transfers between devices, on_device(): right = lax.ppermute(right_env[0], BOTH, spread)  13.8 us
    all_to_all x1, starting transfers between devices, on_device(): lax.all_to_all(results, BOTH, 0, 0, axis_index_groups=exchange, tiled=True)  12.2 us
    all_gather x1, waiting for transfers between devices, on_device(): payloads = lax.all_gather(payload, 'term')  11.4 us
    ppermute x1, waiting for transfers between devices, on_device(): lax.ppermute(turned, 'sec', [(i, i + 1) if i % 2 else (i, i - 1) for i in...  6.97 us
    all_to_all x1, starting transfers between devices, on_device(): lax.all_to_all(sent, 'sec', 0, 0, axis_index_groups=by_core, tiled=True)  6.23 us
    pallas_call x1, Pallas kernels, on_device(): pl.pallas_call(all_products, out_shape=jax.ShapeDtypeStruct((G, 2, M, M),...  4.72 us
    all_to_all x1, waiting for transfers between devices, on_device(): lax.all_to_all(sent, 'sec', 0, 0, axis_index_groups=by_core, tiled=True)  4.03 us
  transfers between devices with their start and end apart: 8, of which 5 were waited for; matrix products, arithmetic and copies ran while one was open for 0% of the time, Pallas kernels for 5%

profile of v10, /device:TPU:4, one launch (start us, length us, event | category | flops | bytes accessed | tf_op | source)
XLA Modules:
  0.0 106.8 jit_solution(10437105798504882535)
XLA Ops:
  6.5 0.0 all-gather.3.cloned.1.call-start
  6.5 1.8 %shard_map.64 = bf16[656,128]{1,0:T(8,128)(2,1)} custom-call(s32[1,5]{1,0:T(1,128)} %shift_ref.1, bf16[640,128]{1,0:T(8,128)(2,1)} %bitcast.7, f32[5,64,64]{2,1,0:T(8,128)} %bitcast.8, s32[64,64]{1,0:T(8,128)} %allowed_ref.3), custom_call_target="tpu_custom_call" | custom-call | tf_op jit(solution)/shard_map/pallas_call | solution.py:156
  8.3 0.0 all-gather.3.cloned.1.call-update
  8.3 13.8 %collective-permute-start.1 = (bf16[1,128,128]{2,1,0:T(8,128)(2,1)}, bf16[1,128,128]{2,1,0:T(8,128)(2,1)S(1)}, u32[]{:S(2)}, u32[]{:S(2)}) collective-permute-start(bf16[1,128,128]{2,1,0:T(8,128)(2,1)} %bitcast.9), channel_id=1, source_target_pairs={{0,352},{1,480},{2,224},{3,96},{4,112},{5,240},{6,496},{7,368},{8,... | collective-permute-start | bytes 98312 | tf_op jit(solution)/shard_map/ppermute | solution.py:155
  22.2 1.8 %shard_map.65.turned_ref = bf16[1024,128]{1,0:T(8,128)(2,1)} custom-call(bf16[1,64,128,128]{3,2,1,0:T(8,128)(2,1)} %psi_ref.1), custom_call_target="tpu_custom_call" | custom-call | tf_op jit(solution)/shard_map/pallas_call | solution.py:164
  24.0 1.9 %collective-permute-start.2 = (bf16[1024,128]{1,0:T(8,128)(2,1)}, bf16[1024,128]{1,0:T(8,128)(2,1)S(1)}, u32[]{:S(2)}, u32[]{:S(2)}) collective-permute-start(bf16[1024,128]{1,0:T(8,128)(2,1)} %shard_map.65.turned_ref), channel_id=1, source_target_pairs={{8,16},{16,8},{24,32},{32,24},{40,48},{48,40},{56,64},{64,56},{72,... | collective-permute-start | bytes 786440 | tf_op jit(solution)/shard_map/ppermute | solution.py:175
  25.9 0.0 collective-permute-done.1.block_ref
  25.9 1.1 %shard_map.66 = bf16[32,128,128]{2,1,0:T(8,128)(2,1)} custom-call(bf16[1,128,128]{2,1,0:T(8,128)(2,1)S(1)} %collective-permute-done.1.block_ref), custom_call_target="tpu_custom_call" | custom-call | flops 6291456000 | bytes 1048576 | tf_op jit(solution)/shard_map/pallas_call | solution.py:176
  27.0 0.0 copy-start
  27.0 7.0 %collective-permute-done.2.near_ref = bf16[1024,128]{1,0:T(8,128)(2,1)S(1)} collective-permute-done((bf16[1024,128]{1,0:T(8,128)(2,1)}, bf16[1024,128]{1,0:T(8,128)(2,1)S(1)}, u32[]{:S(2)}, u32[]{:S(2)}) %collective-permute-start.2) | collective-permute-done | bytes 262176 | tf_op jit(solution)/shard_map/ppermute | solution.py:175
  34.0 6.2 %all-to-all-start = ((bf16[32,128,128]{2,1,0:T(8,128)(2,1)}), bf16[32,128,128]{2,1,0:T(8,128)(2,1)S(1)}, u32[]{:S(2)}, u32[]{:S(2)}) async-start(bf16[32,128,128]{2,1,0:T(8,128)(2,1)} %shard_map.66), calls=%async_computation | async-start | bytes 2097152 | tf_op jit(solution)/shard_map/all_to_all | solution.py:187
  40.2 0.0 copy-done
  40.2 1.9 %collective-permute-start = (bf16[512,128]{1,0:T(8,128)(2,1)S(1)}, bf16[512,128]{1,0:T(8,128)(2,1)S(1)}, u32[]{:S(2)}, u32[]{:S(2)}) collective-permute-start(bf16[512,128]{1,0:T(8,128)(2,1)S(1)} %slice.8), channel_id=1, source_target_pairs={{0,8},{8,0},{16,24},{24,16},{32,40},{40,32},{48,56},{56,48},{64,72... | collective-permute-start | bytes 393224 | tf_op jit(solution)/shard_map/ppermute | solution.py:185
  42.2 2.4 %collective-permute-start.3 = (bf16[512,128]{1,0:T(8,128)(2,1)S(1)}, bf16[512,128]{1,0:T(8,128)(2,1)S(1)}, u32[]{:S(2)}, u32[]{:S(2)}) collective-permute-start(bf16[512,128]{1,0:T(8,128)(2,1)S(1)} %slice.7), channel_id=1, source_target_pairs={{0,8},{8,0},{16,24},{24,16},{32,40},{40,32},{48,56},{56,48},{64,72... | collective-permute-start | bytes 393224 | tf_op jit(solution)/shard_map/ppermute | solution.py:186
  44.6 0.0 collective-permute-done.inner_ref
  44.6 1.0 collective-permute-done.3.far_ref
  45.6 11.4 %all-gather.3.cloned.1.call-done = bf16[5248,128]{1,0:T(8,128)(2,1)} async-done(((bf16[656,128]{1,0:T(8,128)(2,1)}), bf16[5248,128]{1,0:T(8,128)(2,1)}) %all-gather.3.cloned.1.call-update) | async-done | bytes 1343504 | tf_op jit(solution)/shard_map/all_gather | solution.py:173
  57.0 1.9 %collective-permute-start.4 = (bf16[8,656,128]{2,1,0:T(8,128)(2,1)}, bf16[8,656,128]{2,1,0:T(8,128)(2,1)}, u32[]{:S(2)}, u32[]{:S(2)}) collective-permute-start(bf16[8,656,128]{2,1,0:T(8,128)(2,1)} %bitcast.5), channel_id=1, source_target_pairs={{0,8},{8,0},{16,24},{24,16},{32,40},{40,32},{48,56},{56,48},{64,72... | collective-permute-start | bytes 4030472 | tf_op jit(solution)/shard_map/ppermute | solution.py:189
  58.9 0.0 copy-start.1
  58.9 1.3 %copy-done.1 = bf16[5248,128]{1,0:T(8,128)(2,1)S(1)} copy-done((bf16[5248,128]{1,0:T(8,128)(2,1)S(1)}, bf16[5248,128]{1,0:T(8,128)(2,1)}, u32[]{:S(2)}) %copy-start.1) | copy-done | bytes 1343512
  60.2 0.0 copy-start.2
  60.2 2.0 %shard_map.67.own_ref = bf16[4,1024,128]{2,1,0:T(8,128)(2,1)S(1)} custom-call(bf16[8,656,128]{2,1,0:T(8,128)(2,1)S(1)} %bitcast.6, bf16[1024,128]{1,0:T(8,128)(2,1)S(1)} %collective-permute-done.2.near_ref, bf16[1024,128]{1,0:T(8,128)(2,1)S(1)} %copy-done, bf16[512,128]{1,0:T(8,128)(2,1)S(1)} %collective-permute-done.inner_ref, ...), custom_call_target="tpu_custom_call" | custom-call | flops 671088640 | bytes 3145728 | tf_op jit(solution)/shard_map/pallas_call | solution.py:191
  62.3 4.0 %all-to-all-done.right_ref = bf16[32,128,128]{2,1,0:T(8,128)(2,1)S(1)} async-done(((bf16[32,128,128]{2,1,0:T(8,128)(2,1)}), bf16[32,128,128]{2,1,0:T(8,128)(2,1)S(1)}, u32[]{:S(2)}, u32[]{:S(2)}) %all-to-all-start) | async-done | bytes 1048608 | tf_op jit(solution)/shard_map/all_to_all | solution.py:187
  66.3 0.0 collective-permute-done.4.slots
  66.3 0.0 copy-done.2
  66.3 4.7 %shard_map.68 = bf16[8,2,128,128]{3,2,1,0:T(8,128)(2,1)} custom-call(s32[64,64]{1,0:T(8,128)S(1)} %copy-done.2, bf16[8,656,128]{2,1,0:T(8,128)(2,1)} %collective-permute-done.4.slots, bf16[1024,128]{1,0:T(8,128)(2,1)S(1)} %collective-permute-done.2.near_ref, bf16[1024,128]{1,0:T(8,128)(2,1)S(1)} %copy-done, ...), custom_call_target="tpu_custom_call" | custom-call | flops 939524096 | bytes 6291456 | tf_op jit(solution)/shard_map/pallas_call | solution.py:200
  71.0 12.2 %all-to-all-start.1 = ((bf16[8,2,128,128]{3,2,1,0:T(8,128)(2,1)}), bf16[8,2,128,128]{3,2,1,0:T(8,128)(2,1)S(1)}, u32[]{:S(2)}, u32[]{:S(2)}) async-start(bf16[8,2,128,128]{3,2,1,0:T(8,128)(2,1)} %shard_map.68), calls=%async_computation.1 | async-start | bytes 1048576 | tf_op jit(solution)/shard_map/all_to_all | solution.py:210
  83.2 16.0 %all-to-all-done.1 = bf16[8,2,128,128]{3,2,1,0:T(8,128)(2,1)S(1)} async-done(((bf16[8,2,128,128]{3,2,1,0:T(8,128)(2,1)}), bf16[8,2,128,128]{3,2,1,0:T(8,128)(2,1)S(1)}, u32[]{:S(2)}, u32[]{:S(2)}) %all-to-all-start.1) | async-done | bytes 524320 | tf_op jit(solution)/shard_map/all_to_all | solution.py:210
  99.2 0.7 constant_dynamic-slice_fusion
  (2 shorter events, 0.0 us)
Async XLA Ops:
  6.5 50.5 %all-gather.3.cloned.1.call-start = ((), (), s32[]{:S(2)}) async-start(), calls=%async_computation.2 | async-start | bytes 1511424 | tf_op jit(solution)/shard_map/all_gather | solution.py:173
  8.3 17.6 %collective-permute-start.1 = (bf16[1,128,128]{2,1,0:T(8,128)(2,1)}, bf16[1,128,128]{2,1,0:T(8,128)(2,1)S(1)}, u32[]{:S(2)}, u32[]{:S(2)}) collective-permute-start(bf16[1,128,128]{2,1,0:T(8,128)(2,1)} %bitcast.9), channel_id=1, source_target_pairs={{0,352},{1,480},{2,224},{3,96},{4,112},{5,240},{6,496},{7,368},{8,... | collective-permute-start | bytes 98312 | tf_op jit(solution)/shard_map/ppermute | solution.py:155
  24.0 10.0 %collective-permute-start.2 = (bf16[1024,128]{1,0:T(8,128)(2,1)}, bf16[1024,128]{1,0:T(8,128)(2,1)S(1)}, u32[]{:S(2)}, u32[]{:S(2)}) collective-permute-start(bf16[1024,128]{1,0:T(8,128)(2,1)} %shard_map.65.turned_ref), channel_id=1, source_target_pairs={{8,16},{16,8},{24,32},{32,24},{40,48},{48,40},{56,64},{64,56},{72,... | collective-permute-start | bytes 786440 | tf_op jit(solution)/shard_map/ppermute | solution.py:175
  27.0 13.2 %copy-start = (bf16[1024,128]{1,0:T(8,128)(2,1)S(1)}, bf16[1024,128]{1,0:T(8,128)(2,1)}, u32[]{:S(2)}) copy-start(bf16[1024,128]{1,0:T(8,128)(2,1)} %shard_map.65.turned_ref) | copy-start | bytes 786436
  34.0 32.3 %all-to-all-start = ((bf16[32,128,128]{2,1,0:T(8,128)(2,1)}), bf16[32,128,128]{2,1,0:T(8,128)(2,1)S(1)}, u32[]{:S(2)}, u32[]{:S(2)}) async-start(bf16[32,128,128]{2,1,0:T(8,128)(2,1)} %shard_map.66), calls=%async_computation | async-start | bytes 2097152 | tf_op jit(solution)/shard_map/all_to_all | solution.py:187
  40.2 4.4 %collective-permute-start = (bf16[512,128]{1,0:T(8,128)(2,1)S(1)}, bf16[512,128]{1,0:T(8,128)(2,1)S(1)}, u32[]{:S(2)}, u32[]{:S(2)}) collective-permute-start(bf16[512,128]{1,0:T(8,128)(2,1)S(1)} %slice.8), channel_id=1, source_target_pairs={{0,8},{8,0},{16,24},{24,16},{32,40},{40,32},{48,56},{56,48},{64,72... | collective-permute-start | bytes 393224 | tf_op jit(solution)/shard_map/ppermute | solution.py:185
  42.2 3.4 %collective-permute-start.3 = (bf16[512,128]{1,0:T(8,128)(2,1)S(1)}, bf16[512,128]{1,0:T(8,128)(2,1)S(1)}, u32[]{:S(2)}, u32[]{:S(2)}) collective-permute-start(bf16[512,128]{1,0:T(8,128)(2,1)S(1)} %slice.7), channel_id=1, source_target_pairs={{0,8},{8,0},{16,24},{24,16},{32,40},{40,32},{48,56},{56,48},{64,72... | collective-permute-start | bytes 393224 | tf_op jit(solution)/shard_map/ppermute | solution.py:186
  57.0 9.3 %collective-permute-start.4 = (bf16[8,656,128]{2,1,0:T(8,128)(2,1)}, bf16[8,656,128]{2,1,0:T(8,128)(2,1)}, u32[]{:S(2)}, u32[]{:S(2)}) collective-permute-start(bf16[8,656,128]{2,1,0:T(8,128)(2,1)} %bitcast.5), channel_id=1, source_target_pairs={{0,8},{8,0},{16,24},{24,16},{32,40},{40,32},{48,56},{56,48},{64,72... | collective-permute-start | bytes 4030472 | tf_op jit(solution)/shard_map/ppermute | solution.py:189
  58.9 1.3 %copy-start.1 = (bf16[5248,128]{1,0:T(8,128)(2,1)S(1)}, bf16[5248,128]{1,0:T(8,128)(2,1)}, u32[]{:S(2)}) copy-start(bf16[5248,128]{1,0:T(8,128)(2,1)} %all-gather.3.cloned.1.call-done) | copy-start | bytes 4030468
  60.2 6.1 %copy-start.2 = (s32[64,64]{1,0:T(8,128)S(1)}, s32[64,64]{1,0:T(8,128)}, u32[]{:S(2)}) copy-start(s32[64,64]{1,0:T(8,128)} %allowed_ref.3) | copy-start | bytes 49156
  71.0 28.2 %all-to-all-start.1 = ((bf16[8,2,128,128]{3,2,1,0:T(8,128)(2,1)}), bf16[8,2,128,128]{3,2,1,0:T(8,128)(2,1)S(1)}, u32[]{:S(2)}, u32[]{:S(2)}) async-start(bf16[8,2,128,128]{3,2,1,0:T(8,128)(2,1)} %shard_map.68), calls=%async_computation.1 | async-start | bytes 1048576 | tf_op jit(solution)/shard_map/all_to_all | solution.py:210
Sparse Core Ops, SparseCore 0:
  9.4 47.5 all-gather.2

commit v11 on v10

v11 whole, which is shorter than its diff:
```python
import functools

import jax
import jax.numpy as jnp
from jax import lax
from jax.experimental import pallas as pl
from jax.experimental.pallas import tpu as pltpu
from jax.sharding import PartitionSpec as P

M = 128
LB = 5
NW = 8
G = 8
H = G // 2
BOTH = ("sec", "term")
ROWS = LB * M
F32 = jnp.float32
BF16 = jnp.bfloat16
VMEM = pl.BlockSpec(memory_space=pltpu.VMEM)
SMEM = pl.BlockSpec(memory_space=pltpu.SMEM)
PARAMS = pltpu.CompilerParams(vmem_limit_bytes=16 * 1024 * 1024)
FIRST = pltpu.CompilerParams(vmem_limit_bytes=56 * 1024 * 1024)
SPREAD_COST = 100


def together(*arrays):
    return lax.optimization_barrier(arrays)


def right_chip(t, w, i):
    ahead = (w - t) & 7
    far = ahead >> 2
    pair = far * (ahead - 4) + (1 - far) * (3 - ahead)
    x = ((t >> 1) + (pair ^ (pair >> 1))) & 3
    y = (4 * (t & 1) + far * (-1, 1, 2, 4)[i] + (1 - far) * (-2, 0, 3, 5)[i]) & 7
    return x * 8 + y


def pack(shift_ref, env_ref, coupling_ref, allowed_ref, payload_ref, table_ref):
    s = lax.axis_index("sec")
    n_sec = allowed_ref.shape[0]
    payload_ref[:ROWS, :] = env_ref[...]
    table_ref[...] = jnp.zeros_like(table_ref)
    lane = lax.broadcasted_iota(jnp.int32, (1, M), 1)
    shifts = jnp.zeros((1, M), F32)
    for c in range(LB):
        shift = shift_ref[0, c]
        source = s + shift
        inside = jnp.logical_and(source >= 0, source < n_sec).astype(F32)
        kept = allowed_ref[pl.ds(jnp.clip(source, 0, n_sec - 1), 1), :].astype(F32) * inside
        factor = coupling_ref[c, pl.ds(s, 1), :] * kept
        high = factor.astype(BF16).astype(F32)
        middle = (factor - high).astype(BF16).astype(F32)
        low = (factor - high - middle).astype(BF16).astype(F32)
        table_ref[c : c + 1, :] = jnp.concatenate([high, middle], axis=1)
        table_ref[8 + c : 9 + c, :n_sec] = low
        shifts = jnp.where(lane == c, shift.astype(F32), shifts)
    table_ref[15:16, :] = shifts
    payload_ref[ROWS:, :] = table_ref[...].astype(BF16)


def turn(psi_ref, turned_ref, block_ref, sem):
    copy = pltpu.make_async_copy(psi_ref.at[0, pl.ds(lax.axis_index("term") * G, G)], block_ref, sem)
    copy.start()
    copy.wait()
    for j in range(G):
        turned_ref[j * M : (j + 1) * M, :] = block_ref[j].T


def copies(block_ref, out_ref):
    for n in range(out_ref.shape[0]):
        out_ref[n] = block_ref[0]


def left_products(slots, below_ref, turned_ref, above_ref, out_ref, psi_ref):
    for row, ref in enumerate((below_ref, turned_ref, above_ref)):
        psi_ref[row] = ref[...]
    t = lax.axis_index("term")
    sector = lax.broadcasted_iota(jnp.int32, (M, G * M), 0)
    wanted = lax.broadcasted_iota(jnp.int32, (M, G * M), 1) // M + t * G
    pick = jnp.where((sector == wanted) | (sector == wanted + M // 2), 1.0, 0.0).astype(BF16)
    for w in range(H):
        table = slots[w, ROWS : ROWS + 16, :]
        spread = jnp.dot(table, pick, preferred_element_type=F32)
        factors = spread[:8] + spread[8:]
        shifts = table.astype(F32)[15:16, :]
        rows = [shifts[0, c].astype(jnp.int32) + 1 for c in range(LB)]
        for start in range(0, G * M, 2 * M):
            totals = [None, None]
            for c in range(LB):
                product = lax.dot_general(
                    psi_ref[rows[c], start : start + 2 * M, :],
                    slots[w, c * M : (c + 1) * M, :],
                    (((1,), (1,)), ((), ())),
                    preferred_element_type=F32,
                )
                for h in range(2):
                    at = start + h * M
                    term = product[h * M : (h + 1) * M] * factors[c : c + 1, at : at + M]
                    totals[h] = term if totals[h] is None else totals[h] + term
            for h in range(2):
                out_ref[start // M + h, w * M : (w + 1) * M, :] = totals[h].astype(BF16)


def right_sum(i, side, right_ref, same_ref, next_ref, allowed_ref):
    s, t = lax.axis_index("sec"), lax.axis_index("term")
    parity = lax.rem(t, 2)
    j = 2 * i + side
    same = jnp.concatenate([right_ref[right_chip(t, 2 * m + parity, i)] for m in range(H)], axis=1)
    following = jnp.concatenate([right_ref[right_chip(t, 2 * m + 1 - parity, i)] for m in range(H)], axis=1)
    total = jnp.dot(same, same_ref[j], preferred_element_type=F32)
    total += jnp.dot(following, next_ref[j], preferred_element_type=F32)
    return (total * allowed_ref[s, t * G + j].astype(F32)).T.astype(BF16)


def right_own(allowed_ref, right_ref, same_ref, next_ref, out_ref):
    core = lax.rem(lax.axis_index("sec"), 2)
    for i in range(H):
        out_ref[i] = right_sum(i, core, right_ref, same_ref, next_ref, allowed_ref)


def right_other(allowed_ref, right_ref, same_ref, next_ref, own_ref, out_ref):
    core = lax.rem(lax.axis_index("sec"), 2)
    for i in range(H):
        value = right_sum(i, 1 - core, right_ref, same_ref, next_ref, allowed_ref)
        out_ref[2 * i + 1 - core] = value
        out_ref[G + 2 * i + 1 - core] = value
        mine = own_ref[i]
        out_ref[2 * i + core] = mine
        out_ref[G + 2 * i + core] = mine


def on_device(wavefunction, left_env, right_env, coupling, left_shift, allowed, *, n_sec, n_term):
    s, t = lax.axis_index("sec"), lax.axis_index("term")
    groups = n_sec // G

    def device(sec, term):
        return sec * n_term + term

    spread = [
        (device(b, w), device(2 * right_chip(b // G, w, b % G // 2) + b % 2, b // G))
        for b in range(n_sec)
        for w in range(n_term)
    ]
    by_core = [[2 * chip + core for chip in range(n_sec // 2)] for core in range(2)]
    def members(A, B):
        return [device(A * G + i, B) for i in range(G)]

    exchange = [members(A, B) + members(B, A) for A in range(groups) for B in range(A + 1, groups)]
    exchange += [members(A, A) + members(A + 1, A + 1) for A in range(0, groups, 2)]

    right = lax.ppermute(right_env[0], BOTH, spread)
    payload = pl.pallas_call(
        pack,
        out_shape=jax.ShapeDtypeStruct((ROWS + 16, M), BF16),
        in_specs=[SMEM] + [VMEM] * 3,
        out_specs=VMEM,
        scratch_shapes=[pltpu.VMEM((16, M), F32)],
        compiler_params=FIRST,
    )(left_shift, left_env.reshape(ROWS, M), coupling[0], allowed)
    turned = pl.pallas_call(
        turn,
        out_shape=jax.ShapeDtypeStruct((G * M, M), BF16),
        in_specs=[pl.BlockSpec(memory_space=pl.ANY)],
        out_specs=VMEM,
        scratch_shapes=[pltpu.VMEM((G, M, M), BF16), pltpu.SemaphoreType.DMA],
        compiler_params=FIRST,
    )(wavefunction)

    below = lax.ppermute(turned, "sec", [(i, i + 1) for i in range(n_sec - 1)])
    above = lax.ppermute(turned, "sec", [(i + 1, i) for i in range(n_sec - 1)])
    sent = pl.pallas_call(
        copies,
        out_shape=jax.ShapeDtypeStruct((n_sec // 2, M, M), BF16),
        in_specs=[VMEM],
        out_specs=VMEM,
        compiler_params=PARAMS,
        cost_estimate=pl.CostEstimate(flops=SPREAD_COST * M**3, bytes_accessed=1 << 20, transcendentals=0),
    )(right)
    sent, below, above, payload = together(sent, below, above, payload)
    right = lax.all_to_all(sent, "sec", 0, 0, axis_index_groups=by_core, tiled=True)
    same = lax.all_gather(
        payload, "term", axis_index_groups=[list(range(parity, n_term, 2)) for parity in range(2)]
    )
    following = lax.ppermute(same, "term", [(i, i ^ 1) for i in range(n_term)])

    def left_call(slots):
        return pl.pallas_call(
            left_products,
            out_shape=jax.ShapeDtypeStruct((G, H * M, M), BF16),
            in_specs=[VMEM] * 4,
            out_specs=VMEM,
            scratch_shapes=[pltpu.VMEM((3, G * M, M), BF16)],
            compiler_params=PARAMS,
            cost_estimate=pl.CostEstimate(flops=2 * 160 * M**3, bytes_accessed=3 << 20, transcendentals=0),
        )(slots, below, turned, above)

    partial_same = left_call(same)
    following, partial_same, right = together(following, partial_same, right)
    partial_next = left_call(following)
    others = lax.ppermute(right, "sec", [(i, i ^ 1) for i in range(n_sec)])
    cost = pl.CostEstimate(flops=2 * 32 * M**3, bytes_accessed=2 << 20, transcendentals=0)
    own = pl.pallas_call(
        right_own,
        out_shape=jax.ShapeDtypeStruct((H, M, M), BF16),
        in_specs=[SMEM] + [VMEM] * 3,
        out_specs=VMEM,
        compiler_params=PARAMS,
        cost_estimate=cost,
    )(allowed, right, partial_same, partial_next)
    results = pl.pallas_call(
        right_other,
        out_shape=jax.ShapeDtypeStruct((2 * G, M, M), BF16),
        in_specs=[SMEM] + [VMEM] * 4,
        out_specs=VMEM,
        compiler_params=PARAMS,
        cost_estimate=cost,
    )(allowed, others, partial_same, partial_next, own)

    received = lax.all_to_all(results, BOTH, 0, 0, axis_index_groups=exchange, tiled=True)
    A = s // G
    first = jnp.where(A < t, G, jnp.where(A > t, 0, lax.rem(A, 2) * G))
    return lax.dynamic_slice_in_dim(received, first, G, 0)[:, None]


def solution(mesh):
    in_specs = (
        P("sec", None, None, None),
        P("term", None, "sec", None, None),
        P("term", "sec", None, None),
        P("term", None, None, None),
        P("term", None),
        P(),
    )
    body = functools.partial(on_device, n_sec=mesh.shape["sec"], n_term=mesh.shape["term"])
    return jax.shard_map(
        body, mesh=mesh, in_specs=in_specs, out_specs=P("term", "sec", None, None), check_vma=False
    )
```

time: 107 us -> 111 us (1.037)
  the two profiles are of different devices: /device:TPU:4 before, /device:TPU:256 now
where the time goes in v11:
time: 111 us; the launch traced here: 110 us
  waiting for transfers between devices  45.5 us (41%)
  starting transfers between devices  34 us (31%)
  blocking collectives  17.1 us (15%)
  Pallas kernels  12.6 us (11%)
    all_to_all x1, waiting for transfers between devices, on_device(): lax.all_to_all(results, BOTH, 0, 0, axis_index_groups=exchange, tiled=True)  26.1 us
    all_gather x1, blocking collectives, on_device(): lax.all_gather(payload, 'term', axis_index_groups=[list(range(parity, n_t...  17.1 us
    ppermute x1, waiting for transfers between devices, on_device(): following = lax.ppermute(same, 'term', [(i, i ^ 1) for i in range(n_term)])  14.8 us
    all_to_all x1, starting transfers between devices, on_device(): lax.all_to_all(sent, 'sec', 0, 0, axis_index_groups=by_core, tiled=True)  14.1 us
    all_to_all x1, starting transfers between devices, on_device(): lax.all_to_all(results, BOTH, 0, 0, axis_index_groups=exchange, tiled=True)  9.56 us
    ppermute x1, waiting for transfers between devices, on_device(): right = lax.ppermute(right_env[0], BOTH, spread)  4.54 us
    pallas_call x2, Pallas kernels, left_call(): pl.pallas_call(left_products, out_shape=jax.ShapeDtypeStruct((G, H * M, M...  3.94 us
    ppermute x1, starting transfers between devices, on_device(): below = lax.ppermute(turned, 'sec', [(i, i + 1) for i in range(n_sec - 1)])  3.05 us
  transfers between devices with their start and end apart: 7, of which 3 were waited for; matrix products, arithmetic and copies ran while one was open for 0% of the time, Pallas kernels for 8%

profile of v11, /device:TPU:256, one launch (start us, length us, event | category | flops | bytes accessed | tf_op | source)
XLA Modules:
  0.0 110.0 jit_solution(7294540805811013520)
XLA Ops:
  0.0 0.0 copy-start.3
  0.0 1.8 %shard_map.65.turned_ref = bf16[1024,128]{1,0:T(8,128)(2,1)} custom-call(bf16[1,64,128,128]{3,2,1,0:T(8,128)(2,1)} %psi_ref.1), custom_call_target="tpu_custom_call" | custom-call | tf_op jit(solution)/shard_map/pallas_call | solution.py:161
  1.8 1.3 %collective-permute-start.2 = (bf16[1024,128]{1,0:T(8,128)(2,1)}, bf16[1024,128]{1,0:T(8,128)(2,1)S(1)}, u32[]{:S(2)}, u32[]{:S(2)}) collective-permute-start(bf16[1024,128]{1,0:T(8,128)(2,1)} %shard_map.65.turned_ref), channel_id=1, source_target_pairs={{8,0},{16,8},{24,16},{32,24},{40,32},{48,40},{56,48},{64,56},{72,6... | collective-permute-start | bytes 786440 | tf_op jit(solution)/shard_map/ppermute | solution.py:171
  3.1 3.0 %collective-permute-start.1 = (bf16[1024,128]{1,0:T(8,128)(2,1)}, bf16[1024,128]{1,0:T(8,128)(2,1)S(1)}, u32[]{:S(2)}, u32[]{:S(2)}) collective-permute-start(bf16[1024,128]{1,0:T(8,128)(2,1)} %shard_map.65.turned_ref), channel_id=1, source_target_pairs={{0,8},{8,16},{16,24},{24,32},{32,40},{40,48},{48,56},{56,64},{64,7... | collective-permute-start | bytes 786440 | tf_op jit(solution)/shard_map/ppermute | solution.py:170
  6.2 0.0 copy-done.3
  6.2 2.0 %collective-permute-start = (bf16[1,128,128]{2,1,0:T(8,128)(2,1)S(1)}, bf16[1,128,128]{2,1,0:T(8,128)(2,1)S(1)}, u32[]{:S(2)}, u32[]{:S(2)}) collective-permute-start(bf16[1,128,128]{2,1,0:T(8,128)(2,1)S(1)} %bitcast.10), channel_id=1, source_target_pairs={{0,352},{1,480},{2,224},{3,96},{4,112},{5,240},{6,496},{7,368},{8,... | collective-permute-start | bytes 98312 | tf_op jit(solution)/shard_map/ppermute | solution.py:152
  8.2 1.8 %shard_map.66 = bf16[656,128]{1,0:T(8,128)(2,1)} custom-call(s32[1,5]{1,0:T(1,128)} %shift_ref.1, bf16[640,128]{1,0:T(8,128)(2,1)} %bitcast.8, f32[5,64,64]{2,1,0:T(8,128)} %bitcast.9, s32[64,64]{1,0:T(8,128)} %allowed_ref.5), custom_call_target="tpu_custom_call" | custom-call | tf_op jit(solution)/shard_map/pallas_call | solution.py:153
  10.0 0.0 copy-start.2
  10.0 0.0 copy-start
  10.0 4.5 %collective-permute-done.block_ref = bf16[1,128,128]{2,1,0:T(8,128)(2,1)S(1)} collective-permute-done((bf16[1,128,128]{2,1,0:T(8,128)(2,1)S(1)}, bf16[1,128,128]{2,1,0:T(8,128)(2,1)S(1)}, u32[]{:S(2)}, u32[]{:S(2)}) %collective-permute-start) | collective-permute-done | bytes 32800 | tf_op jit(solution)/shard_map/ppermute | solution.py:152
  14.5 1.1 %shard_map.64 = bf16[32,128,128]{2,1,0:T(8,128)(2,1)} custom-call(bf16[1,128,128]{2,1,0:T(8,128)(2,1)S(1)} %collective-permute-done.block_ref), custom_call_target="tpu_custom_call" | custom-call | flops 209715200 | bytes 1048576 | tf_op jit(solution)/shard_map/pallas_call | solution.py:172
  15.6 0.0 collective-permute-done.2.above_ref
  15.6 0.0 collective-permute-done.1.below_ref
  15.6 14.1 %all-to-all-start = ((bf16[32,128,128]{2,1,0:T(8,128)(2,1)}), bf16[32,128,128]{2,1,0:T(8,128)(2,1)S(1)}, u32[]{:S(2)}, u32[]{:S(2)}) async-start(bf16[32,128,128]{2,1,0:T(8,128)(2,1)} %shard_map.64), calls=%async_computation | async-start | bytes 2097152 | tf_op jit(solution)/shard_map/all_to_all | solution.py:181
  29.7 0.0 copy-done.2
  29.7 17.1 %all-gather = bf16[2624,128]{1,0:T(8,128)(2,1)S(1)} all-gather(bf16[656,128]{1,0:T(8,128)(2,1)S(1)} %copy-done.2), channel_id=2, replica_groups={{0,2,4,6},{1,3,5,7},{8,10,12,14},{9,11,13,15},{16,18,20,22},{17,19,21,2..., dimensions={0}, use_global_device_ids=true | all-gather | bytes 839680 | tf_op jit(solution)/shard_map/all_gather | solution.py:182
  46.8 1.9 %collective-permute-start.3 = (bf16[4,656,128]{2,1,0:T(8,128)(2,1)S(1)}, bf16[4,656,128]{2,1,0:T(8,128)(2,1)S(1)}, u32[]{:S(2)}, u32[]{:S(2)}) collective-permute-start(bf16[4,656,128]{2,1,0:T(8,128)(2,1)S(1)} %bitcast.6), channel_id=1, source_target_pairs={{0,1},{1,0},{2,3},{3,2},{4,5},{5,4},{6,7},{7,6},{8,9},{9,8},{10,11... | collective-permute-start | bytes 2015240 | tf_op jit(solution)/shard_map/ppermute | solution.py:185
  48.8 0.0 copy-done
  48.8 2.0 %shard_map.67.same_ref = bf16[8,512,128]{2,1,0:T(8,128)(2,1)S(1)} custom-call(bf16[4,656,128]{2,1,0:T(8,128)(2,1)S(1)} %bitcast.7, bf16[1024,128]{1,0:T(8,128)(2,1)S(1)} %collective-permute-done.1.below_ref, bf16[1024,128]{1,0:T(8,128)(2,1)S(1)} %copy-done, bf16[1024,128]{1,0:T(8,128)(2,1)S(1)} %collective-permute-done.2.above_ref), custom_call_target="tpu_custom_call" | custom-call | flops 671088640 | bytes 3145728 | tf_op jit(solution)/shard_map/pallas_call | solution.py:188
  50.7 14.8 %collective-permute-done.3.slots = bf16[4,656,128]{2,1,0:T(8,128)(2,1)S(1)} collective-permute-done((bf16[4,656,128]{2,1,0:T(8,128)(2,1)S(1)}, bf16[4,656,128]{2,1,0:T(8,128)(2,1)S(1)}, u32[]{:S(2)}, u32[]{:S(2)}) %collective-permute-start.3) | collective-permute-done | bytes 671776 | tf_op jit(solution)/shard_map/ppermute | solution.py:185
  65.5 0.0 all-to-all-done.right_ref
  65.5 0.0 copy-start.1
  65.5 2.0 %collective-permute-start.4 = (bf16[32,128,128]{2,1,0:T(8,128)(2,1)S(1)}, bf16[32,128,128]{2,1,0:T(8,128)(2,1)S(1)}, u32[]{:S(2)}, u32[]{:S(2)}) collective-permute-start(bf16[32,128,128]{2,1,0:T(8,128)(2,1)S(1)} %all-to-all-done.right_ref), channel_id=1, source_target_pairs={{0,8},{8,0},{16,24},{24,16},{32,40},{40,32},{48,56},{56,48},{64,72... | collective-permute-start | bytes 3145736 | tf_op jit(solution)/shard_map/ppermute | solution.py:201
  67.6 2.0 %shard_map.68.next_ref = bf16[8,512,128]{2,1,0:T(8,128)(2,1)S(1)} custom-call(bf16[4,656,128]{2,1,0:T(8,128)(2,1)S(1)} %collective-permute-done.3.slots, bf16[1024,128]{1,0:T(8,128)(2,1)S(1)} %collective-permute-done.1.below_ref, bf16[1024,128]{1,0:T(8,128)(2,1)S(1)} %copy-done, bf16[1024,128]{1,0:T(8,128)(2,1)S(1)} %collective-permute-done.2.above_ref), custom_call_target="tpu_custom_call" | custom-call | flops 671088640 | bytes 3145728 | tf_op jit(solution)/shard_map/pallas_call | solution.py:188
  69.5 0.0 copy-done.1
  69.6 1.6 %shard_map.69.own_ref = bf16[4,128,128]{2,1,0:T(8,128)(2,1)S(1)} custom-call(s32[64,64]{1,0:T(8,128)S(1)} %copy-done.1, bf16[32,128,128]{2,1,0:T(8,128)(2,1)S(1)} %all-to-all-done.right_ref, bf16[8,512,128]{2,1,0:T(8,128)(2,1)S(1)} %shard_map.67.same_ref, bf16[8,512,128]{2,1,0:T(8,128)(2,1)S(1)} %shard_map.68.next_ref), custom_call_target="tpu_custom_call" | custom-call | flops 134217728 | bytes 2097152 | tf_op jit(solution)/shard_map/pallas_call | solution.py:203
  71.1 0.0 collective-permute-done.4.right_ref
  71.2 2.4 %shard_map.70 = bf16[16,128,128]{2,1,0:T(8,128)(2,1)} custom-call(s32[64,64]{1,0:T(8,128)S(1)} %copy-done.1, bf16[32,128,128]{2,1,0:T(8,128)(2,1)S(1)} %collective-permute-done.4.right_ref, bf16[8,512,128]{2,1,0:T(8,128)(2,1)S(1)} %shard_map.67.same_ref, bf16[8,512,128]{2,1,0:T(8,128)(2,1)S(1)} %shard_map.68.next_ref, bf16[4,128,128]{2,1,0:T(8,128)(2,1)S(1)} %shard_map.69.own_ref), custom_call_target="tpu_custom_call" | custom-call | flops 134217728 | bytes 2097152 | tf_op jit(solution)/shard_map/pallas_call | solution.py:211
  73.6 9.6 %all-to-all-start.1 = ((bf16[16,128,128]{2,1,0:T(8,128)(2,1)}), bf16[16,128,128]{2,1,0:T(8,128)(2,1)S(1)}, u32[]{:S(2)}, u32[]{:S(2)}) async-start(bf16[16,128,128]{2,1,0:T(8,128)(2,1)} %shard_map.70), calls=%async_computation.1 | async-start | bytes 1048576 | tf_op jit(solution)/shard_map/all_to_all | solution.py:220
  83.2 26.1 %all-to-all-done.1 = bf16[16,128,128]{2,1,0:T(8,128)(2,1)S(1)} async-done(((bf16[16,128,128]{2,1,0:T(8,128)(2,1)}), bf16[16,128,128]{2,1,0:T(8,128)(2,1)S(1)}, u32[]{:S(2)}, u32[]{:S(2)}) %all-to-all-start.1) | async-done | bytes 524320 | tf_op jit(solution)/shard_map/all_to_all | solution.py:220
  109.3 0.7 dynamic-slice_bitcast_fusion
Async XLA Ops:
  0.0 6.2 %copy-start.3 = (bf16[1,1,128,128]{3,2,1,0:T(8,128)(2,1)S(1)}, bf16[1,1,128,128]{3,2,1,0:T(8,128)(2,1)}, u32[]{:S(2)}) copy-start(bf16[1,1,128,128]{3,2,1,0:T(8,128)(2,1)} %param.8) | copy-start | bytes 98308
  1.8 13.8 %collective-permute-start.2 = (bf16[1024,128]{1,0:T(8,128)(2,1)}, bf16[1024,128]{1,0:T(8,128)(2,1)S(1)}, u32[]{:S(2)}, u32[]{:S(2)}) collective-permute-start(bf16[1024,128]{1,0:T(8,128)(2,1)} %shard_map.65.turned_ref), channel_id=1, source_target_pairs={{8,0},{16,8},{24,16},{32,24},{40,32},{48,40},{56,48},{64,56},{72,6... | collective-permute-start | bytes 786440 | tf_op jit(solution)/shard_map/ppermute | solution.py:171
  3.1 12.5 %collective-permute-start.1 = (bf16[1024,128]{1,0:T(8,128)(2,1)}, bf16[1024,128]{1,0:T(8,128)(2,1)S(1)}, u32[]{:S(2)}, u32[]{:S(2)}) collective-permute-start(bf16[1024,128]{1,0:T(8,128)(2,1)} %shard_map.65.turned_ref), channel_id=1, source_target_pairs={{0,8},{8,16},{16,24},{24,32},{32,40},{40,48},{48,56},{56,64},{64,7... | collective-permute-start | bytes 786440 | tf_op jit(solution)/shard_map/ppermute | solution.py:170
  6.2 8.3 %collective-permute-start = (bf16[1,128,128]{2,1,0:T(8,128)(2,1)S(1)}, bf16[1,128,128]{2,1,0:T(8,128)(2,1)S(1)}, u32[]{:S(2)}, u32[]{:S(2)}) collective-permute-start(bf16[1,128,128]{2,1,0:T(8,128)(2,1)S(1)} %bitcast.10), channel_id=1, source_target_pairs={{0,352},{1,480},{2,224},{3,96},{4,112},{5,240},{6,496},{7,368},{8,... | collective-permute-start | bytes 98312 | tf_op jit(solution)/shard_map/ppermute | solution.py:152
  10.0 19.8 %copy-start.2 = (bf16[656,128]{1,0:T(8,128)(2,1)S(1)}, bf16[656,128]{1,0:T(8,128)(2,1)}, u32[]{:S(2)}) copy-start(bf16[656,128]{1,0:T(8,128)(2,1)} %shard_map.66) | copy-start | bytes 503812
  10.0 38.8 %copy-start = (bf16[1024,128]{1,0:T(8,128)(2,1)S(1)}, bf16[1024,128]{1,0:T(8,128)(2,1)}, u32[]{:S(2)}) copy-start(bf16[1024,128]{1,0:T(8,128)(2,1)} %shard_map.65.turned_ref) | copy-start | bytes 786436
  15.6 49.9 %all-to-all-start = ((bf16[32,128,128]{2,1,0:T(8,128)(2,1)}), bf16[32,128,128]{2,1,0:T(8,128)(2,1)S(1)}, u32[]{:S(2)}, u32[]{:S(2)}) async-start(bf16[32,128,128]{2,1,0:T(8,128)(2,1)} %shard_map.64), calls=%async_computation | async-start | bytes 2097152 | tf_op jit(solution)/shard_map/all_to_all | solution.py:181
  46.8 18.7 %collective-permute-start.3 = (bf16[4,656,128]{2,1,0:T(8,128)(2,1)S(1)}, bf16[4,656,128]{2,1,0:T(8,128)(2,1)S(1)}, u32[]{:S(2)}, u32[]{:S(2)}) collective-permute-start(bf16[4,656,128]{2,1,0:T(8,128)(2,1)S(1)} %bitcast.6), channel_id=1, source_target_pairs={{0,1},{1,0},{2,3},{3,2},{4,5},{5,4},{6,7},{7,6},{8,9},{9,8},{10,11... | collective-permute-start | bytes 2015240 | tf_op jit(solution)/shard_map/ppermute | solution.py:185
  65.5 4.0 %copy-start.1 = (s32[64,64]{1,0:T(8,128)S(1)}, s32[64,64]{1,0:T(8,128)}, u32[]{:S(2)}) copy-start(s32[64,64]{1,0:T(8,128)} %allowed_ref.5) | copy-start | bytes 49156
  65.5 5.6 %collective-permute-start.4 = (bf16[32,128,128]{2,1,0:T(8,128)(2,1)S(1)}, bf16[32,128,128]{2,1,0:T(8,128)(2,1)S(1)}, u32[]{:S(2)}, u32[]{:S(2)}) collective-permute-start(bf16[32,128,128]{2,1,0:T(8,128)(2,1)S(1)} %all-to-all-done.right_ref), channel_id=1, source_target_pairs={{0,8},{8,0},{16,24},{24,16},{32,40},{40,32},{48,56},{56,48},{64,72... | collective-permute-start | bytes 3145736 | tf_op jit(solution)/shard_map/ppermute | solution.py:201
  73.6 35.8 %all-to-all-start.1 = ((bf16[16,128,128]{2,1,0:T(8,128)(2,1)}), bf16[16,128,128]{2,1,0:T(8,128)(2,1)S(1)}, u32[]{:S(2)}, u32[]{:S(2)}) async-start(bf16[16,128,128]{2,1,0:T(8,128)(2,1)} %shard_map.70), calls=%async_computation.1 | async-start | bytes 1048576 | tf_op jit(solution)/shard_map/all_to_all | solution.py:220

commit v12 on v11

--- a/solution.py
+++ b/solution.py
@@ -72,15 +72,17 @@
         out_ref[n] = block_ref[0]
 
 
-def left_products(slots, below_ref, turned_ref, above_ref, out_ref, psi_ref):
+def left_products(count, *refs):
+    below_ref, turned_ref, above_ref, out_ref, psi_ref = refs[count:]
     for row, ref in enumerate((below_ref, turned_ref, above_ref)):
         psi_ref[row] = ref[...]
+    slots = [ref.at[w] for ref in refs[:count] for w in range(ref.shape[0])]
     t = lax.axis_index("term")
     sector = lax.broadcasted_iota(jnp.int32, (M, G * M), 0)
     wanted = lax.broadcasted_iota(jnp.int32, (M, G * M), 1) // M + t * G
     pick = jnp.where((sector == wanted) | (sector == wanted + M // 2), 1.0, 0.0).astype(BF16)
-    for w in range(H):
-        table = slots[w, ROWS : ROWS + 16, :]
+    for w, slot in enumerate(slots):
+        table = slot[ROWS : ROWS + 16, :]
         spread = jnp.dot(table, pick, preferred_element_type=F32)
         factors = spread[:8] + spread[8:]
         shifts = table.astype(F32)[15:16, :]
@@ -90,7 +92,7 @@
             for c in range(LB):
                 product = lax.dot_general(
                     psi_ref[rows[c], start : start + 2 * M, :],
-                    slots[w, c * M : (c + 1) * M, :],
+                    slot[c * M : (c + 1) * M, :],
                     (((1,), (1,)), ((), ())),
                     preferred_element_type=F32,
                 )
@@ -182,22 +184,23 @@
     same = lax.all_gather(
         payload, "term", axis_index_groups=[list(range(parity, n_term, 2)) for parity in range(2)]
     )
-    following = lax.ppermute(same, "term", [(i, i ^ 1) for i in range(n_term)])
-
-    def left_call(slots):
+    from_below = lax.ppermute(same[: H // 2], "term", [(i, (i + 1) % n_term) for i in range(n_term)])
+    from_above = lax.ppermute(same[H // 2 :], "term", [(i, (i - 1) % n_term) for i in range(n_term)])
+
+    def left_call(*slots):
         return pl.pallas_call(
-            left_products,
+            functools.partial(left_products, len(slots)),
             out_shape=jax.ShapeDtypeStruct((G, H * M, M), BF16),
-            in_specs=[VMEM] * 4,
+            in_specs=[VMEM] * (len(slots) + 3),
             out_specs=VMEM,
             scratch_shapes=[pltpu.VMEM((3, G * M, M), BF16)],
             compiler_params=PARAMS,
             cost_estimate=pl.CostEstimate(flops=2 * 160 * M**3, bytes_accessed=3 << 20, transcendentals=0),
-        )(slots, below, turned, above)
+        )(*slots, below, turned, above)
 
     partial_same = left_call(same)
-    following, partial_same, right = together(following, partial_same, right)
-    partial_next = left_call(following)
+    from_below, from_above, partial_same, right = together(from_below, from_above, partial_same, right)
+    partial_next = left_call(from_below, from_above)
     others = lax.ppermute(right, "sec", [(i, i ^ 1) for i in range(n_sec)])
     cost = pl.CostEstimate(flops=2 * 32 * M**3, bytes_accessed=2 << 20, transcendentals=0)
     own = pl.pallas_call(

time: 111 us -> 106 us (0.955)
  the two profiles are of different devices: /device:TPU:256 before, /device:TPU:4 now
where the time goes in v12:
time: 106 us; the launch traced here: 105 us
  starting transfers between devices  47.8 us (45%)
  blocking collectives  22.2 us (21%)
  waiting for transfers between devices  21.9 us (21%)
  Pallas kernels  12.6 us (12%)
    all_gather x1, blocking collectives, on_device(): lax.all_gather(payload, 'term', axis_index_groups=[list(range(parity, n_t...  22.2 us
    all_to_all x1, waiting for transfers between devices, on_device(): lax.all_to_all(results, BOTH, 0, 0, axis_index_groups=exchange, tiled=True)  17.3 us
    all_to_all x1, starting transfers between devices, on_device(): lax.all_to_all(results, BOTH, 0, 0, axis_index_groups=exchange, tiled=True)  12.3 us
    ppermute x1, starting transfers between devices, on_device(): right = lax.ppermute(right_env[0], BOTH, spread)  11.7 us
    all_to_all x1, starting transfers between devices, on_device(): lax.all_to_all(sent, 'sec', 0, 0, axis_index_groups=by_core, tiled=True)  7.96 us
    ppermute x1, starting transfers between devices, on_device(): lax.ppermute(same[H // 2:], 'term', [(i, (i - 1) % n_term) for i in range...  5.13 us
    ppermute x1, starting transfers between devices, on_device(): above = lax.ppermute(turned, 'sec', [(i + 1, i) for i in range(n_sec - 1)])  4.79 us
    pallas_call x2, Pallas kernels, left_call(): pl.pallas_call(functools.partial(left_products, len(slots)), out_shape=ja...  3.95 us
  transfers between devices with their start and end apart: 8, of which 3 were waited for; matrix products, arithmetic and copies ran while one was open for 0% of the time, Pallas kernels for 8%

profile of v12, /device:TPU:4, one launch (start us, length us, event | category | flops | bytes accessed | tf_op | source)
XLA Modules:
  0.0 105.5 jit_solution(18034586289027549991)
XLA Ops:
  0.0 0.0 copy-start.3
  0.0 1.8 %shard_map.65.refs_2_.refs_3_ = bf16[1024,128]{1,0:T(8,128)(2,1)} custom-call(bf16[1,64,128,128]{3,2,1,0:T(8,128)(2,1)} %psi_ref.1), custom_call_target="tpu_custom_call" | custom-call | tf_op jit(solution)/shard_map/pallas_call | solution.py:163
  1.8 4.8 %collective-permute-start.2 = (bf16[1024,128]{1,0:T(8,128)(2,1)}, bf16[1024,128]{1,0:T(8,128)(2,1)S(1)}, u32[]{:S(2)}, u32[]{:S(2)}) collective-permute-start(bf16[1024,128]{1,0:T(8,128)(2,1)} %shard_map.65.refs_2_.refs_3_), channel_id=1, source_target_pairs={{8,0},{16,8},{24,16},{32,24},{40,32},{48,40},{56,48},{64,56},{72,6... | collective-permute-start | bytes 786440 | tf_op jit(solution)/shard_map/ppermute | solution.py:173
  6.6 1.9 %collective-permute-start.1 = (bf16[1024,128]{1,0:T(8,128)(2,1)}, bf16[1024,128]{1,0:T(8,128)(2,1)S(1)}, u32[]{:S(2)}, u32[]{:S(2)}) collective-permute-start(bf16[1024,128]{1,0:T(8,128)(2,1)} %shard_map.65.refs_2_.refs_3_), channel_id=1, source_target_pairs={{0,8},{8,16},{16,24},{24,32},{32,40},{40,48},{48,56},{56,64},{64,7... | collective-permute-start | bytes 786440 | tf_op jit(solution)/shard_map/ppermute | solution.py:172
  8.5 0.0 copy-done.3
  8.5 11.7 %collective-permute-start = (bf16[1,128,128]{2,1,0:T(8,128)(2,1)S(1)}, bf16[1,128,128]{2,1,0:T(8,128)(2,1)S(1)}, u32[]{:S(2)}, u32[]{:S(2)}) collective-permute-start(bf16[1,128,128]{2,1,0:T(8,128)(2,1)S(1)} %bitcast.13), channel_id=1, source_target_pairs={{0,352},{1,480},{2,224},{3,96},{4,112},{5,240},{6,496},{7,368},{8,... | collective-permute-start | bytes 98312 | tf_op jit(solution)/shard_map/ppermute | solution.py:154
  20.3 1.8 %shard_map.66 = bf16[656,128]{1,0:T(8,128)(2,1)} custom-call(s32[1,5]{1,0:T(1,128)} %shift_ref.1, bf16[640,128]{1,0:T(8,128)(2,1)} %bitcast.11, f32[5,64,64]{2,1,0:T(8,128)} %bitcast.12, s32[64,64]{1,0:T(8,128)} %allowed_ref.5), custom_call_target="tpu_custom_call" | custom-call | tf_op jit(solution)/shard_map/pallas_call | solution.py:155
  22.1 0.0 copy-start.2
  22.1 0.0 collective-permute-done.block_ref
  22.1 1.1 %shard_map.64 = bf16[32,128,128]{2,1,0:T(8,128)(2,1)} custom-call(bf16[1,128,128]{2,1,0:T(8,128)(2,1)S(1)} %collective-permute-done.block_ref), custom_call_target="tpu_custom_call" | custom-call | flops 209715200 | bytes 1048576 | tf_op jit(solution)/shard_map/pallas_call | solution.py:174
  23.2 0.0 copy-start
  23.2 0.0 collective-permute-done.2.refs_3_.refs_4_
  23.2 0.0 collective-permute-done.1.refs_1_.refs_2_
  23.2 8.0 %all-to-all-start = ((bf16[32,128,128]{2,1,0:T(8,128)(2,1)}), bf16[32,128,128]{2,1,0:T(8,128)(2,1)S(1)}, u32[]{:S(2)}, u32[]{:S(2)}) async-start(bf16[32,128,128]{2,1,0:T(8,128)(2,1)} %shard_map.64), calls=%async_computation | async-start | bytes 2097152 | tf_op jit(solution)/shard_map/all_to_all | solution.py:183
  31.2 0.0 copy-done.2
  31.2 22.2 %all-gather = bf16[2624,128]{1,0:T(8,128)(2,1)S(1)} all-gather(bf16[656,128]{1,0:T(8,128)(2,1)S(1)} %copy-done.2), channel_id=2, replica_groups={{0,2,4,6},{1,3,5,7},{8,10,12,14},{9,11,13,15},{16,18,20,22},{17,19,21,2..., dimensions={0}, use_global_device_ids=true | all-gather | bytes 839680 | tf_op jit(solution)/shard_map/all_gather | solution.py:184
  53.4 1.9 %collective-permute-start.3 = (bf16[2,656,128]{2,1,0:T(8,128)(2,1)S(1)}, bf16[2,656,128]{2,1,0:T(8,128)(2,1)S(1)}, u32[]{:S(2)}, u32[]{:S(2)}) collective-permute-start(bf16[2,656,128]{2,1,0:T(8,128)(2,1)S(1)} %bitcast.10), channel_id=1, source_target_pairs={{0,1},{1,2},{2,3},{3,4},{4,5},{5,6},{6,7},{7,0},{8,9},{9,10},{10,1... | collective-permute-start | bytes 1007624 | tf_op jit(solution)/shard_map/ppermute | solution.py:187
  55.3 5.1 %collective-permute-start.4 = (bf16[2,656,128]{2,1,0:T(8,128)(2,1)S(1)}, bf16[2,656,128]{2,1,0:T(8,128)(2,1)S(1)}, u32[]{:S(2)}, u32[]{:S(2)}) collective-permute-start(bf16[2,656,128]{2,1,0:T(8,128)(2,1)S(1)} %bitcast.9), channel_id=1, source_target_pairs={{0,7},{1,0},{2,1},{3,2},{4,3},{5,4},{6,5},{7,6},{8,15},{9,8},{10,9... | collective-permute-start | bytes 1007624 | tf_op jit(solution)/shard_map/ppermute | solution.py:188
  60.5 0.0 copy-done
  60.5 2.0 %shard_map.67.same_ref = bf16[8,512,128]{2,1,0:T(8,128)(2,1)S(1)} custom-call(bf16[4,656,128]{2,1,0:T(8,128)(2,1)S(1)} %bitcast.8, bf16[1024,128]{1,0:T(8,128)(2,1)S(1)} %collective-permute-done.1.refs_1_.refs_2_, bf16[1024,128]{1,0:T(8,128)(2,1)S(1)} %copy-done, bf16[1024,128]{1,0:T(8,128)(2,1)S(1)} %collective-permute-done.2.refs_3_.refs_4_), custom_call_target="tpu_custom_call" | custom-call | flops 671088640 | bytes 3145728 | tf_op jit(solution)/shard_map/pallas_call | solution.py:191
  62.4 3.4 %collective-permute-done.3.refs_0_ = bf16[2,656,128]{2,1,0:T(8,128)(2,1)S(1)} collective-permute-done((bf16[2,656,128]{2,1,0:T(8,128)(2,1)S(1)}, bf16[2,656,128]{2,1,0:T(8,128)(2,1)S(1)}, u32[]{:S(2)}, u32[]{:S(2)}) %collective-permute-start.3) | collective-permute-done | bytes 335904 | tf_op jit(solution)/shard_map/ppermute | solution.py:187
  65.8 1.2 %collective-permute-done.4.refs_1_ = bf16[2,656,128]{2,1,0:T(8,128)(2,1)S(1)} collective-permute-done((bf16[2,656,128]{2,1,0:T(8,128)(2,1)S(1)}, bf16[2,656,128]{2,1,0:T(8,128)(2,1)S(1)}, u32[]{:S(2)}, u32[]{:S(2)}) %collective-permute-start.4) | collective-permute-done | bytes 335904 | tf_op jit(solution)/shard_map/ppermute | solution.py:188
  67.0 0.0 all-to-all-done.right_ref
  67.0 0.0 copy-start.1
  67.0 2.0 %collective-permute-start.5 = (bf16[32,128,128]{2,1,0:T(8,128)(2,1)S(1)}, bf16[32,128,128]{2,1,0:T(8,128)(2,1)S(1)}, u32[]{:S(2)}, u32[]{:S(2)}) collective-permute-start(bf16[32,128,128]{2,1,0:T(8,128)(2,1)S(1)} %all-to-all-done.right_ref), channel_id=1, source_target_pairs={{0,8},{8,0},{16,24},{24,16},{32,40},{40,32},{48,56},{56,48},{64,72... | collective-permute-start | bytes 3145736 | tf_op jit(solution)/shard_map/ppermute | solution.py:204
  69.1 2.0 %shard_map.68.next_ref = bf16[8,512,128]{2,1,0:T(8,128)(2,1)S(1)} custom-call(bf16[2,656,128]{2,1,0:T(8,128)(2,1)S(1)} %collective-permute-done.3.refs_0_, bf16[2,656,128]{2,1,0:T(8,128)(2,1)S(1)} %collective-permute-done.4.refs_1_, bf16[1024,128]{1,0:T(8,128)(2,1)S(1)} %collective-permute-done.1.refs_1_.refs_2_, bf16[1024,128]{1,0:T(8,128)(2,1)S(1)} %copy-done, ...), custom_call_target="tpu_custom_call" | custom-call | flops 671088640 | bytes 3145728 | tf_op jit(solution)/shard_map/pallas_call | solution.py:191
  71.1 0.0 copy-done.1
  71.1 1.6 %shard_map.69.own_ref = bf16[4,128,128]{2,1,0:T(8,128)(2,1)S(1)} custom-call(s32[64,64]{1,0:T(8,128)S(1)} %copy-done.1, bf16[32,128,128]{2,1,0:T(8,128)(2,1)S(1)} %all-to-all-done.right_ref, bf16[8,512,128]{2,1,0:T(8,128)(2,1)S(1)} %shard_map.67.same_ref, bf16[8,512,128]{2,1,0:T(8,128)(2,1)S(1)} %shard_map.68.next_ref), custom_call_target="tpu_custom_call" | custom-call | flops 134217728 | bytes 2097152 | tf_op jit(solution)/shard_map/pallas_call | solution.py:206
  72.7 0.0 collective-permute-done.5.right_ref
  72.7 2.4 %shard_map.70 = bf16[16,128,128]{2,1,0:T(8,128)(2,1)} custom-call(s32[64,64]{1,0:T(8,128)S(1)} %copy-done.1, bf16[32,128,128]{2,1,0:T(8,128)(2,1)S(1)} %collective-permute-done.5.right_ref, bf16[8,512,128]{2,1,0:T(8,128)(2,1)S(1)} %shard_map.67.same_ref, bf16[8,512,128]{2,1,0:T(8,128)(2,1)S(1)} %shard_map.68.next_ref, bf16[4,128,128]{2,1,0:T(8,128)(2,1)S(1)} %shard_map.69.own_ref), custom_call_target="tpu_custom_call" | custom-call | flops 134217728 | bytes 2097152 | tf_op jit(solution)/shard_map/pallas_call | solution.py:214
  75.1 12.3 %all-to-all-start.1 = ((bf16[16,128,128]{2,1,0:T(8,128)(2,1)}), bf16[16,128,128]{2,1,0:T(8,128)(2,1)S(1)}, u32[]{:S(2)}, u32[]{:S(2)}) async-start(bf16[16,128,128]{2,1,0:T(8,128)(2,1)} %shard_map.70), calls=%async_computation.1 | async-start | bytes 1048576 | tf_op jit(solution)/shard_map/all_to_all | solution.py:223
  87.4 17.3 %all-to-all-done.1 = bf16[16,128,128]{2,1,0:T(8,128)(2,1)S(1)} async-done(((bf16[16,128,128]{2,1,0:T(8,128)(2,1)}), bf16[16,128,128]{2,1,0:T(8,128)(2,1)S(1)}, u32[]{:S(2)}, u32[]{:S(2)}) %all-to-all-start.1) | async-done | bytes 524320 | tf_op jit(solution)/shard_map/all_to_all | solution.py:223
  104.7 0.7 dynamic-slice_bitcast_fusion
  (1 shorter events, 0.0 us)
Async XLA Ops:
  0.0 8.5 %copy-start.3 = (bf16[1,1,128,128]{3,2,1,0:T(8,128)(2,1)S(1)}, bf16[1,1,128,128]{3,2,1,0:T(8,128)(2,1)}, u32[]{:S(2)}) copy-start(bf16[1,1,128,128]{3,2,1,0:T(8,128)(2,1)} %param.8) | copy-start | bytes 98308
  1.8 21.4 %collective-permute-start.2 = (bf16[1024,128]{1,0:T(8,128)(2,1)}, bf16[1024,128]{1,0:T(8,128)(2,1)S(1)}, u32[]{:S(2)}, u32[]{:S(2)}) collective-permute-start(bf16[1024,128]{1,0:T(8,128)(2,1)} %shard_map.65.refs_2_.refs_3_), channel_id=1, source_target_pairs={{8,0},{16,8},{24,16},{32,24},{40,32},{48,40},{56,48},{64,56},{72,6... | collective-permute-start | bytes 786440 | tf_op jit(solution)/shard_map/ppermute | solution.py:173
  6.6 16.6 %collective-permute-start.1 = (bf16[1024,128]{1,0:T(8,128)(2,1)}, bf16[1024,128]{1,0:T(8,128)(2,1)S(1)}, u32[]{:S(2)}, u32[]{:S(2)}) collective-permute-start(bf16[1024,128]{1,0:T(8,128)(2,1)} %shard_map.65.refs_2_.refs_3_), channel_id=1, source_target_pairs={{0,8},{8,16},{16,24},{24,32},{32,40},{40,48},{48,56},{56,64},{64,7... | collective-permute-start | bytes 786440 | tf_op jit(solution)/shard_map/ppermute | solution.py:172
  8.5 13.5 %collective-permute-start = (bf16[1,128,128]{2,1,0:T(8,128)(2,1)S(1)}, bf16[1,128,128]{2,1,0:T(8,128)(2,1)S(1)}, u32[]{:S(2)}, u32[]{:S(2)}) collective-permute-start(bf16[1,128,128]{2,1,0:T(8,128)(2,1)S(1)} %bitcast.13), channel_id=1, source_target_pairs={{0,352},{1,480},{2,224},{3,96},{4,112},{5,240},{6,496},{7,368},{8,... | collective-permute-start | bytes 98312 | tf_op jit(solution)/shard_map/ppermute | solution.py:154
  22.1 9.1 %copy-start.2 = (bf16[656,128]{1,0:T(8,128)(2,1)S(1)}, bf16[656,128]{1,0:T(8,128)(2,1)}, u32[]{:S(2)}) copy-start(bf16[656,128]{1,0:T(8,128)(2,1)} %shard_map.66) | copy-start | bytes 503812
  23.2 37.3 %copy-start = (bf16[1024,128]{1,0:T(8,128)(2,1)S(1)}, bf16[1024,128]{1,0:T(8,128)(2,1)}, u32[]{:S(2)}) copy-start(bf16[1024,128]{1,0:T(8,128)(2,1)} %shard_map.65.refs_2_.refs_3_) | copy-start | bytes 786436
  23.2 43.8 %all-to-all-start = ((bf16[32,128,128]{2,1,0:T(8,128)(2,1)}), bf16[32,128,128]{2,1,0:T(8,128)(2,1)S(1)}, u32[]{:S(2)}, u32[]{:S(2)}) async-start(bf16[32,128,128]{2,1,0:T(8,128)(2,1)} %shard_map.64), calls=%async_computation | async-start | bytes 2097152 | tf_op jit(solution)/shard_map/all_to_all | solution.py:183
  53.4 12.4 %collective-permute-start.3 = (bf16[2,656,128]{2,1,0:T(8,128)(2,1)S(1)}, bf16[2,656,128]{2,1,0:T(8,128)(2,1)S(1)}, u32[]{:S(2)}, u32[]{:S(2)}) collective-permute-start(bf16[2,656,128]{2,1,0:T(8,128)(2,1)S(1)} %bitcast.10), channel_id=1, source_target_pairs={{0,1},{1,2},{2,3},{3,4},{4,5},{5,6},{6,7},{7,0},{8,9},{9,10},{10,1... | collective-permute-start | bytes 1007624 | tf_op jit(solution)/shard_map/ppermute | solution.py:187
  55.3 11.7 %collective-permute-start.4 = (bf16[2,656,128]{2,1,0:T(8,128)(2,1)S(1)}, bf16[2,656,128]{2,1,0:T(8,128)(2,1)S(1)}, u32[]{:S(2)}, u32[]{:S(2)}) collective-permute-start(bf16[2,656,128]{2,1,0:T(8,128)(2,1)S(1)} %bitcast.9), channel_id=1, source_target_pairs={{0,7},{1,0},{2,1},{3,2},{4,3},{5,4},{6,5},{7,6},{8,15},{9,8},{10,9... | collective-permute-start | bytes 1007624 | tf_op jit(solution)/shard_map/ppermute | solution.py:188
  67.0 4.0 %copy-start.1 = (s32[64,64]{1,0:T(8,128)S(1)}, s32[64,64]{1,0:T(8,128)}, u32[]{:S(2)}) copy-start(s32[64,64]{1,0:T(8,128)} %allowed_ref.5) | copy-start | bytes 49156
  67.0 5.6 %collective-permute-start.5 = (bf16[32,128,128]{2,1,0:T(8,128)(2,1)S(1)}, bf16[32,128,128]{2,1,0:T(8,128)(2,1)S(1)}, u32[]{:S(2)}, u32[]{:S(2)}) collective-permute-start(bf16[32,128,128]{2,1,0:T(8,128)(2,1)S(1)} %all-to-all-done.right_ref), channel_id=1, source_target_pairs={{0,8},{8,0},{16,24},{24,16},{32,40},{40,32},{48,56},{56,48},{64,72... | collective-permute-start | bytes 3145736 | tf_op jit(solution)/shard_map/ppermute | solution.py:204
  75.1 29.7 %all-to-all-start.1 = ((bf16[16,128,128]{2,1,0:T(8,128)(2,1)}), bf16[16,128,128]{2,1,0:T(8,128)(2,1)S(1)}, u32[]{:S(2)}, u32[]{:S(2)}) async-start(bf16[16,128,128]{2,1,0:T(8,128)(2,1)} %shard_map.70), calls=%async_computation.1 | async-start | bytes 1048576 | tf_op jit(solution)/shard_map/all_to_all | solution.py:223

commit v13 on v12

--- a/solution.py
+++ b/solution.py
@@ -73,11 +73,12 @@
 
 
 def left_products(count, *refs):
-    below_ref, turned_ref, above_ref, out_ref, psi_ref = refs[count:]
-    for row, ref in enumerate((below_ref, turned_ref, above_ref)):
+    near_ref, turned_ref, inner_ref, out_ref, psi_ref = refs[count:]
+    for row, ref in enumerate((near_ref, turned_ref, inner_ref)):
         psi_ref[row] = ref[...]
     slots = [ref.at[w] for ref in refs[:count] for w in range(ref.shape[0])]
     t = lax.axis_index("term")
+    step = 1 - 2 * lax.rem(lax.axis_index("sec"), 2)
     sector = lax.broadcasted_iota(jnp.int32, (M, G * M), 0)
     wanted = lax.broadcasted_iota(jnp.int32, (M, G * M), 1) // M + t * G
     pick = jnp.where((sector == wanted) | (sector == wanted + M // 2), 1.0, 0.0).astype(BF16)
@@ -86,7 +87,7 @@
         spread = jnp.dot(table, pick, preferred_element_type=F32)
         factors = spread[:8] + spread[8:]
         shifts = table.astype(F32)[15:16, :]
-        rows = [shifts[0, c].astype(jnp.int32) + 1 for c in range(LB)]
+        rows = [shifts[0, c].astype(jnp.int32) * step + 1 for c in range(LB)]
         for start in range(0, G * M, 2 * M):
             totals = [None, None]
             for c in range(LB):
@@ -115,13 +116,15 @@
     return (total * allowed_ref[s, t * G + j].astype(F32)).T.astype(BF16)
 
 
-def right_own(allowed_ref, right_ref, same_ref, next_ref, out_ref):
+def next_products(allowed_ref, *refs):
+    left_refs, (right_ref, same_ref, next_ref, out_ref, psi_ref) = refs[:5], refs[5:]
+    left_products(2, *left_refs, next_ref, psi_ref)
     core = lax.rem(lax.axis_index("sec"), 2)
     for i in range(H):
         out_ref[i] = right_sum(i, core, right_ref, same_ref, next_ref, allowed_ref)
 
 
-def right_other(allowed_ref, right_ref, same_ref, next_ref, own_ref, out_ref):
+def other_products(allowed_ref, right_ref, same_ref, next_ref, own_ref, out_ref):
     core = lax.rem(lax.axis_index("sec"), 2)
     for i in range(H):
         value = right_sum(i, 1 - core, right_ref, same_ref, next_ref, allowed_ref)
@@ -169,8 +172,7 @@
         compiler_params=FIRST,
     )(wavefunction)
 
-    below = lax.ppermute(turned, "sec", [(i, i + 1) for i in range(n_sec - 1)])
-    above = lax.ppermute(turned, "sec", [(i + 1, i) for i in range(n_sec - 1)])
+    near = lax.ppermute(turned, "sec", [(i, i + 1) if i % 2 else (i, i - 1) for i in range(1, n_sec - 1)])
     sent = pl.pallas_call(
         copies,
         out_shape=jax.ShapeDtypeStruct((n_sec // 2, M, M), BF16),
@@ -179,40 +181,39 @@
         compiler_params=PARAMS,
         cost_estimate=pl.CostEstimate(flops=SPREAD_COST * M**3, bytes_accessed=1 << 20, transcendentals=0),
     )(right)
-    sent, below, above, payload = together(sent, below, above, payload)
+    sent, near, payload = together(sent, near, payload)
     right = lax.all_to_all(sent, "sec", 0, 0, axis_index_groups=by_core, tiled=True)
     same = lax.all_gather(
         payload, "term", axis_index_groups=[list(range(parity, n_term, 2)) for parity in range(2)]
     )
+    across = [(i, i ^ 1) for i in range(n_sec)]
+    inner = lax.ppermute(turned, "sec", across)
     from_below = lax.ppermute(same[: H // 2], "term", [(i, (i + 1) % n_term) for i in range(n_term)])
     from_above = lax.ppermute(same[H // 2 :], "term", [(i, (i - 1) % n_term) for i in range(n_term)])
 
-    def left_call(*slots):
-        return pl.pallas_call(
-            functools.partial(left_products, len(slots)),
-            out_shape=jax.ShapeDtypeStruct((G, H * M, M), BF16),
-            in_specs=[VMEM] * (len(slots) + 3),
-            out_specs=VMEM,
-            scratch_shapes=[pltpu.VMEM((3, G * M, M), BF16)],
-            compiler_params=PARAMS,
-            cost_estimate=pl.CostEstimate(flops=2 * 160 * M**3, bytes_accessed=3 << 20, transcendentals=0),
-        )(*slots, below, turned, above)
-
-    partial_same = left_call(same)
+    partial_same = pl.pallas_call(
+        functools.partial(left_products, 1),
+        out_shape=jax.ShapeDtypeStruct((G, H * M, M), BF16),
+        in_specs=[VMEM] * 4,
+        out_specs=VMEM,
+        scratch_shapes=[pltpu.VMEM((3, G * M, M), BF16)],
+        compiler_params=PARAMS,
+        cost_estimate=pl.CostEstimate(flops=2 * 160 * M**3, bytes_accessed=3 << 20, transcendentals=0),
+    )(same, near, turned, inner)
     from_below, from_above, partial_same, right = together(from_below, from_above, partial_same, right)
-    partial_next = left_call(from_below, from_above)
-    others = lax.ppermute(right, "sec", [(i, i ^ 1) for i in range(n_sec)])
-    cost = pl.CostEstimate(flops=2 * 32 * M**3, bytes_accessed=2 << 20, transcendentals=0)
-    own = pl.pallas_call(
-        right_own,
-        out_shape=jax.ShapeDtypeStruct((H, M, M), BF16),
-        in_specs=[SMEM] + [VMEM] * 3,
-        out_specs=VMEM,
+    others = lax.ppermute(right, "sec", across)
+    cost = pl.CostEstimate(flops=2 * 112 * M**3, bytes_accessed=3 << 20, transcendentals=0)
+    partial_next, own = pl.pallas_call(
+        next_products,
+        out_shape=[jax.ShapeDtypeStruct((G, H * M, M), BF16), jax.ShapeDtypeStruct((H, M, M), BF16)],
+        in_specs=[SMEM] + [VMEM] * 7,
+        out_specs=[VMEM] * 2,
+        scratch_shapes=[pltpu.VMEM((3, G * M, M), BF16)],
         compiler_params=PARAMS,
         cost_estimate=cost,
-    )(allowed, right, partial_same, partial_next)
+    )(allowed, from_below, from_above, near, turned, inner, right, partial_same)
     results = pl.pallas_call(
-        right_other,
+        other_products,
         out_shape=jax.ShapeDtypeStruct((2 * G, M, M), BF16),
         in_specs=[SMEM] + [VMEM] * 4,
         out_specs=VMEM,

time: 106 us -> 104 us (0.981)
  waiting for transfers between devices: 21.9 us -> 20.6 us
    ppermute x1, waiting for transfers between devices: 3.38 us -> 0.01 us  [on_device(): lax.ppermute(same[:H // 2], 'term', [(i, (i + 1) % n_term) for i in range...]
    ppermute x3, waiting for transfers between devices: 0.01 us -> 1.51 us  [the longest x1 1.5 us: on_device(): inner = lax.ppermute(turned, 'sec', across)]
    pallas_call x4 -> x3, Pallas kernels: 7.94 us -> 7.82 us  [the longest x1 3.44 us: on_device(): pl.pallas_call(next_products, out_shape=[jax.ShapeDtypeStruct((G, H * M,...]
where the time goes in v13:
time: 104 us; the launch traced here: 103 us
  starting transfers between devices  47.1 us (45%)
  blocking collectives  21.5 us (21%)
  waiting for transfers between devices  20.6 us (20%)
  Pallas kernels  12.5 us (12%)
  local copies, waits for them, and re-layouts  1.53 us (1%)
    all_gather x1, blocking collectives, on_device(): lax.all_gather(payload, 'term', axis_index_groups=[list(range(parity, n_t...  21.5 us
    all_to_all x1, waiting for transfers between devices, on_device(): lax.all_to_all(results, BOTH, 0, 0, axis_index_groups=exchange, tiled=True)  18 us
    all_to_all x1, starting transfers between devices, on_device(): lax.all_to_all(results, BOTH, 0, 0, axis_index_groups=exchange, tiled=True)  12.4 us
    ppermute x1, starting transfers between devices, on_device(): right = lax.ppermute(right_env[0], BOTH, spread)  11.7 us
    all_to_all x1, starting transfers between devices, on_device(): lax.all_to_all(sent, 'sec', 0, 0, axis_index_groups=by_core, tiled=True)  7.24 us
    ppermute x1, starting transfers between devices, on_device(): lax.ppermute(same[H // 2:], 'term', [(i, (i - 1) % n_term) for i in range...  4.92 us
    ppermute x1, starting transfers between devices, on_device(): lax.ppermute(turned, 'sec', [(i, i + 1) if i % 2 else (i, i - 1) for i in...  4.79 us
    pallas_call x1, Pallas kernels, on_device(): pl.pallas_call(next_products, out_shape=[jax.ShapeDtypeStruct((G, H * M,...  3.44 us
  transfers between devices with their start and end apart: 8, of which 3 were waited for; matrix products, arithmetic and copies ran while one was open for 0% of the time, Pallas kernels for 8%

profile of v13, /device:TPU:4, one launch (start us, length us, event | category | flops | bytes accessed | tf_op | source)
XLA Modules:
  0.0 103.4 jit_solution(9826620667976448699)
XLA Ops:
  0.0 0.0 copy-start.4
  0.0 1.8 %shard_map.65.refs_2_.refs_3_ = bf16[1024,128]{1,0:T(8,128)(2,1)} custom-call(bf16[1,64,128,128]{3,2,1,0:T(8,128)(2,1)} %psi_ref.1), custom_call_target="tpu_custom_call" | custom-call | tf_op jit(solution)/shard_map/pallas_call | solution.py:166
  1.8 4.8 %collective-permute-start.1 = (bf16[1024,128]{1,0:T(8,128)(2,1)}, bf16[1024,128]{1,0:T(8,128)(2,1)S(1)}, u32[]{:S(2)}, u32[]{:S(2)}) collective-permute-start(bf16[1024,128]{1,0:T(8,128)(2,1)} %shard_map.65.refs_2_.refs_3_), channel_id=1, source_target_pairs={{8,16},{16,8},{24,32},{32,24},{40,48},{48,40},{56,64},{64,56},{72,... | collective-permute-start | bytes 786440 | tf_op jit(solution)/shard_map/ppermute | solution.py:175
  6.6 0.0 copy-done.4
  6.6 11.7 %collective-permute-start = (bf16[1,128,128]{2,1,0:T(8,128)(2,1)S(1)}, bf16[1,128,128]{2,1,0:T(8,128)(2,1)S(1)}, u32[]{:S(2)}, u32[]{:S(2)}) collective-permute-start(bf16[1,128,128]{2,1,0:T(8,128)(2,1)S(1)} %bitcast.13), channel_id=1, source_target_pairs={{0,352},{1,480},{2,224},{3,96},{4,112},{5,240},{6,496},{7,368},{8,... | collective-permute-start | bytes 98312 | tf_op jit(solution)/shard_map/ppermute | solution.py:157
  18.3 1.8 %shard_map.66 = bf16[656,128]{1,0:T(8,128)(2,1)} custom-call(s32[1,5]{1,0:T(1,128)} %shift_ref.1, bf16[640,128]{1,0:T(8,128)(2,1)} %bitcast.11, f32[5,64,64]{2,1,0:T(8,128)} %bitcast.12, s32[64,64]{1,0:T(8,128)} %allowed_ref.5), custom_call_target="tpu_custom_call" | custom-call | tf_op jit(solution)/shard_map/pallas_call | solution.py:158
  20.1 0.0 copy-start.3
  20.1 0.0 collective-permute-done.block_ref
  20.1 1.1 %shard_map.64 = bf16[32,128,128]{2,1,0:T(8,128)(2,1)} custom-call(bf16[1,128,128]{2,1,0:T(8,128)(2,1)S(1)} %collective-permute-done.block_ref), custom_call_target="tpu_custom_call" | custom-call | flops 209715200 | bytes 1048576 | tf_op jit(solution)/shard_map/pallas_call | solution.py:176
  21.3 0.0 copy-start
  21.3 0.0 collective-permute-done.1.refs_1_.refs_2_
  21.3 7.2 %all-to-all-start = ((bf16[32,128,128]{2,1,0:T(8,128)(2,1)}), bf16[32,128,128]{2,1,0:T(8,128)(2,1)S(1)}, u32[]{:S(2)}, u32[]{:S(2)}) async-start(bf16[32,128,128]{2,1,0:T(8,128)(2,1)} %shard_map.64), calls=%async_computation | async-start | bytes 2097152 | tf_op jit(solution)/shard_map/all_to_all | solution.py:185
  28.5 0.0 copy-done.3
  28.5 21.5 %all-gather = bf16[2624,128]{1,0:T(8,128)(2,1)S(1)} all-gather(bf16[656,128]{1,0:T(8,128)(2,1)S(1)} %copy-done.3), channel_id=2, replica_groups={{0,2,4,6},{1,3,5,7},{8,10,12,14},{9,11,13,15},{16,18,20,22},{17,19,21,2..., dimensions={0}, use_global_device_ids=true | all-gather | bytes 839680 | tf_op jit(solution)/shard_map/all_gather | solution.py:186
  50.1 2.1 %collective-permute-start.2 = (bf16[2,656,128]{2,1,0:T(8,128)(2,1)S(1)}, bf16[2,656,128]{2,1,0:T(8,128)(2,1)S(1)}, u32[]{:S(2)}, u32[]{:S(2)}) collective-permute-start(bf16[2,656,128]{2,1,0:T(8,128)(2,1)S(1)} %bitcast.10), channel_id=1, source_target_pairs={{0,1},{1,2},{2,3},{3,4},{4,5},{5,6},{6,7},{7,0},{8,9},{9,10},{10,1... | collective-permute-start | bytes 1007624 | tf_op jit(solution)/shard_map/ppermute | solution.py:191
  52.2 4.9 %collective-permute-start.3 = (bf16[2,656,128]{2,1,0:T(8,128)(2,1)S(1)}, bf16[2,656,128]{2,1,0:T(8,128)(2,1)S(1)}, u32[]{:S(2)}, u32[]{:S(2)}) collective-permute-start(bf16[2,656,128]{2,1,0:T(8,128)(2,1)S(1)} %bitcast.9), channel_id=1, source_target_pairs={{0,7},{1,0},{2,1},{3,2},{4,3},{5,4},{6,5},{7,6},{8,15},{9,8},{10,9... | collective-permute-start | bytes 1007624 | tf_op jit(solution)/shard_map/ppermute | solution.py:192
  57.2 0.0 copy-done
  57.2 1.9 %collective-permute-start.4 = (bf16[1024,128]{1,0:T(8,128)(2,1)S(1)}, bf16[1024,128]{1,0:T(8,128)(2,1)S(1)}, u32[]{:S(2)}, u32[]{:S(2)}) collective-permute-start(bf16[1024,128]{1,0:T(8,128)(2,1)S(1)} %copy-done), channel_id=1, source_target_pairs={{0,8},{8,0},{16,24},{24,16},{32,40},{40,32},{48,56},{56,48},{64,72... | collective-permute-start | bytes 786440 | tf_op jit(solution)/shard_map/ppermute | solution.py:190
  59.1 1.5 %collective-permute-done.4.refs_3_.refs_4_ = bf16[1024,128]{1,0:T(8,128)(2,1)S(1)} collective-permute-done((bf16[1024,128]{1,0:T(8,128)(2,1)S(1)}, bf16[1024,128]{1,0:T(8,128)(2,1)S(1)}, u32[]{:S(2)}, u32[]{:S(2)}) %collective-permute-start.4) | collective-permute-done | bytes 262176 | tf_op jit(solution)/shard_map/ppermute | solution.py:190
  60.6 2.0 %shard_map.67.refs_6_.same_ref = bf16[8,512,128]{2,1,0:T(8,128)(2,1)S(1)} custom-call(bf16[4,656,128]{2,1,0:T(8,128)(2,1)S(1)} %bitcast.8, bf16[1024,128]{1,0:T(8,128)(2,1)S(1)} %collective-permute-done.1.refs_1_.refs_2_, bf16[1024,128]{1,0:T(8,128)(2,1)S(1)} %copy-done, bf16[1024,128]{1,0:T(8,128)(2,1)S(1)} %collective-permute-done.4.refs_3_.refs_4_), custom_call_target="tpu_custom_call" | custom-call | flops 671088640 | bytes 3145728 | tf_op jit(solution)/shard_map/pallas_call | solution.py:194
  62.6 0.0 collective-permute-done.2.refs_0_
  62.6 1.0 collective-permute-done.3.refs_1_
  63.6 0.0 all-to-all-done.refs_5_
  63.6 1.9 %collective-permute-start.5 = (bf16[32,128,128]{2,1,0:T(8,128)(2,1)S(1)}, bf16[32,128,128]{2,1,0:T(8,128)(2,1)S(1)}, u32[]{:S(2)}, u32[]{:S(2)}) collective-permute-start(bf16[32,128,128]{2,1,0:T(8,128)(2,1)S(1)} %all-to-all-done.refs_5_), channel_id=1, source_target_pairs={{0,8},{8,0},{16,24},{24,16},{32,40},{40,32},{48,56},{56,48},{64,72... | collective-permute-start | bytes 3145736 | tf_op jit(solution)/shard_map/ppermute | solution.py:204
  65.6 0.0 copy-start.1
  65.6 0.7 copy-done.1
  66.3 0.0 copy-start.2
  66.3 3.4 %shard_map.68 = (bf16[8,512,128]{2,1,0:T(8,128)(2,1)S(1)}, bf16[4,128,128]{2,1,0:T(8,128)(2,1)S(1)}) custom-call(s32[64,64]{1,0:T(8,128)S(1)} %copy-done.1, bf16[2,656,128]{2,1,0:T(8,128)(2,1)S(1)} %collective-permute-done.2.refs_0_, bf16[2,656,128]{2,1,0:T(8,128)(2,1)S(1)} %collective-permute-done.3.refs_1_, ...), custom_call_target="tpu_custom_call" | custom-call | flops 469762048 | bytes 3145728 | tf_op jit(solution)/shard_map/pallas_call | solution.py:206
  69.8 0.0 collective-permute-done.5.right_ref
  69.8 0.0 copy-done.2
  69.8 2.4 %shard_map.69 = bf16[16,128,128]{2,1,0:T(8,128)(2,1)} custom-call(s32[64,64]{1,0:T(8,128)S(1)} %copy-done.2, bf16[32,128,128]{2,1,0:T(8,128)(2,1)S(1)} %collective-permute-done.5.right_ref, bf16[8,512,128]{2,1,0:T(8,128)(2,1)S(1)} %shard_map.67.refs_6_.same_ref, bf16[8,512,128]{2,1,0:T(8,128)(2,1)S(1)} %get-tuple-element.21.next_ref, ...), custom_call_target="tpu_custom_call" | custom-call | flops 469762048 | bytes 3145728 | tf_op jit(solution)/shard_map/pallas_call | solution.py:215
  72.2 12.4 %all-to-all-start.1 = ((bf16[16,128,128]{2,1,0:T(8,128)(2,1)}), bf16[16,128,128]{2,1,0:T(8,128)(2,1)S(1)}, u32[]{:S(2)}, u32[]{:S(2)}) async-start(bf16[16,128,128]{2,1,0:T(8,128)(2,1)} %shard_map.69), calls=%async_computation.1 | async-start | bytes 1048576 | tf_op jit(solution)/shard_map/all_to_all | solution.py:224
  84.6 18.0 %all-to-all-done.1 = bf16[16,128,128]{2,1,0:T(8,128)(2,1)S(1)} async-done(((bf16[16,128,128]{2,1,0:T(8,128)(2,1)}), bf16[16,128,128]{2,1,0:T(8,128)(2,1)S(1)}, u32[]{:S(2)}, u32[]{:S(2)}) %all-to-all-start.1) | async-done | bytes 524320 | tf_op jit(solution)/shard_map/all_to_all | solution.py:224
  102.6 0.7 dynamic-slice_bitcast_fusion
  (1 shorter events, 0.0 us)
Async XLA Ops:
  0.0 6.6 %copy-start.4 = (bf16[1,1,128,128]{3,2,1,0:T(8,128)(2,1)S(1)}, bf16[1,1,128,128]{3,2,1,0:T(8,128)(2,1)}, u32[]{:S(2)}) copy-start(bf16[1,1,128,128]{3,2,1,0:T(8,128)(2,1)} %param.8) | copy-start | bytes 98308
  1.8 19.5 %collective-permute-start.1 = (bf16[1024,128]{1,0:T(8,128)(2,1)}, bf16[1024,128]{1,0:T(8,128)(2,1)S(1)}, u32[]{:S(2)}, u32[]{:S(2)}) collective-permute-start(bf16[1024,128]{1,0:T(8,128)(2,1)} %shard_map.65.refs_2_.refs_3_), channel_id=1, source_target_pairs={{8,16},{16,8},{24,32},{32,24},{40,48},{48,40},{56,64},{64,56},{72,... | collective-permute-start | bytes 786440 | tf_op jit(solution)/shard_map/ppermute | solution.py:175
  6.6 13.5 %collective-permute-start = (bf16[1,128,128]{2,1,0:T(8,128)(2,1)S(1)}, bf16[1,128,128]{2,1,0:T(8,128)(2,1)S(1)}, u32[]{:S(2)}, u32[]{:S(2)}) collective-permute-start(bf16[1,128,128]{2,1,0:T(8,128)(2,1)S(1)} %bitcast.13), channel_id=1, source_target_pairs={{0,352},{1,480},{2,224},{3,96},{4,112},{5,240},{6,496},{7,368},{8,... | collective-permute-start | bytes 98312 | tf_op jit(solution)/shard_map/ppermute | solution.py:157
  20.1 8.4 %copy-start.3 = (bf16[656,128]{1,0:T(8,128)(2,1)S(1)}, bf16[656,128]{1,0:T(8,128)(2,1)}, u32[]{:S(2)}) copy-start(bf16[656,128]{1,0:T(8,128)(2,1)} %shard_map.66) | copy-start | bytes 503812
  21.3 35.9 %copy-start = (bf16[1024,128]{1,0:T(8,128)(2,1)S(1)}, bf16[1024,128]{1,0:T(8,128)(2,1)}, u32[]{:S(2)}) copy-start(bf16[1024,128]{1,0:T(8,128)(2,1)} %shard_map.65.refs_2_.refs_3_) | copy-start | bytes 786436
  21.3 42.4 %all-to-all-start = ((bf16[32,128,128]{2,1,0:T(8,128)(2,1)}), bf16[32,128,128]{2,1,0:T(8,128)(2,1)S(1)}, u32[]{:S(2)}, u32[]{:S(2)}) async-start(bf16[32,128,128]{2,1,0:T(8,128)(2,1)} %shard_map.64), calls=%async_computation | async-start | bytes 2097152 | tf_op jit(solution)/shard_map/all_to_all | solution.py:185
  50.1 12.5 %collective-permute-start.2 = (bf16[2,656,128]{2,1,0:T(8,128)(2,1)S(1)}, bf16[2,656,128]{2,1,0:T(8,128)(2,1)S(1)}, u32[]{:S(2)}, u32[]{:S(2)}) collective-permute-start(bf16[2,656,128]{2,1,0:T(8,128)(2,1)S(1)} %bitcast.10), channel_id=1, source_target_pairs={{0,1},{1,2},{2,3},{3,4},{4,5},{5,6},{6,7},{7,0},{8,9},{9,10},{10,1... | collective-permute-start | bytes 1007624 | tf_op jit(solution)/shard_map/ppermute | solution.py:191
  52.2 11.4 %collective-permute-start.3 = (bf16[2,656,128]{2,1,0:T(8,128)(2,1)S(1)}, bf16[2,656,128]{2,1,0:T(8,128)(2,1)S(1)}, u32[]{:S(2)}, u32[]{:S(2)}) collective-permute-start(bf16[2,656,128]{2,1,0:T(8,128)(2,1)S(1)} %bitcast.9), channel_id=1, source_target_pairs={{0,7},{1,0},{2,1},{3,2},{4,3},{5,4},{6,5},{7,6},{8,15},{9,8},{10,9... | collective-permute-start | bytes 1007624 | tf_op jit(solution)/shard_map/ppermute | solution.py:192
  57.2 3.4 %collective-permute-start.4 = (bf16[1024,128]{1,0:T(8,128)(2,1)S(1)}, bf16[1024,128]{1,0:T(8,128)(2,1)S(1)}, u32[]{:S(2)}, u32[]{:S(2)}) collective-permute-start(bf16[1024,128]{1,0:T(8,128)(2,1)S(1)} %copy-done), channel_id=1, source_target_pairs={{0,8},{8,0},{16,24},{24,16},{32,40},{40,32},{48,56},{56,48},{64,72... | collective-permute-start | bytes 786440 | tf_op jit(solution)/shard_map/ppermute | solution.py:190
  63.6 6.1 %collective-permute-start.5 = (bf16[32,128,128]{2,1,0:T(8,128)(2,1)S(1)}, bf16[32,128,128]{2,1,0:T(8,128)(2,1)S(1)}, u32[]{:S(2)}, u32[]{:S(2)}) collective-permute-start(bf16[32,128,128]{2,1,0:T(8,128)(2,1)S(1)} %all-to-all-done.refs_5_), channel_id=1, source_target_pairs={{0,8},{8,0},{16,24},{24,16},{32,40},{40,32},{48,56},{56,48},{64,72... | collective-permute-start | bytes 3145736 | tf_op jit(solution)/shard_map/ppermute | solution.py:204
  65.6 0.8 copy-start.1
  66.3 3.5 %copy-start.2 = (s32[64,64]{1,0:T(8,128)S(1)}, s32[64,64]{1,0:T(8,128)}, u32[]{:S(2)}) copy-start(s32[64,64]{1,0:T(8,128)} %allowed_ref.5) | copy-start | bytes 49156
  72.2 30.5 %all-to-all-start.1 = ((bf16[16,128,128]{2,1,0:T(8,128)(2,1)}), bf16[16,128,128]{2,1,0:T(8,128)(2,1)S(1)}, u32[]{:S(2)}, u32[]{:S(2)}) async-start(bf16[16,128,128]{2,1,0:T(8,128)(2,1)} %shard_map.69), calls=%async_computation.1 | async-start | bytes 1048576 | tf_op jit(solution)/shard_map/all_to_all | solution.py:224

commit v14 on v13

--- a/solution.py
+++ b/solution.py
@@ -20,6 +20,7 @@
 SMEM = pl.BlockSpec(memory_space=pltpu.SMEM)
 PARAMS = pltpu.CompilerParams(vmem_limit_bytes=16 * 1024 * 1024)
 FIRST = pltpu.CompilerParams(vmem_limit_bytes=56 * 1024 * 1024)
+WEIGHTS = (4000, 8000)
 SPREAD_COST = 100
 
 
@@ -43,11 +44,12 @@
     table_ref[...] = jnp.zeros_like(table_ref)
     lane = lax.broadcasted_iota(jnp.int32, (1, M), 1)
     shifts = jnp.zeros((1, M), F32)
+    result = allowed_ref[pl.ds(s, 1), :].astype(F32)
     for c in range(LB):
         shift = shift_ref[0, c]
         source = s + shift
         inside = jnp.logical_and(source >= 0, source < n_sec).astype(F32)
-        kept = allowed_ref[pl.ds(jnp.clip(source, 0, n_sec - 1), 1), :].astype(F32) * inside
+        kept = allowed_ref[pl.ds(jnp.clip(source, 0, n_sec - 1), 1), :].astype(F32) * inside * result
         factor = coupling_ref[c, pl.ds(s, 1), :] * kept
         high = factor.astype(BF16).astype(F32)
         middle = (factor - high).astype(BF16).astype(F32)
@@ -105,34 +107,20 @@
                 out_ref[start // M + h, w * M : (w + 1) * M, :] = totals[h].astype(BF16)
 
 
-def right_sum(i, side, right_ref, same_ref, next_ref, allowed_ref):
-    s, t = lax.axis_index("sec"), lax.axis_index("term")
+def right_products(right_ref, others_ref, same_ref, next_ref, out_ref):
+    t = lax.axis_index("term")
+    core = lax.rem(lax.axis_index("sec"), 2)
     parity = lax.rem(t, 2)
-    j = 2 * i + side
-    same = jnp.concatenate([right_ref[right_chip(t, 2 * m + parity, i)] for m in range(H)], axis=1)
-    following = jnp.concatenate([right_ref[right_chip(t, 2 * m + 1 - parity, i)] for m in range(H)], axis=1)
-    total = jnp.dot(same, same_ref[j], preferred_element_type=F32)
-    total += jnp.dot(following, next_ref[j], preferred_element_type=F32)
-    return (total * allowed_ref[s, t * G + j].astype(F32)).T.astype(BF16)
-
-
-def next_products(allowed_ref, *refs):
-    left_refs, (right_ref, same_ref, next_ref, out_ref, psi_ref) = refs[:5], refs[5:]
-    left_products(2, *left_refs, next_ref, psi_ref)
-    core = lax.rem(lax.axis_index("sec"), 2)
-    for i in range(H):
-        out_ref[i] = right_sum(i, core, right_ref, same_ref, next_ref, allowed_ref)
-
-
-def other_products(allowed_ref, right_ref, same_ref, next_ref, own_ref, out_ref):
-    core = lax.rem(lax.axis_index("sec"), 2)
-    for i in range(H):
-        value = right_sum(i, 1 - core, right_ref, same_ref, next_ref, allowed_ref)
-        out_ref[2 * i + 1 - core] = value
-        out_ref[G + 2 * i + 1 - core] = value
-        mine = own_ref[i]
-        out_ref[2 * i + core] = mine
-        out_ref[G + 2 * i + core] = mine
+    for ref, side in ((right_ref, core), (others_ref, 1 - core)):
+        for i in range(H):
+            j = 2 * i + side
+            same = jnp.concatenate([ref[right_chip(t, 2 * m + parity, i)] for m in range(H)], axis=1)
+            following = jnp.concatenate([ref[right_chip(t, 2 * m + 1 - parity, i)] for m in range(H)], axis=1)
+            total = jnp.dot(same, same_ref[j], preferred_element_type=F32)
+            total += jnp.dot(following, next_ref[j], preferred_element_type=F32)
+            value = total.T.astype(BF16)
+            out_ref[j] = value
+            out_ref[G + j] = value
 
 
 def on_device(wavefunction, left_env, right_env, coupling, left_shift, allowed, *, n_sec, n_term):
@@ -191,35 +179,29 @@
     from_below = lax.ppermute(same[: H // 2], "term", [(i, (i + 1) % n_term) for i in range(n_term)])
     from_above = lax.ppermute(same[H // 2 :], "term", [(i, (i - 1) % n_term) for i in range(n_term)])
 
-    partial_same = pl.pallas_call(
-        functools.partial(left_products, 1),
-        out_shape=jax.ShapeDtypeStruct((G, H * M, M), BF16),
+    def left_call(weight, *slots):
+        return pl.pallas_call(
+            functools.partial(left_products, len(slots)),
+            out_shape=jax.ShapeDtypeStruct((G, H * M, M), BF16),
+            in_specs=[VMEM] * (len(slots) + 3),
+            out_specs=VMEM,
+            scratch_shapes=[pltpu.VMEM((3, G * M, M), BF16)],
+            compiler_params=PARAMS,
+            cost_estimate=pl.CostEstimate(flops=weight * M**3, bytes_accessed=3 << 20, transcendentals=0),
+        )(*slots, near, turned, inner)
+
+    partial_same = left_call(WEIGHTS[0], same)
+    right, partial_same = together(right, partial_same)
+    others = lax.ppermute(right, "sec", across)
+    partial_next = left_call(WEIGHTS[1], from_below, from_above)
+    results = pl.pallas_call(
+        right_products,
+        out_shape=jax.ShapeDtypeStruct((2 * G, M, M), BF16),
         in_specs=[VMEM] * 4,
         out_specs=VMEM,
-        scratch_shapes=[pltpu.VMEM((3, G * M, M), BF16)],
         compiler_params=PARAMS,
-        cost_estimate=pl.CostEstimate(flops=2 * 160 * M**3, bytes_accessed=3 << 20, transcendentals=0),
-    )(same, near, turned, inner)
-    from_below, from_above, partial_same, right = together(from_below, from_above, partial_same, right)
-    others = lax.ppermute(right, "sec", across)
-    cost = pl.CostEstimate(flops=2 * 112 * M**3, bytes_accessed=3 << 20, transcendentals=0)
-    partial_next, own = pl.pallas_call(
-        next_products,
-        out_shape=[jax.ShapeDtypeStruct((G, H * M, M), BF16), jax.ShapeDtypeStruct((H, M, M), BF16)],
-        in_specs=[SMEM] + [VMEM] * 7,
-        out_specs=[VMEM] * 2,
-        scratch_shapes=[pltpu.VMEM((3, G * M, M), BF16)],
-        compiler_params=PARAMS,
-        cost_estimate=cost,
-    )(allowed, from_below, from_above, near, turned, inner, right, partial_same)
-    results = pl.pallas_call(
-        other_products,
-        out_shape=jax.ShapeDtypeStruct((2 * G, M, M), BF16),
-        in_specs=[SMEM] + [VMEM] * 4,
-        out_specs=VMEM,
-        compiler_params=PARAMS,
-        cost_estimate=cost,
-    )(allowed, others, partial_same, partial_next, own)
+        cost_estimate=pl.CostEstimate(flops=2 * 64 * M**3, bytes_accessed=3 << 20, transcendentals=0),
+    )(right, others, partial_same, partial_next)
 
     received = lax.all_to_all(results, BOTH, 0, 0, axis_index_groups=exchange, tiled=True)
     A = s // G

time: 104 us -> 104 us (level)
  Pallas kernels: 12.5 us -> 10.3 us
  starting transfers between devices: 47.1 us -> 49.1 us
    ppermute x1, starting transfers between devices: 1.92 us -> 4.36 us  [on_device(): inner = lax.ppermute(turned, 'sec', across)]
    pallas_call x3, Pallas kernels: 7.82 us -> 5.58 us  [the longest x2 3.99 us: left_call(): pl.pallas_call(functools.partial(left_products, len(slots)), out_shape=ja...]
    ppermute x1, waiting for transfers between devices: 0.01 us -> 2.11 us  [on_device(): lax.ppermute(same[:H // 2], 'term', [(i, (i + 1) % n_term) for i in range...]
    ppermute x1, waiting for transfers between devices: 1.5 us -> 0.01 us  [on_device(): inner = lax.ppermute(turned, 'sec', across)]
  transfers between devices with their start and end apart: 8 -> 8, of which waited for: 3 -> 3; matrix products, arithmetic and copies ran while one was open for 0% -> 1% of each run, Pallas kernels for 8% -> 7%
where the time goes in v14:
time: 104 us; the launch traced here: 103 us
  starting transfers between devices  49.1 us (47%)
  waiting for transfers between devices  21.2 us (20%)
  blocking collectives  20.8 us (20%)
  Pallas kernels  10.3 us (10%)
  local copies, waits for them, and re-layouts  1.66 us (2%)
    all_gather x1, blocking collectives, on_device(): lax.all_gather(payload, 'term', axis_index_groups=[list(range(parity, n_t...  20.8 us
    all_to_all x1, waiting for transfers between devices, on_device(): lax.all_to_all(results, BOTH, 0, 0, axis_index_groups=exchange, tiled=True)  17.8 us
    all_to_all x1, starting transfers between devices, on_device(): lax.all_to_all(results, BOTH, 0, 0, axis_index_groups=exchange, tiled=True)  12 us
    ppermute x1, starting transfers between devices, on_device(): right = lax.ppermute(right_env[0], BOTH, spread)  11.7 us
    all_to_all x1, starting transfers between devices, on_device(): lax.all_to_all(sent, 'sec', 0, 0, axis_index_groups=by_core, tiled=True)  7.11 us
    ppermute x1, starting transfers between devices, on_device(): lax.ppermute(same[H // 2:], 'term', [(i, (i - 1) % n_term) for i in range...  5.13 us
    ppermute x1, starting transfers between devices, on_device(): lax.ppermute(turned, 'sec', [(i, i + 1) if i % 2 else (i, i - 1) for i in...  4.92 us
    ppermute x1, starting transfers between devices, on_device(): inner = lax.ppermute(turned, 'sec', across)  4.36 us
  transfers between devices with their start and end apart: 8, of which 3 were waited for; matrix products, arithmetic and copies ran while one was open for 1% of the time, Pallas kernels for 7%

profile of v14, /device:TPU:4, one launch (start us, length us, event | category | flops | bytes accessed | tf_op | source)
XLA Modules:
  0.0 103.2 jit_solution(5322867050153591975)
XLA Ops:
  0.0 0.0 copy-start.2
  0.0 1.8 %shard_map.65.refs_2_.refs_3_ = bf16[1024,128]{1,0:T(8,128)(2,1)} custom-call(bf16[1,64,128,128]{3,2,1,0:T(8,128)(2,1)} %psi_ref.1), custom_call_target="tpu_custom_call" | custom-call | tf_op jit(solution)/shard_map/pallas_call | solution.py:154
  1.8 0.0 copy-start
  1.8 4.9 %collective-permute-start.1 = (bf16[1024,128]{1,0:T(8,128)(2,1)}, bf16[1024,128]{1,0:T(8,128)(2,1)S(1)}, u32[]{:S(2)}, u32[]{:S(2)}) collective-permute-start(bf16[1024,128]{1,0:T(8,128)(2,1)} %shard_map.65.refs_2_.refs_3_), channel_id=1, source_target_pairs={{8,16},{16,8},{24,32},{32,24},{40,48},{48,40},{56,64},{64,56},{72,... | collective-permute-start | bytes 786440 | tf_op jit(solution)/shard_map/ppermute | solution.py:163
  6.7 0.0 copy-done.2
  6.7 11.7 %collective-permute-start = (bf16[1,128,128]{2,1,0:T(8,128)(2,1)S(1)}, bf16[1,128,128]{2,1,0:T(8,128)(2,1)S(1)}, u32[]{:S(2)}, u32[]{:S(2)}) collective-permute-start(bf16[1,128,128]{2,1,0:T(8,128)(2,1)S(1)} %bitcast.11), channel_id=1, source_target_pairs={{0,352},{1,480},{2,224},{3,96},{4,112},{5,240},{6,496},{7,368},{8,... | collective-permute-start | bytes 98312 | tf_op jit(solution)/shard_map/ppermute | solution.py:145
  18.5 1.8 %shard_map.66 = bf16[656,128]{1,0:T(8,128)(2,1)} custom-call(s32[1,5]{1,0:T(1,128)} %shift_ref.1, bf16[640,128]{1,0:T(8,128)(2,1)} %bitcast.9, f32[5,64,64]{2,1,0:T(8,128)} %bitcast.10, s32[64,64]{1,0:T(8,128)} %allowed_ref.1), custom_call_target="tpu_custom_call" | custom-call | tf_op jit(solution)/shard_map/pallas_call | solution.py:146
  20.3 0.0 copy-start.1
  20.3 0.0 collective-permute-done.block_ref
  20.3 1.1 %shard_map.64 = bf16[32,128,128]{2,1,0:T(8,128)(2,1)} custom-call(bf16[1,128,128]{2,1,0:T(8,128)(2,1)S(1)} %collective-permute-done.block_ref), custom_call_target="tpu_custom_call" | custom-call | flops 209715200 | bytes 1048576 | tf_op jit(solution)/shard_map/pallas_call | solution.py:164
  21.4 0.0 collective-permute-done.1.refs_1_.refs_2_
  21.4 7.1 %all-to-all-start = ((bf16[32,128,128]{2,1,0:T(8,128)(2,1)}), bf16[32,128,128]{2,1,0:T(8,128)(2,1)S(1)}, u32[]{:S(2)}, u32[]{:S(2)}) async-start(bf16[32,128,128]{2,1,0:T(8,128)(2,1)} %shard_map.64), calls=%async_computation | async-start | bytes 2097152 | tf_op jit(solution)/shard_map/all_to_all | solution.py:173
  28.5 0.0 copy-done
  28.5 4.4 %collective-permute-start.2 = (bf16[1024,128]{1,0:T(8,128)(2,1)S(1)}, bf16[1024,128]{1,0:T(8,128)(2,1)S(1)}, u32[]{:S(2)}, u32[]{:S(2)}) collective-permute-start(bf16[1024,128]{1,0:T(8,128)(2,1)S(1)} %copy-done), channel_id=1, source_target_pairs={{0,8},{8,0},{16,24},{24,16},{32,40},{40,32},{48,56},{56,48},{64,72... | collective-permute-start | bytes 786440 | tf_op jit(solution)/shard_map/ppermute | solution.py:178
  32.9 0.0 copy-done.1
  32.9 20.8 %all-gather = bf16[2624,128]{1,0:T(8,128)(2,1)S(1)} all-gather(bf16[656,128]{1,0:T(8,128)(2,1)S(1)} %copy-done.1), channel_id=2, replica_groups={{0,2,4,6},{1,3,5,7},{8,10,12,14},{9,11,13,15},{16,18,20,22},{17,19,21,2..., dimensions={0}, use_global_device_ids=true | all-gather | bytes 839680 | tf_op jit(solution)/shard_map/all_gather | solution.py:174
  53.7 0.9 fusion
  54.6 1.9 %collective-permute-start.4 = (bf16[2,656,128]{2,1,0:T(8,128)(2,1)}, bf16[2,656,128]{2,1,0:T(8,128)(2,1)S(1)}, u32[]{:S(2)}, u32[]{:S(2)}) collective-permute-start(bf16[2,656,128]{2,1,0:T(8,128)(2,1)} %bitcast.4), channel_id=1, source_target_pairs={{0,1},{1,2},{2,3},{3,4},{4,5},{5,6},{6,7},{7,0},{8,9},{9,10},{10,1... | collective-permute-start | bytes 1007624 | tf_op jit(solution)/shard_map/ppermute | solution.py:179
  56.5 5.1 %collective-permute-start.5 = (bf16[2,656,128]{2,1,0:T(8,128)(2,1)}, bf16[2,656,128]{2,1,0:T(8,128)(2,1)S(1)}, u32[]{:S(2)}, u32[]{:S(2)}) collective-permute-start(bf16[2,656,128]{2,1,0:T(8,128)(2,1)} %bitcast.5), channel_id=1, source_target_pairs={{0,7},{1,0},{2,1},{3,2},{4,3},{5,4},{6,5},{7,6},{8,15},{9,8},{10,9... | collective-permute-start | bytes 1007624 | tf_op jit(solution)/shard_map/ppermute | solution.py:180
  61.7 0.0 collective-permute-done.2.refs_3_.refs_4_
  61.7 2.0 %shard_map.67.same_ref = bf16[8,512,128]{2,1,0:T(8,128)(2,1)S(1)} custom-call(bf16[4,656,128]{2,1,0:T(8,128)(2,1)S(1)} %bitcast.8, bf16[1024,128]{1,0:T(8,128)(2,1)S(1)} %collective-permute-done.1.refs_1_.refs_2_, bf16[1024,128]{1,0:T(8,128)(2,1)S(1)} %copy-done, bf16[1024,128]{1,0:T(8,128)(2,1)S(1)} %collective-permute-done.2.refs_3_.refs_4_), custom_call_target="tpu_custom_call" | custom-call | flops 8388608000 | bytes 3145728 | tf_op jit(solution)/shard_map/pallas_call | solution.py:183
  63.7 0.0 all-to-all-done.right_ref
  63.7 1.9 %collective-permute-start.3 = (bf16[32,128,128]{2,1,0:T(8,128)(2,1)S(1)}, bf16[32,128,128]{2,1,0:T(8,128)(2,1)S(1)}, u32[]{:S(2)}, u32[]{:S(2)}) collective-permute-start(bf16[32,128,128]{2,1,0:T(8,128)(2,1)S(1)} %all-to-all-done.right_ref), channel_id=1, source_target_pairs={{0,8},{8,0},{16,24},{24,16},{32,40},{40,32},{48,56},{56,48},{64,72... | collective-permute-start | bytes 3145736 | tf_op jit(solution)/shard_map/ppermute | solution.py:195
  65.6 2.1 %collective-permute-done.4.refs_0_ = bf16[2,656,128]{2,1,0:T(8,128)(2,1)S(1)} collective-permute-done((bf16[2,656,128]{2,1,0:T(8,128)(2,1)}, bf16[2,656,128]{2,1,0:T(8,128)(2,1)S(1)}, u32[]{:S(2)}, u32[]{:S(2)}) %collective-permute-start.4) | collective-permute-done | bytes 335904 | tf_op jit(solution)/shard_map/ppermute | solution.py:179
  67.7 1.3 %collective-permute-done.5.refs_1_ = bf16[2,656,128]{2,1,0:T(8,128)(2,1)S(1)} collective-permute-done((bf16[2,656,128]{2,1,0:T(8,128)(2,1)}, bf16[2,656,128]{2,1,0:T(8,128)(2,1)S(1)}, u32[]{:S(2)}, u32[]{:S(2)}) %collective-permute-start.5) | collective-permute-done | bytes 335904 | tf_op jit(solution)/shard_map/ppermute | solution.py:180
  69.0 2.0 %shard_map.68.next_ref = bf16[8,512,128]{2,1,0:T(8,128)(2,1)S(1)} custom-call(bf16[2,656,128]{2,1,0:T(8,128)(2,1)S(1)} %collective-permute-done.4.refs_0_, bf16[2,656,128]{2,1,0:T(8,128)(2,1)S(1)} %collective-permute-done.5.refs_1_, bf16[1024,128]{1,0:T(8,128)(2,1)S(1)} %collective-permute-done.1.refs_1_.refs_2_, bf16[1024,128]{1,0:T(8,128)(2,1)S(1)} %copy-done, ...), custom_call_target="tpu_custom_call" | custom-call | flops 16777216000 | bytes 3145728 | tf_op jit(solution)/shard_map/pallas_call | solution.py:183
  71.0 0.0 collective-permute-done.3.others_ref
  71.0 1.6 %shard_map.69 = bf16[16,128,128]{2,1,0:T(8,128)(2,1)} custom-call(bf16[32,128,128]{2,1,0:T(8,128)(2,1)S(1)} %all-to-all-done.right_ref, bf16[32,128,128]{2,1,0:T(8,128)(2,1)S(1)} %collective-permute-done.3.others_ref, bf16[8,512,128]{2,1,0:T(8,128)(2,1)S(1)} %shard_map.67.same_ref, bf16[8,512,128]{2,1,0:T(8,128)(2,1)S(1)} %shard_map.68.next_ref), custom_call_target="tpu_custom_call" | custom-call | flops 268435456 | bytes 3145728 | tf_op jit(solution)/shard_map/pallas_call | solution.py:197
  72.6 12.0 %all-to-all-start.1 = ((bf16[16,128,128]{2,1,0:T(8,128)(2,1)}), bf16[16,128,128]{2,1,0:T(8,128)(2,1)S(1)}, u32[]{:S(2)}, u32[]{:S(2)}) async-start(bf16[16,128,128]{2,1,0:T(8,128)(2,1)} %shard_map.69), calls=%async_computation.1 | async-start | bytes 1048576 | tf_op jit(solution)/shard_map/all_to_all | solution.py:206
  84.7 17.8 %all-to-all-done.1 = bf16[16,128,128]{2,1,0:T(8,128)(2,1)S(1)} async-done(((bf16[16,128,128]{2,1,0:T(8,128)(2,1)}), bf16[16,128,128]{2,1,0:T(8,128)(2,1)S(1)}, u32[]{:S(2)}, u32[]{:S(2)}) %all-to-all-start.1) | async-done | bytes 524320 | tf_op jit(solution)/shard_map/all_to_all | solution.py:206
  102.5 0.7 dynamic-slice_bitcast_fusion
Async XLA Ops:
  0.0 6.7 %copy-start.2 = (bf16[1,1,128,128]{3,2,1,0:T(8,128)(2,1)S(1)}, bf16[1,1,128,128]{3,2,1,0:T(8,128)(2,1)}, u32[]{:S(2)}) copy-start(bf16[1,1,128,128]{3,2,1,0:T(8,128)(2,1)} %param.8) | copy-start | bytes 98308
  1.8 26.7 %copy-start = (bf16[1024,128]{1,0:T(8,128)(2,1)S(1)}, bf16[1024,128]{1,0:T(8,128)(2,1)}, u32[]{:S(2)}) copy-start(bf16[1024,128]{1,0:T(8,128)(2,1)} %shard_map.65.refs_2_.refs_3_) | copy-start | bytes 786436
  1.8 19.6 %collective-permute-start.1 = (bf16[1024,128]{1,0:T(8,128)(2,1)}, bf16[1024,128]{1,0:T(8,128)(2,1)S(1)}, u32[]{:S(2)}, u32[]{:S(2)}) collective-permute-start(bf16[1024,128]{1,0:T(8,128)(2,1)} %shard_map.65.refs_2_.refs_3_), channel_id=1, source_target_pairs={{8,16},{16,8},{24,32},{32,24},{40,48},{48,40},{56,64},{64,56},{72,... | collective-permute-start | bytes 786440 | tf_op jit(solution)/shard_map/ppermute | solution.py:163
  6.7 13.5 %collective-permute-start = (bf16[1,128,128]{2,1,0:T(8,128)(2,1)S(1)}, bf16[1,128,128]{2,1,0:T(8,128)(2,1)S(1)}, u32[]{:S(2)}, u32[]{:S(2)}) collective-permute-start(bf16[1,128,128]{2,1,0:T(8,128)(2,1)S(1)} %bitcast.11), channel_id=1, source_target_pairs={{0,352},{1,480},{2,224},{3,96},{4,112},{5,240},{6,496},{7,368},{8,... | collective-permute-start | bytes 98312 | tf_op jit(solution)/shard_map/ppermute | solution.py:145
  20.3 12.6 %copy-start.1 = (bf16[656,128]{1,0:T(8,128)(2,1)S(1)}, bf16[656,128]{1,0:T(8,128)(2,1)}, u32[]{:S(2)}) copy-start(bf16[656,128]{1,0:T(8,128)(2,1)} %shard_map.66) | copy-start | bytes 503812
  21.4 42.3 %all-to-all-start = ((bf16[32,128,128]{2,1,0:T(8,128)(2,1)}), bf16[32,128,128]{2,1,0:T(8,128)(2,1)S(1)}, u32[]{:S(2)}, u32[]{:S(2)}) async-start(bf16[32,128,128]{2,1,0:T(8,128)(2,1)} %shard_map.64), calls=%async_computation | async-start | bytes 2097152 | tf_op jit(solution)/shard_map/all_to_all | solution.py:173
  28.5 33.2 %collective-permute-start.2 = (bf16[1024,128]{1,0:T(8,128)(2,1)S(1)}, bf16[1024,128]{1,0:T(8,128)(2,1)S(1)}, u32[]{:S(2)}, u32[]{:S(2)}) collective-permute-start(bf16[1024,128]{1,0:T(8,128)(2,1)S(1)} %copy-done), channel_id=1, source_target_pairs={{0,8},{8,0},{16,24},{24,16},{32,40},{40,32},{48,56},{56,48},{64,72... | collective-permute-start | bytes 786440 | tf_op jit(solution)/shard_map/ppermute | solution.py:178
  54.6 13.1 %collective-permute-start.4 = (bf16[2,656,128]{2,1,0:T(8,128)(2,1)}, bf16[2,656,128]{2,1,0:T(8,128)(2,1)S(1)}, u32[]{:S(2)}, u32[]{:S(2)}) collective-permute-start(bf16[2,656,128]{2,1,0:T(8,128)(2,1)} %bitcast.4), channel_id=1, source_target_pairs={{0,1},{1,2},{2,3},{3,4},{4,5},{5,6},{6,7},{7,0},{8,9},{9,10},{10,1... | collective-permute-start | bytes 1007624 | tf_op jit(solution)/shard_map/ppermute | solution.py:179
  56.5 12.5 %collective-permute-start.5 = (bf16[2,656,128]{2,1,0:T(8,128)(2,1)}, bf16[2,656,128]{2,1,0:T(8,128)(2,1)S(1)}, u32[]{:S(2)}, u32[]{:S(2)}) collective-permute-start(bf16[2,656,128]{2,1,0:T(8,128)(2,1)} %bitcast.5), channel_id=1, source_target_pairs={{0,7},{1,0},{2,1},{3,2},{4,3},{5,4},{6,5},{7,6},{8,15},{9,8},{10,9... | collective-permute-start | bytes 1007624 | tf_op jit(solution)/shard_map/ppermute | solution.py:180
  63.7 7.3 %collective-permute-start.3 = (bf16[32,128,128]{2,1,0:T(8,128)(2,1)S(1)}, bf16[32,128,128]{2,1,0:T(8,128)(2,1)S(1)}, u32[]{:S(2)}, u32[]{:S(2)}) collective-permute-start(bf16[32,128,128]{2,1,0:T(8,128)(2,1)S(1)} %all-to-all-done.right_ref), channel_id=1, source_target_pairs={{0,8},{8,0},{16,24},{24,16},{32,40},{40,32},{48,56},{56,48},{64,72... | collective-permute-start | bytes 3145736 | tf_op jit(solution)/shard_map/ppermute | solution.py:195
  72.6 29.9 %all-to-all-start.1 = ((bf16[16,128,128]{2,1,0:T(8,128)(2,1)}), bf16[16,128,128]{2,1,0:T(8,128)(2,1)S(1)}, u32[]{:S(2)}, u32[]{:S(2)}) async-start(bf16[16,128,128]{2,1,0:T(8,128)(2,1)} %shard_map.69), calls=%async_computation.1 | async-start | bytes 1048576 | tf_op jit(solution)/shard_map/all_to_all | solution.py:206

commit v15 on v14

--- a/solution.py
+++ b/solution.py
@@ -175,7 +175,8 @@
         payload, "term", axis_index_groups=[list(range(parity, n_term, 2)) for parity in range(2)]
     )
     across = [(i, i ^ 1) for i in range(n_sec)]
-    inner = lax.ppermute(turned, "sec", across)
+    same, late = together(same, turned)
+    inner = lax.ppermute(late, "sec", across)
     from_below = lax.ppermute(same[: H // 2], "term", [(i, (i + 1) % n_term) for i in range(n_term)])
     from_above = lax.ppermute(same[H // 2 :], "term", [(i, (i - 1) % n_term) for i in range(n_term)])
 

time: 104 us -> 104 us (level)
  starting transfers between devices: 49.1 us -> 46.4 us
  waiting for transfers between devices: 21.2 us -> 23.4 us
    ppermute x1, starting transfers between devices: 4.36 us -> 1.91 us  [on_device(): inner = lax.ppermute(late, 'sec', across)]
where the time goes in v15:
time: 104 us; the launch traced here: 103 us
  starting transfers between devices  46.4 us (45%)
  waiting for transfers between devices  23.4 us (22%)
  blocking collectives  21.5 us (21%)
  Pallas kernels  10.3 us (10%)
  local copies, waits for them, and re-layouts  1.66 us (2%)
    all_gather x1, blocking collectives, on_device(): lax.all_gather(payload, 'term', axis_index_groups=[list(range(parity, n_t...  21.5 us
    all_to_all x1, waiting for transfers between devices, on_device(): lax.all_to_all(results, BOTH, 0, 0, axis_index_groups=exchange, tiled=True)  18.5 us
    ppermute x1, starting transfers between devices, on_device(): right = lax.ppermute(right_env[0], BOTH, spread)  11.7 us
    all_to_all x1, starting transfers between devices, on_device(): lax.all_to_all(results, BOTH, 0, 0, axis_index_groups=exchange, tiled=True)  11.7 us
    all_to_all x1, starting transfers between devices, on_device(): lax.all_to_all(sent, 'sec', 0, 0, axis_index_groups=by_core, tiled=True)  7.11 us
    ppermute x1, starting transfers between devices, on_device(): lax.ppermute(same[H // 2:], 'term', [(i, (i - 1) % n_term) for i in range...  4.91 us
    ppermute x1, starting transfers between devices, on_device(): lax.ppermute(turned, 'sec', [(i, i + 1) if i % 2 else (i, i - 1) for i in...  4.79 us
    pallas_call x2, Pallas kernels, left_call(): pl.pallas_call(functools.partial(left_products, len(slots)), out_shape=ja...  3.98 us
  transfers between devices with their start and end apart: 8, of which 3 were waited for; matrix products, arithmetic and copies ran while one was open for 1% of the time, Pallas kernels for 7%

profile of v15, /device:TPU:4, one launch (start us, length us, event | category | flops | bytes accessed | tf_op | source)
XLA Modules:
  0.0 103.4 jit_solution(10421894628801044702)
XLA Ops:
  0.0 0.0 copy-start.2
  0.0 1.8 %shard_map.65.refs_2_.refs_3_ = bf16[1024,128]{1,0:T(8,128)(2,1)} custom-call(bf16[1,64,128,128]{3,2,1,0:T(8,128)(2,1)} %psi_ref.1), custom_call_target="tpu_custom_call" | custom-call | tf_op jit(solution)/shard_map/pallas_call | solution.py:154
  1.8 4.8 %collective-permute-start.1 = (bf16[1024,128]{1,0:T(8,128)(2,1)}, bf16[1024,128]{1,0:T(8,128)(2,1)S(1)}, u32[]{:S(2)}, u32[]{:S(2)}) collective-permute-start(bf16[1024,128]{1,0:T(8,128)(2,1)} %shard_map.65.refs_2_.refs_3_), channel_id=1, source_target_pairs={{8,16},{16,8},{24,32},{32,24},{40,48},{48,40},{56,64},{64,56},{72,... | collective-permute-start | bytes 786440 | tf_op jit(solution)/shard_map/ppermute | solution.py:163
  6.6 0.0 copy-done.2
  6.6 11.7 %collective-permute-start = (bf16[1,128,128]{2,1,0:T(8,128)(2,1)S(1)}, bf16[1,128,128]{2,1,0:T(8,128)(2,1)S(1)}, u32[]{:S(2)}, u32[]{:S(2)}) collective-permute-start(bf16[1,128,128]{2,1,0:T(8,128)(2,1)S(1)} %bitcast.10), channel_id=1, source_target_pairs={{0,352},{1,480},{2,224},{3,96},{4,112},{5,240},{6,496},{7,368},{8,... | collective-permute-start | bytes 98312 | tf_op jit(solution)/shard_map/ppermute | solution.py:145
  18.3 1.8 %shard_map.66 = bf16[656,128]{1,0:T(8,128)(2,1)} custom-call(s32[1,5]{1,0:T(1,128)} %shift_ref.1, bf16[640,128]{1,0:T(8,128)(2,1)} %bitcast.8, f32[5,64,64]{2,1,0:T(8,128)} %bitcast.9, s32[64,64]{1,0:T(8,128)} %allowed_ref.1), custom_call_target="tpu_custom_call" | custom-call | tf_op jit(solution)/shard_map/pallas_call | solution.py:146
  20.1 0.0 copy-start.1
  20.1 0.0 copy-start
  20.1 0.0 collective-permute-done.block_ref
  20.1 1.1 %shard_map.64 = bf16[32,128,128]{2,1,0:T(8,128)(2,1)} custom-call(bf16[1,128,128]{2,1,0:T(8,128)(2,1)S(1)} %collective-permute-done.block_ref), custom_call_target="tpu_custom_call" | custom-call | flops 209715200 | bytes 1048576 | tf_op jit(solution)/shard_map/pallas_call | solution.py:164
  21.2 0.0 collective-permute-done.1.refs_1_.refs_2_
  21.2 7.1 %all-to-all-start = ((bf16[32,128,128]{2,1,0:T(8,128)(2,1)}), bf16[32,128,128]{2,1,0:T(8,128)(2,1)S(1)}, u32[]{:S(2)}, u32[]{:S(2)}) async-start(bf16[32,128,128]{2,1,0:T(8,128)(2,1)} %shard_map.64), calls=%async_computation | async-start | bytes 2097152 | tf_op jit(solution)/shard_map/all_to_all | solution.py:173
  28.4 0.0 copy-done.1
  28.4 21.5 %all-gather = bf16[2624,128]{1,0:T(8,128)(2,1)S(1)} all-gather(bf16[656,128]{1,0:T(8,128)(2,1)S(1)} %copy-done.1), channel_id=2, replica_groups={{0,2,4,6},{1,3,5,7},{8,10,12,14},{9,11,13,15},{16,18,20,22},{17,19,21,2..., dimensions={0}, use_global_device_ids=true | all-gather | bytes 839680 | tf_op jit(solution)/shard_map/all_gather | solution.py:174
  49.9 0.0 copy-done
  49.9 1.9 %collective-permute-start.2 = (bf16[1024,128]{1,0:T(8,128)(2,1)S(1)}, bf16[1024,128]{1,0:T(8,128)(2,1)S(1)}, u32[]{:S(2)}, u32[]{:S(2)}) collective-permute-start(bf16[1024,128]{1,0:T(8,128)(2,1)S(1)} %copy-done), channel_id=1, source_target_pairs={{0,8},{8,0},{16,24},{24,16},{32,40},{40,32},{48,56},{56,48},{64,72... | collective-permute-start | bytes 786440 | tf_op jit(solution)/shard_map/ppermute | solution.py:179
  51.8 0.9 fusion
  52.8 2.1 %collective-permute-start.4 = (bf16[2,656,128]{2,1,0:T(8,128)(2,1)}, bf16[2,656,128]{2,1,0:T(8,128)(2,1)S(1)}, u32[]{:S(2)}, u32[]{:S(2)}) collective-permute-start(bf16[2,656,128]{2,1,0:T(8,128)(2,1)} %get-tuple-element.20), channel_id=1, source_target_pairs={{0,1},{1,2},{2,3},{3,4},{4,5},{5,6},{6,7},{7,0},{8,9},{9,10},{10,1... | collective-permute-start | bytes 1007624 | tf_op jit(solution)/shard_map/ppermute | solution.py:180
  54.9 4.9 %collective-permute-start.5 = (bf16[2,656,128]{2,1,0:T(8,128)(2,1)}, bf16[2,656,128]{2,1,0:T(8,128)(2,1)S(1)}, u32[]{:S(2)}, u32[]{:S(2)}) collective-permute-start(bf16[2,656,128]{2,1,0:T(8,128)(2,1)} %get-tuple-element.19), channel_id=1, source_target_pairs={{0,7},{1,0},{2,1},{3,2},{4,3},{5,4},{6,5},{7,6},{8,15},{9,8},{10,9... | collective-permute-start | bytes 1007624 | tf_op jit(solution)/shard_map/ppermute | solution.py:181
  59.8 0.0 collective-permute-done.2.refs_3_.refs_4_
  59.8 2.0 %shard_map.67.same_ref = bf16[8,512,128]{2,1,0:T(8,128)(2,1)S(1)} custom-call(bf16[4,656,128]{2,1,0:T(8,128)(2,1)S(1)} %bitcast.7, bf16[1024,128]{1,0:T(8,128)(2,1)S(1)} %collective-permute-done.1.refs_1_.refs_2_, bf16[1024,128]{1,0:T(8,128)(2,1)S(1)} %copy-done, bf16[1024,128]{1,0:T(8,128)(2,1)S(1)} %collective-permute-done.2.refs_3_.refs_4_), custom_call_target="tpu_custom_call" | custom-call | flops 8388608000 | bytes 3145728 | tf_op jit(solution)/shard_map/pallas_call | solution.py:184
  61.8 0.0 all-to-all-done.right_ref
  61.8 2.1 %collective-permute-start.3 = (bf16[32,128,128]{2,1,0:T(8,128)(2,1)S(1)}, bf16[32,128,128]{2,1,0:T(8,128)(2,1)S(1)}, u32[]{:S(2)}, u32[]{:S(2)}) collective-permute-start(bf16[32,128,128]{2,1,0:T(8,128)(2,1)S(1)} %all-to-all-done.right_ref), channel_id=1, source_target_pairs={{0,8},{8,0},{16,24},{24,16},{32,40},{40,32},{48,56},{56,48},{64,72... | collective-permute-start | bytes 3145736 | tf_op jit(solution)/shard_map/ppermute | solution.py:196
  63.9 2.7 %collective-permute-done.4.refs_0_ = bf16[2,656,128]{2,1,0:T(8,128)(2,1)S(1)} collective-permute-done((bf16[2,656,128]{2,1,0:T(8,128)(2,1)}, bf16[2,656,128]{2,1,0:T(8,128)(2,1)S(1)}, u32[]{:S(2)}, u32[]{:S(2)}) %collective-permute-start.4) | collective-permute-done | bytes 335904 | tf_op jit(solution)/shard_map/ppermute | solution.py:180
  66.6 2.2 %collective-permute-done.5.refs_1_ = bf16[2,656,128]{2,1,0:T(8,128)(2,1)S(1)} collective-permute-done((bf16[2,656,128]{2,1,0:T(8,128)(2,1)}, bf16[2,656,128]{2,1,0:T(8,128)(2,1)S(1)}, u32[]{:S(2)}, u32[]{:S(2)}) %collective-permute-start.5) | collective-permute-done | bytes 335904 | tf_op jit(solution)/shard_map/ppermute | solution.py:181
  68.8 2.0 %shard_map.68.next_ref = bf16[8,512,128]{2,1,0:T(8,128)(2,1)S(1)} custom-call(bf16[2,656,128]{2,1,0:T(8,128)(2,1)S(1)} %collective-permute-done.4.refs_0_, bf16[2,656,128]{2,1,0:T(8,128)(2,1)S(1)} %collective-permute-done.5.refs_1_, bf16[1024,128]{1,0:T(8,128)(2,1)S(1)} %collective-permute-done.1.refs_1_.refs_2_, bf16[1024,128]{1,0:T(8,128)(2,1)S(1)} %copy-done, ...), custom_call_target="tpu_custom_call" | custom-call | flops 16777216000 | bytes 3145728 | tf_op jit(solution)/shard_map/pallas_call | solution.py:184
  70.8 0.0 collective-permute-done.3.others_ref
  70.8 1.6 %shard_map.69 = bf16[16,128,128]{2,1,0:T(8,128)(2,1)} custom-call(bf16[32,128,128]{2,1,0:T(8,128)(2,1)S(1)} %all-to-all-done.right_ref, bf16[32,128,128]{2,1,0:T(8,128)(2,1)S(1)} %collective-permute-done.3.others_ref, bf16[8,512,128]{2,1,0:T(8,128)(2,1)S(1)} %shard_map.67.same_ref, bf16[8,512,128]{2,1,0:T(8,128)(2,1)S(1)} %shard_map.68.next_ref), custom_call_target="tpu_custom_call" | custom-call | flops 268435456 | bytes 3145728 | tf_op jit(solution)/shard_map/pallas_call | solution.py:198
  72.4 11.7 %all-to-all-start.1 = ((bf16[16,128,128]{2,1,0:T(8,128)(2,1)}), bf16[16,128,128]{2,1,0:T(8,128)(2,1)S(1)}, u32[]{:S(2)}, u32[]{:S(2)}) async-start(bf16[16,128,128]{2,1,0:T(8,128)(2,1)} %shard_map.69), calls=%async_computation.1 | async-start | bytes 1048576 | tf_op jit(solution)/shard_map/all_to_all | solution.py:207
  84.1 18.5 %all-to-all-done.1 = bf16[16,128,128]{2,1,0:T(8,128)(2,1)S(1)} async-done(((bf16[16,128,128]{2,1,0:T(8,128)(2,1)}), bf16[16,128,128]{2,1,0:T(8,128)(2,1)S(1)}, u32[]{:S(2)}, u32[]{:S(2)}) %all-to-all-start.1) | async-done | bytes 524320 | tf_op jit(solution)/shard_map/all_to_all | solution.py:207
  102.7 0.7 dynamic-slice_bitcast_fusion
Async XLA Ops:
  0.0 6.6 %copy-start.2 = (bf16[1,1,128,128]{3,2,1,0:T(8,128)(2,1)S(1)}, bf16[1,1,128,128]{3,2,1,0:T(8,128)(2,1)}, u32[]{:S(2)}) copy-start(bf16[1,1,128,128]{3,2,1,0:T(8,128)(2,1)} %param.8) | copy-start | bytes 98308
  1.8 19.4 %collective-permute-start.1 = (bf16[1024,128]{1,0:T(8,128)(2,1)}, bf16[1024,128]{1,0:T(8,128)(2,1)S(1)}, u32[]{:S(2)}, u32[]{:S(2)}) collective-permute-start(bf16[1024,128]{1,0:T(8,128)(2,1)} %shard_map.65.refs_2_.refs_3_), channel_id=1, source_target_pairs={{8,16},{16,8},{24,32},{32,24},{40,48},{48,40},{56,64},{64,56},{72,... | collective-permute-start | bytes 786440 | tf_op jit(solution)/shard_map/ppermute | solution.py:163
  6.6 13.5 %collective-permute-start = (bf16[1,128,128]{2,1,0:T(8,128)(2,1)S(1)}, bf16[1,128,128]{2,1,0:T(8,128)(2,1)S(1)}, u32[]{:S(2)}, u32[]{:S(2)}) collective-permute-start(bf16[1,128,128]{2,1,0:T(8,128)(2,1)S(1)} %bitcast.10), channel_id=1, source_target_pairs={{0,352},{1,480},{2,224},{3,96},{4,112},{5,240},{6,496},{7,368},{8,... | collective-permute-start | bytes 98312 | tf_op jit(solution)/shard_map/ppermute | solution.py:145
  20.1 8.2 %copy-start.1 = (bf16[656,128]{1,0:T(8,128)(2,1)S(1)}, bf16[656,128]{1,0:T(8,128)(2,1)}, u32[]{:S(2)}) copy-start(bf16[656,128]{1,0:T(8,128)(2,1)} %shard_map.66) | copy-start | bytes 503812
  20.1 29.8 %copy-start = (bf16[1024,128]{1,0:T(8,128)(2,1)S(1)}, bf16[1024,128]{1,0:T(8,128)(2,1)}, u32[]{:S(2)}) copy-start(bf16[1024,128]{1,0:T(8,128)(2,1)} %shard_map.65.refs_2_.refs_3_) | copy-start | bytes 786436
  21.2 40.6 %all-to-all-start = ((bf16[32,128,128]{2,1,0:T(8,128)(2,1)}), bf16[32,128,128]{2,1,0:T(8,128)(2,1)S(1)}, u32[]{:S(2)}, u32[]{:S(2)}) async-start(bf16[32,128,128]{2,1,0:T(8,128)(2,1)} %shard_map.64), calls=%async_computation | async-start | bytes 2097152 | tf_op jit(solution)/shard_map/all_to_all | solution.py:173
  49.9 9.9 %collective-permute-start.2 = (bf16[1024,128]{1,0:T(8,128)(2,1)S(1)}, bf16[1024,128]{1,0:T(8,128)(2,1)S(1)}, u32[]{:S(2)}, u32[]{:S(2)}) collective-permute-start(bf16[1024,128]{1,0:T(8,128)(2,1)S(1)} %copy-done), channel_id=1, source_target_pairs={{0,8},{8,0},{16,24},{24,16},{32,40},{40,32},{48,56},{56,48},{64,72... | collective-permute-start | bytes 786440 | tf_op jit(solution)/shard_map/ppermute | solution.py:179
  52.8 13.8 %collective-permute-start.4 = (bf16[2,656,128]{2,1,0:T(8,128)(2,1)}, bf16[2,656,128]{2,1,0:T(8,128)(2,1)S(1)}, u32[]{:S(2)}, u32[]{:S(2)}) collective-permute-start(bf16[2,656,128]{2,1,0:T(8,128)(2,1)} %get-tuple-element.20), channel_id=1, source_target_pairs={{0,1},{1,2},{2,3},{3,4},{4,5},{5,6},{6,7},{7,0},{8,9},{9,10},{10,1... | collective-permute-start | bytes 1007624 | tf_op jit(solution)/shard_map/ppermute | solution.py:180
  54.9 13.9 %collective-permute-start.5 = (bf16[2,656,128]{2,1,0:T(8,128)(2,1)}, bf16[2,656,128]{2,1,0:T(8,128)(2,1)S(1)}, u32[]{:S(2)}, u32[]{:S(2)}) collective-permute-start(bf16[2,656,128]{2,1,0:T(8,128)(2,1)} %get-tuple-element.19), channel_id=1, source_target_pairs={{0,7},{1,0},{2,1},{3,2},{4,3},{5,4},{6,5},{7,6},{8,15},{9,8},{10,9... | collective-permute-start | bytes 1007624 | tf_op jit(solution)/shard_map/ppermute | solution.py:181
  61.8 9.0 %collective-permute-start.3 = (bf16[32,128,128]{2,1,0:T(8,128)(2,1)S(1)}, bf16[32,128,128]{2,1,0:T(8,128)(2,1)S(1)}, u32[]{:S(2)}, u32[]{:S(2)}) collective-permute-start(bf16[32,128,128]{2,1,0:T(8,128)(2,1)S(1)} %all-to-all-done.right_ref), channel_id=1, source_target_pairs={{0,8},{8,0},{16,24},{24,16},{32,40},{40,32},{48,56},{56,48},{64,72... | collective-permute-start | bytes 3145736 | tf_op jit(solution)/shard_map/ppermute | solution.py:196
  72.4 30.2 %all-to-all-start.1 = ((bf16[16,128,128]{2,1,0:T(8,128)(2,1)}), bf16[16,128,128]{2,1,0:T(8,128)(2,1)S(1)}, u32[]{:S(2)}, u32[]{:S(2)}) async-start(bf16[16,128,128]{2,1,0:T(8,128)(2,1)} %shard_map.69), calls=%async_computation.1 | async-start | bytes 1048576 | tf_op jit(solution)/shard_map/all_to_all | solution.py:207
